TPU v7x, 32 devices: a whole 2x2x4 slice. The times are simulated.
32 devices in a mesh: fsdp: 8 (over z, x), expert: 4 (over y, core).
Axes of the slice: x: 2, y: 2, z: 4, core: 2. Of those that a mesh axis runs over, the one named last changes fastest.
Arguments:
- tokens: bfloat16 [512, 3072], P('expert'), may hold values from -6 to 6
- cotangent: bfloat16 [512, 3072], P('expert'), may hold values from -6 to 6
- expert_ids: int32 [512, 4], P('expert'), may hold values from 0 to 15, all different within a row; in each aligned block of 128 rows (0 to 127, 128 to 255, ...) at most 40 rows name the same one
- gate_values: bfloat16 [512, 4], P('expert'), may hold values from 0.049804688 to 0.5
- w_in: bfloat16 [3072, 16, 6144], P(None, 'expert', 'fsdp'), may hold values from -0.109375 to 0.109375
- w_out: bfloat16 [6144, 16, 3072], P('fsdp', 'expert'), may hold values from -0.078125 to 0.078125
Outputs:
- grad_tokens: bfloat16 [512, 3072], P('expert')
- grad_gates: bfloat16 [512, 4], P('expert')
- grad_w_in: bfloat16 [3072, 16, 6144], P(None, 'expert', 'fsdp')
- grad_w_out: bfloat16 [6144, 16, 3072], P('fsdp', 'expert')
Inputs may be any that keep to these rules, and one draw needn't show every extreme that they name: `expert_ids`: in each aligned block of 128 rows (the rows of one index of the expert axis) the 4 entries of a row differ, no expert is named by more than 40 rows, a bound that some block reaches.
All inputs are finite; a program needn't handle non-finite values.
Results may differ from a plain program's by a relative error of at most 0.0049.
Values may be sent and summed in bfloat16 or wider, within the bound.
No kernel may reach another device: no remote copies, remote signals or barrier semaphores. Data moves between devices by JAX's collectives and lax.ppermute only.
A program may use at most 192 MiB of HBM per device.

v0:
```python
import jax
import jax.numpy as jnp
from jax import lax
from jax.sharding import PartitionSpec as P

EXPERTS = 16
CAP = 40


def slot_targets(expert_ids):
    flat = expert_ids.reshape(-1)
    table = (flat[:, None] == jnp.arange(EXPERTS, dtype=jnp.int32)[None, :]).astype(jnp.int32)
    earlier = jnp.cumsum(table, axis=0) - table
    position = jnp.sum(earlier * table, axis=1)
    return flat * CAP + position


def fill_slots(rows, target):
    holder = jnp.zeros((EXPERTS * CAP,) + rows.shape[1:], rows.dtype)
    return holder.at[target].set(rows)


def local(tokens, cotangent, expert_ids, gate_values, w_in, w_out):
    tok_rows, model_width = tokens.shape
    top_count = expert_ids.shape[1]
    n_source = lax.axis_size("expert")
    local_count = EXPERTS // n_source
    target = slot_targets(expert_ids)
    send_x = fill_slots(jnp.repeat(tokens, top_count, axis=0), target).reshape(
        EXPERTS, CAP, model_width
    )
    send_g = fill_slots(jnp.repeat(cotangent, top_count, axis=0), target).reshape(
        EXPERTS, CAP, model_width
    )
    send_gate = fill_slots(gate_values.reshape(-1), target).reshape(EXPERTS, CAP)
    arrived_x, arrived_g, arrived_gate = (
        lax.all_to_all(send_x, "expert", split_axis=0, concat_axis=0, tiled=True),
        lax.all_to_all(send_g, "expert", split_axis=0, concat_axis=0, tiled=True),
        lax.all_to_all(send_gate, "expert", split_axis=0, concat_axis=0, tiled=True),
    )
    slot_x = arrived_x.reshape(n_source, local_count, CAP, model_width)
    slot_g = arrived_g.reshape(n_source, local_count, CAP, model_width)
    gate_four = arrived_gate.reshape(n_source, local_count, CAP, 1).astype(jnp.float32)
    pre_act = jnp.einsum("blcd,dlf->blcf", slot_x, w_in, preferred_element_type=jnp.float32)
    upstream = jnp.einsum("blcd,fld->blcf", slot_g, w_out, preferred_element_type=jnp.float32)
    squash = jax.nn.sigmoid(pre_act)
    active = pre_act * squash
    gate_part = jnp.sum(active * upstream, axis=-1)
    act_gated = (gate_four * active).astype(jnp.bfloat16)
    grad_pre = (gate_four * squash * (1.0 + pre_act * (1.0 - squash)) * upstream).astype(
        jnp.bfloat16
    )
    part_x = jnp.einsum("blcf,dlf->blcd", grad_pre, w_in, preferred_element_type=jnp.float32)
    grad_in = jnp.einsum(
        "blcd,blcf->dlf", slot_x, grad_pre, preferred_element_type=jnp.float32
    ).astype(jnp.bfloat16)
    grad_out = jnp.einsum(
        "blcf,blcd->fld", act_gated, slot_g, preferred_element_type=jnp.float32
    ).astype(jnp.bfloat16)
    sum_x, sum_gate = lax.psum((part_x, gate_part), "fsdp")
    back_x, back_gate = (
        lax.all_to_all(
            sum_x.reshape(EXPERTS, CAP, model_width),
            "expert",
            split_axis=0,
            concat_axis=0,
            tiled=True,
        ),
        lax.all_to_all(
            sum_gate.reshape(EXPERTS, CAP), "expert", split_axis=0, concat_axis=0, tiled=True
        ),
    )
    picked = back_x.reshape(EXPERTS * CAP, model_width)[target]
    grad_tokens = picked.reshape(tok_rows, top_count, model_width).sum(axis=1).astype(jnp.bfloat16)
    grad_gates = (
        back_gate.reshape(EXPERTS * CAP)[target].reshape(tok_rows, top_count).astype(jnp.bfloat16)
    )
    return (grad_tokens, grad_gates, grad_in, grad_out)


def solution(mesh):
    return jax.shard_map(
        local,
        mesh=mesh,
        in_specs=(
            P("expert", None),
            P("expert", None),
            P("expert", None),
            P("expert", None),
            P(None, "expert", "fsdp"),
            P("fsdp", "expert", None),
        ),
        out_specs=(
            P("expert", None),
            P("expert", None),
            P(None, "expert", "fsdp"),
            P("fsdp", "expert", None),
        ),
        check_vma=False,
    )
```

profile of v0, /device:TPU:0, one launch (start us, length us, event | category | flops | bytes accessed | tf_op | source)
XLA Modules:
  0.0 573.1 jit_solution(7586629435702043604)
XLA Ops:
  11.5 3.8 scatter_custom_fusion
  16.0 4.2 all-to-all-start
  24.7 8.6 %scatter_custom_fusion.1 = bf16[640,3072]{1,0:T(8,128)(2,1)} fusion(s32[512]{0:T(512)S(1)} %bitcast.88, bf16[512,3072]{1,0:T(8,128)(2,1)} %reshape.145, bf16[]{:T(256)} %constant.6.clone.1), kind=kCustom, calls=%fused_computation.34 | custom fusion | bytes 3932672 | tf_op jit(solution)/shard_map/scatter | solution.py:20
  33.4 5.1 all-to-all-start.1
  42.9 8.6 %scatter_custom_fusion.2 = bf16[640,3072]{1,0:T(8,128)(2,1)} fusion(s32[512]{0:T(512)S(1)} %bitcast.89, bf16[512,3072]{1,0:T(8,128)(2,1)} %reshape.153, bf16[]{:T(256)} %constant.6.clone.1), kind=kCustom, calls=%fused_computation.32 | custom fusion | bytes 3932672 | tf_op jit(solution)/shard_map/scatter | solution.py:20
  51.6 32.3 %all-to-all-done.1 = bf16[16,40,3072]{2,1,0:T(8,128)(2,1)} async-done(((bf16[16,40,3072]{2,1,0:T(8,128)(2,1)}), bf16[16,40,3072]{2,1,0:T(8,128)(2,1)}, u32[]{:S(2)}, u32[]{:S(2)}) %all-to-all-start.1) | async-done | bytes 3932192 | tf_op jit(solution)/shard_map/all_to_all | solution.py:37
  83.8 4.8 all-to-all-start.2
  88.7 13.7 %fusion.6 = f32[4,4,40,768]{3,2,1,0:T(8,128)S(1)} fusion(bf16[3072,4,768,1]{2,1,0,3:T(4,128)(2,1)} %bitcast.82, bf16[4,4,40,3072]{3,2,1,0:T(8,128)(2,1)} %bitcast.4), kind=kOutput, calls=%fused_computation.13 | convolution fusion | flops 3019898880 | bytes 24772608 | tf_op jit(solution)/shard_map/blcd,dlf->blcf/dot_general | solution.py:44
  102.4 31.7 %all-to-all-done.2 = bf16[16,40,3072]{2,1,0:T(8,128)(2,1)} async-done(((bf16[16,40,3072]{2,1,0:T(8,128)(2,1)}), bf16[16,40,3072]{2,1,0:T(8,128)(2,1)}, u32[]{:S(2)}, u32[]{:S(2)}) %all-to-all-start.2) | async-done | bytes 3932192 | tf_op jit(solution)/shard_map/all_to_all | solution.py:38
  134.1 35.3 %fusion.15 = (f32[4,4,40]{2,0,1:T(4,128)S(1)}, bf16[4,4,40,768]{3,2,0,1:T(8,128)(2,1)}, bf16[4,4,40,768]{3,2,0,1:T(8,128)(2,1)}) fusion(f32[4,4,40,768]{3,2,1,0:T(8,128)S(1)} %fusion.6, f32[4,4,40]{2,0,1:T(4,128)S(1)} %copy.72, bf16[768,4,3072,1]{2,1,0,3:T(4,128)(2,1)} %bitcast.92, bf16[4,4,40,3072]{3,2,1,0:T(8,128)(2,1)} %bitcast.8), kind=kOutput, calls=%fused_computation.22 | convolution fusion | flops 3027271168 | bytes 26743808 | tf_op jit(solution)/shard_map/blcd,fld->blcf/dot_general | solution.py:45
  169.4 14.2 %fusion.8 = f32[4,4,40,3072]{3,2,0,1:T(8,128)S(1)} fusion(bf16[4,4,40,768]{3,2,0,1:T(8,128)(2,1)} %get-tuple-element.25, bf16[3072,4,768,1]{2,1,0,3:T(4,128)(2,1)} %bitcast.83), kind=kOutput, calls=%fused_computation.15 | convolution fusion | flops 3019898880 | bytes 27721728 | tf_op jit(solution)/shard_map/blcf,dlf->blcd/dot_general | solution.py:53
  183.6 3.7 copy.78
  187.3 23.3 %psum.15 = bf16[4,4,40]{2,0,1:T(4,128)(2,1)S(1)} all-reduce(f32[4,4,40]{2,0,1:T(4,128)S(1)} %get-tuple-element.24), channel_id=1, replica_groups=mesh['fsdp'=8,'expert'=4] {'fsdp'}, use_global_device_ids=true, to_apply=%region_9.10 | all-reduce | flops 640 | bytes 3840 | tf_op jit(solution)/shard_map/psum | solution.py:60
  210.7 6.1 %all_to_all.30 = bf16[4,4,40]{2,1,0:T(4,128)(2,1)S(1)} all-to-all(bf16[4,4,40]{2,1,0:T(4,128)(2,1)S(1)} %copy.79), channel_id=1, replica_groups=mesh['fsdp'=8,'expert'=4] {'expert'}, dimensions={0} | all-to-all | bytes 2560 | tf_op jit(solution)/shard_map/all_to_all | solution.py:69
  216.8 227.3 %all-reduce.2.cloned.1.call-done = f32[16,40,3072]{2,1,0:T(8,128)} async-done(((f32[16,40,3072]{2,1,0:T(8,128)}), f32[16,40,3072]{2,1,0:T(8,128)}) %all-reduce.2.cloned.1.call-update) | async-done | bytes 7864336 | tf_op jit(solution)/shard_map/psum | solution.py:60
  444.1 5.7 all-to-all-start.3
  449.9 11.6 %fusion = bf16[3072,4,768]{0,2,1:T(8,128)(2,1)} fusion(bf16[4,4,40,768]{3,2,0,1:T(8,128)(2,1)S(1)} %copy-done, bf16[4,4,40,3072]{3,2,1,0:T(8,128)(2,1)} %bitcast.4), kind=kOutput, calls=%fused_computation.7 | convolution fusion | flops 3029336064 | bytes 23789568 | tf_op jit(solution)/shard_map/blcd,blcf->dlf/dot_general | solution.py:54
  461.5 29.5 %copy.83 = bf16[3072,4,768]{2,1,0:T(4,128)(2,1)} copy(bf16[3072,4,768]{0,2,1:T(8,128)(2,1)} %fusion) | data formatting | bytes 37748736
  491.0 12.7 %fusion.1 = bf16[768,4,3072]{0,2,1:T(8,128)(2,1)} fusion(bf16[4,4,40,3072]{3,2,1,0:T(8,128)(2,1)} %bitcast.8, bf16[4,4,40,768]{3,2,0,1:T(8,128)(2,1)S(1)} %copy-done.1), kind=kOutput, calls=%fused_computation.8 | convolution fusion | flops 3029336064 | bytes 23789568 | tf_op jit(solution)/shard_map/blcf,blcd->fld/dot_general | solution.py:57
  503.7 31.9 %copy.84 = bf16[768,4,3072]{2,1,0:T(4,128)(2,1)} copy(bf16[768,4,3072]{0,2,1:T(8,128)(2,1)} %fusion.1) | data formatting | bytes 37748736
  535.7 3.5 gather_fusion.1
  540.0 10.5 %gather_fusion = f32[512,3072]{1,0:T(8,128)} fusion(f32[640,3072]{1,0:T(8,128)} %bitcast.14, s32[1024]{0:T(1024)S(1)} %pad_clamp_fusion), kind=kCustom, calls=%fused_computation | custom fusion | bytes 12584960 | tf_op jit(solution)/shard_map/gather | solution.py:73
  550.5 7.8 %reshape.115 = f32[128,4,3072]{2,1,0:T(4,128)} reshape(f32[512,3072]{1,0:T(8,128)} %gather_fusion) | data formatting | bytes 12582912 | tf_op jit(solution)/shard_map/reshape | solution.py:74
  558.3 7.5 %reduce_sum.31 = bf16[128,3072]{1,0:T(8,128)(2,1)} reduce(f32[128,4,3072]{2,1,0:T(4,128)} %reshape.115, f32[]{:T(128)} %constant.5.clone.1), dimensions={1}, to_apply=%region_7.8 | reduce | flops 1179648 | bytes 7077892 | tf_op jit(solution)/shard_map/reduce_sum | solution.py:74
  (34 shorter events, 15.0 us)
Async XLA Ops:
  16.0 17.3 %all-to-all-start = ((bf16[4,4,40]{2,1,0:T(4,128)(2,1)}), bf16[4,4,40]{2,1,0:T(4,128)(2,1)S(1)}, u32[]{:S(2)}, u32[]{:S(2)}) async-start(bf16[4,4,40]{2,1,0:T(4,128)(2,1)} %all_to_all.19), calls=%async_computation | async-start | bytes 8192 | tf_op jit(solution)/shard_map/all_to_all | solution.py:39
  33.4 50.5 %all-to-all-start.1 = ((bf16[16,40,3072]{2,1,0:T(8,128)(2,1)}), bf16[16,40,3072]{2,1,0:T(8,128)(2,1)}, u32[]{:S(2)}, u32[]{:S(2)}) async-start(bf16[16,40,3072]{2,1,0:T(8,128)(2,1)} %bitcast.85), calls=%async_computation.1 | async-start | bytes 7864320 | tf_op jit(solution)/shard_map/all_to_all | solution.py:37
  83.8 50.3 %all-to-all-start.2 = ((bf16[16,40,3072]{2,1,0:T(8,128)(2,1)}), bf16[16,40,3072]{2,1,0:T(8,128)(2,1)}, u32[]{:S(2)}, u32[]{:S(2)}) async-start(bf16[16,40,3072]{2,1,0:T(8,128)(2,1)} %bitcast.86), calls=%async_computation.2 | async-start | bytes 7864320 | tf_op jit(solution)/shard_map/all_to_all | solution.py:38
  88.7 355.4 %all-reduce.2.cloned.1.call-start = ((), (), s32[]{:S(2)}) async-start(), calls=%async_computation.5 | async-start | bytes 15728640 | tf_op jit(solution)/shard_map/psum | solution.py:60
  216.8 233.0 %copy-start = (bf16[4,4,40,768]{3,2,0,1:T(8,128)(2,1)S(1)}, bf16[4,4,40,768]{3,2,0,1:T(8,128)(2,1)}, u32[]{:S(2)}) copy-start(bf16[4,4,40,768]{3,2,0,1:T(8,128)(2,1)} %get-tuple-element.25) | copy-start | bytes 2949124
  444.1 95.9 %all-to-all-start.3 = ((f32[16,40,3072]{2,1,0:T(8,128)}), f32[16,40,3072]{2,1,0:T(8,128)}, u32[]{:S(2)}, u32[]{:S(2)}) async-start(f32[16,40,3072]{2,1,0:T(8,128)} %all-reduce.2.cloned.1.call-done), calls=%async_computation.3 | async-start | bytes 15728640 | tf_op jit(solution)/shard_map/all_to_all | solution.py:62
  461.5 29.5 %copy-start.1 = (bf16[4,4,40,768]{3,2,0,1:T(8,128)(2,1)S(1)}, bf16[4,4,40,768]{3,2,0,1:T(8,128)(2,1)}, u32[]{:S(2)}) copy-start(bf16[4,4,40,768]{3,2,0,1:T(8,128)(2,1)} %get-tuple-element.26) | copy-start | bytes 2949124
Sparse Core Ops, SparseCore 0:
  187.5 256.5 all-reduce.1
where the time goes:
time: 584 us; the launch traced here: 573 us
  waiting for transfers between devices  291 us (50%)
  local copies, waits for them, and re-layouts  121 us (21%)
  matrix products  87.5 us (15%)
  blocking collectives  29.4 us (5%)
  starting transfers between devices  19.9 us (3%)
  between operations  14.6 us (2%)
  other arithmetic  9.51 us (2%)
    psum x1, waiting for transfers between devices, local(): sum_x, sum_gate = lax.psum((part_x, gate_part), 'fsdp')  227 us
    unnamed x9, local copies, waits for them, and re-layouts  63.6 us
    dot_general x1, matrix products, local(): jnp.einsum('blcd,fld->blcf', slot_g, w_out, preferred_element_type=jnp.fl...  35.3 us
    all_to_all x1, waiting for transfers between devices, local(): lax.all_to_all(send_x, 'expert', split_axis=0, concat_axis=0, tiled=True)  32.3 us
    all_to_all x1, waiting for transfers between devices, local(): lax.all_to_all(send_g, 'expert', split_axis=0, concat_axis=0, tiled=True)  31.7 us
    psum x1, blocking collectives, local(): sum_x, sum_gate = lax.psum((part_x, gate_part), 'fsdp')  23.3 us
    scatter x3, local copies, waits for them, and re-layouts, fill_slots(): return holder.at[target].set(rows)  21 us
    dot_general x1, matrix products, local(): jnp.einsum('blcf,dlf->blcd', grad_pre, w_in, preferred_element_type=jnp.f...  14.2 us
  transfers between devices with their start and end apart: 5, of which 3 were waited for; matrix products, arithmetic and copies ran while one was open for 23% of the time, Pallas kernels for 0%

commit v1 on v0

v1 whole, which is shorter than its diff:
```python
import jax
import jax.numpy as jnp
from jax import lax
from jax.sharding import PartitionSpec as P

EXPERTS = 16
CAP = 40
AXES = ("fsdp", "expert")
CORE, Y, X, Z = 1, 2, 4, 8


def swap(value, mask):
    size = lax.axis_size("fsdp") * lax.axis_size("expert")
    return lax.ppermute(value, AXES, [(i, i ^ mask) for i in range(size)])


def is_small():
    return lax.axis_size("fsdp") == 8 and lax.axis_size("expert") == 4


def own_order(rows):
    x_index = lax.axis_index("fsdp") % 2
    half = rows.shape[0] // 2
    return jnp.where(x_index == 0, rows, jnp.concatenate([rows[half:], rows[:half]], axis=0))


def spread(rows):
    if not is_small():
        return list(lax.all_gather(rows, "expert", axis=0))
    half = rows.shape[0] // 2
    other_core = swap(rows, CORE)
    near = swap(rows[:half], Y)
    far = swap(near, X)
    other_y = jnp.concatenate([near, far], axis=0)
    both = jnp.concatenate([swap(near, CORE), swap(far, CORE)], axis=0)
    return [rows, other_core, other_y, both]


def spread_small(rows):
    if not is_small():
        return list(lax.all_gather(rows, "expert", axis=0))
    return [rows, swap(rows, CORE), swap(rows, Y), swap(rows, CORE | Y)]


def collect(parts):
    if not is_small():
        stacked = jnp.stack(parts, axis=0)
        mine = lax.psum_scatter(stacked, "expert", scatter_dimension=0, tiled=False)
        return lax.psum(mine, "fsdp").astype(jnp.bfloat16)
    narrow, wide = jnp.bfloat16, jnp.float32
    fsdp = lax.axis_index("fsdp")
    x_index, z_index = fsdp % 2, fsdp // 2
    half = parts[0].shape[0] // 2
    own = parts[0] + swap(parts[1].astype(narrow), CORE).astype(wide)
    other = parts[2] + swap(parts[3].astype(narrow), CORE).astype(wide)
    total = own[:half]
    total = total + swap(own[half:].astype(narrow), X).astype(wide)
    total = total + swap(other[:half].astype(narrow), Y).astype(wide)
    total = total + swap(other[half:].astype(narrow), X | Y).astype(wide)
    quarter = half // 4

    def chunk(array, index):
        return lax.dynamic_slice_in_dim(array, index * quarter, quarter, axis=0)

    final = chunk(total, z_index)
    packed = total.astype(narrow)
    for step in (1, 2, 3):
        final = final + swap(chunk(packed, z_index ^ step), step * Z).astype(wide)
    final = final.astype(narrow)
    near = jnp.zeros((half, final.shape[1]), narrow)
    near = lax.dynamic_update_slice_in_dim(near, final, z_index * quarter, axis=0)
    for step in (1, 2, 3):
        near = lax.dynamic_update_slice_in_dim(near, swap(final, step * Z), (z_index ^ step) * quarter, axis=0)
    far = swap(near, X)
    return jnp.where(
        x_index == 0, jnp.concatenate([near, far], axis=0), jnp.concatenate([far, near], axis=0)
    )


def local(tokens, cotangent, expert_ids, gate_values, w_in, w_out):
    tok_rows, model_width = tokens.shape
    local_count = w_in.shape[1]
    narrow, wide = jnp.bfloat16, jnp.float32
    first = lax.axis_index("expert") * local_count
    if is_small():
        tokens, cotangent = own_order(tokens), own_order(cotangent)
        expert_ids, gate_values = own_order(expert_ids), own_order(gate_values)
    meta = jnp.concatenate([expert_ids.astype(wide), gate_values.astype(wide)], axis=1).T
    meta_blocks = jnp.stack(spread_small(meta))
    top_count = expert_ids.shape[1]
    ids = meta_blocks[:, :top_count].astype(jnp.int32)
    gates = meta_blocks[:, top_count:]
    blocks = ids.shape[0]
    x_blocks = jnp.stack(spread(tokens))
    g_blocks = jnp.stack(spread(cotangent))
    names = first + jnp.arange(local_count, dtype=jnp.int32)
    named = ids[:, None] == names[None, :, None, None]
    hit = jnp.any(named, axis=2)
    gate_tok = jnp.sum(jnp.where(named, gates[:, None], 0.0), axis=2)
    earlier = jnp.tril(jnp.ones((tok_rows, tok_rows), wide), -1)
    position = jnp.einsum("tu,blu->blt", earlier, hit.astype(wide)).astype(jnp.int32)
    slots = jnp.arange(CAP, dtype=jnp.int32)
    choose = hit[:, :, None] & (position[:, :, None] == slots[None, None, :, None])
    pick = choose.astype(narrow)
    slot_x = jnp.einsum("blst,btd->lbsd", pick, x_blocks, preferred_element_type=wide).astype(narrow)
    slot_g = jnp.einsum("blst,btd->lbsd", pick, g_blocks, preferred_element_type=wide).astype(narrow)
    gate_slot = jnp.sum(jnp.where(choose, gate_tok[:, :, None], 0.0), axis=3)
    rows = blocks * CAP
    slot_x = slot_x.reshape(local_count, rows, model_width)
    slot_g = slot_g.reshape(local_count, rows, model_width)
    gate_slot = jnp.swapaxes(gate_slot, 0, 1).reshape(local_count, rows, 1)
    pre_act = jnp.einsum("lrd,dlf->lrf", slot_x, w_in, preferred_element_type=wide)
    upstream = jnp.einsum("lrd,fld->lrf", slot_g, w_out, preferred_element_type=wide)
    squash = jax.nn.sigmoid(pre_act)
    active = pre_act * squash
    gate_part = jnp.sum(active * upstream, axis=-1)
    act_gated = (gate_slot * active).astype(narrow)
    grad_pre = (gate_slot * squash * (1.0 + pre_act * (1.0 - squash)) * upstream).astype(narrow)
    gate_part = gate_part.reshape(local_count, blocks, CAP)
    gate_tok = jnp.sum(jnp.where(choose, jnp.swapaxes(gate_part, 0, 1)[..., None], 0.0), axis=2)
    gate_back = jnp.sum(jnp.where(named, gate_tok[:, :, None], 0.0), axis=1)
    part_x = jnp.einsum("lrf,dlf->lrd", grad_pre, w_in, preferred_element_type=wide)
    high = part_x.astype(narrow)
    low = (part_x - high.astype(wide)).astype(narrow)
    high = high.reshape(local_count, blocks, CAP, model_width)
    low = low.reshape(local_count, blocks, CAP, model_width)
    token_part = jnp.einsum("blst,lbsd->btd", pick, high, preferred_element_type=wide)
    token_part = token_part + jnp.einsum("blst,lbsd->btd", pick, low, preferred_element_type=wide)
    grad_tokens = collect([token_part[b] for b in range(blocks)])
    if is_small():
        gates_own = gate_back[0]
        for b, mask in ((1, CORE), (2, Y), (3, CORE | Y)):
            gates_own = gates_own + swap(gate_back[b], mask)
        half = tok_rows // 2
        x_index = lax.axis_index("fsdp") % 2
        gates_own = jnp.where(
            x_index == 0,
            gates_own,
            jnp.concatenate([gates_own[:, half:], gates_own[:, :half]], axis=1),
        )
    else:
        gates_own = lax.psum_scatter(gate_back, "expert", scatter_dimension=0, tiled=False)
    grad_gates = lax.psum(gates_own, "fsdp").T.astype(narrow)
    grad_in = jnp.einsum("lrd,lrf->dlf", slot_x, grad_pre, preferred_element_type=wide).astype(narrow)
    grad_out = jnp.einsum("lrf,lrd->fld", act_gated, slot_g, preferred_element_type=wide).astype(narrow)
    return (grad_tokens, grad_gates, grad_in, grad_out)


def solution(mesh):
    return jax.shard_map(
        local,
        mesh=mesh,
        in_specs=(
            P("expert", None),
            P("expert", None),
            P("expert", None),
            P("expert", None),
            P(None, "expert", "fsdp"),
            P("fsdp", "expert", None),
        ),
        out_specs=(
            P("expert", None),
            P("expert", None),
            P(None, "expert", "fsdp"),
            P("fsdp", "expert", None),
        ),
        check_vma=False,
    )
```

time: 584 us -> 254 us (0.43); the launches traced: 573 us -> 252 us
  waiting for transfers between devices: 291 us -> 39.8 us
  local copies, waits for them, and re-layouts: 121 us -> 67.3 us
  between operations: 14.6 us -> 0.98 us
  blocking collectives: 29.4 us -> 21.3 us
    psum x1 -> x0, waiting for transfers between devices: 227 us -> none  [local(): sum_x, sum_gate = lax.psum((part_x, gate_part), 'fsdp')]
    all_to_all x4 -> x0, waiting for transfers between devices: 63.9 us -> none  [the longest x1 32.3 us: local(): lax.all_to_all(send_x, 'expert', split_axis=0, concat_axis=0, tiled=True)]
    ppermute x0 -> x28, waiting for transfers between devices: none -> 39.8 us  [swap(): return lax.ppermute(value, AXES, [(i, i ^ mask) for i in range(size)])]
    ppermute x0 -> x28, starting transfers between devices: none -> 24.8 us  [swap(): return lax.ppermute(value, AXES, [(i, i ^ mask) for i in range(size)])]
    scatter x3 -> x0, local copies, waits for them, and re-layouts: 21 us -> none  [fill_slots(): return holder.at[target].set(rows)]
    all_to_all x4 -> x0, starting transfers between devices: 19.9 us -> none  [the longest x1 5.73 us: local(): lax.all_to_all(sum_x.reshape(EXPERTS, CAP, model_width), 'expert', split_...]
    gather x2 -> x0, local copies, waits for them, and re-layouts: 14.1 us -> none  [the longest x1 10.5 us: local(): picked = back_x.reshape(EXPERTS * CAP, model_width)[target]]
    reshape x5 -> x1, local copies, waits for them, and re-layouts: 12.8 us -> 0.09 us  [local(): gate_part = gate_part.reshape(local_count, blocks, CAP)]
  transfers between devices with their start and end apart: 5 -> 28, of which waited for: 3 -> 8; matrix products, arithmetic and copies ran while one was open for 23% -> 36% of each run, Pallas kernels for 0% -> 0%
where the time goes in v1:
time: 254 us; the launch traced here: 252 us
  matrix products  86.3 us (34%)
  local copies, waits for them, and re-layouts  67.3 us (26%)
  waiting for transfers between devices  39.8 us (16%)
  starting transfers between devices  24.8 us (10%)
  blocking collectives  21.3 us (8%)
  other arithmetic  11.5 us (5%)
    unnamed x12, local copies, waits for them, and re-layouts  62.1 us
    ppermute x28, waiting for transfers between devices, swap(): return lax.ppermute(value, AXES, [(i, i ^ mask) for i in range(size)])  39.8 us
    ppermute x28, starting transfers between devices, swap(): return lax.ppermute(value, AXES, [(i, i ^ mask) for i in range(size)])  24.8 us
    dot_general x1, matrix products, local(): jnp.einsum('lrd,fld->lrf', slot_g, w_out, preferred_element_type=wide)  24.1 us
    psum x1, blocking collectives, local(): grad_gates = lax.psum(gates_own, 'fsdp').T.astype(narrow)  21.3 us
    dot_general x1, matrix products, local(): jnp.einsum('lrf,dlf->lrd', grad_pre, w_in, preferred_element_type=wide)  15.4 us
    dot_general x1, matrix products, local(): jnp.einsum('lrf,lrd->fld', act_gated, slot_g, preferred_element_type=wide)  12.8 us
    dot_general x1, matrix products, local(): jnp.einsum('lrd,dlf->lrf', slot_x, w_in, preferred_element_type=wide)  12.5 us
  transfers between devices with their start and end apart: 28, of which 8 were waited for; matrix products, arithmetic and copies ran while one was open for 36% of the time, Pallas kernels for 0%

profile of v1, /device:TPU:0, one launch (start us, length us, event | category | flops | bytes accessed | tf_op | source)
XLA Modules:
  0.0 252.0 jit_solution(13907324555723588670)
XLA Ops:
  3.8 3.0 %collective-permute-start.1 = (f32[8,128]{1,0:T(8,128)S(1)}, f32[8,128]{1,0:T(8,128)S(1)}, u32[]{:S(2)}, u32[]{:S(2)}) collective-permute-start(f32[8,128]{1,0:T(8,128)S(1)} %get-tuple-element.51), channel_id=1, source_target_pairs={{0,2},{1,3},{2,0},{3,1},{4,6},{5,7},{6,4},{7,5},{8,10},{9,11},{10,... | collective-permute-start | bytes 12296 | tf_op jit(solution)/shard_map/ppermute | solution.py:14
  14.5 7.5 %collective-permute-done.9 = bf16[64,3072]{1,0:T(8,128)(2,1)S(1)} collective-permute-done((bf16[64,3072]{1,0:T(8,128)(2,1)S(1)}, bf16[64,3072]{1,0:T(8,128)(2,1)S(1)}, u32[]{:S(2)}, u32[]{:S(2)}) %collective-permute-start.9) | collective-permute-done | bytes 393248 | tf_op jit(solution)/shard_map/ppermute | solution.py:14
  22.3 7.6 %collective-permute-done.4 = bf16[64,3072]{1,0:T(8,128)(2,1)S(1)} collective-permute-done((bf16[64,3072]{1,0:T(8,128)(2,1)S(1)}, bf16[64,3072]{1,0:T(8,128)(2,1)S(1)}, u32[]{:S(2)}, u32[]{:S(2)}) %collective-permute-start.4) | collective-permute-done | bytes 393248 | tf_op jit(solution)/shard_map/ppermute | solution.py:14
  30.1 2.0 collective-permute-done.10
  32.2 8.4 %collective-permute-done.5 = bf16[64,3072]{1,0:T(8,128)(2,1)S(1)} collective-permute-done((bf16[64,3072]{1,0:T(8,128)(2,1)S(1)}, bf16[64,3072]{1,0:T(8,128)(2,1)S(1)}, u32[]{:S(2)}, u32[]{:S(2)}) %collective-permute-start.5) | collective-permute-done | bytes 393248 | tf_op jit(solution)/shard_map/ppermute | solution.py:14
  41.2 2.3 fusion.7
  44.0 2.9 %fusion.6 = bf16[4,4,40,3072]{3,2,0,1:T(8,128)(2,1)S(1)} fusion(bf16[1,128,3072]{2,1,0:T(8,128)(2,1)S(1)} %maximum_bitcast_fusion.5, bf16[1,128,3072]{2,1,0:T(8,128)(2,1)S(1)} %maximum_bitcast_fusion.4, bf16[1,128,3072]{2,1,0:T(8,128)(2,1)S(1)} %bitcast.104, bf16[1,128,3072]{2,1,0:T(8,128)(2,1)} %bitcast.7, s32[4,4,128]{2,1,0:T(4,128)S(1)} %convolution_convert_fusion.2, ...), kind=kOutput, calls=%fused_computation.12 | convolution fusion | flops 518029312 | bytes 7088128 | tf_op jit(solution)/shard_map/blst,btd->lbsd/dot_general | solution.py:105
  47.3 12.5 %fusion.4 = f32[4,160,768]{2,1,0:T(8,128)} fusion(bf16[4,160,3072]{2,1,0:T(8,128)(2,1)S(1)} %bitcast.93, bf16[3072,4,768]{2,1,0:T(4,128)(2,1)} %param.10), kind=kOutput, calls=%fused_computation.6 | convolution fusion | flops 3019898880 | bytes 24772608 | tf_op jit(solution)/shard_map/lrd,dlf->lrf/dot_general | solution.py:112
  59.8 24.1 %multiply_reduce_fusion = (f32[4,160]{1,0:T(4,128)S(1)}, f32[4,160,768]{2,1,0:T(8,128)}) fusion(f32[4,160,768]{2,1,0:T(8,128)} %fusion.4, bf16[4,160,3072]{2,1,0:T(8,128)(2,1)S(1)} %bitcast.95, bf16[768,4,3072]{2,1,0:T(4,128)(2,1)} %param.11), kind=kOutput, calls=%fused_computation.32 | convolution fusion | flops 3022847488 | bytes 26741248 | tf_op jit(solution)/shard_map/lrd,fld->lrf/dot_general | solution.py:113
  84.4 2.9 %multiply_convert_fusion.1 = bf16[4,160,768]{2,1,0:T(8,128)(2,1)S(1)} fusion(f32[4,160,768]{2,1,0:T(8,128)} %get-tuple-element.59, f32[4,160,768]{2,1,0:T(8,128)} %fusion.4, f32[4,160]{1,0:T(4,128)S(1)} %mul.51), kind=kLoop, calls=%fused_computation.33 | loop fusion | flops 4915200 | bytes 4917760 | tf_op jit(solution)/shard_map/convert_element_type | solution.py:118
  87.3 15.4 %subtract_convert_fusion = (bf16[4,160,3072]{2,1,0:T(8,128)(2,1)S(1)}, bf16[4,160,3072]{2,1,0:T(8,128)(2,1)}) fusion(bf16[4,160,768]{2,1,0:T(8,128)(2,1)S(1)} %multiply_convert_fusion.1, bf16[3072,4,768]{2,1,0:T(4,128)(2,1)} %param.10), kind=kOutput, calls=%fused_computation.8 | convolution fusion | flops 3027763200 | bytes 27721728 | tf_op jit(solution)/shard_map/lrf,dlf->lrd/dot_general | solution.py:122
  102.7 3.1 %fusion.9 = f32[4,128,3072,1]{2,1,3,0:T(8,128)S(1)} fusion(bf16[4,4,40,3072]{3,2,1,0:T(8,128)(2,1)} %bitcast.92, s32[4,4,128]{2,1,0:T(4,128)S(1)} %convolution_convert_fusion.2, pred[4,4,128]{2,1,0:T(4,128)(4,1)S(1)} %compare_reduce_fusion), kind=kOutput, calls=%fused_computation.15 | convolution fusion | flops 503480320 | bytes 10233856 | tf_op jit(solution)/shard_map/blst,lbsd->btd/dot_general | solution.py:127
  105.8 3.9 %fusion.72 = (bf16[4,128,3072]{2,1,0:T(8,128)(2,1)S(1)}, f32[4,128,3072]{2,1,0:T(8,128)}) fusion(bf16[4,4,40,3072]{3,2,1,0:T(8,128)(2,1)S(1)} %bitcast.91, s32[4,4,128]{2,1,0:T(4,128)S(1)} %convolution_convert_fusion.2, pred[4,4,128]{2,1,0:T(4,128)(4,1)S(1)} %compare_reduce_fusion, f32[4,128,3072,1]{2,1,3,0:T(8,128)S(1)} %fusion.9), kind=kOutput, calls=%fused_computation.120 | convolution fusion | flops 506626048 | bytes 19671040 | tf_op jit(solution)/shard_map/blst,lbsd->btd/dot_general | solution.py:128
  111.3 12.8 %convert_bitcast_fusion = bf16[768,4,3072]{0,2,1:T(8,128)(2,1)} fusion(bf16[4,160,3072]{2,1,0:T(8,128)(2,1)} %bitcast.96, f32[4,160]{1,0:T(4,128)S(1)} %mul.51, f32[4,160,768]{2,1,0:T(8,128)S(1)} %copy-done.3), kind=kOutput, calls=%fused_computation.2 | convolution fusion | flops 3032285184 | bytes 24775168 | tf_op jit(solution)/shard_map/lrf,lrd->fld/dot_general | solution.py:145
  124.1 2.4 fusion.26
  130.2 9.1 %convert_bitcast_fusion.1 = bf16[3072,4,768]{0,2,1:T(8,128)(2,1)} fusion(bf16[4,160,768]{2,1,0:T(8,128)(2,1)S(1)} %multiply_convert_fusion.1, bf16[4,160,3072]{2,1,0:T(8,128)(2,1)S(1)} %bitcast.94), kind=kOutput, calls=%fused_computation.3 | convolution fusion | flops 3029336064 | bytes 23789568 | tf_op jit(solution)/shard_map/lrd,lrf->dlf/dot_general | solution.py:144
  139.4 6.3 %collective-permute-done.16 = bf16[64,3072]{1,0:T(8,128)(2,1)S(1)} collective-permute-done((bf16[64,3072]{1,0:T(8,128)(2,1)S(1)}, bf16[64,3072]{1,0:T(8,128)(2,1)S(1)}, u32[]{:S(2)}, u32[]{:S(2)}) %collective-permute-start.16) | collective-permute-done | bytes 393248 | tf_op jit(solution)/shard_map/ppermute | solution.py:14
  149.4 2.5 collective-permute-start.20
  152.7 31.9 %copy.58 = bf16[768,4,3072]{2,1,0:T(4,128)(2,1)} copy(bf16[768,4,3072]{0,2,1:T(8,128)(2,1)} %convert_bitcast_fusion) | data formatting | bytes 37748736
  184.6 29.4 %copy.57 = bf16[3072,4,768]{2,1,0:T(4,128)(2,1)} copy(bf16[3072,4,768]{0,2,1:T(8,128)(2,1)} %convert_bitcast_fusion.1) | data formatting | bytes 37748736
  215.5 1.9 collective-permute-start.21
  217.6 2.8 %collective-permute-start.22 = (bf16[16,3072]{1,0:T(8,128)(2,1)S(1)}, bf16[16,3072]{1,0:T(8,128)(2,1)S(1)}, u32[]{:S(2)}, u32[]{:S(2)}) collective-permute-start(bf16[16,3072]{1,0:T(8,128)(2,1)S(1)} %get-tuple-element.27), channel_id=1, source_target_pairs={{0,16},{1,17},{2,18},{3,19},{4,20},{5,21},{6,22},{7,23},{8,24},{9,... | collective-permute-start | bytes 294920 | tf_op jit(solution)/shard_map/ppermute | solution.py:14
  221.7 6.0 %collective-permute-done.22 = bf16[16,3072]{1,0:T(8,128)(2,1)S(1)} collective-permute-done((bf16[16,3072]{1,0:T(8,128)(2,1)S(1)}, bf16[16,3072]{1,0:T(8,128)(2,1)S(1)}, u32[]{:S(2)}, u32[]{:S(2)}) %collective-permute-start.22) | collective-permute-done | bytes 98336 | tf_op jit(solution)/shard_map/ppermute | solution.py:14
  229.6 21.3 %psum.7 = bf16[4,128]{1,0:T(4,128)(2,1)} all-reduce(f32[4,128]{1,0:T(4,128)S(1)} %maximum_select_fusion.3), channel_id=1, replica_groups=mesh['fsdp'=8,'expert'=4] {'fsdp'}, use_global_device_ids=true, to_apply=%region_6.7 | all-reduce | flops 512 | bytes 3072 | tf_op jit(solution)/shard_map/psum | solution.py:143
  (101 shorter events, 29.1 us)
Async XLA Ops:
  3.8 10.1 %collective-permute-start.1 = (f32[8,128]{1,0:T(8,128)S(1)}, f32[8,128]{1,0:T(8,128)S(1)}, u32[]{:S(2)}, u32[]{:S(2)}) collective-permute-start(f32[8,128]{1,0:T(8,128)S(1)} %get-tuple-element.51), channel_id=1, source_target_pairs={{0,2},{1,3},{2,0},{3,1},{4,6},{5,7},{6,4},{7,5},{8,10},{9,11},{10,... | collective-permute-start | bytes 12296 | tf_op jit(solution)/shard_map/ppermute | solution.py:14
  6.9 7.3 %collective-permute-start = (f32[8,128]{1,0:T(8,128)S(1)}, f32[8,128]{1,0:T(8,128)S(1)}, u32[]{:S(2)}, u32[]{:S(2)}) collective-permute-start(f32[8,128]{1,0:T(8,128)S(1)} %get-tuple-element.51), channel_id=1, source_target_pairs={{0,1},{1,0},{2,3},{3,2},{4,5},{5,4},{6,7},{7,6},{8,9},{9,8},{10,11... | collective-permute-start | bytes 12296 | tf_op jit(solution)/shard_map/ppermute | solution.py:14
  6.9 7.6 %collective-permute-start.2 = (f32[8,128]{1,0:T(8,128)S(1)}, f32[8,128]{1,0:T(8,128)S(1)}, u32[]{:S(2)}, u32[]{:S(2)}) collective-permute-start(f32[8,128]{1,0:T(8,128)S(1)} %get-tuple-element.51), channel_id=1, source_target_pairs={{0,3},{1,2},{2,1},{3,0},{4,7},{5,6},{6,5},{7,4},{8,11},{9,10},{10,... | collective-permute-start | bytes 12296 | tf_op jit(solution)/shard_map/ppermute | solution.py:14
  9.6 31.6 %collective-permute-start.8 = (bf16[128,3072]{1,0:T(8,128)(2,1)S(1)}, bf16[128,3072]{1,0:T(8,128)(2,1)}, u32[]{:S(2)}, u32[]{:S(2)}) collective-permute-start(bf16[128,3072]{1,0:T(8,128)(2,1)S(1)} %maximum_select_fusion.1), channel_id=1, source_target_pairs={{0,1},{1,0},{2,3},{3,2},{4,5},{5,4},{6,7},{7,6},{8,9},{9,8},{10,11... | collective-permute-start | bytes 2359304 | tf_op jit(solution)/shard_map/ppermute | solution.py:14
  10.0 12.0 %collective-permute-start.9 = (bf16[64,3072]{1,0:T(8,128)(2,1)S(1)}, bf16[64,3072]{1,0:T(8,128)(2,1)S(1)}, u32[]{:S(2)}, u32[]{:S(2)}) collective-permute-start(bf16[64,3072]{1,0:T(8,128)(2,1)S(1)} %slice.112), channel_id=1, source_target_pairs={{0,2},{1,3},{2,0},{3,1},{4,6},{5,7},{6,4},{7,5},{8,10},{9,11},{10,... | collective-permute-start | bytes 1179656 | tf_op jit(solution)/shard_map/ppermute | solution.py:14
  13.9 30.1 %collective-permute-start.3 = (bf16[128,3072]{1,0:T(8,128)(2,1)}, bf16[128,3072]{1,0:T(8,128)(2,1)S(1)}, u32[]{:S(2)}, u32[]{:S(2)}) collective-permute-start(bf16[128,3072]{1,0:T(8,128)(2,1)} %maximum_select_fusion), channel_id=1, source_target_pairs={{0,1},{1,0},{2,3},{3,2},{4,5},{5,4},{6,7},{7,6},{8,9},{9,8},{10,11... | collective-permute-start | bytes 2359304 | tf_op jit(solution)/shard_map/ppermute | solution.py:14
  14.2 15.7 %collective-permute-start.4 = (bf16[64,3072]{1,0:T(8,128)(2,1)S(1)}, bf16[64,3072]{1,0:T(8,128)(2,1)S(1)}, u32[]{:S(2)}, u32[]{:S(2)}) collective-permute-start(bf16[64,3072]{1,0:T(8,128)(2,1)S(1)} %slice.111), channel_id=1, source_target_pairs={{0,2},{1,3},{2,0},{3,1},{4,6},{5,7},{6,4},{7,5},{8,10},{9,11},{10,... | collective-permute-start | bytes 1179656 | tf_op jit(solution)/shard_map/ppermute | solution.py:14
  22.0 10.1 %collective-permute-start.10 = (bf16[64,3072]{1,0:T(8,128)(2,1)S(1)}, bf16[64,3072]{1,0:T(8,128)(2,1)S(1)}, u32[]{:S(2)}, u32[]{:S(2)}) collective-permute-start(bf16[64,3072]{1,0:T(8,128)(2,1)S(1)} %collective-permute-done.9), channel_id=1, source_target_pairs={{0,4},{1,5},{2,6},{3,7},{4,0},{5,1},{6,2},{7,3},{8,12},{9,13},{10,... | collective-permute-start | bytes 1179656 | tf_op jit(solution)/shard_map/ppermute | solution.py:14
  29.9 10.6 %collective-permute-start.5 = (bf16[64,3072]{1,0:T(8,128)(2,1)S(1)}, bf16[64,3072]{1,0:T(8,128)(2,1)S(1)}, u32[]{:S(2)}, u32[]{:S(2)}) collective-permute-start(bf16[64,3072]{1,0:T(8,128)(2,1)S(1)} %collective-permute-done.4), channel_id=1, source_target_pairs={{0,4},{1,5},{2,6},{3,7},{4,0},{5,1},{6,2},{7,3},{8,12},{9,13},{10,... | collective-permute-start | bytes 1179656 | tf_op jit(solution)/shard_map/ppermute | solution.py:14
  30.0 10.6 %collective-permute-start.11 = (bf16[64,3072]{1,0:T(8,128)(2,1)S(1)}, bf16[64,3072]{1,0:T(8,128)(2,1)S(1)}, u32[]{:S(2)}, u32[]{:S(2)}) collective-permute-start(bf16[64,3072]{1,0:T(8,128)(2,1)S(1)} %collective-permute-done.9), channel_id=1, source_target_pairs={{0,1},{1,0},{2,3},{3,2},{4,5},{5,4},{6,7},{7,6},{8,9},{9,8},{10,11... | collective-permute-start | bytes 1179656 | tf_op jit(solution)/shard_map/ppermute | solution.py:14
  32.1 9.1 %collective-permute-start.12 = (bf16[64,3072]{1,0:T(8,128)(2,1)S(1)}, bf16[64,3072]{1,0:T(8,128)(2,1)S(1)}, u32[]{:S(2)}, u32[]{:S(2)}) collective-permute-start(bf16[64,3072]{1,0:T(8,128)(2,1)S(1)} %collective-permute-done.10), channel_id=1, source_target_pairs={{0,1},{1,0},{2,3},{3,2},{4,5},{5,4},{6,7},{7,6},{8,9},{9,8},{10,11... | collective-permute-start | bytes 1179656 | tf_op jit(solution)/shard_map/ppermute | solution.py:14
  109.9 14.2 %collective-permute-start.13 = (bf16[128,3072]{1,0:T(8,128)(2,1)S(1)}, bf16[128,3072]{1,0:T(8,128)(2,1)S(1)}, u32[]{:S(2)}, u32[]{:S(2)}) collective-permute-start(bf16[128,3072]{1,0:T(8,128)(2,1)S(1)} %get-tuple-element.34), channel_id=1, source_target_pairs={{0,1},{1,0},{2,3},{3,2},{4,5},{5,4},{6,7},{7,6},{8,9},{9,8},{10,11... | collective-permute-start | bytes 2359304 | tf_op jit(solution)/shard_map/ppermute | solution.py:14
  110.0 14.1 %collective-permute-start.15 = (bf16[128,3072]{1,0:T(8,128)(2,1)S(1)}, bf16[128,3072]{1,0:T(8,128)(2,1)S(1)}, u32[]{:S(2)}, u32[]{:S(2)}) collective-permute-start(bf16[128,3072]{1,0:T(8,128)(2,1)S(1)} %get-tuple-element.35), channel_id=1, source_target_pairs={{0,1},{1,0},{2,3},{3,2},{4,5},{5,4},{6,7},{7,6},{8,9},{9,8},{10,11... | collective-permute-start | bytes 2359304 | tf_op jit(solution)/shard_map/ppermute | solution.py:14
  126.7 12.7 %collective-permute-start.14 = (bf16[64,3072]{1,0:T(8,128)(2,1)S(1)}, bf16[64,3072]{1,0:T(8,128)(2,1)S(1)}, u32[]{:S(2)}, u32[]{:S(2)}) collective-permute-start(bf16[64,3072]{1,0:T(8,128)(2,1)S(1)} %slice.152), channel_id=1, source_target_pairs={{0,4},{1,5},{2,6},{3,7},{4,0},{5,1},{6,2},{7,3},{8,12},{9,13},{10,... | collective-permute-start | bytes 1179656 | tf_op jit(solution)/shard_map/ppermute | solution.py:14
  127.0 18.7 %collective-permute-start.16 = (bf16[64,3072]{1,0:T(8,128)(2,1)S(1)}, bf16[64,3072]{1,0:T(8,128)(2,1)S(1)}, u32[]{:S(2)}, u32[]{:S(2)}) collective-permute-start(bf16[64,3072]{1,0:T(8,128)(2,1)S(1)} %get-tuple-element.36), channel_id=1, source_target_pairs={{0,2},{1,3},{2,0},{3,1},{4,6},{5,7},{6,4},{7,5},{8,10},{9,11},{10,... | collective-permute-start | bytes 1179656 | tf_op jit(solution)/shard_map/ppermute | solution.py:14
  128.8 18.6 %collective-permute-start.17 = (bf16[64,3072]{1,0:T(8,128)(2,1)S(1)}, bf16[64,3072]{1,0:T(8,128)(2,1)S(1)}, u32[]{:S(2)}, u32[]{:S(2)}) collective-permute-start(bf16[64,3072]{1,0:T(8,128)(2,1)S(1)} %get-tuple-element.37), channel_id=1, source_target_pairs={{0,6},{1,7},{2,4},{3,5},{4,2},{5,3},{6,0},{7,1},{8,14},{9,15},{10,... | collective-permute-start | bytes 1179656 | tf_op jit(solution)/shard_map/ppermute | solution.py:14
  147.7 66.3 %collective-permute-start.18 = (bf16[16,3072]{1,0:T(8,128)(2,1)S(1)}, bf16[16,3072]{1,0:T(8,128)(2,1)S(1)}, u32[]{:S(2)}, u32[]{:S(2)}) collective-permute-start(bf16[16,3072]{1,0:T(8,128)(2,1)S(1)} %get-tuple-element.42), channel_id=1, source_target_pairs={{0,8},{1,9},{2,10},{3,11},{4,12},{5,13},{6,14},{7,15},{8,0},{9,1},... | collective-permute-start | bytes 294920 | tf_op jit(solution)/shard_map/ppermute | solution.py:14
  149.4 66.0 %collective-permute-start.20 = (bf16[16,3072]{1,0:T(8,128)(2,1)S(1)}, bf16[16,3072]{1,0:T(8,128)(2,1)S(1)}, u32[]{:S(2)}, u32[]{:S(2)}) collective-permute-start(bf16[16,3072]{1,0:T(8,128)(2,1)S(1)} %get-tuple-element.43), channel_id=1, source_target_pairs={{0,24},{1,25},{2,26},{3,27},{4,28},{5,29},{6,30},{7,31},{8,16},{9,... | collective-permute-start | bytes 294920 | tf_op jit(solution)/shard_map/ppermute | solution.py:14
  151.8 63.5 %collective-permute-start.19 = (bf16[16,3072]{1,0:T(8,128)(2,1)S(1)}, bf16[16,3072]{1,0:T(8,128)(2,1)S(1)}, u32[]{:S(2)}, u32[]{:S(2)}) collective-permute-start(bf16[16,3072]{1,0:T(8,128)(2,1)S(1)} %get-tuple-element.44), channel_id=1, source_target_pairs={{0,16},{1,17},{2,18},{3,19},{4,20},{5,21},{6,22},{7,23},{8,24},{9,... | collective-permute-start | bytes 294920 | tf_op jit(solution)/shard_map/ppermute | solution.py:14
  151.9 65.4 %collective-permute-start.25 = (f32[4,128]{1,0:T(4,128)S(1)}, f32[4,128]{1,0:T(4,128)S(1)}, u32[]{:S(2)}, u32[]{:S(2)}) collective-permute-start(f32[4,128]{1,0:T(4,128)S(1)} %get-tuple-element.47), channel_id=1, source_target_pairs={{0,1},{1,0},{2,3},{3,2},{4,5},{5,4},{6,7},{7,6},{8,9},{9,8},{10,11... | collective-permute-start | bytes 6152 | tf_op jit(solution)/shard_map/ppermute | solution.py:14
  152.0 65.4 %collective-permute-start.27 = (f32[4,128]{1,0:T(4,128)S(1)}, f32[4,128]{1,0:T(4,128)S(1)}, u32[]{:S(2)}, u32[]{:S(2)}) collective-permute-start(f32[4,128]{1,0:T(4,128)S(1)} %get-tuple-element.48), channel_id=1, source_target_pairs={{0,3},{1,2},{2,1},{3,0},{4,7},{5,6},{6,5},{7,4},{8,11},{9,10},{10,... | collective-permute-start | bytes 6152 | tf_op jit(solution)/shard_map/ppermute | solution.py:14
  217.6 10.1 %collective-permute-start.22 = (bf16[16,3072]{1,0:T(8,128)(2,1)S(1)}, bf16[16,3072]{1,0:T(8,128)(2,1)S(1)}, u32[]{:S(2)}, u32[]{:S(2)}) collective-permute-start(bf16[16,3072]{1,0:T(8,128)(2,1)S(1)} %get-tuple-element.27), channel_id=1, source_target_pairs={{0,16},{1,17},{2,18},{3,19},{4,20},{5,21},{6,22},{7,23},{8,24},{9,... | collective-permute-start | bytes 294920 | tf_op jit(solution)/shard_map/ppermute | solution.py:14
  220.4 7.4 %collective-permute-start.23 = (bf16[16,3072]{1,0:T(8,128)(2,1)S(1)}, bf16[16,3072]{1,0:T(8,128)(2,1)S(1)}, u32[]{:S(2)}, u32[]{:S(2)}) collective-permute-start(bf16[16,3072]{1,0:T(8,128)(2,1)S(1)} %get-tuple-element.27), channel_id=1, source_target_pairs={{0,24},{1,25},{2,26},{3,27},{4,28},{5,29},{6,30},{7,31},{8,16},{9,... | collective-permute-start | bytes 294920 | tf_op jit(solution)/shard_map/ppermute | solution.py:14
  227.8 23.1 %collective-permute-start.24 = (bf16[64,3072]{1,0:T(8,128)(2,1)S(1)}, bf16[64,3072]{1,0:T(8,128)(2,1)S(1)}, u32[]{:S(2)}, u32[]{:S(2)}) collective-permute-start(bf16[64,3072]{1,0:T(8,128)(2,1)S(1)} %constant_dynamic-update-slice_fusion), channel_id=1, source_target_pairs={{0,4},{1,5},{2,6},{3,7},{4,0},{5,1},{6,2},{7,3},{8,12},{9,13},{10,... | collective-permute-start | bytes 1179656 | tf_op jit(solution)/shard_map/ppermute | solution.py:14
  (9 other events, 63.7 us)

commit v2 on v1

v2 whole, which is shorter than its diff:
```python
import functools
import jax
import jax.numpy as jnp
from jax import lax
from jax.experimental import pallas as pl
from jax.experimental.pallas import tpu as pltpu
from jax.sharding import PartitionSpec as P

EXPERTS = 16
CAP = 40
AXES = ("fsdp", "expert")
CORE, Y, X, Z = 1, 2, 4, 8
LANES = 128
NARROW, WIDE = jnp.bfloat16, jnp.float32
MIB = 1 << 20
TN = (((0,), (0,)), ((), ()))
NT = (((1,), (1,)), ((), ()))
NN = (((1,), (0,)), ((), ()))


def mm(a, b, dims):
    return lax.dot_general(a, b, dims, preferred_element_type=WIDE)


def swap(value, mask):
    size = lax.axis_size("fsdp") * lax.axis_size("expert")
    return lax.ppermute(value, AXES, [(i, i ^ mask) for i in range(size)])


def is_small():
    return lax.axis_size("fsdp") == 8 and lax.axis_size("expert") == 4


def own_order(rows):
    x_index = lax.axis_index("fsdp") % 2
    half = rows.shape[0] // 2
    return jnp.where(x_index == 0, rows, jnp.concatenate([rows[half:], rows[:half]], axis=0))


def spread(rows):
    half = rows.shape[0] // 2
    other_core = swap(rows, CORE)
    near = swap(rows[:half], Y)
    far = swap(near, X)
    return [rows, other_core, near, far, swap(near, CORE), swap(far, CORE)]


def collect(keep, send):
    fsdp = lax.axis_index("fsdp")
    x_index, z_index = fsdp % 2, fsdp // 2
    rows = keep.shape[0] // 2
    half = rows // 2
    total = keep + swap(send, CORE).astype(WIDE)
    own, other = total[:rows], total[rows:]
    total = own[:half]
    total = total + swap(own[half:].astype(NARROW), X).astype(WIDE)
    total = total + swap(other[:half].astype(NARROW), Y).astype(WIDE)
    total = total + swap(other[half:].astype(NARROW), X | Y).astype(WIDE)
    quarter = half // 4

    def chunk(array, index):
        return lax.dynamic_slice_in_dim(array, index * quarter, quarter, axis=0)

    final = chunk(total, z_index)
    packed = total.astype(NARROW)
    for step in (1, 2, 3):
        final = final + swap(chunk(packed, z_index ^ step), step * Z).astype(WIDE)
    final = final.astype(NARROW)
    near = jnp.zeros((half, final.shape[1]), NARROW)
    near = lax.dynamic_update_slice_in_dim(near, final, z_index * quarter, axis=0)
    for step in (1, 2, 3):
        near = lax.dynamic_update_slice_in_dim(near, swap(final, step * Z), (z_index ^ step) * quarter, axis=0)
    far = swap(near, X)
    return jnp.where(
        x_index == 0, jnp.concatenate([near, far], axis=0), jnp.concatenate([far, near], axis=0)
    )


def collect_gates(parts):
    total = parts[0]
    for block, mask in ((1, CORE), (2, Y), (3, CORE | Y)):
        total = total + swap(parts[block], mask)
    half = total.shape[1] // 2
    x_index = lax.axis_index("fsdp") % 2
    total = jnp.where(
        x_index == 0, total, jnp.concatenate([total[:, half:], total[:, :half]], axis=1)
    )
    for mask in (X, Z, 2 * Z):
        total = total + swap(total, mask)
    return total


def tiled_view(weight):
    rows, experts, columns = weight.shape
    return weight.reshape(rows, experts, columns // LANES, LANES).transpose(0, 2, 1, 3)


def split_body(w_ref, out_ref, wide_ref):
    rows, tiles, experts, _ = w_ref.shape
    stride = tiles * experts
    wide_ref[...] = w_ref.reshape(rows * stride, LANES)[...].astype(WIDE)
    for expert in range(experts):
        for tile in range(tiles):
            part = wide_ref[pl.ds(tile * experts + expert, rows, stride), :]
            out_ref[expert, :, tile * LANES : (tile + 1) * LANES] = part.astype(NARROW)


def split_experts(view, start, rows, block):
    _, tiles, experts, _ = view.shape
    columns = tiles * LANES
    first = start // block
    return pl.pallas_call(
        split_body,
        out_shape=jax.ShapeDtypeStruct((experts, rows, columns), NARROW),
        grid=(rows // block,),
        in_specs=[pl.BlockSpec((block, tiles, experts, LANES), lambda i: (first + i, 0, 0, 0))],
        out_specs=pl.BlockSpec((experts, block, columns), lambda i: (0, i, 0)),
        scratch_shapes=[pltpu.VMEM((block * tiles * experts, LANES), WIDE)],
        compiler_params=pltpu.CompilerParams(vmem_limit_bytes=24 * MIB),
        cost_estimate=pl.CostEstimate(
            flops=0, bytes_accessed=4 * experts * rows * columns, transcendentals=0
        ),
        name="split_experts",
    )(view)


def forward_body(
    target_ref, gate_ref, x_ref, g_ref, w0_ref, w1_ref, v0_ref, v1_ref,
    xs_ref, gs_ref, gp_ref, ag_ref, gate_out_ref, keep_ref, send_ref,
    back_ref, pick_ref,
):
    step = pl.program_id(0)
    slots, model_width = xs_ref.shape[1:]
    tokens = x_ref.shape[0]
    half_d = w0_ref.shape[1]
    columns = 512
    target = target_ref[0]
    choose = lax.broadcasted_iota(jnp.int32, (slots, tokens), 0) == target
    pick = choose.astype(WIDE).astype(NARROW)
    rows = pl.ds(pl.multiple_of(step * slots, slots), slots)
    pick_ref[rows, :] = pick
    gate = jnp.sum(jnp.where(choose, gate_ref[0], 0.0), axis=1, keepdims=True)
    for begin in range(0, model_width, columns):
        part = slice(begin, begin + columns)
        xs_ref[0, :, part] = mm(pick, x_ref[:, part], NN).astype(NARROW)
        gs_ref[0, :, part] = mm(pick, g_ref[:, part], NN).astype(NARROW)
    pre_act = mm(xs_ref[0, :, :half_d], w0_ref[0], NN) + mm(xs_ref[0, :, half_d:], w1_ref[0], NN)
    squash = jax.nn.sigmoid(pre_act)
    active = pre_act * squash
    slope = gate * squash * (1.0 + pre_act * (1.0 - squash))
    ag_ref[0] = (gate * active).astype(NARROW)
    half_f = v0_ref.shape[1]
    gate_part = jnp.zeros((slots, 1), WIDE)
    for begin, v_ref in ((0, v0_ref), (half_f, v1_ref)):
        upstream = mm(gs_ref[0], v_ref[0], NT)
        part = slice(begin, begin + half_f)
        gate_part = gate_part + jnp.sum(active[:, part] * upstream, axis=1, keepdims=True)
        gp_ref[0, :, part] = (slope[:, part] * upstream).astype(NARROW)
    gate_out_ref[0] = jnp.sum(jnp.where(choose, gate_part, 0.0), axis=0, keepdims=True)
    for begin in range(0, model_width, columns):
        w_ref = w0_ref if begin < half_d else w1_ref
        inner = begin % half_d
        back = mm(gp_ref[0], w_ref[0, inner : inner + columns, :], NT)
        back_ref[rows, begin : begin + columns] = back.astype(NARROW)

    @pl.when(step == pl.num_programs(0) - 1)
    def _():
        quarter = tokens // 4
        for begin in range(0, model_width, columns):
            part = slice(begin, begin + columns)
            summed = mm(pick_ref[...], back_ref[:, part], TN)
            for pair in range(2):
                lower = 2 * pair * quarter
                keep_ref[pair * quarter : (pair + 1) * quarter, part] = summed[lower : lower + quarter]
                send_ref[pair * quarter : (pair + 1) * quarter, part] = summed[
                    lower + quarter : lower + 2 * quarter
                ].astype(NARROW)


def forward(target, gate_tok, x_rows, g_rows, w_parts, v_parts):
    experts, _, tokens = target.shape
    model_width = x_rows.shape[1]
    hidden = w_parts[0].shape[2]
    slots = tokens // 128 * CAP
    whole = lambda i: (0, 0)
    expert = lambda i: (i, 0, 0)
    one = pl.Buffered(1)
    flops = 2 * slots * experts * model_width * (3 * hidden + 3 * tokens)
    weight_specs = [
        pl.BlockSpec((1,) + part.shape[1:], expert) for part in (*w_parts, *v_parts)
    ]
    return pl.pallas_call(
        forward_body,
        out_shape=[
            jax.ShapeDtypeStruct((experts, slots, model_width), NARROW),
            jax.ShapeDtypeStruct((experts, slots, model_width), NARROW),
            jax.ShapeDtypeStruct((experts, slots, hidden), NARROW),
            jax.ShapeDtypeStruct((experts, slots, hidden), NARROW),
            jax.ShapeDtypeStruct((experts, 1, tokens), WIDE),
            jax.ShapeDtypeStruct((tokens // 2, model_width), WIDE),
            jax.ShapeDtypeStruct((tokens // 2, model_width), NARROW),
        ],
        grid=(experts,),
        in_specs=[
            pl.BlockSpec((1, 1, tokens), expert),
            pl.BlockSpec((1, 1, tokens), expert),
            pl.BlockSpec((tokens, model_width), whole, pipeline_mode=one),
            pl.BlockSpec((tokens, model_width), whole, pipeline_mode=one),
            *weight_specs,
        ],
        out_specs=[
            pl.BlockSpec((1, slots, model_width), expert),
            pl.BlockSpec((1, slots, model_width), expert),
            pl.BlockSpec((1, slots, hidden), expert),
            pl.BlockSpec((1, slots, hidden), expert),
            pl.BlockSpec((1, 1, tokens), expert),
            pl.BlockSpec((tokens // 2, model_width), whole, pipeline_mode=one),
            pl.BlockSpec((tokens // 2, model_width), whole, pipeline_mode=one),
        ],
        scratch_shapes=[
            pltpu.VMEM((experts * slots, model_width), NARROW),
            pltpu.VMEM((experts * slots, tokens), NARROW),
        ],
        compiler_params=pltpu.CompilerParams(vmem_limit_bytes=58 * MIB),
        cost_estimate=pl.CostEstimate(
            flops=flops, bytes_accessed=4 * experts * model_width * hidden, transcendentals=0
        ),
        name="forward",
    )(target, gate_tok, x_rows, g_rows, *w_parts, *v_parts)


def outer_body(a_ref, b_ref, _, out_ref, wide_ref):
    rows, tiles, experts, _ = out_ref.shape
    stride = wide_ref.shape[0] // rows
    group = stride // experts
    out = out_ref.reshape(rows, tiles * experts, LANES)
    for begin in range(0, tiles, group):
        for expert in range(experts):
            part = mm(a_ref[expert], b_ref[expert, :, begin * LANES : (begin + group) * LANES], TN)
            for tile in range(group):
                wide_ref[pl.ds(tile * experts + expert, rows, stride), :] = part[
                    :, tile * LANES : (tile + 1) * LANES
                ]
        out[:, begin * experts : (begin + group) * experts, :] = (
            wide_ref[...].astype(NARROW).reshape(rows, stride, LANES)
        )


def outer(a, b, holder, start, count, block, group):
    experts, slots, total = a.shape
    columns = b.shape[2]
    tiles = columns // LANES
    first = start // block
    shape = (total, tiles, experts, LANES)
    inputs = [a, b]
    specs = [
        pl.BlockSpec((experts, slots, block), lambda i: (0, 0, first + i)),
        pl.BlockSpec((experts, slots, columns), lambda i: (0, 0, 0), pipeline_mode=pl.Buffered(1)),
    ]
    body, aliases = outer_body, {2: 0}
    if holder is None:
        body, aliases = (lambda a_ref, b_ref, *rest: outer_body(a_ref, b_ref, None, *rest)), {}
    else:
        inputs.append(holder)
        specs.append(pl.BlockSpec(memory_space=pl.ANY))
    return pl.pallas_call(
        body,
        out_shape=jax.ShapeDtypeStruct(shape, NARROW),
        grid=(count // block,),
        in_specs=specs,
        out_specs=pl.BlockSpec((block, tiles, experts, LANES), lambda i: (first + i, 0, 0, 0)),
        scratch_shapes=[pltpu.VMEM((block * group * experts, LANES), WIDE)],
        input_output_aliases=aliases,
        compiler_params=pltpu.CompilerParams(vmem_limit_bytes=32 * MIB),
        cost_estimate=pl.CostEstimate(
            flops=2 * experts * slots * count * columns,
            bytes_accessed=4 * experts * count * columns,
            transcendentals=0,
        ),
        name="weight_gradient",
    )(*inputs)


def stored_view(tiled):
    rows, tiles, experts, _ = tiled.shape
    return tiled.transpose(0, 2, 1, 3).reshape(rows, experts, tiles * LANES)


def local(tokens, cotangent, expert_ids, gate_values, w_in, w_out):
    if not is_small():
        return local_general(tokens, cotangent, expert_ids, gate_values, w_in, w_out)
    tok_rows, model_width = tokens.shape
    top_count = expert_ids.shape[1]
    local_count = w_in.shape[1]
    hidden = w_in.shape[2]
    first = lax.axis_index("expert") * local_count
    meta = own_order(jnp.concatenate([expert_ids.astype(WIDE), gate_values.astype(WIDE)], axis=1)).T
    meta = jnp.stack([meta, swap(meta, CORE), swap(meta, Y), swap(meta, CORE | Y)])
    x_rows = jnp.concatenate(spread(own_order(tokens)), axis=0)
    g_rows = jnp.concatenate(spread(own_order(cotangent)), axis=0)
    w_view, v_view = tiled_view(w_in), tiled_view(w_out)
    w_parts = [split_experts(w_view, s, model_width // 2, 128) for s in (0, model_width // 2)]
    v_parts = [split_experts(v_view, s, hidden // 2, 32) for s in (0, hidden // 2)]

    ids, gates = meta[:, :top_count].astype(jnp.int32), meta[:, top_count:]
    blocks = ids.shape[0]
    names = first + jnp.arange(local_count, dtype=jnp.int32)
    named = ids[:, None] == names[None, :, None, None]
    hit = jnp.any(named, axis=2)
    gate_tok = jnp.sum(jnp.where(named, gates[:, None], 0.0), axis=2)
    earlier = jnp.tril(jnp.ones((tok_rows, tok_rows), WIDE), -1)
    position = jnp.einsum("tu,blu->blt", earlier, hit.astype(WIDE)).astype(jnp.int32)
    base = jnp.arange(blocks, dtype=jnp.int32)[:, None, None] * CAP
    target = jnp.where(hit, base + position, -1)

    def by_expert(value):
        return jnp.swapaxes(value, 0, 1).reshape(local_count, 1, blocks * tok_rows)

    xs, gs, gp, ag, gate_out, keep, send = forward(
        by_expert(target), by_expert(gate_tok), x_rows, g_rows, w_parts, v_parts
    )
    gate_out = jnp.swapaxes(gate_out.reshape(local_count, blocks, tok_rows), 0, 1)
    gate_back = jnp.sum(jnp.where(named, gate_out[:, :, None], 0.0), axis=1)
    grad_gates = collect_gates(gate_back).T.astype(NARROW)
    grad_tokens = collect(keep, send)
    grad_in = outer(xs, gp, None, 0, model_width // 2, 128, 6)
    grad_in = outer(xs, gp, grad_in, model_width // 2, model_width // 2, 128, 6)
    grad_out = outer(ag, gs, None, 0, hidden // 2, 128, 4)
    grad_out = outer(ag, gs, grad_out, hidden // 2, hidden // 2, 128, 4)
    return (grad_tokens, grad_gates, stored_view(grad_in), stored_view(grad_out))


def local_general(tokens, cotangent, expert_ids, gate_values, w_in, w_out):
    tok_rows, model_width = tokens.shape
    local_count = w_in.shape[1]
    first = lax.axis_index("expert") * local_count
    gather = functools.partial(lax.all_gather, axis_name="expert", axis=0)
    ids, gates = gather(expert_ids), gather(gate_values).astype(WIDE)
    x_blocks, g_blocks = gather(tokens), gather(cotangent)
    blocks = ids.shape[0]
    names = first + jnp.arange(local_count, dtype=jnp.int32)
    named = ids[:, None] == names[None, :, None, None]
    hit = jnp.any(named, axis=3)
    gate_tok = jnp.sum(jnp.where(named, gates[:, None], 0.0), axis=3)
    earlier = jnp.tril(jnp.ones((tok_rows, tok_rows), WIDE), -1)
    position = jnp.einsum("tu,blu->blt", earlier, hit.astype(WIDE)).astype(jnp.int32)
    slots = jnp.arange(CAP, dtype=jnp.int32)
    choose = hit[:, :, None] & (position[:, :, None] == slots[None, None, :, None])
    pick = choose.astype(NARROW)
    slot_x = jnp.einsum("blst,btd->lbsd", pick, x_blocks, preferred_element_type=WIDE).astype(NARROW)
    slot_g = jnp.einsum("blst,btd->lbsd", pick, g_blocks, preferred_element_type=WIDE).astype(NARROW)
    gate_slot = jnp.sum(jnp.where(choose, gate_tok[:, :, None], 0.0), axis=3)
    rows = blocks * CAP
    slot_x = slot_x.reshape(local_count, rows, model_width)
    slot_g = slot_g.reshape(local_count, rows, model_width)
    gate_slot = jnp.swapaxes(gate_slot, 0, 1).reshape(local_count, rows, 1)
    pre_act = jnp.einsum("lrd,dlf->lrf", slot_x, w_in, preferred_element_type=WIDE)
    upstream = jnp.einsum("lrd,fld->lrf", slot_g, w_out, preferred_element_type=WIDE)
    squash = jax.nn.sigmoid(pre_act)
    active = pre_act * squash
    gate_part = jnp.sum(active * upstream, axis=-1)
    act_gated = (gate_slot * active).astype(NARROW)
    grad_pre = (gate_slot * squash * (1.0 + pre_act * (1.0 - squash)) * upstream).astype(NARROW)
    gate_part = jnp.swapaxes(gate_part.reshape(local_count, blocks, CAP), 0, 1)
    gate_tok = jnp.sum(jnp.where(choose, gate_part[..., None], 0.0), axis=2)
    gate_back = jnp.sum(jnp.where(named, gate_tok[..., None], 0.0), axis=1)
    part_x = jnp.einsum("lrf,dlf->lrd", grad_pre, w_in, preferred_element_type=WIDE)
    part_x = part_x.astype(NARROW).reshape(local_count, blocks, CAP, model_width)
    token_part = jnp.einsum("blst,lbsd->btd", pick, part_x, preferred_element_type=WIDE)
    scatter = functools.partial(lax.psum_scatter, axis_name="expert", scatter_dimension=0)
    grad_tokens = lax.psum(scatter(token_part), "fsdp").astype(NARROW)
    grad_gates = lax.psum(scatter(gate_back), "fsdp").astype(NARROW)
    grad_in = jnp.einsum("lrd,lrf->dlf", slot_x, grad_pre, preferred_element_type=WIDE).astype(NARROW)
    grad_out = jnp.einsum("lrf,lrd->fld", act_gated, slot_g, preferred_element_type=WIDE).astype(NARROW)
    return (grad_tokens, grad_gates, grad_in, grad_out)


def solution(mesh):
    return jax.shard_map(
        local,
        mesh=mesh,
        in_specs=(
            P("expert", None),
            P("expert", None),
            P("expert", None),
            P("expert", None),
            P(None, "expert", "fsdp"),
            P("fsdp", "expert", None),
        ),
        out_specs=(
            P("expert", None),
            P("expert", None),
            P(None, "expert", "fsdp"),
            P("fsdp", "expert", None),
        ),
        check_vma=False,
    )
```

time: 254 us -> 251 us (0.988)
  Pallas kernels: 0 us -> 126 us
  matrix products: 86.3 us -> 0.21 us
  local copies, waits for them, and re-layouts: 67.3 us -> 42.6 us
  blocking collectives: 21.3 us -> 0 us
  waiting for transfers between devices: 39.8 us -> 45.2 us
    pallas_call x0 -> x9, Pallas kernels: none -> 126 us  [the longest x4 48.7 us: split_experts(): pl.pallas_call(split_body, out_shape=jax.ShapeDtypeStruct((experts, rows,...]
    dot_general x10 -> x1, matrix products: 86.3 us -> 0.21 us  [local(): jnp.einsum('tu,blu->blt', earlier, hit.astype(WIDE)).astype(jnp.int32)]
    unnamed x12 -> x36, local copies, waits for them, and re-layouts: 62.1 us -> 37.5 us
    psum x1 -> x0, blocking collectives: 21.3 us -> none  [local(): grad_gates = lax.psum(gates_own, 'fsdp').T.astype(narrow)]
    ppermute x28 -> x30, waiting for transfers between devices: 39.8 us -> 45.2 us  [swap(): return lax.ppermute(value, AXES, [(i, i ^ mask) for i in range(size)])]
    unnamed x0 -> x2, other arithmetic: none -> 3.45 us
    ppermute x28 -> x30, starting transfers between devices: 24.8 us -> 26.6 us  [swap(): return lax.ppermute(value, AXES, [(i, i ^ mask) for i in range(size)])]
  transfers between devices with their start and end apart: 28 -> 30, of which waited for: 8 -> 10; matrix products, arithmetic and copies ran while one was open for 36% -> 7% of each run, Pallas kernels for 0% -> 38%
where the time goes in v2:
time: 251 us
  Pallas kernels  126 us (50%)
  waiting for transfers between devices  45.2 us (18%)
  local copies, waits for them, and re-layouts  42.6 us (17%)
  starting transfers between devices  26.6 us (11%)
  other arithmetic  9.55 us (4%)
    pallas_call x4, Pallas kernels, split_experts(): pl.pallas_call(split_body, out_shape=jax.ShapeDtypeStruct((experts, rows,...  48.7 us
    pallas_call x4, Pallas kernels, outer(): pl.pallas_call(body, out_shape=jax.ShapeDtypeStruct(shape, NARROW), grid=...  45.8 us
    ppermute x30, waiting for transfers between devices, swap(): return lax.ppermute(value, AXES, [(i, i ^ mask) for i in range(size)])  45.2 us
    unnamed x36, local copies, waits for them, and re-layouts  37.5 us
    pallas_call x1, Pallas kernels, forward(): pl.pallas_call(forward_body, out_shape=[jax.ShapeDtypeStruct((experts, sl...  31.2 us
    ppermute x30, starting transfers between devices, swap(): return lax.ppermute(value, AXES, [(i, i ^ mask) for i in range(size)])  26.6 us
  transfers between devices with their start and end apart: 30, of which 10 were waited for; matrix products, arithmetic and copies ran while one was open for 7% of the time, Pallas kernels for 38%

profile of v2, /device:TPU:0, one launch (start us, length us, event | category | flops | bytes accessed | tf_op | source)
XLA Modules:
  0.0 250.7 jit_solution(9967188085904660479)
XLA Ops:
  2.3 3.0 %collective-permute-start.1 = (f32[8,128]{1,0:T(8,128)S(1)}, f32[8,128]{1,0:T(8,128)S(1)}, u32[]{:S(2)}, u32[]{:S(2)}) collective-permute-start(f32[8,128]{1,0:T(8,128)S(1)} %bitcast.53), channel_id=1, source_target_pairs={{0,2},{1,3},{2,0},{3,1},{4,6},{5,7},{6,4},{7,5},{8,10},{9,11},{10,... | collective-permute-start | bytes 12296 | tf_op jit(solution)/shard_map/ppermute | solution.py:27
  13.4 6.4 %copy-done = bf16[3072,4,768]{2,1,0:T(4,128)(2,1)S(1)} copy-done((bf16[3072,4,768]{2,1,0:T(4,128)(2,1)S(1)}, bf16[3072,4,768]{2,1,0:T(4,128)(2,1)}, u32[]{:S(2)}) %copy-start) | copy-done | bytes 18874392
  19.7 8.6 %split_experts.5.w1_ref = bf16[4,1536,768]{2,1,0:T(8,128)(2,1)S(1)} custom-call(bf16[3072,6,4,128]{3,2,1,0:T(4,128)(2,1)S(1)} %bitcast.46), custom_call_target="tpu_custom_call" | custom-call | bytes 18874368 | tf_op jit(solution)/shard_map/split_experts/pallas_call | solution.py:112
  28.3 3.7 %copy-done.4 = bf16[4,1536,768]{2,1,0:T(8,128)(2,1)} copy-done((bf16[4,1536,768]{2,1,0:T(8,128)(2,1)}, bf16[4,1536,768]{2,1,0:T(8,128)(2,1)S(1)}, u32[]{:S(2)}) %copy-start.4) | copy-done | bytes 9437208
  32.1 8.6 %split_experts.4.w0_ref = bf16[4,1536,768]{2,1,0:T(8,128)(2,1)S(1)} custom-call(bf16[3072,6,4,128]{3,2,1,0:T(4,128)(2,1)S(1)} %bitcast.47), custom_call_target="tpu_custom_call" | custom-call | bytes 18874368 | tf_op jit(solution)/shard_map/split_experts/pallas_call | solution.py:112
  40.7 3.7 %copy-done.5 = bf16[4,1536,768]{2,1,0:T(8,128)(2,1)} copy-done((bf16[4,1536,768]{2,1,0:T(8,128)(2,1)}, bf16[4,1536,768]{2,1,0:T(8,128)(2,1)S(1)}, u32[]{:S(2)}) %copy-start.5) | copy-done | bytes 9437208
  44.4 6.4 %copy-done.1 = bf16[768,4,3072]{2,1,0:T(4,128)(2,1)S(1)} copy-done((bf16[768,4,3072]{2,1,0:T(4,128)(2,1)S(1)}, bf16[768,4,3072]{2,1,0:T(4,128)(2,1)}, u32[]{:S(2)}) %copy-start.1) | copy-done | bytes 18874392
  50.8 15.8 %split_experts.7.v1_ref = bf16[4,384,3072]{2,1,0:T(8,128)(2,1)S(1)} custom-call(bf16[768,24,4,128]{3,2,1,0:T(4,128)(2,1)S(1)} %bitcast.48), custom_call_target="tpu_custom_call" | custom-call | bytes 18874368 | tf_op jit(solution)/shard_map/split_experts/pallas_call | solution.py:112
  66.6 3.7 %copy-done.6 = bf16[4,384,3072]{2,1,0:T(8,128)(2,1)} copy-done((bf16[4,384,3072]{2,1,0:T(8,128)(2,1)}, bf16[4,384,3072]{2,1,0:T(8,128)(2,1)S(1)}, u32[]{:S(2)}) %copy-start.6) | copy-done | bytes 9437208
  70.2 15.8 %split_experts.6.v0_ref = bf16[4,384,3072]{2,1,0:T(8,128)(2,1)S(1)} custom-call(bf16[768,24,4,128]{3,2,1,0:T(4,128)(2,1)S(1)} %bitcast.49), custom_call_target="tpu_custom_call" | custom-call | bytes 18874368 | tf_op jit(solution)/shard_map/split_experts/pallas_call | solution.py:112
  86.0 3.6 %copy-done.7 = bf16[4,384,3072]{2,1,0:T(8,128)(2,1)} copy-done((bf16[4,384,3072]{2,1,0:T(8,128)(2,1)}, bf16[4,384,3072]{2,1,0:T(8,128)(2,1)S(1)}, u32[]{:S(2)}) %copy-start.7) | copy-done | bytes 9437208
  94.6 8.3 %collective-permute-done.10 = bf16[64,3072]{1,0:T(8,128)(2,1)S(1)} collective-permute-done((bf16[64,3072]{1,0:T(8,128)(2,1)S(1)}, bf16[64,3072]{1,0:T(8,128)(2,1)S(1)}, u32[]{:S(2)}, u32[]{:S(2)}) %collective-permute-start.10) | collective-permute-done | bytes 393248 | tf_op jit(solution)/shard_map/ppermute | solution.py:27
  103.4 7.0 %collective-permute-done.5 = bf16[64,3072]{1,0:T(8,128)(2,1)S(1)} collective-permute-done((bf16[64,3072]{1,0:T(8,128)(2,1)S(1)}, bf16[64,3072]{1,0:T(8,128)(2,1)S(1)}, u32[]{:S(2)}, u32[]{:S(2)}) %collective-permute-start.5) | collective-permute-done | bytes 393248 | tf_op jit(solution)/shard_map/ppermute | solution.py:27
  118.7 31.2 %forward.1 = (bf16[4,160,3072]{2,1,0:T(8,128)(2,1)}, bf16[4,160,3072]{2,1,0:T(8,128)(2,1)}, bf16[4,160,768]{2,1,0:T(8,128)(2,1)}, bf16[4,160,768]{2,1,0:T(8,128)...) custom-call(s32[4,1,512]{2,1,0:T(1,128)} %bitcast.58, f32[4,1,512]{2,1,0:T(1,128)} %bitcast.57, ...), custom_call_target="tpu_custom_call" | custom-call | flops 15099494400 | bytes 37748736 | tf_op jit(solution)/shard_map/forward/pallas_call | solution.py:192
  156.8 10.7 %weight_gradient.4._ = bf16[3072,6,4,128]{3,2,1,0:T(4,128)(2,1)} custom-call(bf16[4,160,3072]{2,1,0:T(8,128)(2,1)S(1)} %copy-done.3, bf16[4,160,768]{2,1,0:T(8,128)(2,1)S(1)} %copy-done.9), custom_call_target="tpu_custom_call" | custom-call | flops 1509949440 | bytes 18874368 | tf_op jit(solution)/shard_map/weight_gradient/pallas_call | solution.py:266
  169.1 2.6 %collective-permute-start.16 = (bf16[64,3072]{1,0:T(8,128)(2,1)S(1)}, bf16[64,3072]{1,0:T(8,128)(2,1)S(1)}, u32[]{:S(2)}, u32[]{:S(2)}) collective-permute-start(bf16[64,3072]{1,0:T(8,128)(2,1)S(1)} %get-tuple-element.29), channel_id=1, source_target_pairs={{0,6},{1,7},{2,4},{3,5},{4,2},{5,3},{6,0},{7,1},{8,14},{9,15},{10,... | collective-permute-start | bytes 1179656 | tf_op jit(solution)/shard_map/ppermute | solution.py:27
  171.9 8.4 %collective-permute-done.14 = bf16[64,3072]{1,0:T(8,128)(2,1)S(1)} collective-permute-done((bf16[64,3072]{1,0:T(8,128)(2,1)S(1)}, bf16[64,3072]{1,0:T(8,128)(2,1)S(1)}, u32[]{:S(2)}, u32[]{:S(2)}) %collective-permute-start.14) | collective-permute-done | bytes 393248 | tf_op jit(solution)/shard_map/ppermute | solution.py:27
  180.3 8.7 %collective-permute-done.16 = bf16[64,3072]{1,0:T(8,128)(2,1)S(1)} collective-permute-done((bf16[64,3072]{1,0:T(8,128)(2,1)S(1)}, bf16[64,3072]{1,0:T(8,128)(2,1)S(1)}, u32[]{:S(2)}, u32[]{:S(2)}) %collective-permute-start.16) | collective-permute-done | bytes 393248 | tf_op jit(solution)/shard_map/ppermute | solution.py:27
  196.2 2.6 %collective-permute-done.19 = bf16[16,3072]{1,0:T(8,128)(2,1)S(1)} collective-permute-done((bf16[16,3072]{1,0:T(8,128)(2,1)S(1)}, bf16[16,3072]{1,0:T(8,128)(2,1)S(1)}, u32[]{:S(2)}, u32[]{:S(2)}) %collective-permute-start.19) | collective-permute-done | bytes 98336 | tf_op jit(solution)/shard_map/ppermute | solution.py:27
  198.8 2.7 %collective-permute-done.18 = bf16[16,3072]{1,0:T(8,128)(2,1)S(1)} collective-permute-done((bf16[16,3072]{1,0:T(8,128)(2,1)S(1)}, bf16[16,3072]{1,0:T(8,128)(2,1)S(1)}, u32[]{:S(2)}, u32[]{:S(2)}) %collective-permute-start.18) | collective-permute-done | bytes 98336 | tf_op jit(solution)/shard_map/ppermute | solution.py:27
  201.7 10.7 %weight_gradient.5 = bf16[3072,6,4,128]{3,2,1,0:T(4,128)(2,1)} custom-call(bf16[4,160,3072]{2,1,0:T(8,128)(2,1)S(1)} %copy-done.3, bf16[4,160,768]{2,1,0:T(8,128)(2,1)S(1)} %copy-done.9, bf16[3072,6,4,128]{3,2,1,0:T(4,128)(2,1)} %weight_gradient.4._), custom_call_target="tpu_custom_call", output_to_operand_aliasing={{}: (2, {})} | custom-call | flops 1509949440 | bytes 18874368 | tf_op jit(solution)/shard_map/weight_gradient/pallas_call | solution.py:266
  217.0 3.9 %collective-permute-done.21 = bf16[16,3072]{1,0:T(8,128)(2,1)S(1)} collective-permute-done((bf16[16,3072]{1,0:T(8,128)(2,1)S(1)}, bf16[16,3072]{1,0:T(8,128)(2,1)S(1)}, u32[]{:S(2)}, u32[]{:S(2)}) %collective-permute-start.21) | collective-permute-done | bytes 98336 | tf_op jit(solution)/shard_map/ppermute | solution.py:27
  222.6 12.2 %weight_gradient.6._ = bf16[768,24,4,128]{3,2,1,0:T(4,128)(2,1)} custom-call(bf16[4,160,768]{2,1,0:T(8,128)(2,1)S(1)} %copy-done.8, bf16[4,160,3072]{2,1,0:T(8,128)(2,1)S(1)} %copy-done.2), custom_call_target="tpu_custom_call" | custom-call | flops 1509949440 | bytes 18874368 | tf_op jit(solution)/shard_map/weight_gradient/pallas_call | solution.py:266
  236.9 12.2 %weight_gradient.7 = bf16[768,24,4,128]{3,2,1,0:T(4,128)(2,1)} custom-call(bf16[4,160,768]{2,1,0:T(8,128)(2,1)S(1)} %copy-done.8, bf16[4,160,3072]{2,1,0:T(8,128)(2,1)S(1)} %copy-done.2, bf16[768,24,4,128]{3,2,1,0:T(4,128)(2,1)} %weight_gradient.6._), custom_call_target="tpu_custom_call", output_to_operand_aliasing={{}: (2, {})} | custom-call | flops 1509949440 | bytes 18874368 | tf_op jit(solution)/shard_map/weight_gradient/pallas_call | solution.py:266
  (123 shorter events, 49.4 us)
Async XLA Ops:
  2.3 87.4 %collective-permute-start.1 = (f32[8,128]{1,0:T(8,128)S(1)}, f32[8,128]{1,0:T(8,128)S(1)}, u32[]{:S(2)}, u32[]{:S(2)}) collective-permute-start(f32[8,128]{1,0:T(8,128)S(1)} %bitcast.53), channel_id=1, source_target_pairs={{0,2},{1,3},{2,0},{3,1},{4,6},{5,7},{6,4},{7,5},{8,10},{9,11},{10,... | collective-permute-start | bytes 12296 | tf_op jit(solution)/shard_map/ppermute | solution.py:27
  5.2 84.4 %collective-permute-start = (f32[8,128]{1,0:T(8,128)S(1)}, f32[8,128]{1,0:T(8,128)S(1)}, u32[]{:S(2)}, u32[]{:S(2)}) collective-permute-start(f32[8,128]{1,0:T(8,128)S(1)} %bitcast.54), channel_id=1, source_target_pairs={{0,1},{1,0},{2,3},{3,2},{4,5},{5,4},{6,7},{7,6},{8,9},{9,8},{10,11... | collective-permute-start | bytes 12296 | tf_op jit(solution)/shard_map/ppermute | solution.py:27
  5.2 84.9 %collective-permute-start.2 = (f32[8,128]{1,0:T(8,128)S(1)}, f32[8,128]{1,0:T(8,128)}, u32[]{:S(2)}, u32[]{:S(2)}) collective-permute-start(f32[8,128]{1,0:T(8,128)S(1)} %bitcast.55), channel_id=1, source_target_pairs={{0,3},{1,2},{2,1},{3,0},{4,7},{5,6},{6,5},{7,4},{8,11},{9,10},{10,... | collective-permute-start | bytes 12296 | tf_op jit(solution)/shard_map/ppermute | solution.py:27
  8.9 81.9 %collective-permute-start.9 = (bf16[64,3072]{1,0:T(8,128)(2,1)S(1)}, bf16[64,3072]{1,0:T(8,128)(2,1)S(1)}, u32[]{:S(2)}, u32[]{:S(2)}) collective-permute-start(bf16[64,3072]{1,0:T(8,128)(2,1)S(1)} %slice.92), channel_id=1, source_target_pairs={{0,2},{1,3},{2,0},{3,1},{4,6},{5,7},{6,4},{7,5},{8,10},{9,11},{10,... | collective-permute-start | bytes 1179656 | tf_op jit(solution)/shard_map/ppermute | solution.py:27
  12.2 79.6 %collective-permute-start.4 = (bf16[64,3072]{1,0:T(8,128)(2,1)S(1)}, bf16[64,3072]{1,0:T(8,128)(2,1)S(1)}, u32[]{:S(2)}, u32[]{:S(2)}) collective-permute-start(bf16[64,3072]{1,0:T(8,128)(2,1)S(1)} %slice.91), channel_id=1, source_target_pairs={{0,2},{1,3},{2,0},{3,1},{4,6},{5,7},{6,4},{7,5},{8,10},{9,11},{10,... | collective-permute-start | bytes 1179656 | tf_op jit(solution)/shard_map/ppermute | solution.py:27
  89.7 13.3 %collective-permute-start.8 = (bf16[128,3072]{1,0:T(8,128)(2,1)S(1)}, bf16[128,3072]{1,0:T(8,128)(2,1)S(1)}, u32[]{:S(2)}, u32[]{:S(2)}) collective-permute-start(bf16[128,3072]{1,0:T(8,128)(2,1)S(1)} %get-tuple-element.25), channel_id=1, source_target_pairs={{0,1},{1,0},{2,3},{3,2},{4,5},{5,4},{6,7},{7,6},{8,9},{9,8},{10,11... | collective-permute-start | bytes 2359304 | tf_op jit(solution)/shard_map/ppermute | solution.py:27
  89.7 23.3 %collective-permute-start.3 = (bf16[128,3072]{1,0:T(8,128)(2,1)S(1)}, bf16[128,3072]{1,0:T(8,128)(2,1)S(1)}, u32[]{:S(2)}, u32[]{:S(2)}) collective-permute-start(bf16[128,3072]{1,0:T(8,128)(2,1)S(1)} %get-tuple-element.27), channel_id=1, source_target_pairs={{0,1},{1,0},{2,3},{3,2},{4,5},{5,4},{6,7},{7,6},{8,9},{9,8},{10,11... | collective-permute-start | bytes 2359304 | tf_op jit(solution)/shard_map/ppermute | solution.py:27
  90.9 12.0 %collective-permute-start.10 = (bf16[64,3072]{1,0:T(8,128)(2,1)S(1)}, bf16[64,3072]{1,0:T(8,128)(2,1)S(1)}, u32[]{:S(2)}, u32[]{:S(2)}) collective-permute-start(bf16[64,3072]{1,0:T(8,128)(2,1)S(1)} %collective-permute-done.9), channel_id=1, source_target_pairs={{0,4},{1,5},{2,6},{3,7},{4,0},{5,1},{6,2},{7,3},{8,12},{9,13},{10,... | collective-permute-start | bytes 1179656 | tf_op jit(solution)/shard_map/ppermute | solution.py:27
  91.7 18.7 %collective-permute-start.5 = (bf16[64,3072]{1,0:T(8,128)(2,1)S(1)}, bf16[64,3072]{1,0:T(8,128)(2,1)S(1)}, u32[]{:S(2)}, u32[]{:S(2)}) collective-permute-start(bf16[64,3072]{1,0:T(8,128)(2,1)S(1)} %collective-permute-done.4), channel_id=1, source_target_pairs={{0,4},{1,5},{2,6},{3,7},{4,0},{5,1},{6,2},{7,3},{8,12},{9,13},{10,... | collective-permute-start | bytes 1179656 | tf_op jit(solution)/shard_map/ppermute | solution.py:27
  94.6 20.9 %collective-permute-start.11 = (bf16[64,3072]{1,0:T(8,128)(2,1)S(1)}, bf16[64,3072]{1,0:T(8,128)(2,1)S(1)}, u32[]{:S(2)}, u32[]{:S(2)}) collective-permute-start(bf16[64,3072]{1,0:T(8,128)(2,1)S(1)} %collective-permute-done.9), channel_id=1, source_target_pairs={{0,1},{1,0},{2,3},{3,2},{4,5},{5,4},{6,7},{7,6},{8,9},{9,8},{10,11... | collective-permute-start | bytes 1179656 | tf_op jit(solution)/shard_map/ppermute | solution.py:27
  102.9 13.4 %collective-permute-start.6 = (bf16[64,3072]{1,0:T(8,128)(2,1)S(1)}, bf16[64,3072]{1,0:T(8,128)(2,1)S(1)}, u32[]{:S(2)}, u32[]{:S(2)}) collective-permute-start(bf16[64,3072]{1,0:T(8,128)(2,1)S(1)} %collective-permute-done.4), channel_id=1, source_target_pairs={{0,1},{1,0},{2,3},{3,2},{4,5},{5,4},{6,7},{7,6},{8,9},{9,8},{10,11... | collective-permute-start | bytes 1179656 | tf_op jit(solution)/shard_map/ppermute | solution.py:27
  102.9 14.2 %collective-permute-start.12 = (bf16[64,3072]{1,0:T(8,128)(2,1)S(1)}, bf16[64,3072]{1,0:T(8,128)(2,1)S(1)}, u32[]{:S(2)}, u32[]{:S(2)}) collective-permute-start(bf16[64,3072]{1,0:T(8,128)(2,1)S(1)} %collective-permute-done.10), channel_id=1, source_target_pairs={{0,1},{1,0},{2,3},{3,2},{4,5},{5,4},{6,7},{7,6},{8,9},{9,8},{10,11... | collective-permute-start | bytes 1179656 | tf_op jit(solution)/shard_map/ppermute | solution.py:27
  149.9 17.6 %collective-permute-start.13 = (bf16[256,3072]{1,0:T(8,128)(2,1)}, bf16[256,3072]{1,0:T(8,128)(2,1)S(1)}, u32[]{:S(2)}, u32[]{:S(2)}) collective-permute-start(bf16[256,3072]{1,0:T(8,128)(2,1)} %get-tuple-element.12), channel_id=1, source_target_pairs={{0,1},{1,0},{2,3},{3,2},{4,5},{5,4},{6,7},{7,6},{8,9},{9,8},{10,11... | collective-permute-start | bytes 4718600 | tf_op jit(solution)/shard_map/ppermute | solution.py:27
  151.2 20.5 %collective-permute-start.24 = (f32[4,128]{1,0:T(4,128)S(1)}, f32[4,128]{1,0:T(4,128)S(1)}, u32[]{:S(2)}, u32[]{:S(2)}) collective-permute-start(f32[4,128]{1,0:T(4,128)S(1)} %get-tuple-element.40), channel_id=1, source_target_pairs={{0,1},{1,0},{2,3},{3,2},{4,5},{5,4},{6,7},{7,6},{8,9},{9,8},{10,11... | collective-permute-start | bytes 6152 | tf_op jit(solution)/shard_map/ppermute | solution.py:27
  151.4 20.4 %collective-permute-start.26 = (f32[4,128]{1,0:T(4,128)S(1)}, f32[4,128]{1,0:T(4,128)S(1)}, u32[]{:S(2)}, u32[]{:S(2)}) collective-permute-start(f32[4,128]{1,0:T(4,128)S(1)} %get-tuple-element.41), channel_id=1, source_target_pairs={{0,3},{1,2},{2,1},{3,0},{4,7},{5,6},{6,5},{7,4},{8,11},{9,10},{10,... | collective-permute-start | bytes 6152 | tf_op jit(solution)/shard_map/ppermute | solution.py:27
  153.4 18.4 %collective-permute-start.25 = (f32[4,128]{1,0:T(4,128)S(1)}, f32[4,128]{1,0:T(4,128)S(1)}, u32[]{:S(2)}, u32[]{:S(2)}) collective-permute-start(f32[4,128]{1,0:T(4,128)S(1)} %get-tuple-element.42), channel_id=1, source_target_pairs={{0,2},{1,3},{2,0},{3,1},{4,6},{5,7},{6,4},{7,5},{8,10},{9,11},{10,... | collective-permute-start | bytes 6152 | tf_op jit(solution)/shard_map/ppermute | solution.py:27
  168.2 12.0 %collective-permute-start.14 = (bf16[64,3072]{1,0:T(8,128)(2,1)S(1)}, bf16[64,3072]{1,0:T(8,128)(2,1)S(1)}, u32[]{:S(2)}, u32[]{:S(2)}) collective-permute-start(bf16[64,3072]{1,0:T(8,128)(2,1)S(1)} %get-tuple-element.28), channel_id=1, source_target_pairs={{0,4},{1,5},{2,6},{3,7},{4,0},{5,1},{6,2},{7,3},{8,12},{9,13},{10,... | collective-permute-start | bytes 1179656 | tf_op jit(solution)/shard_map/ppermute | solution.py:27
  169.1 19.9 %collective-permute-start.16 = (bf16[64,3072]{1,0:T(8,128)(2,1)S(1)}, bf16[64,3072]{1,0:T(8,128)(2,1)S(1)}, u32[]{:S(2)}, u32[]{:S(2)}) collective-permute-start(bf16[64,3072]{1,0:T(8,128)(2,1)S(1)} %get-tuple-element.29), channel_id=1, source_target_pairs={{0,6},{1,7},{2,4},{3,5},{4,2},{5,3},{6,0},{7,1},{8,14},{9,15},{10,... | collective-permute-start | bytes 1179656 | tf_op jit(solution)/shard_map/ppermute | solution.py:27
  171.7 18.7 %collective-permute-start.15 = (bf16[64,3072]{1,0:T(8,128)(2,1)S(1)}, bf16[64,3072]{1,0:T(8,128)(2,1)S(1)}, u32[]{:S(2)}, u32[]{:S(2)}) collective-permute-start(bf16[64,3072]{1,0:T(8,128)(2,1)S(1)} %get-tuple-element.30), channel_id=1, source_target_pairs={{0,2},{1,3},{2,0},{3,1},{4,6},{5,7},{6,4},{7,5},{8,10},{9,11},{10,... | collective-permute-start | bytes 1179656 | tf_op jit(solution)/shard_map/ppermute | solution.py:27
  194.9 17.5 %collective-permute-start.27 = (f32[4,128]{1,0:T(4,128)S(1)}, f32[4,128]{1,0:T(4,128)S(1)}, u32[]{:S(2)}, u32[]{:S(2)}) collective-permute-start(f32[4,128]{1,0:T(4,128)S(1)} %maximum_select_fusion.4), channel_id=1, source_target_pairs={{0,4},{1,5},{2,6},{3,7},{4,0},{5,1},{6,2},{7,3},{8,12},{9,13},{10,... | collective-permute-start | bytes 6152 | tf_op jit(solution)/shard_map/ppermute | solution.py:27
  201.6 15.4 %collective-permute-start.20 = (bf16[16,3072]{1,0:T(8,128)(2,1)S(1)}, bf16[16,3072]{1,0:T(8,128)(2,1)S(1)}, u32[]{:S(2)}, u32[]{:S(2)}) collective-permute-start(bf16[16,3072]{1,0:T(8,128)(2,1)S(1)} %get-tuple-element.19), channel_id=1, source_target_pairs={{0,8},{1,9},{2,10},{3,11},{4,12},{5,13},{6,14},{7,15},{8,0},{9,1},... | collective-permute-start | bytes 294920 | tf_op jit(solution)/shard_map/ppermute | solution.py:27
  212.4 22.4 %collective-permute-start.28 = (f32[4,128]{1,0:T(4,128)S(1)}, f32[4,128]{1,0:T(4,128)S(1)}, u32[]{:S(2)}, u32[]{:S(2)}) collective-permute-start(f32[4,128]{1,0:T(4,128)S(1)} %add.114), channel_id=1, source_target_pairs={{0,8},{1,9},{2,10},{3,11},{4,12},{5,13},{6,14},{7,15},{8,0},{9,1},... | collective-permute-start | bytes 6152 | tf_op jit(solution)/shard_map/ppermute | solution.py:27
  222.2 27.5 %collective-permute-start.23 = (bf16[64,3072]{1,0:T(8,128)(2,1)S(1)}, bf16[64,3072]{1,0:T(8,128)(2,1)S(1)}, u32[]{:S(2)}, u32[]{:S(2)}) collective-permute-start(bf16[64,3072]{1,0:T(8,128)(2,1)S(1)} %constant_dynamic-update-slice_fusion.12), channel_id=1, source_target_pairs={{0,4},{1,5},{2,6},{3,7},{4,0},{5,1},{6,2},{7,3},{8,12},{9,13},{10,... | collective-permute-start | bytes 1179656 | tf_op jit(solution)/shard_map/ppermute | solution.py:27
  234.8 14.3 %collective-permute-start.29 = (f32[4,128]{1,0:T(4,128)S(1)}, f32[4,128]{1,0:T(4,128)S(1)}, u32[]{:S(2)}, u32[]{:S(2)}) collective-permute-start(f32[4,128]{1,0:T(4,128)S(1)} %add.115), channel_id=1, source_target_pairs={{0,16},{1,17},{2,18},{3,19},{4,20},{5,21},{6,22},{7,23},{8,24},{9,... | collective-permute-start | bytes 6152 | tf_op jit(solution)/shard_map/ppermute | solution.py:27
  (20 other events, 180.3 us)

commit v3 on v2

--- a/solution.py
+++ b/solution.py
@@ -33,58 +33,103 @@
 
 def own_order(rows):
     x_index = lax.axis_index("fsdp") % 2
-    half = rows.shape[0] // 2
-    return jnp.where(x_index == 0, rows, jnp.concatenate([rows[half:], rows[:half]], axis=0))
-
-
-def spread(rows):
-    half = rows.shape[0] // 2
-    other_core = swap(rows, CORE)
-    near = swap(rows[:half], Y)
-    far = swap(near, X)
-    return [rows, other_core, near, far, swap(near, CORE), swap(far, CORE)]
-
-
-def collect(keep, send):
-    fsdp = lax.axis_index("fsdp")
-    x_index, z_index = fsdp % 2, fsdp // 2
-    rows = keep.shape[0] // 2
-    half = rows // 2
-    total = keep + swap(send, CORE).astype(WIDE)
-    own, other = total[:rows], total[rows:]
-    total = own[:half]
-    total = total + swap(own[half:].astype(NARROW), X).astype(WIDE)
-    total = total + swap(other[:half].astype(NARROW), Y).astype(WIDE)
-    total = total + swap(other[half:].astype(NARROW), X | Y).astype(WIDE)
-    quarter = half // 4
-
-    def chunk(array, index):
-        return lax.dynamic_slice_in_dim(array, index * quarter, quarter, axis=0)
-
-    final = chunk(total, z_index)
-    packed = total.astype(NARROW)
-    for step in (1, 2, 3):
-        final = final + swap(chunk(packed, z_index ^ step), step * Z).astype(WIDE)
-    final = final.astype(NARROW)
-    near = jnp.zeros((half, final.shape[1]), NARROW)
-    near = lax.dynamic_update_slice_in_dim(near, final, z_index * quarter, axis=0)
-    for step in (1, 2, 3):
-        near = lax.dynamic_update_slice_in_dim(near, swap(final, step * Z), (z_index ^ step) * quarter, axis=0)
-    far = swap(near, X)
+    half = rows.shape[-1] // 2
     return jnp.where(
-        x_index == 0, jnp.concatenate([near, far], axis=0), jnp.concatenate([far, near], axis=0)
-    )
+        x_index == 0, rows, jnp.concatenate([rows[..., half:], rows[..., :half]], axis=-1)
+    )
+
+
+ANY = pl.BlockSpec(memory_space=pl.ANY)
+FLAG = jax.ShapeDtypeStruct((8, LANES), WIDE)
+
+
+def small_call(body, place, inputs, after, outs, name):
+    given = len(inputs)
+
+    def run(place_ref, *refs):
+        body(place_ref, refs[:given], refs[given + len(after) :])
+
+    def whole(array):
+        return pl.BlockSpec(array.shape, lambda: (0,) * len(array.shape))
+
+    return pl.pallas_call(
+        run,
+        out_shape=outs,
+        in_specs=[pl.BlockSpec(memory_space=pltpu.SMEM)]
+        + [whole(array) for array in inputs]
+        + [ANY] * len(after),
+        out_specs=[whole(out) for out in outs],
+        compiler_params=pltpu.CompilerParams(vmem_limit_bytes=32 * MIB),
+        cost_estimate=pl.CostEstimate(flops=0, bytes_accessed=1 << 20, transcendentals=0),
+        name=name,
+    )(place, *inputs, *after)
+
+
+def hold(arrays, after):
+    count = len(arrays)
+    return pl.pallas_call(
+        lambda *refs: None,
+        out_shape=[jax.ShapeDtypeStruct(array.shape, array.dtype) for array in arrays],
+        in_specs=[ANY] * (count + len(after)),
+        out_specs=[ANY] * count,
+        input_output_aliases={number: number for number in range(count)},
+        cost_estimate=pl.CostEstimate(flops=0, bytes_accessed=1 << 18, transcendentals=0),
+        name="hold",
+    )(*arrays, *after)
+
+
+def at(index, size):
+    return pl.ds(pl.multiple_of(index * size, size), size)
+
+
+def first_sum(place_ref, ins, outs):
+    keep_ref, got_ref = ins
+    mine_ref, x_ref, y_ref, xy_ref = outs
+    half = mine_ref.shape[0]
+    x_index = place_ref[0]
+
+    def total(rows):
+        return keep_ref[rows, :] + got_ref[rows, :].astype(WIDE)
+
+    mine_ref[...] = total(at(x_index, half))
+    x_ref[...] = total(at(1 - x_index, half)).astype(NARROW)
+    y_ref[...] = total(slice(2 * half, 3 * half)).astype(NARROW)
+    xy_ref[...] = total(slice(3 * half, 4 * half)).astype(NARROW)
+
+
+def second_sum(place_ref, ins, outs):
+    mine_ref, x_ref, y_ref, xy_ref = ins
+    quarter = outs[0].shape[0]
+    z_index = place_ref[1]
+    for step in range(4):
+        rows = at(z_index ^ step, quarter)
+        total = mine_ref[rows, :] + x_ref[rows, :].astype(WIDE)
+        total = total + (y_ref[rows, :].astype(WIDE) + xy_ref[rows, :].astype(WIDE))
+        outs[step][...] = total.astype(outs[step].dtype)
+
+
+def third_sum(place_ref, ins, outs):
+    total = ins[0][...]
+    for got in ins[1:]:
+        total = total + got[...].astype(WIDE)
+    outs[0][...] = total.astype(NARROW)
+
+
+def join_z(place_ref, ins, outs):
+    quarter = ins[0].shape[0]
+    for step in range(4):
+        outs[0][at(place_ref[1] ^ step, quarter), :] = ins[step][...]
+
+
+def join_x(place_ref, ins, outs):
+    half = ins[0].shape[0]
+    for step in range(2):
+        outs[0][at(place_ref[0] ^ step, half), :] = ins[step][...]
 
 
 def collect_gates(parts):
-    total = parts[0]
-    for block, mask in ((1, CORE), (2, Y), (3, CORE | Y)):
-        total = total + swap(parts[block], mask)
-    half = total.shape[1] // 2
-    x_index = lax.axis_index("fsdp") % 2
-    total = jnp.where(
-        x_index == 0, total, jnp.concatenate([total[:, half:], total[:, :half]], axis=1)
-    )
+    total = parts[0] + swap(parts[1], CORE)
+    total = total + own_order(swap(parts[2], Y) + swap(parts[3], CORE | Y))
     for mask in (X, Z, 2 * Z):
         total = total + swap(total, mask)
     return total
@@ -95,41 +140,74 @@
     return weight.reshape(rows, experts, columns // LANES, LANES).transpose(0, 2, 1, 3)
 
 
-def split_body(w_ref, out_ref, wide_ref):
+def odd_tiles(rows):
+    tiles = -(-rows // 8)
+    return 8 * (tiles + 1 - tiles % 2)
+
+
+def split_body(w_ref, *refs):
+    out_ref, flag_ref, wide_ref = refs[-3:]
+    flag_ref[...] = jnp.zeros_like(flag_ref)
     rows, tiles, experts, _ = w_ref.shape
-    stride = tiles * experts
-    wide_ref[...] = w_ref.reshape(rows * stride, LANES)[...].astype(WIDE)
+    held = tiles * experts
+    stride = wide_ref.shape[1]
+    wide_ref[:, :held, :] = w_ref.reshape(rows, held, LANES)[...].astype(WIDE)
+    flat = wide_ref.reshape(rows * stride, LANES)
     for expert in range(experts):
         for tile in range(tiles):
-            part = wide_ref[pl.ds(tile * experts + expert, rows, stride), :]
+            part = flat[pl.ds(tile * experts + expert, rows, stride), :]
             out_ref[expert, :, tile * LANES : (tile + 1) * LANES] = part.astype(NARROW)
 
 
-def split_experts(view, start, rows, block):
+def split_experts(view, start, rows, block, after):
     _, tiles, experts, _ = view.shape
     columns = tiles * LANES
     first = start // block
     return pl.pallas_call(
         split_body,
-        out_shape=jax.ShapeDtypeStruct((experts, rows, columns), NARROW),
+        out_shape=[jax.ShapeDtypeStruct((experts, rows, columns), NARROW), FLAG],
         grid=(rows // block,),
-        in_specs=[pl.BlockSpec((block, tiles, experts, LANES), lambda i: (first + i, 0, 0, 0))],
-        out_specs=pl.BlockSpec((experts, block, columns), lambda i: (0, i, 0)),
-        scratch_shapes=[pltpu.VMEM((block * tiles * experts, LANES), WIDE)],
-        compiler_params=pltpu.CompilerParams(vmem_limit_bytes=24 * MIB),
+        in_specs=[
+            pl.BlockSpec((block, tiles, experts, LANES), lambda i: (first + i, 0, 0, 0)),
+            *[ANY] * len(after),
+        ],
+        out_specs=[
+            pl.BlockSpec((experts, block, columns), lambda i: (0, i, 0)),
+            pl.BlockSpec(FLAG.shape, lambda i: (0, 0)),
+        ],
+        scratch_shapes=[pltpu.VMEM((block, odd_tiles(tiles * experts), LANES), WIDE)],
+        compiler_params=pltpu.CompilerParams(vmem_limit_bytes=56 * MIB),
         cost_estimate=pl.CostEstimate(
             flops=0, bytes_accessed=4 * experts * rows * columns, transcendentals=0
         ),
         name="split_experts",
-    )(view)
+    )(view, *after)
 
 
 def forward_body(
-    target_ref, gate_ref, x_ref, g_ref, w0_ref, w1_ref, v0_ref, v1_ref,
-    xs_ref, gs_ref, gp_ref, ag_ref, gate_out_ref, keep_ref, send_ref,
-    back_ref, pick_ref,
+    target_ref, gate_ref, w0_ref, w1_ref, v0_ref, v1_ref, *refs
 ):
     step = pl.program_id(0)
+    pieces = refs[:-12]
+    xs_ref, gs_ref, gp_ref, ag_ref, gate_out_ref, keep_ref, send_ref = refs[-12:-5]
+    x_ref, g_ref, back_ref, pick_ref, sem = refs[-5:]
+
+    @pl.when(step == 0)
+    def _():
+        copies = []
+        for number, whole in enumerate((x_ref, g_ref)):
+            begin = 0
+            for piece in pieces[number * len(pieces) // 2 : (number + 1) * len(pieces) // 2]:
+                count = piece.shape[0]
+                copies.append(
+                    pltpu.make_async_copy(piece, whole.at[begin : begin + count], sem.at[len(copies)])
+                )
+                begin += count
+        for copy in copies:
+            copy.start()
+        for copy in copies:
+            copy.wait()
+
     slots, model_width = xs_ref.shape[1:]
     tokens = x_ref.shape[0]
     half_d = w0_ref.shape[1]
@@ -177,9 +255,9 @@
                 ].astype(NARROW)
 
 
-def forward(target, gate_tok, x_rows, g_rows, w_parts, v_parts):
+def forward(target, gate_tok, x_pieces, g_pieces, w_parts, v_parts):
     experts, _, tokens = target.shape
-    model_width = x_rows.shape[1]
+    model_width = x_pieces[0].shape[1]
     hidden = w_parts[0].shape[2]
     slots = tokens // 128 * CAP
     whole = lambda i: (0, 0)
@@ -204,9 +282,8 @@
         in_specs=[
             pl.BlockSpec((1, 1, tokens), expert),
             pl.BlockSpec((1, 1, tokens), expert),
-            pl.BlockSpec((tokens, model_width), whole, pipeline_mode=one),
-            pl.BlockSpec((tokens, model_width), whole, pipeline_mode=one),
             *weight_specs,
+            *[ANY] * (len(x_pieces) + len(g_pieces)),
         ],
         out_specs=[
             pl.BlockSpec((1, slots, model_width), expert),
@@ -218,67 +295,69 @@
             pl.BlockSpec((tokens // 2, model_width), whole, pipeline_mode=one),
         ],
         scratch_shapes=[
+            pltpu.VMEM((tokens, model_width), NARROW),
+            pltpu.VMEM((tokens, model_width), NARROW),
             pltpu.VMEM((experts * slots, model_width), NARROW),
             pltpu.VMEM((experts * slots, tokens), NARROW),
+            pltpu.SemaphoreType.DMA((len(x_pieces) + len(g_pieces),)),
         ],
         compiler_params=pltpu.CompilerParams(vmem_limit_bytes=58 * MIB),
         cost_estimate=pl.CostEstimate(
             flops=flops, bytes_accessed=4 * experts * model_width * hidden, transcendentals=0
         ),
         name="forward",
-    )(target, gate_tok, x_rows, g_rows, *w_parts, *v_parts)
-
-
-def outer_body(a_ref, b_ref, _, out_ref, wide_ref):
+    )(target, gate_tok, *w_parts, *v_parts, *x_pieces, *g_pieces)
+
+
+def outer_body(group, a_ref, b_ref, *refs):
+    out_ref, flag_ref, wide_ref = refs[-3:]
     rows, tiles, experts, _ = out_ref.shape
-    stride = wide_ref.shape[0] // rows
-    group = stride // experts
+    stride = wide_ref.shape[1]
+    held = group * experts
     out = out_ref.reshape(rows, tiles * experts, LANES)
+    flat = wide_ref.reshape(rows * stride, LANES)
     for begin in range(0, tiles, group):
         for expert in range(experts):
             part = mm(a_ref[expert], b_ref[expert, :, begin * LANES : (begin + group) * LANES], TN)
             for tile in range(group):
-                wide_ref[pl.ds(tile * experts + expert, rows, stride), :] = part[
+                flat[pl.ds(tile * experts + expert, rows, stride), :] = part[
                     :, tile * LANES : (tile + 1) * LANES
                 ]
-        out[:, begin * experts : (begin + group) * experts, :] = (
-            wide_ref[...].astype(NARROW).reshape(rows, stride, LANES)
-        )
-
-
-def outer(a, b, holder, start, count, block, group):
+        out[:, begin * experts : begin * experts + held, :] = wide_ref[:, :held, :].astype(NARROW)
+    flag_ref[...] = jnp.zeros_like(flag_ref)
+
+
+def outer(a, b, holder, start, count, block, group, after):
     experts, slots, total = a.shape
     columns = b.shape[2]
     tiles = columns // LANES
     first = start // block
-    shape = (total, tiles, experts, LANES)
-    inputs = [a, b]
-    specs = [
-        pl.BlockSpec((experts, slots, block), lambda i: (0, 0, first + i)),
-        pl.BlockSpec((experts, slots, columns), lambda i: (0, 0, 0), pipeline_mode=pl.Buffered(1)),
-    ]
-    body, aliases = outer_body, {2: 0}
-    if holder is None:
-        body, aliases = (lambda a_ref, b_ref, *rest: outer_body(a_ref, b_ref, None, *rest)), {}
-    else:
-        inputs.append(holder)
-        specs.append(pl.BlockSpec(memory_space=pl.ANY))
+    extra = list(after) if holder is None else [holder, *after]
     return pl.pallas_call(
-        body,
-        out_shape=jax.ShapeDtypeStruct(shape, NARROW),
+        functools.partial(outer_body, group),
+        out_shape=[jax.ShapeDtypeStruct((total, tiles, experts, LANES), NARROW), FLAG],
         grid=(count // block,),
-        in_specs=specs,
-        out_specs=pl.BlockSpec((block, tiles, experts, LANES), lambda i: (first + i, 0, 0, 0)),
-        scratch_shapes=[pltpu.VMEM((block * group * experts, LANES), WIDE)],
-        input_output_aliases=aliases,
-        compiler_params=pltpu.CompilerParams(vmem_limit_bytes=32 * MIB),
+        in_specs=[
+            pl.BlockSpec((experts, slots, block), lambda i: (0, 0, first + i)),
+            pl.BlockSpec(
+                (experts, slots, columns), lambda i: (0, 0, 0), pipeline_mode=pl.Buffered(1)
+            ),
+            *[ANY] * len(extra),
+        ],
+        out_specs=[
+            pl.BlockSpec((block, tiles, experts, LANES), lambda i: (first + i, 0, 0, 0)),
+            pl.BlockSpec(FLAG.shape, lambda i: (0, 0)),
+        ],
+        scratch_shapes=[pltpu.VMEM((block, odd_tiles(group * experts), LANES), WIDE)],
+        input_output_aliases={} if holder is None else {2: 0},
+        compiler_params=pltpu.CompilerParams(vmem_limit_bytes=40 * MIB),
         cost_estimate=pl.CostEstimate(
             flops=2 * experts * slots * count * columns,
             bytes_accessed=4 * experts * count * columns,
             transcendentals=0,
         ),
         name="weight_gradient",
-    )(*inputs)
+    )(a, b, *extra)
 
 
 def stored_view(tiled):
@@ -293,14 +372,34 @@
     top_count = expert_ids.shape[1]
     local_count = w_in.shape[1]
     hidden = w_in.shape[2]
+    half = tok_rows // 2
     first = lax.axis_index("expert") * local_count
-    meta = own_order(jnp.concatenate([expert_ids.astype(WIDE), gate_values.astype(WIDE)], axis=1)).T
-    meta = jnp.stack([meta, swap(meta, CORE), swap(meta, Y), swap(meta, CORE | Y)])
-    x_rows = jnp.concatenate(spread(own_order(tokens)), axis=0)
-    g_rows = jnp.concatenate(spread(own_order(cotangent)), axis=0)
+    fsdp = lax.axis_index("fsdp")
+    x_index = fsdp % 2
+    place = jnp.stack([x_index, fsdp // 2]).astype(jnp.int32)
+
+    meta = jnp.concatenate([expert_ids.astype(WIDE), gate_values.astype(WIDE)], axis=1).T
+    turned = own_order(meta)
+    meta = jnp.stack([meta, swap(meta, CORE), swap(turned, Y), swap(turned, CORE | Y)])
     w_view, v_view = tiled_view(w_in), tiled_view(w_out)
-    w_parts = [split_experts(w_view, s, model_width // 2, 128) for s in (0, model_width // 2)]
-    v_parts = [split_experts(v_view, s, hidden // 2, 32) for s in (0, hidden // 2)]
+    x_near = swap(lax.dynamic_slice_in_dim(tokens, x_index * half, half, axis=0), Y)
+    g_near = swap(lax.dynamic_slice_in_dim(cotangent, x_index * half, half, axis=0), Y)
+    x_core, g_core = swap(tokens, CORE), swap(cotangent, CORE)
+    w_low, flag = split_experts(w_view, 0, model_width // 2, 256, [])
+    (x_near,) = hold([x_near], [flag])
+    x_far = swap(x_near, X)
+    x_near_core = swap(x_near, CORE)
+    w_high, flag = split_experts(w_view, model_width // 2, model_width // 2, 256, [x_near])
+    x_far, g_near = hold([x_far, g_near], [flag])
+    g_far = swap(g_near, X)
+    g_near_core = swap(g_near, CORE)
+    x_far_core = swap(x_far, CORE)
+    v_low, flag = split_experts(v_view, 0, hidden // 2, 64, [x_far])
+    (g_far,) = hold([g_far], [flag])
+    g_far_core = swap(g_far, CORE)
+    v_high, _ = split_experts(v_view, hidden // 2, hidden // 2, 64, [g_far])
+    x_pieces = [tokens, x_core, x_near, x_far, x_near_core, x_far_core]
+    g_pieces = [cotangent, g_core, g_near, g_far, g_near_core, g_far_core]
 
     ids, gates = meta[:, :top_count].astype(jnp.int32), meta[:, top_count:]
     blocks = ids.shape[0]
@@ -317,16 +416,50 @@
         return jnp.swapaxes(value, 0, 1).reshape(local_count, 1, blocks * tok_rows)
 
     xs, gs, gp, ag, gate_out, keep, send = forward(
-        by_expert(target), by_expert(gate_tok), x_rows, g_rows, w_parts, v_parts
+        by_expert(target), by_expert(gate_tok), x_pieces, g_pieces, [w_low, w_high], [v_low, v_high]
     )
     gate_out = jnp.swapaxes(gate_out.reshape(local_count, blocks, tok_rows), 0, 1)
     gate_back = jnp.sum(jnp.where(named, gate_out[:, :, None], 0.0), axis=1)
     grad_gates = collect_gates(gate_back).T.astype(NARROW)
-    grad_tokens = collect(keep, send)
-    grad_in = outer(xs, gp, None, 0, model_width // 2, 128, 6)
-    grad_in = outer(xs, gp, grad_in, model_width // 2, model_width // 2, 128, 6)
-    grad_out = outer(ag, gs, None, 0, hidden // 2, 128, 4)
-    grad_out = outer(ag, gs, grad_out, hidden // 2, hidden // 2, 128, 4)
+
+    def shape(rows, dtype):
+        return jax.ShapeDtypeStruct((rows, model_width), dtype)
+
+    def in_part(holder, number, after):
+        rows = model_width // 4
+        return outer(xs, gp, holder, number * rows, rows, 128, 6, after)
+
+    def out_part(holder, number, after):
+        rows = hidden // 3
+        return outer(ag, gs, holder, number * rows, rows, 128, 8, after)
+
+    got = swap(send, CORE)
+    grad_in, flag = in_part(None, 0, [])
+    mine, *sends = small_call(
+        first_sum, place, [keep, got], [flag],
+        [shape(half, WIDE)] + [shape(half, NARROW)] * 3, "first_sum",
+    )
+    got = [swap(part, mask) for part, mask in zip(sends, (X, Y, X | Y))]
+    grad_in, flag = in_part(grad_in, 1, [mine])
+    grad_in, flag = in_part(grad_in, 2, [flag])
+    grad_in, flag = in_part(grad_in, 3, [flag])
+    mine, *sends = small_call(
+        second_sum, place, [mine, *got], [flag],
+        [shape(half // 4, WIDE)] + [shape(half // 4, NARROW)] * 3, "second_sum",
+    )
+    got = [swap(part, mask * Z) for part, mask in zip(sends, (1, 2, 3))]
+    grad_out, flag = out_part(None, 0, [mine])
+    (final,) = small_call(
+        third_sum, place, [mine, *got], [flag], [shape(half // 4, NARROW)], "third_sum"
+    )
+    got = [swap(final, mask * Z) for mask in (1, 2, 3)]
+    grad_out, flag = out_part(grad_out, 1, [final])
+    (near,) = small_call(join_z, place, [final, *got], [flag], [shape(half, NARROW)], "join_z")
+    far = swap(near, X)
+    grad_out, flag = out_part(grad_out, 2, [near])
+    (grad_tokens,) = small_call(
+        join_x, place, [near, far], [flag], [shape(tok_rows, NARROW)], "join_x"
+    )
     return (grad_tokens, grad_gates, stored_view(grad_in), stored_view(grad_out))
 
 

time: 251 us -> 191 us (0.76)
  local copies, waits for them, and re-layouts: 42.6 us -> 11.9 us
  waiting for transfers between devices: 45.2 us -> 16.1 us
  other arithmetic: 9.55 us -> 2.48 us
  Pallas kernels: 126 us -> 130 us
    unnamed x36 -> x28, local copies, waits for them, and re-layouts: 37.5 us -> 7.81 us
    ppermute x30, waiting for transfers between devices: 45.2 us -> 16.1 us  [swap(): return lax.ppermute(value, AXES, [(i, i ^ mask) for i in range(size)])]
    unnamed x2 -> x0, other arithmetic: 3.45 us -> none
    pallas_call x8 -> x19, Pallas kernels: 94.5 us -> 96.2 us  [the longest x4 48.4 us: split_experts(): pl.pallas_call(split_body, out_shape=[jax.ShapeDtypeStruct((experts, rows...]
  transfers between devices with their start and end apart: 30 -> 30, of which waited for: 10 -> 6; matrix products, arithmetic and copies ran while one was open for 7% -> 4% of each run, Pallas kernels for 38% -> 49%
where the time goes in v3:
time: 191 us; the launch traced here: 190 us
  Pallas kernels  130 us (68%)
  starting transfers between devices  29.1 us (15%)
  waiting for transfers between devices  16.1 us (8%)
  local copies, waits for them, and re-layouts  11.9 us (6%)
  other arithmetic  2.48 us (1%)
    pallas_call x4, Pallas kernels, split_experts(): pl.pallas_call(split_body, out_shape=[jax.ShapeDtypeStruct((experts, rows...  48.4 us
    pallas_call x7, Pallas kernels, outer(): pl.pallas_call(functools.partial(outer_body, group), out_shape=[jax.Shape...  43.6 us
    pallas_call x1, Pallas kernels, forward(): pl.pallas_call(forward_body, out_shape=[jax.ShapeDtypeStruct((experts, sl...  33.5 us
    ppermute x30, starting transfers between devices, swap(): return lax.ppermute(value, AXES, [(i, i ^ mask) for i in range(size)])  29.1 us
    ppermute x30, waiting for transfers between devices, swap(): return lax.ppermute(value, AXES, [(i, i ^ mask) for i in range(size)])  16.1 us
    unnamed x28, local copies, waits for them, and re-layouts  7.81 us
    pallas_call x5, Pallas kernels, small_call(): pl.pallas_call(run, out_shape=outs, in_specs=[pl.BlockSpec(memory_space=p...  4.27 us
  transfers between devices with their start and end apart: 30, of which 6 were waited for; matrix products, arithmetic and copies ran while one was open for 4% of the time, Pallas kernels for 49%

profile of v3, /device:TPU:0, one launch (start us, length us, event | category | flops | bytes accessed | tf_op | source)
XLA Modules:
  0.0 190.5 jit_solution(8457077055342010844)
XLA Ops:
  2.2 2.6 %collective-permute-start.3 = (bf16[64,3072]{1,0:T(8,128)(2,1)S(1)}, bf16[64,3072]{1,0:T(8,128)(2,1)S(1)}, u32[]{:S(2)}, u32[]{:S(2)}) collective-permute-start(bf16[64,3072]{1,0:T(8,128)(2,1)S(1)} %constant_dynamic-slice_fusion.1), channel_id=1, source_target_pairs={{0,2},{1,3},{2,0},{3,1},{4,6},{5,7},{6,4},{7,5},{8,10},{9,11},{10,... | collective-permute-start | bytes 1179656 | tf_op jit(solution)/shard_map/ppermute | solution.py:27
  7.3 12.2 %split_experts.4 = (bf16[4,1536,768]{2,1,0:T(8,128)(2,1)}, f32[8,128]{1,0:T(8,128)}) custom-call(bf16[3072,6,4,128]{3,2,1,0:T(4,128)(2,1)} %bitcast.51), custom_call_target="tpu_custom_call" | custom-call | bytes 18874368 | tf_op jit(solution)/shard_map/split_experts/pallas_call | solution.py:166
  20.2 2.0 %collective-permute-start.4 = (bf16[64,3072]{1,0:T(8,128)(2,1)}, bf16[64,3072]{1,0:T(8,128)(2,1)S(1)}, u32[]{:S(2)}, u32[]{:S(2)}) collective-permute-start(bf16[64,3072]{1,0:T(8,128)(2,1)} %hold.3.refs_0_.refs_2_), channel_id=1, source_target_pairs={{0,4},{1,5},{2,6},{3,7},{4,0},{5,1},{6,2},{7,3},{8,12},{9,13},{10,... | collective-permute-start | bytes 1179656 | tf_op jit(solution)/shard_map/ppermute | solution.py:27
  24.0 12.1 %split_experts.5 = (bf16[4,1536,768]{2,1,0:T(8,128)(2,1)}, f32[8,128]{1,0:T(8,128)}) custom-call(bf16[3072,6,4,128]{3,2,1,0:T(4,128)(2,1)} %bitcast.52, bf16[64,3072]{1,0:T(8,128)(2,1)} %hold.3.refs_0_.refs_2_), custom_call_target="tpu_custom_call" | custom-call | bytes 18874368 | tf_op jit(solution)/shard_map/split_experts/pallas_call | solution.py:166
  38.4 12.0 %split_experts.6 = (bf16[4,384,3072]{2,1,0:T(8,128)(2,1)}, f32[8,128]{1,0:T(8,128)}) custom-call(bf16[768,24,4,128]{3,2,1,0:T(4,128)(2,1)} %bitcast.53, bf16[64,3072]{1,0:T(8,128)(2,1)} %get-tuple-element.46.refs_0_.refs_3_), custom_call_target="tpu_custom_call" | custom-call | bytes 18874368 | tf_op jit(solution)/shard_map/split_experts/pallas_call | solution.py:166
  53.1 12.0 %split_experts.7 = (bf16[4,384,3072]{2,1,0:T(8,128)(2,1)}, f32[8,128]{1,0:T(8,128)}) custom-call(bf16[768,24,4,128]{3,2,1,0:T(4,128)(2,1)} %bitcast.54, bf16[64,3072]{1,0:T(8,128)(2,1)} %hold.5.refs_0_.refs_9_), custom_call_target="tpu_custom_call" | custom-call | bytes 18874368 | tf_op jit(solution)/shard_map/split_experts/pallas_call | solution.py:166
  66.0 33.5 %forward.1 = (bf16[4,160,3072]{2,1,0:T(8,128)(2,1)}, bf16[4,160,3072]{2,1,0:T(8,128)(2,1)}, bf16[4,160,768]{2,1,0:T(8,128)(2,1)}, bf16[4,160,768]{2,1,0:T(8,128)...) custom-call(s32[4,1,512]{2,1,0:T(1,128)} %bitcast.59, f32[4,1,512]{2,1,0:T(1,128)} %bitcast.58, ...), custom_call_target="tpu_custom_call" | custom-call | flops 15099494400 | bytes 37748736 | tf_op jit(solution)/shard_map/forward/pallas_call | solution.py:270
  99.8 2.1 %copy-done = bf16[4,160,3072]{2,1,0:T(8,128)(2,1)S(1)} copy-done((bf16[4,160,3072]{2,1,0:T(8,128)(2,1)S(1)}, bf16[4,160,3072]{2,1,0:T(8,128)(2,1)}, u32[]{:S(2)}) %copy-start) | copy-done | bytes 3932184
  103.1 5.8 %weight_gradient.7 = (bf16[3072,6,4,128]{3,2,1,0:T(4,128)(2,1)}, f32[8,128]{1,0:T(8,128)S(1)}) custom-call(bf16[4,160,3072]{2,1,0:T(8,128)(2,1)S(1)} %copy-done, bf16[4,160,768]{2,1,0:T(8,128)(2,1)S(1)} %copy-done.2), custom_call_target="tpu_custom_call" | custom-call | flops 754974720 | bytes 9437184 | tf_op jit(solution)/shard_map/weight_gradient/pallas_call | solution.py:336
  108.9 1.9 copy-done.4
  111.7 1.8 collective-permute-start.14
  116.1 5.8 %weight_gradient.8 = (bf16[3072,6,4,128]{3,2,1,0:T(4,128)(2,1)}, f32[8,128]{1,0:T(8,128)S(1)}) custom-call(bf16[4,160,3072]{2,1,0:T(8,128)(2,1)S(1)} %copy-done, bf16[4,160,768]{2,1,0:T(8,128)(2,1)S(1)} %copy-done.2, bf16[3072,6,4,128]{3,2,1,0:T(4,128)(2,1)} %get-tuple-element.60.refs_0_, ...), custom_call_target="tpu_custom_call", output_to_operand_aliasing={{0}: (2, {})} | custom-call | flops 754974720 | bytes 9437184 | tf_op jit(solution)/shard_map/weight_gradient/pallas_call | solution.py:336
  121.9 5.8 %weight_gradient.9 = (bf16[3072,6,4,128]{3,2,1,0:T(4,128)(2,1)}, f32[8,128]{1,0:T(8,128)S(1)}) custom-call(bf16[4,160,3072]{2,1,0:T(8,128)(2,1)S(1)} %copy-done, bf16[4,160,768]{2,1,0:T(8,128)(2,1)S(1)} %copy-done.2, bf16[3072,6,4,128]{3,2,1,0:T(4,128)(2,1)} %get-tuple-element.61.refs_0_, ...), custom_call_target="tpu_custom_call", output_to_operand_aliasing={{0}: (2, {})} | custom-call | flops 754974720 | bytes 9437184 | tf_op jit(solution)/shard_map/weight_gradient/pallas_call | solution.py:336
  127.7 5.8 %weight_gradient.10 = (bf16[3072,6,4,128]{3,2,1,0:T(4,128)(2,1)}, f32[8,128]{1,0:T(8,128)S(1)}) custom-call(bf16[4,160,3072]{2,1,0:T(8,128)(2,1)S(1)} %copy-done, bf16[4,160,768]{2,1,0:T(8,128)(2,1)S(1)} %copy-done.2, bf16[3072,6,4,128]{3,2,1,0:T(4,128)(2,1)} %get-tuple-element.63.refs_0_, ...), custom_call_target="tpu_custom_call", output_to_operand_aliasing={{0}: (2, {})} | custom-call | flops 754974720 | bytes 9437184 | tf_op jit(solution)/shard_map/weight_gradient/pallas_call | solution.py:336
  134.3 1.9 collective-permute-start.17
  136.1 2.6 %collective-permute-start.18 = (bf16[16,3072]{1,0:T(8,128)(2,1)S(1)}, bf16[16,3072]{1,0:T(8,128)(2,1)S(1)}, u32[]{:S(2)}, u32[]{:S(2)}) collective-permute-start(bf16[16,3072]{1,0:T(8,128)(2,1)S(1)} %get-tuple-element.68), channel_id=1, source_target_pairs={{0,16},{1,17},{2,18},{3,19},{4,20},{5,21},{6,22},{7,23},{8,24},{9,... | collective-permute-start | bytes 294920 | tf_op jit(solution)/shard_map/ppermute | solution.py:27
  142.5 6.9 %weight_gradient.11 = (bf16[768,24,4,128]{3,2,1,0:T(4,128)(2,1)}, f32[8,128]{1,0:T(8,128)S(1)}) custom-call(bf16[4,160,768]{2,1,0:T(8,128)(2,1)S(1)} %copy-done.3, bf16[4,160,3072]{2,1,0:T(8,128)(2,1)S(1)} %copy-done.1, f32[16,3072]{1,0:T(8,128)S(1)} %get-tuple-element.66.refs_0_), custom_call_target="tpu_custom_call" | custom-call | flops 1006632960 | bytes 12582912 | tf_op jit(solution)/shard_map/weight_gradient/pallas_call | solution.py:336
  150.0 3.8 %collective-permute-start.22 = (bf16[16,3072]{1,0:T(8,128)(2,1)S(1)}, bf16[16,3072]{1,0:T(8,128)(2,1)S(1)}, u32[]{:S(2)}, u32[]{:S(2)}) collective-permute-start(bf16[16,3072]{1,0:T(8,128)(2,1)S(1)} %third_sum.1.refs_1_.refs_0_), channel_id=1, source_target_pairs={{0,24},{1,25},{2,26},{3,27},{4,28},{5,29},{6,30},{7,31},{8,16},{9,... | collective-permute-start | bytes 294920 | tf_op jit(solution)/shard_map/ppermute | solution.py:27
  154.6 6.7 %weight_gradient.12 = (bf16[768,24,4,128]{3,2,1,0:T(4,128)(2,1)}, f32[8,128]{1,0:T(8,128)S(1)}) custom-call(bf16[4,160,768]{2,1,0:T(8,128)(2,1)S(1)} %copy-done.3, bf16[4,160,3072]{2,1,0:T(8,128)(2,1)S(1)} %copy-done.1, bf16[768,24,4,128]{3,2,1,0:T(4,128)(2,1)} %get-tuple-element.73.refs_0_, ...), custom_call_target="tpu_custom_call", output_to_operand_aliasing={{0}: (2, {})} | custom-call | flops 1006632960 | bytes 12582912 | tf_op jit(solution)/shard_map/weight_gradient/pallas_call | solution.py:336
  164.8 8.8 %collective-permute-done.27 = f32[4,128]{1,0:T(4,128)S(1)} collective-permute-done((f32[4,128]{1,0:T(4,128)S(1)}, f32[4,128]{1,0:T(4,128)S(1)}, u32[]{:S(2)}, u32[]{:S(2)}) %collective-permute-start.27) | collective-permute-done | bytes 2080 | tf_op jit(solution)/shard_map/ppermute | solution.py:27
  175.0 2.2 %collective-permute-done.28 = f32[4,128]{1,0:T(4,128)S(1)} collective-permute-done((f32[4,128]{1,0:T(4,128)S(1)}, f32[4,128]{1,0:T(4,128)S(1)}, u32[]{:S(2)}, u32[]{:S(2)}) %collective-permute-start.28) | collective-permute-done | bytes 2080 | tf_op jit(solution)/shard_map/ppermute | solution.py:27
  177.2 1.7 collective-permute-start.29
  179.0 2.7 %collective-permute-done.29 = f32[4,128]{1,0:T(4,128)S(1)} collective-permute-done((f32[4,128]{1,0:T(4,128)S(1)}, f32[4,128]{1,0:T(4,128)S(1)}, u32[]{:S(2)}, u32[]{:S(2)}) %collective-permute-start.29) | collective-permute-done | bytes 2080 | tf_op jit(solution)/shard_map/ppermute | solution.py:27
  182.3 6.7 %weight_gradient.13 = (bf16[768,24,4,128]{3,2,1,0:T(4,128)(2,1)}, f32[8,128]{1,0:T(8,128)S(1)}) custom-call(bf16[4,160,768]{2,1,0:T(8,128)(2,1)S(1)} %copy-done.3, bf16[4,160,3072]{2,1,0:T(8,128)(2,1)S(1)} %copy-done.1, bf16[768,24,4,128]{3,2,1,0:T(4,128)(2,1)} %get-tuple-element.75.refs_0_, ...), custom_call_target="tpu_custom_call", output_to_operand_aliasing={{0}: (2, {})} | custom-call | flops 1006632960 | bytes 12582912 | tf_op jit(solution)/shard_map/weight_gradient/pallas_call | solution.py:336
  (111 shorter events, 29.9 us)
Async XLA Ops:
  0.6 50.5 %collective-permute-start.7 = (bf16[128,3072]{1,0:T(8,128)(2,1)}, bf16[128,3072]{1,0:T(8,128)(2,1)S(1)}, u32[]{:S(2)}, u32[]{:S(2)}) collective-permute-start(bf16[128,3072]{1,0:T(8,128)(2,1)} %refs_0_.1), channel_id=1, source_target_pairs={{0,1},{1,0},{2,3},{3,2},{4,5},{5,4},{6,7},{7,6},{8,9},{9,8},{10,11... | collective-permute-start | bytes 2359304 | tf_op jit(solution)/shard_map/ppermute | solution.py:27
  2.2 17.3 %collective-permute-start.3 = (bf16[64,3072]{1,0:T(8,128)(2,1)S(1)}, bf16[64,3072]{1,0:T(8,128)(2,1)S(1)}, u32[]{:S(2)}, u32[]{:S(2)}) collective-permute-start(bf16[64,3072]{1,0:T(8,128)(2,1)S(1)} %constant_dynamic-slice_fusion.1), channel_id=1, source_target_pairs={{0,2},{1,3},{2,0},{3,1},{4,6},{5,7},{6,4},{7,5},{8,10},{9,11},{10,... | collective-permute-start | bytes 1179656 | tf_op jit(solution)/shard_map/ppermute | solution.py:27
  5.8 30.3 %collective-permute-start.5 = (bf16[64,3072]{1,0:T(8,128)(2,1)S(1)}, bf16[64,3072]{1,0:T(8,128)(2,1)S(1)}, u32[]{:S(2)}, u32[]{:S(2)}) collective-permute-start(bf16[64,3072]{1,0:T(8,128)(2,1)S(1)} %constant_dynamic-slice_fusion), channel_id=1, source_target_pairs={{0,2},{1,3},{2,0},{3,1},{4,6},{5,7},{6,4},{7,5},{8,10},{9,11},{10,... | collective-permute-start | bytes 1179656 | tf_op jit(solution)/shard_map/ppermute | solution.py:27
  20.2 16.2 %collective-permute-start.4 = (bf16[64,3072]{1,0:T(8,128)(2,1)}, bf16[64,3072]{1,0:T(8,128)(2,1)S(1)}, u32[]{:S(2)}, u32[]{:S(2)}) collective-permute-start(bf16[64,3072]{1,0:T(8,128)(2,1)} %hold.3.refs_0_.refs_2_), channel_id=1, source_target_pairs={{0,4},{1,5},{2,6},{3,7},{4,0},{5,1},{6,2},{7,3},{8,12},{9,13},{10,... | collective-permute-start | bytes 1179656 | tf_op jit(solution)/shard_map/ppermute | solution.py:27
  22.4 15.2 %collective-permute-start.2 = (f32[8,128]{1,0:T(8,128)S(1)}, f32[8,128]{1,0:T(8,128)S(1)}, u32[]{:S(2)}, u32[]{:S(2)}) collective-permute-start(f32[8,128]{1,0:T(8,128)S(1)} %maximum_select_fusion), channel_id=1, source_target_pairs={{0,3},{1,2},{2,1},{3,0},{4,7},{5,6},{6,5},{7,4},{8,11},{9,10},{10,... | collective-permute-start | bytes 12296 | tf_op jit(solution)/shard_map/ppermute | solution.py:27
  23.1 14.7 %collective-permute-start.1 = (f32[8,128]{1,0:T(8,128)S(1)}, f32[8,128]{1,0:T(8,128)S(1)}, u32[]{:S(2)}, u32[]{:S(2)}) collective-permute-start(f32[8,128]{1,0:T(8,128)S(1)} %maximum_select_fusion), channel_id=1, source_target_pairs={{0,2},{1,3},{2,0},{3,1},{4,6},{5,7},{6,4},{7,5},{8,10},{9,11},{10,... | collective-permute-start | bytes 12296 | tf_op jit(solution)/shard_map/ppermute | solution.py:27
  37.2 13.2 %collective-permute-start.6 = (bf16[64,3072]{1,0:T(8,128)(2,1)}, bf16[64,3072]{1,0:T(8,128)(2,1)S(1)}, u32[]{:S(2)}, u32[]{:S(2)}) collective-permute-start(bf16[64,3072]{1,0:T(8,128)(2,1)} %get-tuple-element.48.refs_8_), channel_id=1, source_target_pairs={{0,4},{1,5},{2,6},{3,7},{4,0},{5,1},{6,2},{7,3},{8,12},{9,13},{10,... | collective-permute-start | bytes 1179656 | tf_op jit(solution)/shard_map/ppermute | solution.py:27
  37.5 27.6 %collective-permute-start.10 = (bf16[128,3072]{1,0:T(8,128)(2,1)S(1)}, bf16[128,3072]{1,0:T(8,128)(2,1)}, u32[]{:S(2)}, u32[]{:S(2)}) collective-permute-start(bf16[128,3072]{1,0:T(8,128)(2,1)S(1)} %copy-done.11), channel_id=1, source_target_pairs={{0,1},{1,0},{2,3},{3,2},{4,5},{5,4},{6,7},{7,6},{8,9},{9,8},{10,11... | collective-permute-start | bytes 2359304 | tf_op jit(solution)/shard_map/ppermute | solution.py:27
  37.8 27.4 %collective-permute-start.8 = (bf16[64,3072]{1,0:T(8,128)(2,1)S(1)}, bf16[64,3072]{1,0:T(8,128)(2,1)}, u32[]{:S(2)}, u32[]{:S(2)}) collective-permute-start(bf16[64,3072]{1,0:T(8,128)(2,1)S(1)} %copy-done.8), channel_id=1, source_target_pairs={{0,1},{1,0},{2,3},{3,2},{4,5},{5,4},{6,7},{7,6},{8,9},{9,8},{10,11... | collective-permute-start | bytes 1179656 | tf_op jit(solution)/shard_map/ppermute | solution.py:27
  38.2 27.0 %collective-permute-start.9 = (bf16[64,3072]{1,0:T(8,128)(2,1)}, bf16[64,3072]{1,0:T(8,128)(2,1)}, u32[]{:S(2)}, u32[]{:S(2)}) collective-permute-start(bf16[64,3072]{1,0:T(8,128)(2,1)} %get-tuple-element.46.refs_0_.refs_3_), channel_id=1, source_target_pairs={{0,1},{1,0},{2,3},{3,2},{4,5},{5,4},{6,7},{7,6},{8,9},{9,8},{10,11... | collective-permute-start | bytes 1179656 | tf_op jit(solution)/shard_map/ppermute | solution.py:27
  50.4 14.8 %collective-permute-start.11 = (bf16[64,3072]{1,0:T(8,128)(2,1)S(1)}, bf16[64,3072]{1,0:T(8,128)(2,1)}, u32[]{:S(2)}, u32[]{:S(2)}) collective-permute-start(bf16[64,3072]{1,0:T(8,128)(2,1)S(1)} %copy-done.10), channel_id=1, source_target_pairs={{0,1},{1,0},{2,3},{3,2},{4,5},{5,4},{6,7},{7,6},{8,9},{9,8},{10,11... | collective-permute-start | bytes 1179656 | tf_op jit(solution)/shard_map/ppermute | solution.py:27
  51.2 14.0 %collective-permute-start.12 = (bf16[64,3072]{1,0:T(8,128)(2,1)}, bf16[64,3072]{1,0:T(8,128)(2,1)S(1)}, u32[]{:S(2)}, u32[]{:S(2)}) collective-permute-start(bf16[64,3072]{1,0:T(8,128)(2,1)} %hold.5.refs_0_.refs_9_), channel_id=1, source_target_pairs={{0,1},{1,0},{2,3},{3,2},{4,5},{5,4},{6,7},{7,6},{8,9},{9,8},{10,11... | collective-permute-start | bytes 1179656 | tf_op jit(solution)/shard_map/ppermute | solution.py:27
  99.5 9.4 %collective-permute-start.13 = (bf16[256,3072]{1,0:T(8,128)(2,1)}, bf16[256,3072]{1,0:T(8,128)(2,1)S(1)}, u32[]{:S(2)}, u32[]{:S(2)}) collective-permute-start(bf16[256,3072]{1,0:T(8,128)(2,1)} %get-tuple-element.52), channel_id=1, source_target_pairs={{0,1},{1,0},{2,3},{3,2},{4,5},{5,4},{6,7},{7,6},{8,9},{9,8},{10,11... | collective-permute-start | bytes 4718600 | tf_op jit(solution)/shard_map/ppermute | solution.py:27
  111.7 21.8 %collective-permute-start.14 = (bf16[64,3072]{1,0:T(8,128)(2,1)S(1)}, bf16[64,3072]{1,0:T(8,128)(2,1)S(1)}, u32[]{:S(2)}, u32[]{:S(2)}) collective-permute-start(bf16[64,3072]{1,0:T(8,128)(2,1)S(1)} %get-tuple-element.57), channel_id=1, source_target_pairs={{0,4},{1,5},{2,6},{3,7},{4,0},{5,1},{6,2},{7,3},{8,12},{9,13},{10,... | collective-permute-start | bytes 1179656 | tf_op jit(solution)/shard_map/ppermute | solution.py:27
  113.5 20.0 %collective-permute-start.15 = (bf16[64,3072]{1,0:T(8,128)(2,1)S(1)}, bf16[64,3072]{1,0:T(8,128)(2,1)S(1)}, u32[]{:S(2)}, u32[]{:S(2)}) collective-permute-start(bf16[64,3072]{1,0:T(8,128)(2,1)S(1)} %get-tuple-element.58), channel_id=1, source_target_pairs={{0,2},{1,3},{2,0},{3,1},{4,6},{5,7},{6,4},{7,5},{8,10},{9,11},{10,... | collective-permute-start | bytes 1179656 | tf_op jit(solution)/shard_map/ppermute | solution.py:27
  115.0 18.5 %collective-permute-start.16 = (bf16[64,3072]{1,0:T(8,128)(2,1)S(1)}, bf16[64,3072]{1,0:T(8,128)(2,1)S(1)}, u32[]{:S(2)}, u32[]{:S(2)}) collective-permute-start(bf16[64,3072]{1,0:T(8,128)(2,1)S(1)} %get-tuple-element.59), channel_id=1, source_target_pairs={{0,6},{1,7},{2,4},{3,5},{4,2},{5,3},{6,0},{7,1},{8,14},{9,15},{10,... | collective-permute-start | bytes 1179656 | tf_op jit(solution)/shard_map/ppermute | solution.py:27
  134.3 15.1 %collective-permute-start.17 = (bf16[16,3072]{1,0:T(8,128)(2,1)S(1)}, bf16[16,3072]{1,0:T(8,128)(2,1)S(1)}, u32[]{:S(2)}, u32[]{:S(2)}) collective-permute-start(bf16[16,3072]{1,0:T(8,128)(2,1)S(1)} %get-tuple-element.67), channel_id=1, source_target_pairs={{0,8},{1,9},{2,10},{3,11},{4,12},{5,13},{6,14},{7,15},{8,0},{9,1},... | collective-permute-start | bytes 294920 | tf_op jit(solution)/shard_map/ppermute | solution.py:27
  136.1 13.2 %collective-permute-start.18 = (bf16[16,3072]{1,0:T(8,128)(2,1)S(1)}, bf16[16,3072]{1,0:T(8,128)(2,1)S(1)}, u32[]{:S(2)}, u32[]{:S(2)}) collective-permute-start(bf16[16,3072]{1,0:T(8,128)(2,1)S(1)} %get-tuple-element.68), channel_id=1, source_target_pairs={{0,16},{1,17},{2,18},{3,19},{4,20},{5,21},{6,22},{7,23},{8,24},{9,... | collective-permute-start | bytes 294920 | tf_op jit(solution)/shard_map/ppermute | solution.py:27
  138.8 10.6 %collective-permute-start.19 = (bf16[16,3072]{1,0:T(8,128)(2,1)S(1)}, bf16[16,3072]{1,0:T(8,128)(2,1)S(1)}, u32[]{:S(2)}, u32[]{:S(2)}) collective-permute-start(bf16[16,3072]{1,0:T(8,128)(2,1)S(1)} %get-tuple-element.69), channel_id=1, source_target_pairs={{0,24},{1,25},{2,26},{3,27},{4,28},{5,29},{6,30},{7,31},{8,16},{9,... | collective-permute-start | bytes 294920 | tf_op jit(solution)/shard_map/ppermute | solution.py:27
  141.8 22.4 %collective-permute-start.24 = (f32[4,128]{1,0:T(4,128)S(1)}, f32[4,128]{1,0:T(4,128)S(1)}, u32[]{:S(2)}, u32[]{:S(2)}) collective-permute-start(f32[4,128]{1,0:T(4,128)S(1)} %get-tuple-element.84), channel_id=1, source_target_pairs={{0,1},{1,0},{2,3},{3,2},{4,5},{5,4},{6,7},{7,6},{8,9},{9,8},{10,11... | collective-permute-start | bytes 6152 | tf_op jit(solution)/shard_map/ppermute | solution.py:27
  150.0 11.3 %collective-permute-start.22 = (bf16[16,3072]{1,0:T(8,128)(2,1)S(1)}, bf16[16,3072]{1,0:T(8,128)(2,1)S(1)}, u32[]{:S(2)}, u32[]{:S(2)}) collective-permute-start(bf16[16,3072]{1,0:T(8,128)(2,1)S(1)} %third_sum.1.refs_1_.refs_0_), channel_id=1, source_target_pairs={{0,24},{1,25},{2,26},{3,27},{4,28},{5,29},{6,30},{7,31},{8,16},{9,... | collective-permute-start | bytes 294920 | tf_op jit(solution)/shard_map/ppermute | solution.py:27
  153.8 8.2 %collective-permute-start.21 = (bf16[16,3072]{1,0:T(8,128)(2,1)S(1)}, bf16[16,3072]{1,0:T(8,128)(2,1)S(1)}, u32[]{:S(2)}, u32[]{:S(2)}) collective-permute-start(bf16[16,3072]{1,0:T(8,128)(2,1)S(1)} %third_sum.1.refs_1_.refs_0_), channel_id=1, source_target_pairs={{0,16},{1,17},{2,18},{3,19},{4,20},{5,21},{6,22},{7,23},{8,24},{9,... | collective-permute-start | bytes 294920 | tf_op jit(solution)/shard_map/ppermute | solution.py:27
  162.6 26.3 %collective-permute-start.23 = (bf16[64,3072]{1,0:T(8,128)(2,1)S(1)}, bf16[64,3072]{1,0:T(8,128)(2,1)S(1)}, u32[]{:S(2)}, u32[]{:S(2)}) collective-permute-start(bf16[64,3072]{1,0:T(8,128)(2,1)S(1)} %join_z.1.refs_1_.refs_0_), channel_id=1, source_target_pairs={{0,4},{1,5},{2,6},{3,7},{4,0},{5,1},{6,2},{7,3},{8,12},{9,13},{10,... | collective-permute-start | bytes 1179656 | tf_op jit(solution)/shard_map/ppermute | solution.py:27
  164.3 9.3 %collective-permute-start.27 = (f32[4,128]{1,0:T(4,128)S(1)}, f32[4,128]{1,0:T(4,128)S(1)}, u32[]{:S(2)}, u32[]{:S(2)}) collective-permute-start(f32[4,128]{1,0:T(4,128)S(1)} %fusion.13), channel_id=1, source_target_pairs={{0,4},{1,5},{2,6},{3,7},{4,0},{5,1},{6,2},{7,3},{8,12},{9,13},{10,... | collective-permute-start | bytes 6152 | tf_op jit(solution)/shard_map/ppermute | solution.py:27
  (20 other events, 149.7 us)

commit v4 on v3

v4 whole, which is shorter than its diff:
```python
import functools
import jax
import jax.numpy as jnp
import numpy as np
from jax import lax
from jax.experimental import pallas as pl
from jax.experimental.pallas import tpu as pltpu
from jax.sharding import PartitionSpec as P

EXPERTS = 16
CAP = 40
AXES = ("fsdp", "expert")
CORE, Y, X, Z = 1, 2, 4, 8
LANES = 128
NARROW, WIDE = jnp.bfloat16, jnp.float32
MIB = 1 << 20
TN = (((0,), (0,)), ((), ()))
NT = (((1,), (1,)), ((), ()))
NN = (((1,), (0,)), ((), ()))


def mm(a, b, dims):
    return lax.dot_general(a, b, dims, preferred_element_type=WIDE)


def swap(value, mask):
    size = lax.axis_size("fsdp") * lax.axis_size("expert")
    return lax.ppermute(value, AXES, [(i, i ^ mask) for i in range(size)])


def is_small():
    return lax.axis_size("fsdp") == 8 and lax.axis_size("expert") == 4


def own_order(rows):
    x_index = lax.axis_index("fsdp") % 2
    half = rows.shape[-1] // 2
    return jnp.where(
        x_index == 0, rows, jnp.concatenate([rows[..., half:], rows[..., :half]], axis=-1)
    )


ANY = pl.BlockSpec(memory_space=pl.ANY)
FLAG = jax.ShapeDtypeStruct((8, LANES), WIDE)


def small_call(body, place, inputs, after, outs, name, grant=12):
    given = len(inputs)

    def run(place_ref, *refs):
        body(place_ref, refs[:given], refs[given + len(after) :])

    def whole(array):
        return pl.BlockSpec(array.shape, lambda: (0,) * len(array.shape))

    return pl.pallas_call(
        run,
        out_shape=outs,
        in_specs=[pl.BlockSpec(memory_space=pltpu.SMEM)]
        + [whole(array) for array in inputs]
        + [ANY] * len(after),
        out_specs=[whole(out) for out in outs],
        compiler_params=pltpu.CompilerParams(vmem_limit_bytes=grant * MIB),
        cost_estimate=pl.CostEstimate(flops=0, bytes_accessed=1 << 20, transcendentals=0),
        name=name,
    )(place, *inputs, *after)


def hold(arrays, after):
    count = len(arrays)
    return pl.pallas_call(
        lambda *refs: None,
        out_shape=[jax.ShapeDtypeStruct(array.shape, array.dtype) for array in arrays],
        in_specs=[ANY] * (count + len(after)),
        out_specs=[ANY] * count,
        input_output_aliases={number: number for number in range(count)},
        cost_estimate=pl.CostEstimate(flops=0, bytes_accessed=1 << 18, transcendentals=0),
        name="hold",
    )(*arrays, *after)


def at(index, size):
    return pl.ds(pl.multiple_of(index * size, size), size)


def first_sum(place_ref, ins, outs):
    keep_ref, got_ref = ins
    mine_ref, x_ref, y_ref, xy_ref = outs
    half = mine_ref.shape[0]
    x_index = place_ref[0]

    def total(rows):
        return keep_ref[rows, :] + got_ref[rows, :].astype(WIDE)

    mine_ref[...] = total(at(x_index, half))
    x_ref[...] = total(at(1 - x_index, half)).astype(NARROW)
    y_ref[...] = total(slice(2 * half, 3 * half)).astype(NARROW)
    xy_ref[...] = total(slice(3 * half, 4 * half)).astype(NARROW)


def second_sum(place_ref, ins, outs):
    mine_ref, x_ref, y_ref, xy_ref = ins
    quarter = outs[0].shape[0]
    z_index = place_ref[1]
    for step in range(4):
        rows = at(z_index ^ step, quarter)
        total = mine_ref[rows, :] + x_ref[rows, :].astype(WIDE)
        total = total + (y_ref[rows, :].astype(WIDE) + xy_ref[rows, :].astype(WIDE))
        outs[step][...] = total.astype(outs[step].dtype)


def third_sum(place_ref, ins, outs):
    total = ins[0][...]
    for got in ins[1:]:
        total = total + got[...].astype(WIDE)
    outs[0][...] = total.astype(NARROW)


def join_z(place_ref, ins, outs):
    quarter = ins[0].shape[0]
    for step in range(4):
        outs[0][at(place_ref[1] ^ step, quarter), :] = ins[step][...]


def join_x(place_ref, ins, outs):
    half = ins[0].shape[0]
    model_width = outs[0].shape[1]
    for step in range(2):
        rows = at(place_ref[0] ^ step, half)
        outs[0][rows, :] = ins[step][:, :model_width]
        outs[1][rows, :] = ins[step][:, model_width:]


def sorter(rows, tiles, experts):
    size = rows * tiles * experts
    order = np.arange(size).reshape(rows, tiles, experts).transpose(2, 1, 0).reshape(-1)
    return jnp.asarray(np.eye(size, dtype=np.float32)[order], NARROW)


def tiled_view(weight):
    rows, experts, columns = weight.shape
    return weight.reshape(rows, experts, columns // LANES, LANES).transpose(0, 2, 1, 3)


def split_body(group, some, sort_ref, w_ref, *refs):
    out_ref, flag_ref = refs[-2:]
    flag_ref[...] = jnp.zeros_like(flag_ref)
    rows, tiles, experts, _ = w_ref.shape
    held = group * experts
    flat = w_ref.reshape(rows, tiles * experts, LANES)
    places = [(row, tile) for row in range(0, rows, some) for tile in range(0, tiles, group)]
    for pair in zip(places[::2], places[1::2]):
        blocks = [
            flat[row : row + some, tile * experts : tile * experts + held, :].reshape(
                some * held, LANES
            )
            for row, tile in pair
        ]
        result = mm(sort_ref[...], jnp.concatenate(blocks, axis=1), NN)
        for expert in range(experts):
            for tile in range(group):
                begin = (expert * group + tile) * some
                parts = [
                    result[begin : begin + some, side * LANES : (side + 1) * LANES]
                    for side in range(2)
                ]
                if some == 8:
                    row, first = pair[0][0], pair[0][1] + tile
                    out_ref[expert, row : row + 16, first * LANES : (first + 1) * LANES] = (
                        jnp.concatenate(parts, axis=0).astype(NARROW)
                    )
                else:
                    for (row, first), part in zip(pair, parts):
                        column = (first + tile) * LANES
                        out_ref[expert, row : row + some, column : column + LANES] = part.astype(
                            NARROW
                        )


def split_experts(view, sort, block, group, some, after):
    rows, tiles, experts, _ = view.shape
    columns = tiles * LANES
    return pl.pallas_call(
        functools.partial(split_body, group, some),
        out_shape=[jax.ShapeDtypeStruct((experts, rows, columns), NARROW), FLAG],
        grid=(rows // block,),
        in_specs=[
            pl.BlockSpec(sort.shape, lambda i: (0, 0)),
            pl.BlockSpec((block, tiles, experts, LANES), lambda i: (i, 0, 0, 0)),
            *[ANY] * len(after),
        ],
        out_specs=[
            pl.BlockSpec((experts, block, columns), lambda i: (0, i, 0)),
            pl.BlockSpec(FLAG.shape, lambda i: (0, 0)),
        ],
        compiler_params=pltpu.CompilerParams(vmem_limit_bytes=56 * MIB),
        cost_estimate=pl.CostEstimate(
            flops=0, bytes_accessed=4 * experts * rows * columns, transcendentals=0
        ),
        name="split_experts",
    )(sort, view, *after)


def fetch(pieces, whole, sem):
    copies, begin = [], 0
    for number, piece in enumerate(pieces):
        count = piece.shape[0]
        copies.append(
            pltpu.make_async_copy(piece, whole.at[begin : begin + count], sem.at[number])
        )
        begin += count
    for copy in copies:
        copy.start()
    for copy in copies:
        copy.wait()


def chosen(code_ref, slots):
    code = code_ref[0]
    tokens = code.shape[1]
    return lax.broadcasted_iota(jnp.int32, (slots, tokens), 0) == jnp.bitwise_and(code, 1023)


def forward_tokens_body(code_ref, gate_ref, w_ref, *refs):
    pieces, (xs_ref, ag_ref, active_ref, slope_ref, x_ref, sem) = refs[:-6], refs[-6:]
    slots, model_width = xs_ref.shape[1:]
    columns = 512
    pl.when(pl.program_id(0) == 0)(lambda: fetch(pieces, x_ref, sem))
    choose = chosen(code_ref, slots)
    pick = choose.astype(WIDE).astype(NARROW)
    gate = jnp.sum(jnp.where(choose, gate_ref[0], 0.0), axis=1, keepdims=True)
    for begin in range(0, model_width, columns):
        part = slice(begin, begin + columns)
        xs_ref[0, :, part] = mm(pick, x_ref[:, part], NN).astype(NARROW)
    pre_act = mm(xs_ref[0], w_ref[0], NN)
    squash = jax.nn.sigmoid(pre_act)
    active = pre_act * squash
    active_ref[0] = active
    ag_ref[0] = (gate * active).astype(NARROW)
    slope_ref[0] = gate * squash * (1.0 + pre_act * (1.0 - squash))


def forward_tokens(code, gate_tok, x_pieces, w_split):
    experts, model_width, hidden = w_split.shape
    tokens = code.shape[2]
    slots = tokens // 128 * CAP
    expert = lambda i: (i, 0, 0)
    shapes = [(model_width, NARROW), (hidden, NARROW), (hidden, WIDE), (hidden, WIDE)]
    return pl.pallas_call(
        forward_tokens_body,
        out_shape=[jax.ShapeDtypeStruct((experts, slots, width), dtype) for width, dtype in shapes],
        grid=(experts,),
        in_specs=[
            pl.BlockSpec((1, 1, tokens), expert),
            pl.BlockSpec((1, 1, tokens), expert),
            pl.BlockSpec((1, model_width, hidden), expert),
            *[ANY] * len(x_pieces),
        ],
        out_specs=[pl.BlockSpec((1, slots, width), expert) for width, _ in shapes],
        scratch_shapes=[
            pltpu.VMEM((tokens, model_width), NARROW),
            pltpu.SemaphoreType.DMA((len(x_pieces),)),
        ],
        compiler_params=pltpu.CompilerParams(vmem_limit_bytes=56 * MIB),
        cost_estimate=pl.CostEstimate(
            flops=2 * slots * experts * model_width * (hidden + tokens),
            bytes_accessed=2 * experts * model_width * hidden,
            transcendentals=0,
        ),
        name="forward_tokens",
    )(code, gate_tok, w_split, *x_pieces)


def forward_cotangents_body(code_ref, active_ref, slope_ref, w_ref, v_ref, *refs):
    pieces = refs[:-8]
    gs_ref, gp_ref, keep_ref, send_ref, g_ref, back_ref, pick_ref, sem = refs[-8:]
    step = pl.program_id(0)
    slots, model_width = gs_ref.shape[1:]
    columns = 512
    pl.when(step == 0)(lambda: fetch(pieces, g_ref, sem))
    choose = chosen(code_ref, slots)
    pick = choose.astype(WIDE).astype(NARROW)
    rows = pl.ds(pl.multiple_of(step * slots, slots), slots)
    pick_ref[rows, :] = pick
    for begin in range(0, model_width, columns):
        part = slice(begin, begin + columns)
        gs_ref[0, :, part] = mm(pick, g_ref[:, part], NN).astype(NARROW)
    upstream = mm(gs_ref[0], v_ref[0], NT)
    gate_part = jnp.sum(active_ref[0] * upstream, axis=1, keepdims=True)
    gp_ref[0] = (slope_ref[0] * upstream).astype(NARROW)
    for begin in range(0, model_width, columns):
        back = mm(gp_ref[0], w_ref[0, begin : begin + columns, :], NT)
        back_ref[rows, begin : begin + columns] = back.astype(NARROW)
    which = jnp.sum(
        jnp.where(choose, jnp.right_shift(code_ref[0], 10), 0), axis=1, keepdims=True
    )
    lane = lax.broadcasted_iota(jnp.int32, (slots, LANES), 1)
    high = gate_part.astype(NARROW).astype(WIDE)
    gates = jnp.where(lane == which, high, 0.0)
    gates = jnp.where(lane == which + LANES // 2, gate_part - high, gates)
    back_ref[rows, model_width:] = gates.astype(NARROW)

    @pl.when(step == pl.num_programs(0) - 1)
    def _():
        quarter = g_ref.shape[0] // 4
        for begin in range(0, model_width + LANES, columns):
            part = slice(begin, min(begin + columns, model_width + LANES))
            summed = mm(pick_ref[...], back_ref[:, part], TN)
            if begin == model_width:
                summed = summed + pltpu.roll(summed, LANES // 2, 1)
            for pair in range(2):
                lower = 2 * pair * quarter
                into = slice(pair * quarter, (pair + 1) * quarter)
                keep_ref[into, part] = summed[lower : lower + quarter]
                send_ref[into, part] = summed[lower + quarter : lower + 2 * quarter].astype(NARROW)


def forward_cotangents(code, active, slope, g_pieces, w_split, v_split):
    experts, model_width, hidden = w_split.shape
    tokens = code.shape[2]
    slots = tokens // 128 * CAP
    width = model_width + LANES
    expert = lambda i: (i, 0, 0)
    whole = lambda i: (0, 0)
    one = pl.Buffered(1)
    return pl.pallas_call(
        forward_cotangents_body,
        out_shape=[
            jax.ShapeDtypeStruct((experts, slots, model_width), NARROW),
            jax.ShapeDtypeStruct((experts, slots, hidden), NARROW),
            jax.ShapeDtypeStruct((tokens // 2, width), WIDE),
            jax.ShapeDtypeStruct((tokens // 2, width), NARROW),
        ],
        grid=(experts,),
        in_specs=[
            pl.BlockSpec((1, 1, tokens), expert),
            pl.BlockSpec((1, slots, hidden), expert),
            pl.BlockSpec((1, slots, hidden), expert),
            pl.BlockSpec((1, model_width, hidden), expert),
            pl.BlockSpec((1, hidden, model_width), expert),
            *[ANY] * len(g_pieces),
        ],
        out_specs=[
            pl.BlockSpec((1, slots, model_width), expert),
            pl.BlockSpec((1, slots, hidden), expert),
            pl.BlockSpec((tokens // 2, width), whole, pipeline_mode=one),
            pl.BlockSpec((tokens // 2, width), whole, pipeline_mode=one),
        ],
        scratch_shapes=[
            pltpu.VMEM((tokens, model_width), NARROW),
            pltpu.VMEM((experts * slots, width), NARROW),
            pltpu.VMEM((experts * slots, tokens), NARROW),
            pltpu.SemaphoreType.DMA((len(g_pieces),)),
        ],
        compiler_params=pltpu.CompilerParams(vmem_limit_bytes=56 * MIB),
        cost_estimate=pl.CostEstimate(
            flops=2 * slots * experts * model_width * (2 * hidden + 2 * tokens),
            bytes_accessed=4 * experts * model_width * hidden,
            transcendentals=0,
        ),
        name="forward_cotangents",
    )(code, active, slope, w_split, v_split, *g_pieces)


def outer_body(group, some, sort_ref, a_ref, b_ref, *refs):
    out_ref, flag_ref = refs[-2:]
    flag_ref[...] = jnp.zeros_like(flag_ref)
    rows, tiles, experts, _ = out_ref.shape
    held = group * experts
    out = out_ref.reshape(rows, tiles * experts, LANES)
    across = 1 if some == 8 else 2
    for tile in range(0, tiles, group * across):
        wide = group * across * LANES
        parts = [
            mm(a_ref[expert], b_ref[expert, :, tile * LANES : tile * LANES + wide], TN)
            for expert in range(experts)
        ]
        for row in range(0, rows, 16):
            pair = [(row, 0), (row + 8, 0)] if some == 8 else [(row, 0), (row, group)]
            blocks = [
                jnp.concatenate(
                    [
                        part[begin : begin + some, (first + inner) * LANES : (first + inner + 1) * LANES]
                        for part in parts
                        for inner in range(group)
                    ],
                    axis=0,
                )
                for begin, first in pair
            ]
            result = mm(sort_ref[...], jnp.concatenate(blocks, axis=1).astype(NARROW), NN)
            for side, (begin, first) in enumerate(pair):
                at_tile = (tile + first) * experts
                out[begin : begin + some, at_tile : at_tile + held, :] = (
                    result[:, side * LANES : (side + 1) * LANES]
                    .astype(NARROW)
                    .reshape(some, held, LANES)
                )


def outer(sort, a, b, holder, start, count, group, some, after):
    experts, slots, total = a.shape
    columns = b.shape[2]
    tiles = columns // LANES
    block = 128
    first = start // block
    extra = list(after) if holder is None else [holder, *after]
    return pl.pallas_call(
        functools.partial(outer_body, group, some),
        out_shape=[jax.ShapeDtypeStruct((total, tiles, experts, LANES), NARROW), FLAG],
        grid=(count // block,),
        in_specs=[
            pl.BlockSpec(sort.shape, lambda i: (0, 0)),
            pl.BlockSpec((experts, slots, block), lambda i: (0, 0, first + i)),
            pl.BlockSpec(
                (experts, slots, columns), lambda i: (0, 0, 0), pipeline_mode=pl.Buffered(1)
            ),
            *[ANY] * len(extra),
        ],
        out_specs=[
            pl.BlockSpec((block, tiles, experts, LANES), lambda i: (first + i, 0, 0, 0)),
            pl.BlockSpec(FLAG.shape, lambda i: (0, 0)),
        ],
        input_output_aliases={} if holder is None else {3: 0},
        compiler_params=pltpu.CompilerParams(vmem_limit_bytes=56 * MIB),
        cost_estimate=pl.CostEstimate(
            flops=2 * experts * slots * count * columns,
            bytes_accessed=4 * experts * count * columns,
            transcendentals=0,
        ),
        name="weight_gradient",
    )(sort, a, b, *extra)


def stored_view(tiled):
    rows, tiles, experts, _ = tiled.shape
    return tiled.transpose(0, 2, 1, 3).reshape(rows, experts, tiles * LANES)


def local(tokens, cotangent, expert_ids, gate_values, w_in, w_out):
    if not is_small():
        return local_general(tokens, cotangent, expert_ids, gate_values, w_in, w_out)
    tok_rows, model_width = tokens.shape
    top_count = expert_ids.shape[1]
    local_count = w_in.shape[1]
    hidden = w_in.shape[2]
    half = tok_rows // 2
    first = lax.axis_index("expert") * local_count
    fsdp = lax.axis_index("fsdp")
    x_index = fsdp % 2
    place = jnp.stack([x_index, fsdp // 2]).astype(jnp.int32)

    meta = jnp.concatenate([expert_ids.astype(WIDE), gate_values.astype(WIDE)], axis=1).T
    turned = own_order(meta)
    meta = jnp.stack([meta, swap(meta, CORE), swap(turned, Y), swap(turned, CORE | Y)])
    w_view, v_view = tiled_view(w_in), tiled_view(w_out)
    x_near = swap(lax.dynamic_slice_in_dim(tokens, x_index * half, half, axis=0), Y)
    g_near = swap(lax.dynamic_slice_in_dim(cotangent, x_index * half, half, axis=0), Y)
    x_core, g_core = swap(tokens, CORE), swap(cotangent, CORE)
    ids, gates = meta[:, :top_count].astype(jnp.int32), meta[:, top_count:]
    blocks = ids.shape[0]
    names = first + jnp.arange(local_count, dtype=jnp.int32)
    named = ids[:, None] == names[None, :, None, None]
    hit = jnp.any(named, axis=2)
    gate_tok = jnp.sum(jnp.where(named, gates[:, None], 0.0), axis=2)
    earlier = jnp.tril(jnp.ones((tok_rows, tok_rows), WIDE), -1)
    position = jnp.einsum("tu,blu->blt", earlier, hit.astype(WIDE)).astype(jnp.int32)
    base = jnp.arange(blocks, dtype=jnp.int32)[:, None, None] * CAP
    order = jnp.arange(top_count, dtype=jnp.int32)[None, None, :, None]
    which = jnp.sum(jnp.where(named, order, 0), axis=2)
    code = jnp.where(hit, base + position, 1023) + 1024 * which

    def by_expert(value):
        return jnp.swapaxes(value, 0, 1).reshape(local_count, 1, blocks * tok_rows)

    code, gate_tok = by_expert(code), by_expert(gate_tok)
    w_sort, v_sort = sorter(8, 6, local_count), sorter(16, 4, local_count)
    w_split, flag = split_experts(w_view, w_sort, 256, 6, 8, [])
    (x_near,) = hold([x_near], [flag])
    x_far = swap(x_near, X)
    x_near_core = swap(x_near, CORE)
    v_split, flag = split_experts(v_view, v_sort, 64, 4, 16, [x_near])
    x_far, g_near = hold([x_far, g_near], [flag])
    g_far = swap(g_near, X)
    g_near_core = swap(g_near, CORE)
    x_far_core = swap(x_far, CORE)
    x_pieces = [tokens, x_core, x_near, x_far, x_near_core, x_far_core]
    xs, ag, active, slope = forward_tokens(code, gate_tok, x_pieces, w_split)
    g_far_core = swap(g_far, CORE)
    g_pieces = [cotangent, g_core, g_near, g_far, g_near_core, g_far_core]
    gs, gp, keep, send = forward_cotangents(code, active, slope, g_pieces, w_split, v_split)
    w_back, v_back = w_sort.T, v_sort.T
    width = keep.shape[1]

    def shape(rows, dtype, columns=width):
        return jax.ShapeDtypeStruct((rows, columns), dtype)

    def in_part(holder, number, after):
        rows = model_width // 4
        return outer(w_back, xs, gp, holder, number * rows, rows, 6, 8, after)

    def out_part(holder, number, after):
        rows = hidden // 3
        return outer(v_back, ag, gs, holder, number * rows, rows, 4, 16, after)

    got = swap(send, CORE)
    grad_in, flag = in_part(None, 0, [])
    mine, *sends = small_call(
        first_sum, place, [keep, got], [flag],
        [shape(half, WIDE)] + [shape(half, NARROW)] * 3, "first_sum", 56,
    )
    got = [swap(part, mask) for part, mask in zip(sends, (X, Y, X | Y))]
    grad_in, flag = in_part(grad_in, 1, [mine])
    grad_in, flag = in_part(grad_in, 2, [flag])
    grad_in, flag = in_part(grad_in, 3, [flag])
    mine, *sends = small_call(
        second_sum, place, [mine, *got], [flag],
        [shape(half // 4, WIDE)] + [shape(half // 4, NARROW)] * 3, "second_sum",
    )
    got = [swap(part, mask * Z) for part, mask in zip(sends, (1, 2, 3))]
    grad_out, flag = out_part(None, 0, [mine])
    (final,) = small_call(
        third_sum, place, [mine, *got], [flag], [shape(half // 4, NARROW)], "third_sum"
    )
    got = [swap(final, mask * Z) for mask in (1, 2, 3)]
    grad_out, flag = out_part(grad_out, 1, [final])
    (near,) = small_call(join_z, place, [final, *got], [flag], [shape(half, NARROW)], "join_z")
    far = swap(near, X)
    grad_out, flag = out_part(grad_out, 2, [near])
    grad_tokens, grad_gates = small_call(
        join_x, place, [near, far], [flag],
        [shape(tok_rows, NARROW, model_width), shape(tok_rows, NARROW, LANES)], "join_x",
    )
    grad_gates = grad_gates[:, :top_count]
    return (grad_tokens, grad_gates, stored_view(grad_in), stored_view(grad_out))


def local_general(tokens, cotangent, expert_ids, gate_values, w_in, w_out):
    tok_rows, model_width = tokens.shape
    local_count = w_in.shape[1]
    first = lax.axis_index("expert") * local_count
    gather = functools.partial(lax.all_gather, axis_name="expert", axis=0)
    ids, gates = gather(expert_ids), gather(gate_values).astype(WIDE)
    x_blocks, g_blocks = gather(tokens), gather(cotangent)
    blocks = ids.shape[0]
    names = first + jnp.arange(local_count, dtype=jnp.int32)
    named = ids[:, None] == names[None, :, None, None]
    hit = jnp.any(named, axis=3)
    gate_tok = jnp.sum(jnp.where(named, gates[:, None], 0.0), axis=3)
    earlier = jnp.tril(jnp.ones((tok_rows, tok_rows), WIDE), -1)
    position = jnp.einsum("tu,blu->blt", earlier, hit.astype(WIDE)).astype(jnp.int32)
    slots = jnp.arange(CAP, dtype=jnp.int32)
    choose = hit[:, :, None] & (position[:, :, None] == slots[None, None, :, None])
    pick = choose.astype(NARROW)
    slot_x = jnp.einsum("blst,btd->lbsd", pick, x_blocks, preferred_element_type=WIDE).astype(NARROW)
    slot_g = jnp.einsum("blst,btd->lbsd", pick, g_blocks, preferred_element_type=WIDE).astype(NARROW)
    gate_slot = jnp.sum(jnp.where(choose, gate_tok[:, :, None], 0.0), axis=3)
    rows = blocks * CAP
    slot_x = slot_x.reshape(local_count, rows, model_width)
    slot_g = slot_g.reshape(local_count, rows, model_width)
    gate_slot = jnp.swapaxes(gate_slot, 0, 1).reshape(local_count, rows, 1)
    pre_act = jnp.einsum("lrd,dlf->lrf", slot_x, w_in, preferred_element_type=WIDE)
    upstream = jnp.einsum("lrd,fld->lrf", slot_g, w_out, preferred_element_type=WIDE)
    squash = jax.nn.sigmoid(pre_act)
    active = pre_act * squash
    gate_part = jnp.sum(active * upstream, axis=-1)
    act_gated = (gate_slot * active).astype(NARROW)
    grad_pre = (gate_slot * squash * (1.0 + pre_act * (1.0 - squash)) * upstream).astype(NARROW)
    gate_part = jnp.swapaxes(gate_part.reshape(local_count, blocks, CAP), 0, 1)
    gate_tok = jnp.sum(jnp.where(choose, gate_part[..., None], 0.0), axis=2)
    gate_back = jnp.sum(jnp.where(named, gate_tok[..., None], 0.0), axis=1)
    part_x = jnp.einsum("lrf,dlf->lrd", grad_pre, w_in, preferred_element_type=WIDE)
    part_x = part_x.astype(NARROW).reshape(local_count, blocks, CAP, model_width)
    token_part = jnp.einsum("blst,lbsd->btd", pick, part_x, preferred_element_type=WIDE)
    scatter = functools.partial(lax.psum_scatter, axis_name="expert", scatter_dimension=0)
    grad_tokens = lax.psum(scatter(token_part), "fsdp").astype(NARROW)
    grad_gates = lax.psum(scatter(gate_back), "fsdp").astype(NARROW)
    grad_in = jnp.einsum("lrd,lrf->dlf", slot_x, grad_pre, preferred_element_type=WIDE).astype(NARROW)
    grad_out = jnp.einsum("lrf,lrd->fld", act_gated, slot_g, preferred_element_type=WIDE).astype(NARROW)
    return (grad_tokens, grad_gates, grad_in, grad_out)


def solution(mesh):
    return jax.shard_map(
        local,
        mesh=mesh,
        in_specs=(
            P("expert", None),
            P("expert", None),
            P("expert", None),
            P("expert", None),
            P(None, "expert", "fsdp"),
            P("fsdp", "expert", None),
        ),
        out_specs=(
            P("expert", None),
            P("expert", None),
            P(None, "expert", "fsdp"),
            P("fsdp", "expert", None),
        ),
        check_vma=False,
    )
```

time: 191 us -> 202 us (1.058)
  Pallas kernels: 130 us -> 149 us
  waiting for transfers between devices: 16.1 us -> 7.14 us
  starting transfers between devices: 29.1 us -> 22 us
  other arithmetic: 2.48 us -> 6.74 us
  local copies, waits for them, and re-layouts: 11.9 us -> 14.7 us
    pallas_call x12 -> x11, Pallas kernels: 126 us -> 141 us  [the longest x7 56.9 us: outer(): pl.pallas_call(functools.partial(outer_body, group, some), out_shape=[jax...]
    ppermute x30 -> x24, waiting for transfers between devices: 16.1 us -> 7.14 us  [swap(): return lax.ppermute(value, AXES, [(i, i ^ mask) for i in range(size)])]
    ppermute x30 -> x24, starting transfers between devices: 29.1 us -> 22 us  [swap(): return lax.ppermute(value, AXES, [(i, i ^ mask) for i in range(size)])]
    unnamed x28 -> x47, local copies, waits for them, and re-layouts: 7.81 us -> 11.4 us
    pallas_call x5, Pallas kernels: 4.27 us -> 7.26 us  [small_call(): pl.pallas_call(run, out_shape=outs, in_specs=[pl.BlockSpec(memory_space=p...]
  transfers between devices with their start and end apart: 30 -> 24, of which waited for: 6 -> 1; matrix products, arithmetic and copies ran while one was open for 4% -> 5% of each run, Pallas kernels for 49% -> 55%
where the time goes in v4:
time: 202 us; the launch traced here: 201 us
  Pallas kernels  149 us (74%)
  starting transfers between devices  22 us (11%)
  local copies, waits for them, and re-layouts  14.7 us (7%)
  waiting for transfers between devices  7.14 us (4%)
  other arithmetic  6.74 us (3%)
    pallas_call x7, Pallas kernels, outer(): pl.pallas_call(functools.partial(outer_body, group, some), out_shape=[jax...  56.9 us
    pallas_call x2, Pallas kernels, split_experts(): pl.pallas_call(functools.partial(split_body, group, some), out_shape=[jax...  39.5 us
    pallas_call x1, Pallas kernels, forward_cotangents(): pl.pallas_call(forward_cotangents_body, out_shape=[jax.ShapeDtypeStruct((...  30.7 us
    ppermute x24, starting transfers between devices, swap(): return lax.ppermute(value, AXES, [(i, i ^ mask) for i in range(size)])  22 us
    pallas_call x1, Pallas kernels, forward_tokens(): pl.pallas_call(forward_tokens_body, out_shape=[jax.ShapeDtypeStruct((expe...  14.3 us
    unnamed x47, local copies, waits for them, and re-layouts  11.4 us
    pallas_call x5, Pallas kernels, small_call(): pl.pallas_call(run, out_shape=outs, in_specs=[pl.BlockSpec(memory_space=p...  7.26 us
    ppermute x24, waiting for transfers between devices, swap(): return lax.ppermute(value, AXES, [(i, i ^ mask) for i in range(size)])  7.14 us
  transfers between devices with their start and end apart: 24, of which 1 were waited for; matrix products, arithmetic and copies ran while one was open for 5% of the time, Pallas kernels for 55%

profile of v4, /device:TPU:0, one launch (start us, length us, event | category | flops | bytes accessed | tf_op | source)
XLA Modules:
  0.0 201.1 jit_solution(3518567111262545119)
XLA Ops:
  2.3 2.4 %collective-permute-start.2 = (f32[8,128]{1,0:T(8,128)S(1)}, f32[8,128]{1,0:T(8,128)S(1)}, u32[]{:S(2)}, u32[]{:S(2)}) collective-permute-start(f32[8,128]{1,0:T(8,128)S(1)} %maximum_select_fusion), channel_id=1, source_target_pairs={{0,3},{1,2},{2,1},{3,0},{4,7},{5,6},{6,5},{7,4},{8,11},{9,10},{10,... | collective-permute-start | bytes 12296 | tf_op jit(solution)/shard_map/ppermute | solution.py:28
  5.8 1.0 constant_dynamic-slice_fusion.1
  6.8 1.5 collective-permute-start.4
  10.9 19.6 %split_experts.2 = (bf16[4,3072,768]{2,1,0:T(8,128)(2,1)}, f32[8,128]{1,0:T(8,128)}) custom-call(bf16[192,192]{1,0:T(8,128)(2,1)} %constant.62.clone.sort_ref, bf16[3072,6,4,128]{3,2,1,0:T(4,128)(2,1)} %bitcast.37), custom_call_target="tpu_custom_call" | custom-call | bytes 37748736 | tf_op jit(solution)/shard_map/split_experts/pallas_call | solution.py:183
  31.9 1.4 collective-permute-start.5
  34.9 19.9 %split_experts.3 = (bf16[4,768,3072]{2,1,0:T(8,128)(2,1)}, f32[8,128]{1,0:T(8,128)}) custom-call(bf16[256,256]{1,0:T(8,128)(2,1)} %constant.63.clone.sort_ref, bf16[768,24,4,128]{3,2,1,0:T(4,128)(2,1)} %bitcast.38, bf16[64,3072]{1,0:T(8,128)(2,1)} %hold.2.refs_0_.refs_2_), custom_call_target="tpu_custom_call" | custom-call | bytes 37748736 | tf_op jit(solution)/shard_map/split_experts/pallas_call | solution.py:183
  60.4 7.1 %collective-permute-done.10.refs_3_ = bf16[64,3072]{1,0:T(8,128)(2,1)S(1)} collective-permute-done((bf16[64,3072]{1,0:T(8,128)(2,1)}, bf16[64,3072]{1,0:T(8,128)(2,1)S(1)}, u32[]{:S(2)}, u32[]{:S(2)}) %collective-permute-start.10) | collective-permute-done | bytes 393248 | tf_op jit(solution)/shard_map/ppermute | solution.py:28
  68.3 14.3 %forward_tokens.1 = (bf16[4,160,3072]{2,1,0:T(8,128)(2,1)}, bf16[4,160,768]{2,1,0:T(8,128)(2,1)}, f32[4,160,768]{2,1,0:T(8,128)}, f32[4,160,768]{2,1,0:T(8,128)}) custom-call(s32[4,1,512]{2,1,0:T(1,128)} %bitcast.39, f32[4,1,512]{2,1,0:T(1,128)} %bitcast.41, bf16[4,3072,768]{2,1,0:T(8,128)(2,1)} %get-tuple-element.42.w_ref, bf16[128,3072]{1,0:T(8,128)(2,1)} %refs_0_.2, ...), custom_call_target="tpu_custom_call" | custom-call | flops 5033164800 | bytes 18874368 | tf_op jit(solution)/shard_map/forward_tokens/pallas_call | solution.py:249
  83.8 30.7 %forward_cotangents.1 = (bf16[4,160,3072]{2,1,0:T(8,128)(2,1)}, bf16[4,160,768]{2,1,0:T(8,128)(2,1)}, f32[256,3200]{1,0:T(8,128)}, bf16[256,3200]{1,0:T(8,128)(2,1)}) custom-call(s32[4,1,512]{2,1,0:T(1,128)} %bitcast.40, f32[4,160,768]{2,1,0:T(8,128)} %get-tuple-element.46.active_ref, f32[4,160,768]{2,1,0:T(8,128)} %get-tuple-element.47.slope_ref, ...), custom_call_target="tpu_custom_call" | custom-call | flops 10066329600 | bytes 37748736 | tf_op jit(solution)/shard_map/forward_cotangents/pallas_call | solution.py:326
  115.7 7.7 %weight_gradient.7 = (bf16[3072,6,4,128]{3,2,1,0:T(4,128)(2,1)}, f32[8,128]{1,0:T(8,128)}) custom-call(bf16[192,192]{1,0:T(8,128)(2,1)} %constant.64.sort_ref, bf16[4,160,3072]{2,1,0:T(8,128)(2,1)} %get-tuple-element.52.a_ref, bf16[4,160,768]{2,1,0:T(8,128)(2,1)} %get-tuple-element.53.b_ref), custom_call_target="tpu_custom_call" | custom-call | flops 754974720 | bytes 9437184 | tf_op jit(solution)/shard_map/weight_gradient/pallas_call | solution.py:408
  123.4 1.2 copy-done.14
  124.6 3.9 %first_sum.1 = (f32[64,3200]{1,0:T(8,128)}, bf16[64,3200]{1,0:T(8,128)(2,1)}, bf16[64,3200]{1,0:T(8,128)(2,1)}, bf16[64,3200]{1,0:T(8,128)(2,1)}) custom-call(s32[2]{0:T(128)} %pad_add_fusion.place_ref, f32[256,3200]{1,0:T(8,128)} %get-tuple-element.50.refs_0_, bf16[256,3200]{1,0:T(8,128)(2,1)} %copy-done.14, f32[8,128]{1,0:T(8,128)} %get-tuple-element.54.refs_2_), custom_call_target="tpu_custom_call" | custom-call | bytes 1048576 | tf_op jit(solution)/shard_map/first_sum/pallas_call | solution.py:56
  129.0 1.3 collective-permute-start.15
  130.4 1.6 collective-permute-start.16
  131.9 7.7 %weight_gradient.8 = (bf16[3072,6,4,128]{3,2,1,0:T(4,128)(2,1)}, f32[8,128]{1,0:T(8,128)}) custom-call(bf16[192,192]{1,0:T(8,128)(2,1)} %constant.64.sort_ref, bf16[4,160,3072]{2,1,0:T(8,128)(2,1)} %get-tuple-element.52.a_ref, bf16[4,160,768]{2,1,0:T(8,128)(2,1)} %get-tuple-element.53.b_ref, ...), custom_call_target="tpu_custom_call", output_to_operand_aliasing={{0}: (3, {})} | custom-call | flops 754974720 | bytes 9437184 | tf_op jit(solution)/shard_map/weight_gradient/pallas_call | solution.py:408
  139.7 7.8 %weight_gradient.9 = (bf16[3072,6,4,128]{3,2,1,0:T(4,128)(2,1)}, f32[8,128]{1,0:T(8,128)}) custom-call(bf16[192,192]{1,0:T(8,128)(2,1)} %constant.64.sort_ref, bf16[4,160,3072]{2,1,0:T(8,128)(2,1)} %get-tuple-element.52.a_ref, bf16[4,160,768]{2,1,0:T(8,128)(2,1)} %get-tuple-element.53.b_ref, ...), custom_call_target="tpu_custom_call", output_to_operand_aliasing={{0}: (3, {})} | custom-call | flops 754974720 | bytes 9437184 | tf_op jit(solution)/shard_map/weight_gradient/pallas_call | solution.py:408
  147.4 7.7 %weight_gradient.10 = (bf16[3072,6,4,128]{3,2,1,0:T(4,128)(2,1)}, f32[8,128]{1,0:T(8,128)}) custom-call(bf16[192,192]{1,0:T(8,128)(2,1)} %constant.64.sort_ref, bf16[4,160,3072]{2,1,0:T(8,128)(2,1)} %get-tuple-element.52.a_ref, bf16[4,160,768]{2,1,0:T(8,128)(2,1)} %get-tuple-element.53.b_ref, ...), custom_call_target="tpu_custom_call", output_to_operand_aliasing={{0}: (3, {})} | custom-call | flops 754974720 | bytes 9437184 | tf_op jit(solution)/shard_map/weight_gradient/pallas_call | solution.py:408
  157.3 1.6 collective-permute-start.17
  158.9 2.6 %collective-permute-start.18 = (bf16[16,3200]{1,0:T(8,128)(2,1)S(1)}, bf16[16,3200]{1,0:T(8,128)(2,1)S(1)}, u32[]{:S(2)}, u32[]{:S(2)}) collective-permute-start(bf16[16,3200]{1,0:T(8,128)(2,1)S(1)} %get-tuple-element.67), channel_id=1, source_target_pairs={{0,16},{1,17},{2,18},{3,19},{4,20},{5,21},{6,22},{7,23},{8,24},{9,... | collective-permute-start | bytes 307208 | tf_op jit(solution)/shard_map/ppermute | solution.py:28
  161.7 8.7 %weight_gradient.11 = (bf16[768,24,4,128]{3,2,1,0:T(4,128)(2,1)}, f32[8,128]{1,0:T(8,128)}) custom-call(bf16[256,256]{1,0:T(8,128)(2,1)} %constant.65.sort_ref, bf16[4,160,768]{2,1,0:T(8,128)(2,1)} %get-tuple-element.69.a_ref, bf16[4,160,3072]{2,1,0:T(8,128)(2,1)} %get-tuple-element.70.b_ref, f32[16,3200]{1,0:T(8,128)} %copy-done.5), custom_call_target="tpu_custom_call" | custom-call | flops 1006632960 | bytes 12582912 | tf_op jit(solution)/shard_map/weight_gradient/pallas_call | solution.py:408
  172.6 3.7 %collective-permute-start.22 = (bf16[16,3200]{1,0:T(8,128)(2,1)S(1)}, bf16[16,3200]{1,0:T(8,128)(2,1)S(1)}, u32[]{:S(2)}, u32[]{:S(2)}) collective-permute-start(bf16[16,3200]{1,0:T(8,128)(2,1)S(1)} %third_sum.1.refs_1_.refs_0_), channel_id=1, source_target_pairs={{0,24},{1,25},{2,26},{3,27},{4,28},{5,29},{6,30},{7,31},{8,16},{9,... | collective-permute-start | bytes 307208 | tf_op jit(solution)/shard_map/ppermute | solution.py:28
  177.0 8.7 %weight_gradient.12 = (bf16[768,24,4,128]{3,2,1,0:T(4,128)(2,1)}, f32[8,128]{1,0:T(8,128)}) custom-call(bf16[256,256]{1,0:T(8,128)(2,1)} %constant.65.sort_ref, bf16[4,160,768]{2,1,0:T(8,128)(2,1)} %get-tuple-element.69.a_ref, bf16[4,160,3072]{2,1,0:T(8,128)(2,1)} %get-tuple-element.70.b_ref, ...), custom_call_target="tpu_custom_call", output_to_operand_aliasing={{0}: (3, {})} | custom-call | flops 1006632960 | bytes 12582912 | tf_op jit(solution)/shard_map/weight_gradient/pallas_call | solution.py:408
  188.6 8.7 %weight_gradient.13 = (bf16[768,24,4,128]{3,2,1,0:T(4,128)(2,1)}, f32[8,128]{1,0:T(8,128)}) custom-call(bf16[256,256]{1,0:T(8,128)(2,1)} %constant.65.sort_ref, bf16[4,160,768]{2,1,0:T(8,128)(2,1)} %get-tuple-element.69.a_ref, bf16[4,160,3072]{2,1,0:T(8,128)(2,1)} %get-tuple-element.70.b_ref, ...), custom_call_target="tpu_custom_call", output_to_operand_aliasing={{0}: (3, {})} | custom-call | flops 1006632960 | bytes 12582912 | tf_op jit(solution)/shard_map/weight_gradient/pallas_call | solution.py:408
  199.0 1.5 join_x.1
  (108 shorter events, 28.0 us)
Async XLA Ops:
  2.3 29.0 %collective-permute-start.2 = (f32[8,128]{1,0:T(8,128)S(1)}, f32[8,128]{1,0:T(8,128)S(1)}, u32[]{:S(2)}, u32[]{:S(2)}) collective-permute-start(f32[8,128]{1,0:T(8,128)S(1)} %maximum_select_fusion), channel_id=1, source_target_pairs={{0,3},{1,2},{2,1},{3,0},{4,7},{5,6},{6,5},{7,4},{8,11},{9,10},{10,... | collective-permute-start | bytes 12296 | tf_op jit(solution)/shard_map/ppermute | solution.py:28
  4.7 27.3 %collective-permute-start.1 = (f32[8,128]{1,0:T(8,128)S(1)}, f32[8,128]{1,0:T(8,128)S(1)}, u32[]{:S(2)}, u32[]{:S(2)}) collective-permute-start(f32[8,128]{1,0:T(8,128)S(1)} %maximum_select_fusion), channel_id=1, source_target_pairs={{0,2},{1,3},{2,0},{3,1},{4,6},{5,7},{6,4},{7,5},{8,10},{9,11},{10,... | collective-permute-start | bytes 12296 | tf_op jit(solution)/shard_map/ppermute | solution.py:28
  5.3 28.1 %collective-permute-start = (f32[8,128]{1,0:T(8,128)S(1)}, f32[8,128]{1,0:T(8,128)}, u32[]{:S(2)}, u32[]{:S(2)}) collective-permute-start(f32[8,128]{1,0:T(8,128)S(1)} %get-tuple-element.91), channel_id=1, source_target_pairs={{0,1},{1,0},{2,3},{3,2},{4,5},{5,4},{6,7},{7,6},{8,9},{9,8},{10,11... | collective-permute-start | bytes 12296 | tf_op jit(solution)/shard_map/ppermute | solution.py:28
  5.3 55.1 %collective-permute-start.3 = (bf16[128,3072]{1,0:T(8,128)(2,1)}, bf16[128,3072]{1,0:T(8,128)(2,1)S(1)}, u32[]{:S(2)}, u32[]{:S(2)}) collective-permute-start(bf16[128,3072]{1,0:T(8,128)(2,1)} %refs_0_.2), channel_id=1, source_target_pairs={{0,1},{1,0},{2,3},{3,2},{4,5},{5,4},{6,7},{7,6},{8,9},{9,8},{10,11... | collective-permute-start | bytes 2359304 | tf_op jit(solution)/shard_map/ppermute | solution.py:28
  6.8 23.7 %collective-permute-start.4 = (bf16[64,3072]{1,0:T(8,128)(2,1)S(1)}, bf16[64,3072]{1,0:T(8,128)(2,1)S(1)}, u32[]{:S(2)}, u32[]{:S(2)}) collective-permute-start(bf16[64,3072]{1,0:T(8,128)(2,1)S(1)} %constant_dynamic-slice_fusion.1), channel_id=1, source_target_pairs={{0,2},{1,3},{2,0},{3,1},{4,6},{5,7},{6,4},{7,5},{8,10},{9,11},{10,... | collective-permute-start | bytes 1179656 | tf_op jit(solution)/shard_map/ppermute | solution.py:28
  30.5 52.2 %collective-permute-start.9 = (bf16[128,3072]{1,0:T(8,128)(2,1)S(1)}, bf16[128,3072]{1,0:T(8,128)(2,1)S(1)}, u32[]{:S(2)}, u32[]{:S(2)}) collective-permute-start(bf16[128,3072]{1,0:T(8,128)(2,1)S(1)} %copy-done.13), channel_id=1, source_target_pairs={{0,1},{1,0},{2,3},{3,2},{4,5},{5,4},{6,7},{7,6},{8,9},{9,8},{10,11... | collective-permute-start | bytes 2359304 | tf_op jit(solution)/shard_map/ppermute | solution.py:28
  31.3 23.6 %collective-permute-start.6 = (bf16[64,3072]{1,0:T(8,128)(2,1)S(1)}, bf16[64,3072]{1,0:T(8,128)(2,1)S(1)}, u32[]{:S(2)}, u32[]{:S(2)}) collective-permute-start(bf16[64,3072]{1,0:T(8,128)(2,1)S(1)} %constant_dynamic-slice_fusion), channel_id=1, source_target_pairs={{0,2},{1,3},{2,0},{3,1},{4,6},{5,7},{6,4},{7,5},{8,10},{9,11},{10,... | collective-permute-start | bytes 1179656 | tf_op jit(solution)/shard_map/ppermute | solution.py:28
  31.9 22.9 %collective-permute-start.5 = (bf16[64,3072]{1,0:T(8,128)(2,1)}, bf16[64,3072]{1,0:T(8,128)(2,1)S(1)}, u32[]{:S(2)}, u32[]{:S(2)}) collective-permute-start(bf16[64,3072]{1,0:T(8,128)(2,1)} %hold.2.refs_0_.refs_2_), channel_id=1, source_target_pairs={{0,4},{1,5},{2,6},{3,7},{4,0},{5,1},{6,2},{7,3},{8,12},{9,13},{10,... | collective-permute-start | bytes 1179656 | tf_op jit(solution)/shard_map/ppermute | solution.py:28
  34.8 32.7 %collective-permute-start.7 = (bf16[64,3072]{1,0:T(8,128)(2,1)}, bf16[64,3072]{1,0:T(8,128)(2,1)}, u32[]{:S(2)}, u32[]{:S(2)}) collective-permute-start(bf16[64,3072]{1,0:T(8,128)(2,1)} %hold.2.refs_0_.refs_2_), channel_id=1, source_target_pairs={{0,1},{1,0},{2,3},{3,2},{4,5},{5,4},{6,7},{7,6},{8,9},{9,8},{10,11... | collective-permute-start | bytes 1179656 | tf_op jit(solution)/shard_map/ppermute | solution.py:28
  55.8 11.8 %collective-permute-start.8 = (bf16[64,3072]{1,0:T(8,128)(2,1)}, bf16[64,3072]{1,0:T(8,128)(2,1)S(1)}, u32[]{:S(2)}, u32[]{:S(2)}) collective-permute-start(bf16[64,3072]{1,0:T(8,128)(2,1)} %get-tuple-element.45.refs_3_), channel_id=1, source_target_pairs={{0,1},{1,0},{2,3},{3,2},{4,5},{5,4},{6,7},{7,6},{8,9},{9,8},{10,11... | collective-permute-start | bytes 1179656 | tf_op jit(solution)/shard_map/ppermute | solution.py:28
  56.2 11.3 %collective-permute-start.10 = (bf16[64,3072]{1,0:T(8,128)(2,1)}, bf16[64,3072]{1,0:T(8,128)(2,1)S(1)}, u32[]{:S(2)}, u32[]{:S(2)}) collective-permute-start(bf16[64,3072]{1,0:T(8,128)(2,1)} %get-tuple-element.49.refs_2_), channel_id=1, source_target_pairs={{0,4},{1,5},{2,6},{3,7},{4,0},{5,1},{6,2},{7,3},{8,12},{9,13},{10,... | collective-permute-start | bytes 1179656 | tf_op jit(solution)/shard_map/ppermute | solution.py:28
  60.4 22.3 %collective-permute-start.11 = (bf16[64,3072]{1,0:T(8,128)(2,1)}, bf16[64,3072]{1,0:T(8,128)(2,1)S(1)}, u32[]{:S(2)}, u32[]{:S(2)}) collective-permute-start(bf16[64,3072]{1,0:T(8,128)(2,1)} %get-tuple-element.49.refs_2_), channel_id=1, source_target_pairs={{0,1},{1,0},{2,3},{3,2},{4,5},{5,4},{6,7},{7,6},{8,9},{9,8},{10,11... | collective-permute-start | bytes 1179656 | tf_op jit(solution)/shard_map/ppermute | solution.py:28
  67.5 15.2 %collective-permute-start.12 = (bf16[64,3072]{1,0:T(8,128)(2,1)S(1)}, bf16[64,3072]{1,0:T(8,128)(2,1)S(1)}, u32[]{:S(2)}, u32[]{:S(2)}) collective-permute-start(bf16[64,3072]{1,0:T(8,128)(2,1)S(1)} %collective-permute-done.10.refs_3_), channel_id=1, source_target_pairs={{0,1},{1,0},{2,3},{3,2},{4,5},{5,4},{6,7},{7,6},{8,9},{9,8},{10,11... | collective-permute-start | bytes 1179656 | tf_op jit(solution)/shard_map/ppermute | solution.py:28
  114.5 8.9 %collective-permute-start.13 = (bf16[256,3200]{1,0:T(8,128)(2,1)}, bf16[256,3200]{1,0:T(8,128)(2,1)S(1)}, u32[]{:S(2)}, u32[]{:S(2)}) collective-permute-start(bf16[256,3200]{1,0:T(8,128)(2,1)} %get-tuple-element.51), channel_id=1, source_target_pairs={{0,1},{1,0},{2,3},{3,2},{4,5},{5,4},{6,7},{7,6},{8,9},{9,8},{10,11... | collective-permute-start | bytes 4915208 | tf_op jit(solution)/shard_map/ppermute | solution.py:28
  128.4 26.7 %collective-permute-start.14 = (bf16[64,3200]{1,0:T(8,128)(2,1)}, bf16[64,3200]{1,0:T(8,128)(2,1)S(1)}, u32[]{:S(2)}, u32[]{:S(2)}) collective-permute-start(bf16[64,3200]{1,0:T(8,128)(2,1)} %get-tuple-element.56), channel_id=1, source_target_pairs={{0,4},{1,5},{2,6},{3,7},{4,0},{5,1},{6,2},{7,3},{8,12},{9,13},{10,... | collective-permute-start | bytes 1228808 | tf_op jit(solution)/shard_map/ppermute | solution.py:28
  129.0 26.1 %collective-permute-start.15 = (bf16[64,3200]{1,0:T(8,128)(2,1)}, bf16[64,3200]{1,0:T(8,128)(2,1)S(1)}, u32[]{:S(2)}, u32[]{:S(2)}) collective-permute-start(bf16[64,3200]{1,0:T(8,128)(2,1)} %get-tuple-element.57), channel_id=1, source_target_pairs={{0,2},{1,3},{2,0},{3,1},{4,6},{5,7},{6,4},{7,5},{8,10},{9,11},{10,... | collective-permute-start | bytes 1228808 | tf_op jit(solution)/shard_map/ppermute | solution.py:28
  130.4 24.8 %collective-permute-start.16 = (bf16[64,3200]{1,0:T(8,128)(2,1)}, bf16[64,3200]{1,0:T(8,128)(2,1)S(1)}, u32[]{:S(2)}, u32[]{:S(2)}) collective-permute-start(bf16[64,3200]{1,0:T(8,128)(2,1)} %get-tuple-element.58), channel_id=1, source_target_pairs={{0,6},{1,7},{2,4},{3,5},{4,2},{5,3},{6,0},{7,1},{8,14},{9,15},{10,... | collective-permute-start | bytes 1228808 | tf_op jit(solution)/shard_map/ppermute | solution.py:28
  157.3 13.1 %collective-permute-start.17 = (bf16[16,3200]{1,0:T(8,128)(2,1)S(1)}, bf16[16,3200]{1,0:T(8,128)(2,1)S(1)}, u32[]{:S(2)}, u32[]{:S(2)}) collective-permute-start(bf16[16,3200]{1,0:T(8,128)(2,1)S(1)} %get-tuple-element.66), channel_id=1, source_target_pairs={{0,8},{1,9},{2,10},{3,11},{4,12},{5,13},{6,14},{7,15},{8,0},{9,1},... | collective-permute-start | bytes 307208 | tf_op jit(solution)/shard_map/ppermute | solution.py:28
  158.9 11.5 %collective-permute-start.18 = (bf16[16,3200]{1,0:T(8,128)(2,1)S(1)}, bf16[16,3200]{1,0:T(8,128)(2,1)S(1)}, u32[]{:S(2)}, u32[]{:S(2)}) collective-permute-start(bf16[16,3200]{1,0:T(8,128)(2,1)S(1)} %get-tuple-element.67), channel_id=1, source_target_pairs={{0,16},{1,17},{2,18},{3,19},{4,20},{5,21},{6,22},{7,23},{8,24},{9,... | collective-permute-start | bytes 307208 | tf_op jit(solution)/shard_map/ppermute | solution.py:28
  161.5 8.9 %collective-permute-start.19 = (bf16[16,3200]{1,0:T(8,128)(2,1)S(1)}, bf16[16,3200]{1,0:T(8,128)(2,1)S(1)}, u32[]{:S(2)}, u32[]{:S(2)}) collective-permute-start(bf16[16,3200]{1,0:T(8,128)(2,1)S(1)} %get-tuple-element.68), channel_id=1, source_target_pairs={{0,24},{1,25},{2,26},{3,27},{4,28},{5,29},{6,30},{7,31},{8,16},{9,... | collective-permute-start | bytes 307208 | tf_op jit(solution)/shard_map/ppermute | solution.py:28
  172.6 13.1 %collective-permute-start.22 = (bf16[16,3200]{1,0:T(8,128)(2,1)S(1)}, bf16[16,3200]{1,0:T(8,128)(2,1)S(1)}, u32[]{:S(2)}, u32[]{:S(2)}) collective-permute-start(bf16[16,3200]{1,0:T(8,128)(2,1)S(1)} %third_sum.1.refs_1_.refs_0_), channel_id=1, source_target_pairs={{0,24},{1,25},{2,26},{3,27},{4,28},{5,29},{6,30},{7,31},{8,16},{9,... | collective-permute-start | bytes 307208 | tf_op jit(solution)/shard_map/ppermute | solution.py:28
  176.3 9.4 %collective-permute-start.21 = (bf16[16,3200]{1,0:T(8,128)(2,1)S(1)}, bf16[16,3200]{1,0:T(8,128)(2,1)S(1)}, u32[]{:S(2)}, u32[]{:S(2)}) collective-permute-start(bf16[16,3200]{1,0:T(8,128)(2,1)S(1)} %third_sum.1.refs_1_.refs_0_), channel_id=1, source_target_pairs={{0,16},{1,17},{2,18},{3,19},{4,20},{5,21},{6,22},{7,23},{8,24},{9,... | collective-permute-start | bytes 307208 | tf_op jit(solution)/shard_map/ppermute | solution.py:28
  176.3 9.4 %collective-permute-start.20 = (bf16[16,3200]{1,0:T(8,128)(2,1)S(1)}, bf16[16,3200]{1,0:T(8,128)(2,1)S(1)}, u32[]{:S(2)}, u32[]{:S(2)}) collective-permute-start(bf16[16,3200]{1,0:T(8,128)(2,1)S(1)} %third_sum.1.refs_1_.refs_0_), channel_id=1, source_target_pairs={{0,8},{1,9},{2,10},{3,11},{4,12},{5,13},{6,14},{7,15},{8,0},{9,1},... | collective-permute-start | bytes 307208 | tf_op jit(solution)/shard_map/ppermute | solution.py:28
  187.9 9.4 %collective-permute-start.23 = (bf16[64,3200]{1,0:T(8,128)(2,1)S(1)}, bf16[64,3200]{1,0:T(8,128)(2,1)S(1)}, u32[]{:S(2)}, u32[]{:S(2)}) collective-permute-start(bf16[64,3200]{1,0:T(8,128)(2,1)S(1)} %join_z.1.refs_1_.refs_0_), channel_id=1, source_target_pairs={{0,4},{1,5},{2,6},{3,7},{4,0},{5,1},{6,2},{7,3},{8,12},{9,13},{10,... | collective-permute-start | bytes 1228808 | tf_op jit(solution)/shard_map/ppermute | solution.py:28
  (23 other events, 102.0 us)

commit v5 on v4

--- a/solution.py
+++ b/solution.py
@@ -44,18 +44,20 @@
 FLAG = jax.ShapeDtypeStruct((8, LANES), WIDE)
 
 
-def small_call(body, place, inputs, after, outs, name, grant=12):
+def small_call(body, place, inputs, after, outs, name, grant=12, steps=1):
     given = len(inputs)
 
     def run(place_ref, *refs):
         body(place_ref, refs[:given], refs[given + len(after) :])
 
     def whole(array):
-        return pl.BlockSpec(array.shape, lambda: (0,) * len(array.shape))
+        rows, columns = array.shape
+        return pl.BlockSpec((rows, columns // steps), lambda i: (0, i))
 
     return pl.pallas_call(
         run,
         out_shape=outs,
+        grid=(steps,),
         in_specs=[pl.BlockSpec(memory_space=pltpu.SMEM)]
         + [whole(array) for array in inputs]
         + [ANY] * len(after),
@@ -142,9 +144,40 @@
     return weight.reshape(rows, experts, columns // LANES, LANES).transpose(0, 2, 1, 3)
 
 
-def split_body(group, some, sort_ref, w_ref, *refs):
-    out_ref, flag_ref = refs[-2:]
-    flag_ref[...] = jnp.zeros_like(flag_ref)
+def staged(stages, outs, sem, compute):
+    step, steps = pl.program_id(0), pl.num_programs(0)
+
+    def copies(slot, at_step):
+        return [
+            pltpu.make_async_copy(source, target, sem.at[slot, number])
+            for number, (source, target) in enumerate(outs(stages[slot], at_step))
+        ]
+
+    for slot in range(2):
+
+        @pl.when(lax.rem(step, 2) == slot)
+        def _():
+            @pl.when(step >= 2)
+            def _():
+                for copy in copies(slot, step - 2):
+                    copy.wait()
+
+            compute(stages[slot])
+            for copy in copies(slot, step):
+                copy.start()
+
+            @pl.when(step == steps - 1)
+            def _():
+                @pl.when(step >= 1)
+                def _():
+                    for copy in copies(1 - slot, step - 1):
+                        copy.wait()
+
+                for copy in copies(slot, step):
+                    copy.wait()
+
+
+def split_block(group, some, sort_ref, w_ref, out_ref, base):
     rows, tiles, experts, _ = w_ref.shape
     held = group * experts
     flat = w_ref.reshape(rows, tiles * experts, LANES)
@@ -165,40 +198,64 @@
                     for side in range(2)
                 ]
                 if some == 8:
-                    row, first = pair[0][0], pair[0][1] + tile
+                    row, first = base + pair[0][0], pair[0][1] + tile
                     out_ref[expert, row : row + 16, first * LANES : (first + 1) * LANES] = (
                         jnp.concatenate(parts, axis=0).astype(NARROW)
                     )
                 else:
                     for (row, first), part in zip(pair, parts):
                         column = (first + tile) * LANES
-                        out_ref[expert, row : row + some, column : column + LANES] = part.astype(
-                            NARROW
-                        )
+                        out_ref[
+                            expert, base + row : base + row + some, column : column + LANES
+                        ] = part.astype(NARROW)
 
 
 def split_experts(view, sort, block, group, some, after):
     rows, tiles, experts, _ = view.shape
     columns = tiles * LANES
+    streams = 4
+    part = block // streams
+
+    def body(sort_ref, *refs):
+        out_ref, flag_ref, low, high, sem = refs[-5:]
+        flag_ref[...] = jnp.zeros_like(flag_ref)
+
+        def outs(stage, step):
+            into = pl.ds(pl.multiple_of(step * block, block), block)
+            return [(stage.at[expert], out_ref.at[expert, into]) for expert in range(experts)]
+
+        def compute(stage):
+            for number in range(streams):
+                split_block(group, some, sort_ref, refs[number], stage, number * part)
+
+        staged((low, high), outs, sem, compute)
+
+    def piece(number):
+        return pl.BlockSpec(
+            (part, tiles, experts, LANES), lambda i: (i * streams + number, 0, 0, 0)
+        )
+
     return pl.pallas_call(
-        functools.partial(split_body, group, some),
+        body,
         out_shape=[jax.ShapeDtypeStruct((experts, rows, columns), NARROW), FLAG],
         grid=(rows // block,),
         in_specs=[
             pl.BlockSpec(sort.shape, lambda i: (0, 0)),
-            pl.BlockSpec((block, tiles, experts, LANES), lambda i: (i, 0, 0, 0)),
+            *[piece(number) for number in range(streams)],
             *[ANY] * len(after),
         ],
-        out_specs=[
-            pl.BlockSpec((experts, block, columns), lambda i: (0, i, 0)),
-            pl.BlockSpec(FLAG.shape, lambda i: (0, 0)),
+        out_specs=[ANY, pl.BlockSpec(FLAG.shape, lambda i: (0, 0))],
+        scratch_shapes=[
+            pltpu.VMEM((experts, block, columns), NARROW),
+            pltpu.VMEM((experts, block, columns), NARROW),
+            pltpu.SemaphoreType.DMA((2, experts)),
         ],
         compiler_params=pltpu.CompilerParams(vmem_limit_bytes=56 * MIB),
         cost_estimate=pl.CostEstimate(
             flops=0, bytes_accessed=4 * experts * rows * columns, transcendentals=0
         ),
         name="split_experts",
-    )(sort, view, *after)
+    )(sort, *[view] * streams, *after)
 
 
 def fetch(pieces, whole, sem):
@@ -221,7 +278,17 @@
     return lax.broadcasted_iota(jnp.int32, (slots, tokens), 0) == jnp.bitwise_and(code, 1023)
 
 
-def forward_tokens_body(code_ref, gate_ref, w_ref, *refs):
+def weight_parts(weights, streams):
+    _, rows, columns = weights.shape
+    specs = [
+        pl.BlockSpec((1, rows // streams, columns), lambda i, number=number: (i, number, 0))
+        for number in range(streams)
+    ]
+    return specs, [weights] * streams
+
+
+def forward_tokens_body(code_ref, gate_ref, *refs):
+    w_refs, refs = refs[:4], refs[4:]
     pieces, (xs_ref, ag_ref, active_ref, slope_ref, x_ref, sem) = refs[:-6], refs[-6:]
     slots, model_width = xs_ref.shape[1:]
     columns = 512
@@ -232,7 +299,11 @@
     for begin in range(0, model_width, columns):
         part = slice(begin, begin + columns)
         xs_ref[0, :, part] = mm(pick, x_ref[:, part], NN).astype(NARROW)
-    pre_act = mm(xs_ref[0], w_ref[0], NN)
+    pre_act, begin = 0.0, 0
+    for w_ref in w_refs:
+        end = begin + w_ref.shape[1]
+        pre_act = pre_act + mm(xs_ref[0, :, begin:end], w_ref[0], NN)
+        begin = end
     squash = jax.nn.sigmoid(pre_act)
     active = pre_act * squash
     active_ref[0] = active
@@ -245,6 +316,7 @@
     tokens = code.shape[2]
     slots = tokens // 128 * CAP
     expert = lambda i: (i, 0, 0)
+    w_specs, w_operands = weight_parts(w_split, 4)
     shapes = [(model_width, NARROW), (hidden, NARROW), (hidden, WIDE), (hidden, WIDE)]
     return pl.pallas_call(
         forward_tokens_body,
@@ -253,7 +325,7 @@
         in_specs=[
             pl.BlockSpec((1, 1, tokens), expert),
             pl.BlockSpec((1, 1, tokens), expert),
-            pl.BlockSpec((1, model_width, hidden), expert),
+            *w_specs,
             *[ANY] * len(x_pieces),
         ],
         out_specs=[pl.BlockSpec((1, slots, width), expert) for width, _ in shapes],
@@ -268,10 +340,11 @@
             transcendentals=0,
         ),
         name="forward_tokens",
-    )(code, gate_tok, w_split, *x_pieces)
-
-
-def forward_cotangents_body(code_ref, active_ref, slope_ref, w_ref, v_ref, *refs):
+    )(code, gate_tok, *w_operands, *x_pieces)
+
+
+def forward_cotangents_body(code_ref, active_ref, slope_ref, *refs):
+    w_refs, v_refs, refs = refs[:3], refs[3:6], refs[6:]
     pieces = refs[:-8]
     gs_ref, gp_ref, keep_ref, send_ref, g_ref, back_ref, pick_ref, sem = refs[-8:]
     step = pl.program_id(0)
@@ -285,11 +358,17 @@
     for begin in range(0, model_width, columns):
         part = slice(begin, begin + columns)
         gs_ref[0, :, part] = mm(pick, g_ref[:, part], NN).astype(NARROW)
-    upstream = mm(gs_ref[0], v_ref[0], NT)
-    gate_part = jnp.sum(active_ref[0] * upstream, axis=1, keepdims=True)
-    gp_ref[0] = (slope_ref[0] * upstream).astype(NARROW)
+    gate_part, begin = 0.0, 0
+    for v_ref in v_refs:
+        part = slice(begin, begin + v_ref.shape[1])
+        upstream = mm(gs_ref[0], v_ref[0], NT)
+        gate_part = gate_part + jnp.sum(active_ref[0, :, part] * upstream, axis=1, keepdims=True)
+        gp_ref[0, :, part] = (slope_ref[0, :, part] * upstream).astype(NARROW)
+        begin = part.stop
     for begin in range(0, model_width, columns):
-        back = mm(gp_ref[0], w_ref[0, begin : begin + columns, :], NT)
+        held = w_refs[0].shape[1]
+        w_ref, inner = w_refs[begin // held], begin % held
+        back = mm(gp_ref[0], w_ref[0, inner : inner + columns, :], NT)
         back_ref[rows, begin : begin + columns] = back.astype(NARROW)
     which = jnp.sum(
         jnp.where(choose, jnp.right_shift(code_ref[0], 10), 0), axis=1, keepdims=True
@@ -323,6 +402,8 @@
     expert = lambda i: (i, 0, 0)
     whole = lambda i: (0, 0)
     one = pl.Buffered(1)
+    w_specs, w_operands = weight_parts(w_split, 3)
+    v_specs, v_operands = weight_parts(v_split, 3)
     return pl.pallas_call(
         forward_cotangents_body,
         out_shape=[
@@ -336,8 +417,8 @@
             pl.BlockSpec((1, 1, tokens), expert),
             pl.BlockSpec((1, slots, hidden), expert),
             pl.BlockSpec((1, slots, hidden), expert),
-            pl.BlockSpec((1, model_width, hidden), expert),
-            pl.BlockSpec((1, hidden, model_width), expert),
+            *w_specs,
+            *v_specs,
             *[ANY] * len(g_pieces),
         ],
         out_specs=[
@@ -359,69 +440,75 @@
             transcendentals=0,
         ),
         name="forward_cotangents",
-    )(code, active, slope, w_split, v_split, *g_pieces)
-
-
-def outer_body(group, some, sort_ref, a_ref, b_ref, *refs):
-    out_ref, flag_ref = refs[-2:]
-    flag_ref[...] = jnp.zeros_like(flag_ref)
+    )(code, active, slope, *w_operands, *v_operands, *g_pieces)
+
+
+def odd_tiles(rows):
+    tiles = -(-rows // 8)
+    return 8 * (tiles + 1 - tiles % 2)
+
+
+def outer_block(group, a_ref, b_ref, out_ref, wide_ref):
     rows, tiles, experts, _ = out_ref.shape
+    stride = wide_ref.shape[1]
     held = group * experts
     out = out_ref.reshape(rows, tiles * experts, LANES)
-    across = 1 if some == 8 else 2
-    for tile in range(0, tiles, group * across):
-        wide = group * across * LANES
-        parts = [
-            mm(a_ref[expert], b_ref[expert, :, tile * LANES : tile * LANES + wide], TN)
-            for expert in range(experts)
-        ]
-        for row in range(0, rows, 16):
-            pair = [(row, 0), (row + 8, 0)] if some == 8 else [(row, 0), (row, group)]
-            blocks = [
-                jnp.concatenate(
-                    [
-                        part[begin : begin + some, (first + inner) * LANES : (first + inner + 1) * LANES]
-                        for part in parts
-                        for inner in range(group)
-                    ],
-                    axis=0,
-                )
-                for begin, first in pair
-            ]
-            result = mm(sort_ref[...], jnp.concatenate(blocks, axis=1).astype(NARROW), NN)
-            for side, (begin, first) in enumerate(pair):
-                at_tile = (tile + first) * experts
-                out[begin : begin + some, at_tile : at_tile + held, :] = (
-                    result[:, side * LANES : (side + 1) * LANES]
-                    .astype(NARROW)
-                    .reshape(some, held, LANES)
-                )
-
-
-def outer(sort, a, b, holder, start, count, group, some, after):
+    flat = wide_ref.reshape(rows * stride, LANES)
+    for begin in range(0, tiles, group):
+        for expert in range(experts):
+            part = mm(a_ref[expert], b_ref[expert, :, begin * LANES : (begin + group) * LANES], TN)
+            for tile in range(group):
+                flat[pl.ds(tile * experts + expert, rows, stride), :] = part[
+                    :, tile * LANES : (tile + 1) * LANES
+                ]
+        out[:, begin * experts : begin * experts + held, :] = wide_ref[:, :held, :].astype(NARROW)
+
+
+def outer(a, b, holder, start, count, group, after):
     experts, slots, total = a.shape
     columns = b.shape[2]
     tiles = columns // LANES
-    block = 128
+    block, streams = 128, 4
     first = start // block
+    part = block // streams
     extra = list(after) if holder is None else [holder, *after]
+
+    def body(a_ref, b_ref, *refs):
+        out_ref, flag_ref, wide_ref, low, high, sem = refs[-6:]
+        flag_ref[...] = jnp.zeros_like(flag_ref)
+
+        def outs(stage, step):
+            return [
+                (
+                    stage.at[number * part : (number + 1) * part],
+                    out_ref.at[pl.ds(start + step * block + number * part, part)],
+                )
+                for number in range(streams)
+            ]
+
+        staged(
+            (low, high), outs, sem, lambda stage: outer_block(group, a_ref, b_ref, stage, wide_ref)
+        )
+
     return pl.pallas_call(
-        functools.partial(outer_body, group, some),
+        body,
         out_shape=[jax.ShapeDtypeStruct((total, tiles, experts, LANES), NARROW), FLAG],
         grid=(count // block,),
         in_specs=[
-            pl.BlockSpec(sort.shape, lambda i: (0, 0)),
             pl.BlockSpec((experts, slots, block), lambda i: (0, 0, first + i)),
             pl.BlockSpec(
                 (experts, slots, columns), lambda i: (0, 0, 0), pipeline_mode=pl.Buffered(1)
             ),
             *[ANY] * len(extra),
         ],
-        out_specs=[
-            pl.BlockSpec((block, tiles, experts, LANES), lambda i: (first + i, 0, 0, 0)),
-            pl.BlockSpec(FLAG.shape, lambda i: (0, 0)),
-        ],
-        input_output_aliases={} if holder is None else {3: 0},
+        out_specs=[ANY, pl.BlockSpec(FLAG.shape, lambda i: (0, 0))],
+        scratch_shapes=[
+            pltpu.VMEM((block, odd_tiles(group * experts), LANES), WIDE),
+            pltpu.VMEM((block, tiles, experts, LANES), NARROW),
+            pltpu.VMEM((block, tiles, experts, LANES), NARROW),
+            pltpu.SemaphoreType.DMA((2, streams)),
+        ],
+        input_output_aliases={} if holder is None else {2: 0},
         compiler_params=pltpu.CompilerParams(vmem_limit_bytes=56 * MIB),
         cost_estimate=pl.CostEstimate(
             flops=2 * experts * slots * count * columns,
@@ -429,7 +516,7 @@
             transcendentals=0,
         ),
         name="weight_gradient",
-    )(sort, a, b, *extra)
+    )(a, b, *extra)
 
 
 def stored_view(tiled):
@@ -489,7 +576,6 @@
     g_far_core = swap(g_far, CORE)
     g_pieces = [cotangent, g_core, g_near, g_far, g_near_core, g_far_core]
     gs, gp, keep, send = forward_cotangents(code, active, slope, g_pieces, w_split, v_split)
-    w_back, v_back = w_sort.T, v_sort.T
     width = keep.shape[1]
 
     def shape(rows, dtype, columns=width):
@@ -497,17 +583,17 @@
 
     def in_part(holder, number, after):
         rows = model_width // 4
-        return outer(w_back, xs, gp, holder, number * rows, rows, 6, 8, after)
+        return outer(xs, gp, holder, number * rows, rows, 6, after)
 
     def out_part(holder, number, after):
         rows = hidden // 3
-        return outer(v_back, ag, gs, holder, number * rows, rows, 4, 16, after)
+        return outer(ag, gs, holder, number * rows, rows, 8, after)
 
     got = swap(send, CORE)
     grad_in, flag = in_part(None, 0, [])
     mine, *sends = small_call(
         first_sum, place, [keep, got], [flag],
-        [shape(half, WIDE)] + [shape(half, NARROW)] * 3, "first_sum", 56,
+        [shape(half, WIDE)] + [shape(half, NARROW)] * 3, "first_sum", 56, 5,
     )
     got = [swap(part, mask) for part, mask in zip(sends, (X, Y, X | Y))]
     grad_in, flag = in_part(grad_in, 1, [mine])

time: 202 us -> 210 us (1.040)
  Pallas kernels: 149 us -> 156 us
    pallas_call x14, Pallas kernels: 104 us -> 110 us  [the longest x7 61.2 us: outer(): pl.pallas_call(body, out_shape=[jax.ShapeDtypeStruct((total, tiles, exper...]
    unnamed x47 -> x49, local copies, waits for them, and re-layouts: 11.4 us -> 11.5 us
  transfers between devices with their start and end apart: 24 -> 24, of which waited for: 1 -> 1; matrix products, arithmetic and copies ran while one was open for 5% -> 4% of each run, Pallas kernels for 55% -> 56%
where the time goes in v5:
time: 210 us; the launch traced here: 208 us
  Pallas kernels  156 us (74%)
  starting transfers between devices  21.9 us (10%)
  local copies, waits for them, and re-layouts  15.6 us (7%)
  waiting for transfers between devices  7.24 us (3%)
  other arithmetic  5.83 us (3%)
    pallas_call x7, Pallas kernels, outer(): pl.pallas_call(body, out_shape=[jax.ShapeDtypeStruct((total, tiles, exper...  61.2 us
    pallas_call x2, Pallas kernels, split_experts(): pl.pallas_call(body, out_shape=[jax.ShapeDtypeStruct((experts, rows, colu...  40.6 us
    pallas_call x1, Pallas kernels, forward_cotangents(): pl.pallas_call(forward_cotangents_body, out_shape=[jax.ShapeDtypeStruct((...  30.7 us
    ppermute x24, starting transfers between devices, swap(): return lax.ppermute(value, AXES, [(i, i ^ mask) for i in range(size)])  21.9 us
    pallas_call x1, Pallas kernels, forward_tokens(): pl.pallas_call(forward_tokens_body, out_shape=[jax.ShapeDtypeStruct((expe...  15 us
    unnamed x49, local copies, waits for them, and re-layouts  11.5 us
    pallas_call x5, Pallas kernels, small_call(): pl.pallas_call(run, out_shape=outs, grid=(steps,), in_specs=[pl.BlockSpec...  8.43 us
    ppermute x24, waiting for transfers between devices, swap(): return lax.ppermute(value, AXES, [(i, i ^ mask) for i in range(size)])  7.24 us
  transfers between devices with their start and end apart: 24, of which 1 were waited for; matrix products, arithmetic and copies ran while one was open for 4% of the time, Pallas kernels for 56%

profile of v5, /device:TPU:0, one launch (start us, length us, event | category | flops | bytes accessed | tf_op | source)
XLA Modules:
  0.0 208.4 jit_solution(13341042886935852053)
XLA Ops:
  2.2 2.4 %collective-permute-start.2 = (f32[8,128]{1,0:T(8,128)S(1)}, f32[8,128]{1,0:T(8,128)S(1)}, u32[]{:S(2)}, u32[]{:S(2)}) collective-permute-start(f32[8,128]{1,0:T(8,128)S(1)} %maximum_select_fusion), channel_id=1, source_target_pairs={{0,3},{1,2},{2,1},{3,0},{4,7},{5,6},{6,5},{7,4},{8,11},{9,10},{10,... | collective-permute-start | bytes 12296 | tf_op jit(solution)/shard_map/ppermute | solution.py:28
  6.8 1.5 collective-permute-start.4
  9.2 1.8 constant_dynamic-slice_fusion
  11.5 20.2 %split_experts.2 = (bf16[4,3072,768]{2,1,0:T(8,128)(2,1)}, f32[8,128]{1,0:T(8,128)}) custom-call(bf16[192,192]{1,0:T(8,128)(2,1)} %constant.62.clone.sort_ref, bf16[3072,6,4,128]{3,2,1,0:T(4,128)(2,1)} %bitcast.35, bf16[3072,6,4,128]{3,2,1,0:T(4,128)(2,1)} %bitcast.36, bf16[3072,6,4,128]{3,2,1,0:T(4,128)(2,1)} %bitcast.37, bf16[3072,6,4,128]{3,2,1,0:T(4,128)(2,1)} %bitcast.38), custom_call_target="tpu_custom_call" | custom-call | bytes 37748736 | tf_op jit(solution)/shard_map/split_experts/pallas_call | solution.py:238
  33.1 1.5 collective-permute-start.5
  35.4 20.4 %split_experts.3 = (bf16[4,768,3072]{2,1,0:T(8,128)(2,1)}, f32[8,128]{1,0:T(8,128)}) custom-call(bf16[256,256]{1,0:T(8,128)(2,1)} %constant.63.clone.sort_ref, bf16[768,24,4,128]{3,2,1,0:T(4,128)(2,1)} %bitcast.39, bf16[768,24,4,128]{3,2,1,0:T(4,128)(2,1)} %bitcast.40, bf16[768,24,4,128]{3,2,1,0:T(4,128)(2,1)} %bitcast.41, ...), custom_call_target="tpu_custom_call" | custom-call | bytes 37748736 | tf_op jit(solution)/shard_map/split_experts/pallas_call | solution.py:238
  61.4 7.2 %collective-permute-done.10.refs_9_ = bf16[64,3072]{1,0:T(8,128)(2,1)S(1)} collective-permute-done((bf16[64,3072]{1,0:T(8,128)(2,1)}, bf16[64,3072]{1,0:T(8,128)(2,1)S(1)}, u32[]{:S(2)}, u32[]{:S(2)}) %collective-permute-start.10) | collective-permute-done | bytes 393248 | tf_op jit(solution)/shard_map/ppermute | solution.py:28
  69.5 15.0 %forward_tokens.1 = (bf16[4,160,3072]{2,1,0:T(8,128)(2,1)}, bf16[4,160,768]{2,1,0:T(8,128)(2,1)}, f32[4,160,768]{2,1,0:T(8,128)}, f32[4,160,768]{2,1,0:T(8,128)}) custom-call(s32[4,1,512]{2,1,0:T(1,128)} %bitcast.45, f32[4,1,512]{2,1,0:T(1,128)} %bitcast.48, bf16[4,3072,768]{2,1,0:T(8,128)(2,1)} %get-tuple-element.42.refs_0_.refs_1_.refs_2_.refs_3_, ...), custom_call_target="tpu_custom_call" | custom-call | flops 5033164800 | bytes 18874368 | tf_op jit(solution)/shard_map/forward_tokens/pallas_call | solution.py:321
  85.6 30.7 %forward_cotangents.1 = (bf16[4,160,3072]{2,1,0:T(8,128)(2,1)}, bf16[4,160,768]{2,1,0:T(8,128)(2,1)}, f32[256,3200]{1,0:T(8,128)}, bf16[256,3200]{1,0:T(8,128)(2,1)}) custom-call(s32[4,1,512]{2,1,0:T(1,128)} %bitcast.46, f32[4,160,768]{2,1,0:T(8,128)} %get-tuple-element.46.active_ref, f32[4,160,768]{2,1,0:T(8,128)} %get-tuple-element.47.slope_ref, ...), custom_call_target="tpu_custom_call" | custom-call | flops 10066329600 | bytes 37748736 | tf_op jit(solution)/shard_map/forward_cotangents/pallas_call | solution.py:407
  117.4 8.2 %weight_gradient.7 = (bf16[3072,6,4,128]{3,2,1,0:T(4,128)(2,1)}, f32[8,128]{1,0:T(8,128)}) custom-call(bf16[4,160,3072]{2,1,0:T(8,128)(2,1)} %get-tuple-element.52.a_ref, bf16[4,160,768]{2,1,0:T(8,128)(2,1)} %get-tuple-element.53.b_ref), custom_call_target="tpu_custom_call" | custom-call | flops 754974720 | bytes 9437184 | tf_op jit(solution)/shard_map/weight_gradient/pallas_call | solution.py:493
  125.6 1.2 copy-done.14
  126.8 5.0 %first_sum.1 = (f32[64,3200]{1,0:T(8,128)}, bf16[64,3200]{1,0:T(8,128)(2,1)}, bf16[64,3200]{1,0:T(8,128)(2,1)}, bf16[64,3200]{1,0:T(8,128)(2,1)}) custom-call(s32[2]{0:T(128)} %pad_add_fusion.place_ref, f32[256,3200]{1,0:T(8,128)} %get-tuple-element.50.refs_0_, bf16[256,3200]{1,0:T(8,128)(2,1)} %copy-done.14, f32[8,128]{1,0:T(8,128)} %get-tuple-element.54.refs_2_), custom_call_target="tpu_custom_call" | custom-call | bytes 1048576 | tf_op jit(solution)/shard_map/first_sum/pallas_call | solution.py:57
  132.4 1.4 collective-permute-start.15
  133.8 1.6 collective-permute-start.16
  135.3 8.2 %weight_gradient.8 = (bf16[3072,6,4,128]{3,2,1,0:T(4,128)(2,1)}, f32[8,128]{1,0:T(8,128)}) custom-call(bf16[4,160,3072]{2,1,0:T(8,128)(2,1)} %get-tuple-element.52.a_ref, bf16[4,160,768]{2,1,0:T(8,128)(2,1)} %get-tuple-element.53.b_ref, bf16[3072,6,4,128]{3,2,1,0:T(4,128)(2,1)} %get-tuple-element.59.refs_0_, ...), custom_call_target="tpu_custom_call", output_to_operand_aliasing={{0}: (2, {})} | custom-call | flops 754974720 | bytes 9437184 | tf_op jit(solution)/shard_map/weight_gradient/pallas_call | solution.py:493
  143.6 8.3 %weight_gradient.9 = (bf16[3072,6,4,128]{3,2,1,0:T(4,128)(2,1)}, f32[8,128]{1,0:T(8,128)}) custom-call(bf16[4,160,3072]{2,1,0:T(8,128)(2,1)} %get-tuple-element.52.a_ref, bf16[4,160,768]{2,1,0:T(8,128)(2,1)} %get-tuple-element.53.b_ref, bf16[3072,6,4,128]{3,2,1,0:T(4,128)(2,1)} %get-tuple-element.60.refs_0_, ...), custom_call_target="tpu_custom_call", output_to_operand_aliasing={{0}: (2, {})} | custom-call | flops 754974720 | bytes 9437184 | tf_op jit(solution)/shard_map/weight_gradient/pallas_call | solution.py:493
  151.8 8.2 %weight_gradient.10 = (bf16[3072,6,4,128]{3,2,1,0:T(4,128)(2,1)}, f32[8,128]{1,0:T(8,128)}) custom-call(bf16[4,160,3072]{2,1,0:T(8,128)(2,1)} %get-tuple-element.52.a_ref, bf16[4,160,768]{2,1,0:T(8,128)(2,1)} %get-tuple-element.53.b_ref, bf16[3072,6,4,128]{3,2,1,0:T(4,128)(2,1)} %get-tuple-element.62.refs_0_, ...), custom_call_target="tpu_custom_call", output_to_operand_aliasing={{0}: (2, {})} | custom-call | flops 754974720 | bytes 9437184 | tf_op jit(solution)/shard_map/weight_gradient/pallas_call | solution.py:493
  162.2 1.6 collective-permute-start.17
  163.8 2.6 %collective-permute-start.18 = (bf16[16,3200]{1,0:T(8,128)(2,1)S(1)}, bf16[16,3200]{1,0:T(8,128)(2,1)S(1)}, u32[]{:S(2)}, u32[]{:S(2)}) collective-permute-start(bf16[16,3200]{1,0:T(8,128)(2,1)S(1)} %get-tuple-element.67), channel_id=1, source_target_pairs={{0,16},{1,17},{2,18},{3,19},{4,20},{5,21},{6,22},{7,23},{8,24},{9,... | collective-permute-start | bytes 307208 | tf_op jit(solution)/shard_map/ppermute | solution.py:28
  166.6 9.4 %weight_gradient.11 = (bf16[768,24,4,128]{3,2,1,0:T(4,128)(2,1)}, f32[8,128]{1,0:T(8,128)}) custom-call(bf16[4,160,768]{2,1,0:T(8,128)(2,1)} %get-tuple-element.69.a_ref, bf16[4,160,3072]{2,1,0:T(8,128)(2,1)} %get-tuple-element.70.b_ref, f32[16,3200]{1,0:T(8,128)} %copy-done.5), custom_call_target="tpu_custom_call" | custom-call | flops 1006632960 | bytes 12582912 | tf_op jit(solution)/shard_map/weight_gradient/pallas_call | solution.py:493
  178.3 3.7 %collective-permute-start.22 = (bf16[16,3200]{1,0:T(8,128)(2,1)S(1)}, bf16[16,3200]{1,0:T(8,128)(2,1)S(1)}, u32[]{:S(2)}, u32[]{:S(2)}) collective-permute-start(bf16[16,3200]{1,0:T(8,128)(2,1)S(1)} %third_sum.1.refs_1_.refs_0_), channel_id=1, source_target_pairs={{0,24},{1,25},{2,26},{3,27},{4,28},{5,29},{6,30},{7,31},{8,16},{9,... | collective-permute-start | bytes 307208 | tf_op jit(solution)/shard_map/ppermute | solution.py:28
  182.8 9.4 %weight_gradient.12 = (bf16[768,24,4,128]{3,2,1,0:T(4,128)(2,1)}, f32[8,128]{1,0:T(8,128)}) custom-call(bf16[4,160,768]{2,1,0:T(8,128)(2,1)} %get-tuple-element.69.a_ref, bf16[4,160,3072]{2,1,0:T(8,128)(2,1)} %get-tuple-element.70.b_ref, bf16[768,24,4,128]{3,2,1,0:T(4,128)(2,1)} %get-tuple-element.72.refs_0_, ...), custom_call_target="tpu_custom_call", output_to_operand_aliasing={{0}: (2, {})} | custom-call | flops 1006632960 | bytes 12582912 | tf_op jit(solution)/shard_map/weight_gradient/pallas_call | solution.py:493
  195.2 9.4 %weight_gradient.13 = (bf16[768,24,4,128]{3,2,1,0:T(4,128)(2,1)}, f32[8,128]{1,0:T(8,128)}) custom-call(bf16[4,160,768]{2,1,0:T(8,128)(2,1)} %get-tuple-element.69.a_ref, bf16[4,160,3072]{2,1,0:T(8,128)(2,1)} %get-tuple-element.70.b_ref, bf16[768,24,4,128]{3,2,1,0:T(4,128)(2,1)} %get-tuple-element.74.refs_0_, ...), custom_call_target="tpu_custom_call", output_to_operand_aliasing={{0}: (2, {})} | custom-call | flops 1006632960 | bytes 12582912 | tf_op jit(solution)/shard_map/weight_gradient/pallas_call | solution.py:493
  206.3 1.5 join_x.1
  (110 shorter events, 27.1 us)
Async XLA Ops:
  2.2 30.3 %collective-permute-start.2 = (f32[8,128]{1,0:T(8,128)S(1)}, f32[8,128]{1,0:T(8,128)S(1)}, u32[]{:S(2)}, u32[]{:S(2)}) collective-permute-start(f32[8,128]{1,0:T(8,128)S(1)} %maximum_select_fusion), channel_id=1, source_target_pairs={{0,3},{1,2},{2,1},{3,0},{4,7},{5,6},{6,5},{7,4},{8,11},{9,10},{10,... | collective-permute-start | bytes 12296 | tf_op jit(solution)/shard_map/ppermute | solution.py:28
  4.6 28.5 %collective-permute-start.1 = (f32[8,128]{1,0:T(8,128)S(1)}, f32[8,128]{1,0:T(8,128)S(1)}, u32[]{:S(2)}, u32[]{:S(2)}) collective-permute-start(f32[8,128]{1,0:T(8,128)S(1)} %maximum_select_fusion), channel_id=1, source_target_pairs={{0,2},{1,3},{2,0},{3,1},{4,6},{5,7},{6,4},{7,5},{8,10},{9,11},{10,... | collective-permute-start | bytes 12296 | tf_op jit(solution)/shard_map/ppermute | solution.py:28
  5.2 29.4 %collective-permute-start = (f32[8,128]{1,0:T(8,128)S(1)}, f32[8,128]{1,0:T(8,128)S(1)}, u32[]{:S(2)}, u32[]{:S(2)}) collective-permute-start(f32[8,128]{1,0:T(8,128)S(1)} %get-tuple-element.91), channel_id=1, source_target_pairs={{0,1},{1,0},{2,3},{3,2},{4,5},{5,4},{6,7},{7,6},{8,9},{9,8},{10,11... | collective-permute-start | bytes 12296 | tf_op jit(solution)/shard_map/ppermute | solution.py:28
  5.3 56.1 %collective-permute-start.3 = (bf16[128,3072]{1,0:T(8,128)(2,1)}, bf16[128,3072]{1,0:T(8,128)(2,1)S(1)}, u32[]{:S(2)}, u32[]{:S(2)}) collective-permute-start(bf16[128,3072]{1,0:T(8,128)(2,1)} %refs_4_.1), channel_id=1, source_target_pairs={{0,1},{1,0},{2,3},{3,2},{4,5},{5,4},{6,7},{7,6},{8,9},{9,8},{10,11... | collective-permute-start | bytes 2359304 | tf_op jit(solution)/shard_map/ppermute | solution.py:28
  6.8 24.9 %collective-permute-start.4 = (bf16[64,3072]{1,0:T(8,128)(2,1)S(1)}, bf16[64,3072]{1,0:T(8,128)(2,1)S(1)}, u32[]{:S(2)}, u32[]{:S(2)}) collective-permute-start(bf16[64,3072]{1,0:T(8,128)(2,1)S(1)} %constant_dynamic-slice_fusion.1), channel_id=1, source_target_pairs={{0,2},{1,3},{2,0},{3,1},{4,6},{5,7},{6,4},{7,5},{8,10},{9,11},{10,... | collective-permute-start | bytes 1179656 | tf_op jit(solution)/shard_map/ppermute | solution.py:28
  31.7 52.8 %collective-permute-start.9 = (bf16[128,3072]{1,0:T(8,128)(2,1)S(1)}, bf16[128,3072]{1,0:T(8,128)(2,1)S(1)}, u32[]{:S(2)}, u32[]{:S(2)}) collective-permute-start(bf16[128,3072]{1,0:T(8,128)(2,1)S(1)} %copy-done.13), channel_id=1, source_target_pairs={{0,1},{1,0},{2,3},{3,2},{4,5},{5,4},{6,7},{7,6},{8,9},{9,8},{10,11... | collective-permute-start | bytes 2359304 | tf_op jit(solution)/shard_map/ppermute | solution.py:28
  32.4 23.4 %collective-permute-start.6 = (bf16[64,3072]{1,0:T(8,128)(2,1)}, bf16[64,3072]{1,0:T(8,128)(2,1)S(1)}, u32[]{:S(2)}, u32[]{:S(2)}) collective-permute-start(bf16[64,3072]{1,0:T(8,128)(2,1)} %constant_dynamic-slice_fusion), channel_id=1, source_target_pairs={{0,2},{1,3},{2,0},{3,1},{4,6},{5,7},{6,4},{7,5},{8,10},{9,11},{10,... | collective-permute-start | bytes 1179656 | tf_op jit(solution)/shard_map/ppermute | solution.py:28
  33.1 22.8 %collective-permute-start.5 = (bf16[64,3072]{1,0:T(8,128)(2,1)}, bf16[64,3072]{1,0:T(8,128)(2,1)S(1)}, u32[]{:S(2)}, u32[]{:S(2)}) collective-permute-start(bf16[64,3072]{1,0:T(8,128)(2,1)} %hold.2.refs_4_.refs_6_), channel_id=1, source_target_pairs={{0,4},{1,5},{2,6},{3,7},{4,0},{5,1},{6,2},{7,3},{8,12},{9,13},{10,... | collective-permute-start | bytes 1179656 | tf_op jit(solution)/shard_map/ppermute | solution.py:28
  35.4 33.2 %collective-permute-start.7 = (bf16[64,3072]{1,0:T(8,128)(2,1)}, bf16[64,3072]{1,0:T(8,128)(2,1)S(1)}, u32[]{:S(2)}, u32[]{:S(2)}) collective-permute-start(bf16[64,3072]{1,0:T(8,128)(2,1)} %hold.2.refs_4_.refs_6_), channel_id=1, source_target_pairs={{0,1},{1,0},{2,3},{3,2},{4,5},{5,4},{6,7},{7,6},{8,9},{9,8},{10,11... | collective-permute-start | bytes 1179656 | tf_op jit(solution)/shard_map/ppermute | solution.py:28
  56.8 11.8 %collective-permute-start.8 = (bf16[64,3072]{1,0:T(8,128)(2,1)}, bf16[64,3072]{1,0:T(8,128)(2,1)S(1)}, u32[]{:S(2)}, u32[]{:S(2)}) collective-permute-start(bf16[64,3072]{1,0:T(8,128)(2,1)} %get-tuple-element.45.refs_7_), channel_id=1, source_target_pairs={{0,1},{1,0},{2,3},{3,2},{4,5},{5,4},{6,7},{7,6},{8,9},{9,8},{10,11... | collective-permute-start | bytes 1179656 | tf_op jit(solution)/shard_map/ppermute | solution.py:28
  57.3 11.3 %collective-permute-start.10 = (bf16[64,3072]{1,0:T(8,128)(2,1)}, bf16[64,3072]{1,0:T(8,128)(2,1)S(1)}, u32[]{:S(2)}, u32[]{:S(2)}) collective-permute-start(bf16[64,3072]{1,0:T(8,128)(2,1)} %get-tuple-element.49.refs_8_), channel_id=1, source_target_pairs={{0,4},{1,5},{2,6},{3,7},{4,0},{5,1},{6,2},{7,3},{8,12},{9,13},{10,... | collective-permute-start | bytes 1179656 | tf_op jit(solution)/shard_map/ppermute | solution.py:28
  61.4 23.1 %collective-permute-start.11 = (bf16[64,3072]{1,0:T(8,128)(2,1)}, bf16[64,3072]{1,0:T(8,128)(2,1)S(1)}, u32[]{:S(2)}, u32[]{:S(2)}) collective-permute-start(bf16[64,3072]{1,0:T(8,128)(2,1)} %get-tuple-element.49.refs_8_), channel_id=1, source_target_pairs={{0,1},{1,0},{2,3},{3,2},{4,5},{5,4},{6,7},{7,6},{8,9},{9,8},{10,11... | collective-permute-start | bytes 1179656 | tf_op jit(solution)/shard_map/ppermute | solution.py:28
  68.5 16.0 %collective-permute-start.12 = (bf16[64,3072]{1,0:T(8,128)(2,1)S(1)}, bf16[64,3072]{1,0:T(8,128)(2,1)S(1)}, u32[]{:S(2)}, u32[]{:S(2)}) collective-permute-start(bf16[64,3072]{1,0:T(8,128)(2,1)S(1)} %collective-permute-done.10.refs_9_), channel_id=1, source_target_pairs={{0,1},{1,0},{2,3},{3,2},{4,5},{5,4},{6,7},{7,6},{8,9},{9,8},{10,11... | collective-permute-start | bytes 1179656 | tf_op jit(solution)/shard_map/ppermute | solution.py:28
  116.3 9.3 %collective-permute-start.13 = (bf16[256,3200]{1,0:T(8,128)(2,1)}, bf16[256,3200]{1,0:T(8,128)(2,1)S(1)}, u32[]{:S(2)}, u32[]{:S(2)}) collective-permute-start(bf16[256,3200]{1,0:T(8,128)(2,1)} %get-tuple-element.51), channel_id=1, source_target_pairs={{0,1},{1,0},{2,3},{3,2},{4,5},{5,4},{6,7},{7,6},{8,9},{9,8},{10,11... | collective-permute-start | bytes 4915208 | tf_op jit(solution)/shard_map/ppermute | solution.py:28
  131.8 28.2 %collective-permute-start.14 = (bf16[64,3200]{1,0:T(8,128)(2,1)}, bf16[64,3200]{1,0:T(8,128)(2,1)S(1)}, u32[]{:S(2)}, u32[]{:S(2)}) collective-permute-start(bf16[64,3200]{1,0:T(8,128)(2,1)} %get-tuple-element.56), channel_id=1, source_target_pairs={{0,4},{1,5},{2,6},{3,7},{4,0},{5,1},{6,2},{7,3},{8,12},{9,13},{10,... | collective-permute-start | bytes 1228808 | tf_op jit(solution)/shard_map/ppermute | solution.py:28
  132.4 27.7 %collective-permute-start.15 = (bf16[64,3200]{1,0:T(8,128)(2,1)}, bf16[64,3200]{1,0:T(8,128)(2,1)S(1)}, u32[]{:S(2)}, u32[]{:S(2)}) collective-permute-start(bf16[64,3200]{1,0:T(8,128)(2,1)} %get-tuple-element.57), channel_id=1, source_target_pairs={{0,2},{1,3},{2,0},{3,1},{4,6},{5,7},{6,4},{7,5},{8,10},{9,11},{10,... | collective-permute-start | bytes 1228808 | tf_op jit(solution)/shard_map/ppermute | solution.py:28
  133.8 26.3 %collective-permute-start.16 = (bf16[64,3200]{1,0:T(8,128)(2,1)}, bf16[64,3200]{1,0:T(8,128)(2,1)S(1)}, u32[]{:S(2)}, u32[]{:S(2)}) collective-permute-start(bf16[64,3200]{1,0:T(8,128)(2,1)} %get-tuple-element.58), channel_id=1, source_target_pairs={{0,6},{1,7},{2,4},{3,5},{4,2},{5,3},{6,0},{7,1},{8,14},{9,15},{10,... | collective-permute-start | bytes 1228808 | tf_op jit(solution)/shard_map/ppermute | solution.py:28
  162.2 13.8 %collective-permute-start.17 = (bf16[16,3200]{1,0:T(8,128)(2,1)S(1)}, bf16[16,3200]{1,0:T(8,128)(2,1)S(1)}, u32[]{:S(2)}, u32[]{:S(2)}) collective-permute-start(bf16[16,3200]{1,0:T(8,128)(2,1)S(1)} %get-tuple-element.66), channel_id=1, source_target_pairs={{0,8},{1,9},{2,10},{3,11},{4,12},{5,13},{6,14},{7,15},{8,0},{9,1},... | collective-permute-start | bytes 307208 | tf_op jit(solution)/shard_map/ppermute | solution.py:28
  163.8 12.3 %collective-permute-start.18 = (bf16[16,3200]{1,0:T(8,128)(2,1)S(1)}, bf16[16,3200]{1,0:T(8,128)(2,1)S(1)}, u32[]{:S(2)}, u32[]{:S(2)}) collective-permute-start(bf16[16,3200]{1,0:T(8,128)(2,1)S(1)} %get-tuple-element.67), channel_id=1, source_target_pairs={{0,16},{1,17},{2,18},{3,19},{4,20},{5,21},{6,22},{7,23},{8,24},{9,... | collective-permute-start | bytes 307208 | tf_op jit(solution)/shard_map/ppermute | solution.py:28
  166.4 9.7 %collective-permute-start.19 = (bf16[16,3200]{1,0:T(8,128)(2,1)S(1)}, bf16[16,3200]{1,0:T(8,128)(2,1)S(1)}, u32[]{:S(2)}, u32[]{:S(2)}) collective-permute-start(bf16[16,3200]{1,0:T(8,128)(2,1)S(1)} %get-tuple-element.68), channel_id=1, source_target_pairs={{0,24},{1,25},{2,26},{3,27},{4,28},{5,29},{6,30},{7,31},{8,16},{9,... | collective-permute-start | bytes 307208 | tf_op jit(solution)/shard_map/ppermute | solution.py:28
  178.3 13.9 %collective-permute-start.22 = (bf16[16,3200]{1,0:T(8,128)(2,1)S(1)}, bf16[16,3200]{1,0:T(8,128)(2,1)S(1)}, u32[]{:S(2)}, u32[]{:S(2)}) collective-permute-start(bf16[16,3200]{1,0:T(8,128)(2,1)S(1)} %third_sum.1.refs_1_.refs_0_), channel_id=1, source_target_pairs={{0,24},{1,25},{2,26},{3,27},{4,28},{5,29},{6,30},{7,31},{8,16},{9,... | collective-permute-start | bytes 307208 | tf_op jit(solution)/shard_map/ppermute | solution.py:28
  182.0 10.2 %collective-permute-start.21 = (bf16[16,3200]{1,0:T(8,128)(2,1)S(1)}, bf16[16,3200]{1,0:T(8,128)(2,1)S(1)}, u32[]{:S(2)}, u32[]{:S(2)}) collective-permute-start(bf16[16,3200]{1,0:T(8,128)(2,1)S(1)} %third_sum.1.refs_1_.refs_0_), channel_id=1, source_target_pairs={{0,16},{1,17},{2,18},{3,19},{4,20},{5,21},{6,22},{7,23},{8,24},{9,... | collective-permute-start | bytes 307208 | tf_op jit(solution)/shard_map/ppermute | solution.py:28
  182.0 10.3 %collective-permute-start.20 = (bf16[16,3200]{1,0:T(8,128)(2,1)S(1)}, bf16[16,3200]{1,0:T(8,128)(2,1)S(1)}, u32[]{:S(2)}, u32[]{:S(2)}) collective-permute-start(bf16[16,3200]{1,0:T(8,128)(2,1)S(1)} %third_sum.1.refs_1_.refs_0_), channel_id=1, source_target_pairs={{0,8},{1,9},{2,10},{3,11},{4,12},{5,13},{6,14},{7,15},{8,0},{9,1},... | collective-permute-start | bytes 307208 | tf_op jit(solution)/shard_map/ppermute | solution.py:28
  194.4 10.2 %collective-permute-start.23 = (bf16[64,3200]{1,0:T(8,128)(2,1)S(1)}, bf16[64,3200]{1,0:T(8,128)(2,1)S(1)}, u32[]{:S(2)}, u32[]{:S(2)}) collective-permute-start(bf16[64,3200]{1,0:T(8,128)(2,1)S(1)} %join_z.1.refs_1_.refs_0_), channel_id=1, source_target_pairs={{0,4},{1,5},{2,6},{3,7},{4,0},{5,1},{6,2},{7,3},{8,12},{9,13},{10,... | collective-permute-start | bytes 1228808 | tf_op jit(solution)/shard_map/ppermute | solution.py:28
  (24 other events, 96.1 us)

commit v6 on v4

--- a/solution.py
+++ b/solution.py
@@ -44,18 +44,20 @@
 FLAG = jax.ShapeDtypeStruct((8, LANES), WIDE)
 
 
-def small_call(body, place, inputs, after, outs, name, grant=12):
+def small_call(body, place, inputs, after, outs, name, grant=12, steps=1):
     given = len(inputs)
 
     def run(place_ref, *refs):
         body(place_ref, refs[:given], refs[given + len(after) :])
 
     def whole(array):
-        return pl.BlockSpec(array.shape, lambda: (0,) * len(array.shape))
+        rows, columns = array.shape
+        return pl.BlockSpec((rows, columns // steps), lambda i: (0, i))
 
     return pl.pallas_call(
         run,
         out_shape=outs,
+        grid=(steps,),
         in_specs=[pl.BlockSpec(memory_space=pltpu.SMEM)]
         + [whole(array) for array in inputs]
         + [ANY] * len(after),
@@ -177,16 +179,17 @@
                         )
 
 
-def split_experts(view, sort, block, group, some, after):
-    rows, tiles, experts, _ = view.shape
+def split_experts(view, sort, start, rows, block, group, some, after):
+    _, tiles, experts, _ = view.shape
     columns = tiles * LANES
+    first = start // block
     return pl.pallas_call(
         functools.partial(split_body, group, some),
         out_shape=[jax.ShapeDtypeStruct((experts, rows, columns), NARROW), FLAG],
         grid=(rows // block,),
         in_specs=[
             pl.BlockSpec(sort.shape, lambda i: (0, 0)),
-            pl.BlockSpec((block, tiles, experts, LANES), lambda i: (i, 0, 0, 0)),
+            pl.BlockSpec((block, tiles, experts, LANES), lambda i: (first + i, 0, 0, 0)),
             *[ANY] * len(after),
         ],
         out_specs=[
@@ -205,6 +208,8 @@
     copies, begin = [], 0
     for number, piece in enumerate(pieces):
         count = piece.shape[0]
+        if begin == whole.shape[0]:
+            break
         copies.append(
             pltpu.make_async_copy(piece, whole.at[begin : begin + count], sem.at[number])
         )
@@ -215,29 +220,65 @@
         copy.wait()
 
 
-def chosen(code_ref, slots):
-    code = code_ref[0]
+def chosen(code, slots):
     tokens = code.shape[1]
     return lax.broadcasted_iota(jnp.int32, (slots, tokens), 0) == jnp.bitwise_and(code, 1023)
 
 
-def forward_tokens_body(code_ref, gate_ref, w_ref, *refs):
-    pieces, (xs_ref, ag_ref, active_ref, slope_ref, x_ref, sem) = refs[:-6], refs[-6:]
-    slots, model_width = xs_ref.shape[1:]
-    columns = 512
-    pl.when(pl.program_id(0) == 0)(lambda: fetch(pieces, x_ref, sem))
-    choose = chosen(code_ref, slots)
-    pick = choose.astype(WIDE).astype(NARROW)
-    gate = jnp.sum(jnp.where(choose, gate_ref[0], 0.0), axis=1, keepdims=True)
+def weight_parts(weights, streams):
+    specs, operands = [], []
+    for array in weights:
+        _, rows, columns = array.shape
+        for number in range(streams):
+            specs.append(
+                pl.BlockSpec((1, rows // streams, columns), lambda i, number=number: (i, number, 0))
+            )
+            operands.append(array)
+    return specs, operands
+
+
+def gather_slots(code_ref, whole_ref, pick_ref, slot_ref):
+    experts, _, tokens = code_ref.shape
+    slots = pick_ref.shape[0] // experts
+    model_width = whole_ref.shape[1]
+    columns = 256
+    for expert in range(experts):
+        pick_ref[expert * slots : (expert + 1) * slots, :] = (
+            chosen(code_ref[expert], slots).astype(WIDE).astype(NARROW)
+        )
     for begin in range(0, model_width, columns):
         part = slice(begin, begin + columns)
-        xs_ref[0, :, part] = mm(pick, x_ref[:, part], NN).astype(NARROW)
-    pre_act = mm(xs_ref[0], w_ref[0], NN)
+        slot_ref[:, part] = mm(pick_ref[...], whole_ref[:, part], NN).astype(NARROW)
+
+
+def forward_tokens_body(code_ref, gate_ref, *refs):
+    w_refs, refs = refs[:2], refs[2:]
+    pieces, refs = refs[:-9], refs[-9:]
+    xs_ref, ag_ref, active_ref, slope_ref, x_ref, slot_ref, pick_ref, sem, out_sem = refs
+    step = pl.program_id(0)
+    slots = ag_ref.shape[1]
+    out = pltpu.make_async_copy(slot_ref, xs_ref, out_sem)
+
+    @pl.when(step == 0)
+    def _():
+        fetch(pieces, x_ref, sem)
+        gather_slots(code_ref, x_ref, pick_ref, slot_ref)
+        out.start()
+
+    choose = chosen(code_ref[step], slots)
+    gate = jnp.sum(jnp.where(choose, gate_ref[step], 0.0), axis=1, keepdims=True)
+    rows = pl.ds(pl.multiple_of(step * slots, slots), slots)
+    pre_act, begin = 0.0, 0
+    for w_ref in w_refs:
+        end = begin + w_ref.shape[1]
+        pre_act = pre_act + mm(slot_ref[rows, begin:end], w_ref[0], NN)
+        begin = end
     squash = jax.nn.sigmoid(pre_act)
     active = pre_act * squash
     active_ref[0] = active
     ag_ref[0] = (gate * active).astype(NARROW)
     slope_ref[0] = gate * squash * (1.0 + pre_act * (1.0 - squash))
+    pl.when(step == pl.num_programs(0) - 1)(out.wait)
 
 
 def forward_tokens(code, gate_tok, x_pieces, w_split):
@@ -245,21 +286,22 @@
     tokens = code.shape[2]
     slots = tokens // 128 * CAP
     expert = lambda i: (i, 0, 0)
-    shapes = [(model_width, NARROW), (hidden, NARROW), (hidden, WIDE), (hidden, WIDE)]
+    all_experts = pl.BlockSpec((experts, 1, tokens), lambda i: (0, 0, 0))
+    w_specs, w_operands = weight_parts([w_split], 2)
+    shapes = [(hidden, NARROW), (hidden, WIDE), (hidden, WIDE)]
     return pl.pallas_call(
         forward_tokens_body,
-        out_shape=[jax.ShapeDtypeStruct((experts, slots, width), dtype) for width, dtype in shapes],
+        out_shape=[jax.ShapeDtypeStruct((experts * slots, model_width), NARROW)]
+        + [jax.ShapeDtypeStruct((experts, slots, width), dtype) for width, dtype in shapes],
         grid=(experts,),
-        in_specs=[
-            pl.BlockSpec((1, 1, tokens), expert),
-            pl.BlockSpec((1, 1, tokens), expert),
-            pl.BlockSpec((1, model_width, hidden), expert),
-            *[ANY] * len(x_pieces),
-        ],
-        out_specs=[pl.BlockSpec((1, slots, width), expert) for width, _ in shapes],
+        in_specs=[all_experts, all_experts, *w_specs, *[ANY] * len(x_pieces)],
+        out_specs=[ANY] + [pl.BlockSpec((1, slots, width), expert) for width, _ in shapes],
         scratch_shapes=[
             pltpu.VMEM((tokens, model_width), NARROW),
+            pltpu.VMEM((experts * slots, model_width), NARROW),
+            pltpu.VMEM((experts * slots, tokens), NARROW),
             pltpu.SemaphoreType.DMA((len(x_pieces),)),
+            pltpu.SemaphoreType.DMA(()),
         ],
         compiler_params=pltpu.CompilerParams(vmem_limit_bytes=56 * MIB),
         cost_estimate=pl.CostEstimate(
@@ -268,31 +310,41 @@
             transcendentals=0,
         ),
         name="forward_tokens",
-    )(code, gate_tok, w_split, *x_pieces)
-
-
-def forward_cotangents_body(code_ref, active_ref, slope_ref, w_ref, v_ref, *refs):
-    pieces = refs[:-8]
-    gs_ref, gp_ref, keep_ref, send_ref, g_ref, back_ref, pick_ref, sem = refs[-8:]
+    )(code, gate_tok, *w_operands, *x_pieces)
+
+
+def forward_cotangents_body(code_ref, active_ref, slope_ref, *refs):
+    w_refs, v_refs, refs = refs[:2], refs[2:4], refs[4:]
+    pieces, refs = refs[:-10], refs[-10:]
+    gs_ref, gp_ref, keep_ref, send_ref, g_ref, slot_ref, back_ref, pick_ref, sem, out_sem = refs
     step = pl.program_id(0)
-    slots, model_width = gs_ref.shape[1:]
+    slots = gp_ref.shape[1]
+    model_width = g_ref.shape[1]
     columns = 512
-    pl.when(step == 0)(lambda: fetch(pieces, g_ref, sem))
-    choose = chosen(code_ref, slots)
-    pick = choose.astype(WIDE).astype(NARROW)
+    out = pltpu.make_async_copy(slot_ref, gs_ref, out_sem)
+
+    @pl.when(step == 0)
+    def _():
+        fetch(pieces, g_ref, sem)
+        gather_slots(code_ref, g_ref, pick_ref, slot_ref)
+        out.start()
+
+    code = code_ref[step]
     rows = pl.ds(pl.multiple_of(step * slots, slots), slots)
-    pick_ref[rows, :] = pick
+    gate_part, begin = 0.0, 0
+    for v_ref in v_refs:
+        part = slice(begin, begin + v_ref.shape[1])
+        upstream = mm(slot_ref[rows, :], v_ref[0], NT)
+        gate_part = gate_part + jnp.sum(active_ref[0, :, part] * upstream, axis=1, keepdims=True)
+        gp_ref[0, :, part] = (slope_ref[0, :, part] * upstream).astype(NARROW)
+        begin = part.stop
     for begin in range(0, model_width, columns):
-        part = slice(begin, begin + columns)
-        gs_ref[0, :, part] = mm(pick, g_ref[:, part], NN).astype(NARROW)
-    upstream = mm(gs_ref[0], v_ref[0], NT)
-    gate_part = jnp.sum(active_ref[0] * upstream, axis=1, keepdims=True)
-    gp_ref[0] = (slope_ref[0] * upstream).astype(NARROW)
-    for begin in range(0, model_width, columns):
-        back = mm(gp_ref[0], w_ref[0, begin : begin + columns, :], NT)
+        held = w_refs[0].shape[1]
+        w_ref, inner = w_refs[begin // held], begin % held
+        back = mm(gp_ref[0], w_ref[0, inner : inner + columns, :], NT)
         back_ref[rows, begin : begin + columns] = back.astype(NARROW)
     which = jnp.sum(
-        jnp.where(choose, jnp.right_shift(code_ref[0], 10), 0), axis=1, keepdims=True
+        jnp.where(chosen(code, slots), jnp.right_shift(code, 10), 0), axis=1, keepdims=True
     )
     lane = lax.broadcasted_iota(jnp.int32, (slots, LANES), 1)
     high = gate_part.astype(NARROW).astype(WIDE)
@@ -302,6 +354,7 @@
 
     @pl.when(step == pl.num_programs(0) - 1)
     def _():
+        out.wait()
         quarter = g_ref.shape[0] // 4
         for begin in range(0, model_width + LANES, columns):
             part = slice(begin, min(begin + columns, model_width + LANES))
@@ -323,34 +376,38 @@
     expert = lambda i: (i, 0, 0)
     whole = lambda i: (0, 0)
     one = pl.Buffered(1)
+    w_specs, w_operands = weight_parts([w_split], 2)
+    v_specs, v_operands = weight_parts(v_split, 1)
     return pl.pallas_call(
         forward_cotangents_body,
         out_shape=[
-            jax.ShapeDtypeStruct((experts, slots, model_width), NARROW),
+            jax.ShapeDtypeStruct((experts * slots, model_width), NARROW),
             jax.ShapeDtypeStruct((experts, slots, hidden), NARROW),
             jax.ShapeDtypeStruct((tokens // 2, width), WIDE),
             jax.ShapeDtypeStruct((tokens // 2, width), NARROW),
         ],
         grid=(experts,),
         in_specs=[
-            pl.BlockSpec((1, 1, tokens), expert),
+            pl.BlockSpec((experts, 1, tokens), lambda i: (0, 0, 0)),
             pl.BlockSpec((1, slots, hidden), expert),
             pl.BlockSpec((1, slots, hidden), expert),
-            pl.BlockSpec((1, model_width, hidden), expert),
-            pl.BlockSpec((1, hidden, model_width), expert),
+            *w_specs,
+            *v_specs,
             *[ANY] * len(g_pieces),
         ],
         out_specs=[
-            pl.BlockSpec((1, slots, model_width), expert),
+            ANY,
             pl.BlockSpec((1, slots, hidden), expert),
             pl.BlockSpec((tokens // 2, width), whole, pipeline_mode=one),
             pl.BlockSpec((tokens // 2, width), whole, pipeline_mode=one),
         ],
         scratch_shapes=[
             pltpu.VMEM((tokens, model_width), NARROW),
+            pltpu.VMEM((experts * slots, model_width), NARROW),
             pltpu.VMEM((experts * slots, width), NARROW),
             pltpu.VMEM((experts * slots, tokens), NARROW),
             pltpu.SemaphoreType.DMA((len(g_pieces),)),
+            pltpu.SemaphoreType.DMA(()),
         ],
         compiler_params=pltpu.CompilerParams(vmem_limit_bytes=56 * MIB),
         cost_estimate=pl.CostEstimate(
@@ -359,58 +416,43 @@
             transcendentals=0,
         ),
         name="forward_cotangents",
-    )(code, active, slope, w_split, v_split, *g_pieces)
-
-
-def outer_body(group, some, sort_ref, a_ref, b_ref, *refs):
-    out_ref, flag_ref = refs[-2:]
+    )(code, active, slope, *w_operands, *v_operands, *g_pieces)
+
+
+def odd_tiles(rows):
+    tiles = -(-rows // 8)
+    return 8 * (tiles + 1 - tiles % 2)
+
+
+def outer_body(group, a_ref, b_ref, *refs):
+    out_ref, flag_ref, wide_ref = refs[-3:]
     flag_ref[...] = jnp.zeros_like(flag_ref)
     rows, tiles, experts, _ = out_ref.shape
+    stride = wide_ref.shape[1]
     held = group * experts
     out = out_ref.reshape(rows, tiles * experts, LANES)
-    across = 1 if some == 8 else 2
-    for tile in range(0, tiles, group * across):
-        wide = group * across * LANES
-        parts = [
-            mm(a_ref[expert], b_ref[expert, :, tile * LANES : tile * LANES + wide], TN)
-            for expert in range(experts)
-        ]
-        for row in range(0, rows, 16):
-            pair = [(row, 0), (row + 8, 0)] if some == 8 else [(row, 0), (row, group)]
-            blocks = [
-                jnp.concatenate(
-                    [
-                        part[begin : begin + some, (first + inner) * LANES : (first + inner + 1) * LANES]
-                        for part in parts
-                        for inner in range(group)
-                    ],
-                    axis=0,
-                )
-                for begin, first in pair
-            ]
-            result = mm(sort_ref[...], jnp.concatenate(blocks, axis=1).astype(NARROW), NN)
-            for side, (begin, first) in enumerate(pair):
-                at_tile = (tile + first) * experts
-                out[begin : begin + some, at_tile : at_tile + held, :] = (
-                    result[:, side * LANES : (side + 1) * LANES]
-                    .astype(NARROW)
-                    .reshape(some, held, LANES)
-                )
-
-
-def outer(sort, a, b, holder, start, count, group, some, after):
+    flat = wide_ref.reshape(rows * stride, LANES)
+    for begin in range(0, tiles, group):
+        for expert in range(experts):
+            part = mm(a_ref[expert], b_ref[expert, :, begin * LANES : (begin + group) * LANES], TN)
+            for tile in range(group):
+                flat[pl.ds(tile * experts + expert, rows, stride), :] = part[
+                    :, tile * LANES : (tile + 1) * LANES
+                ]
+        out[:, begin * experts : begin * experts + held, :] = wide_ref[:, :held, :].astype(NARROW)
+
+
+def outer(a, b, holder, start, count, block, group, after):
     experts, slots, total = a.shape
     columns = b.shape[2]
     tiles = columns // LANES
-    block = 128
     first = start // block
     extra = list(after) if holder is None else [holder, *after]
     return pl.pallas_call(
-        functools.partial(outer_body, group, some),
+        functools.partial(outer_body, group),
         out_shape=[jax.ShapeDtypeStruct((total, tiles, experts, LANES), NARROW), FLAG],
         grid=(count // block,),
         in_specs=[
-            pl.BlockSpec(sort.shape, lambda i: (0, 0)),
             pl.BlockSpec((experts, slots, block), lambda i: (0, 0, first + i)),
             pl.BlockSpec(
                 (experts, slots, columns), lambda i: (0, 0, 0), pipeline_mode=pl.Buffered(1)
@@ -421,15 +463,16 @@
             pl.BlockSpec((block, tiles, experts, LANES), lambda i: (first + i, 0, 0, 0)),
             pl.BlockSpec(FLAG.shape, lambda i: (0, 0)),
         ],
-        input_output_aliases={} if holder is None else {3: 0},
-        compiler_params=pltpu.CompilerParams(vmem_limit_bytes=56 * MIB),
+        scratch_shapes=[pltpu.VMEM((block, odd_tiles(group * experts), LANES), WIDE)],
+        input_output_aliases={} if holder is None else {2: 0},
+        compiler_params=pltpu.CompilerParams(vmem_limit_bytes=40 * MIB),
         cost_estimate=pl.CostEstimate(
             flops=2 * experts * slots * count * columns,
             bytes_accessed=4 * experts * count * columns,
             transcendentals=0,
         ),
         name="weight_gradient",
-    )(sort, a, b, *extra)
+    )(a, b, *extra)
 
 
 def stored_view(tiled):
@@ -475,21 +518,25 @@
 
     code, gate_tok = by_expert(code), by_expert(gate_tok)
     w_sort, v_sort = sorter(8, 6, local_count), sorter(16, 4, local_count)
-    w_split, flag = split_experts(w_view, w_sort, 256, 6, 8, [])
+    w_split, flag = split_experts(w_view, w_sort, 0, model_width, 256, 6, 8, [])
     (x_near,) = hold([x_near], [flag])
     x_far = swap(x_near, X)
     x_near_core = swap(x_near, CORE)
-    v_split, flag = split_experts(v_view, v_sort, 64, 4, 16, [x_near])
+    v_low, flag = split_experts(v_view, v_sort, 0, hidden // 2, 64, 4, 16, [x_near])
     x_far, g_near = hold([x_far, g_near], [flag])
     g_far = swap(g_near, X)
     g_near_core = swap(g_near, CORE)
     x_far_core = swap(x_far, CORE)
+    v_high, flag = split_experts(v_view, v_sort, hidden // 2, hidden // 2, 64, 4, 16, [x_far])
     x_pieces = [tokens, x_core, x_near, x_far, x_near_core, x_far_core]
-    xs, ag, active, slope = forward_tokens(code, gate_tok, x_pieces, w_split)
+    (g_far,) = hold([g_far], [flag])
     g_far_core = swap(g_far, CORE)
+    xs, ag, active, slope = forward_tokens(code, gate_tok, [*x_pieces, g_far], w_split)
     g_pieces = [cotangent, g_core, g_near, g_far, g_near_core, g_far_core]
-    gs, gp, keep, send = forward_cotangents(code, active, slope, g_pieces, w_split, v_split)
-    w_back, v_back = w_sort.T, v_sort.T
+    gs, gp, keep, send = forward_cotangents(
+        code, active, slope, g_pieces, w_split, [v_low, v_high]
+    )
+    xs, gs = xs.reshape(local_count, -1, model_width), gs.reshape(local_count, -1, model_width)
     width = keep.shape[1]
 
     def shape(rows, dtype, columns=width):
@@ -497,17 +544,17 @@
 
     def in_part(holder, number, after):
         rows = model_width // 4
-        return outer(w_back, xs, gp, holder, number * rows, rows, 6, 8, after)
+        return outer(xs, gp, holder, number * rows, rows, 256, 6, after)
 
     def out_part(holder, number, after):
         rows = hidden // 3
-        return outer(v_back, ag, gs, holder, number * rows, rows, 4, 16, after)
+        return outer(ag, gs, holder, number * rows, rows, 128, 8, after)
 
     got = swap(send, CORE)
     grad_in, flag = in_part(None, 0, [])
     mine, *sends = small_call(
         first_sum, place, [keep, got], [flag],
-        [shape(half, WIDE)] + [shape(half, NARROW)] * 3, "first_sum", 56,
+        [shape(half, WIDE)] + [shape(half, NARROW)] * 3, "first_sum", 32,
     )
     got = [swap(part, mask) for part, mask in zip(sends, (X, Y, X | Y))]
     grad_in, flag = in_part(grad_in, 1, [mine])

time: 202 us -> 180 us (0.89)
  Pallas kernels: 149 us -> 130 us
    pallas_call x12, Pallas kernels: 64.1 us -> 45 us  [the longest x7 40.8 us: outer(): pl.pallas_call(functools.partial(outer_body, group), out_shape=[jax.Shape...]
    unnamed x47 -> x31, local copies, waits for them, and re-layouts: 11.4 us -> 9.97 us
    pallas_call x2 -> x3, Pallas kernels: 39.5 us -> 40.2 us  [split_experts(): pl.pallas_call(functools.partial(split_body, group, some), out_shape=[jax...]
  transfers between devices with their start and end apart: 24 -> 24, of which waited for: 1 -> 3; matrix products, arithmetic and copies ran while one was open for 5% -> 5% of each run, Pallas kernels for 55% -> 54%
where the time goes in v6:
time: 180 us; the launch traced here: 179 us
  Pallas kernels  130 us (72%)
  starting transfers between devices  22.8 us (13%)
  local copies, waits for them, and re-layouts  13.3 us (7%)
  other arithmetic  6.24 us (3%)
  waiting for transfers between devices  5.41 us (3%)
    pallas_call x7, Pallas kernels, outer(): pl.pallas_call(functools.partial(outer_body, group), out_shape=[jax.Shape...  40.8 us
    pallas_call x3, Pallas kernels, split_experts(): pl.pallas_call(functools.partial(split_body, group, some), out_shape=[jax...  40.2 us
    pallas_call x1, Pallas kernels, forward_cotangents(): pl.pallas_call(forward_cotangents_body, out_shape=[jax.ShapeDtypeStruct((...  29.2 us
    ppermute x24, starting transfers between devices, swap(): return lax.ppermute(value, AXES, [(i, i ^ mask) for i in range(size)])  22.8 us
    pallas_call x1, Pallas kernels, forward_tokens(): pl.pallas_call(forward_tokens_body, out_shape=[jax.ShapeDtypeStruct((expe...  15.2 us
    unnamed x31, local copies, waits for them, and re-layouts  9.97 us
    ppermute x24, waiting for transfers between devices, swap(): return lax.ppermute(value, AXES, [(i, i ^ mask) for i in range(size)])  5.41 us
    pallas_call x5, Pallas kernels, small_call(): pl.pallas_call(run, out_shape=outs, grid=(steps,), in_specs=[pl.BlockSpec...  4.21 us
  transfers between devices with their start and end apart: 24, of which 3 were waited for; matrix products, arithmetic and copies ran while one was open for 5% of the time, Pallas kernels for 54%

profile of v6, /device:TPU:0, one launch (start us, length us, event | category | flops | bytes accessed | tf_op | source)
XLA Modules:
  0.0 179.1 jit_solution(7329901448990519703)
XLA Ops:
  2.3 2.4 %collective-permute-start.2 = (f32[8,128]{1,0:T(8,128)S(1)}, f32[8,128]{1,0:T(8,128)S(1)}, u32[]{:S(2)}, u32[]{:S(2)}) collective-permute-start(f32[8,128]{1,0:T(8,128)S(1)} %maximum_select_fusion), channel_id=1, source_target_pairs={{0,3},{1,2},{2,1},{3,0},{4,7},{5,6},{6,5},{7,4},{8,11},{9,10},{10,... | collective-permute-start | bytes 12296 | tf_op jit(solution)/shard_map/ppermute | solution.py:28
  11.0 19.6 %split_experts.3 = (bf16[4,3072,768]{2,1,0:T(8,128)(2,1)}, f32[8,128]{1,0:T(8,128)}) custom-call(bf16[192,192]{1,0:T(8,128)(2,1)} %constant.62.clone.sort_ref, bf16[3072,6,4,128]{3,2,1,0:T(4,128)(2,1)} %bitcast.48), custom_call_target="tpu_custom_call" | custom-call | bytes 37748736 | tf_op jit(solution)/shard_map/split_experts/pallas_call | solution.py:186
  32.0 1.5 collective-permute-start.5
  35.0 10.3 %split_experts.4 = (bf16[4,384,3072]{2,1,0:T(8,128)(2,1)}, f32[8,128]{1,0:T(8,128)}) custom-call(bf16[256,256]{1,0:T(8,128)(2,1)} %constant.63.clone.sort_ref, bf16[768,24,4,128]{3,2,1,0:T(4,128)(2,1)} %bitcast.45, bf16[64,3072]{1,0:T(8,128)(2,1)} %hold.3.refs_0_.refs_4_), custom_call_target="tpu_custom_call" | custom-call | bytes 18874368 | tf_op jit(solution)/shard_map/split_experts/pallas_call | solution.py:186
  50.9 10.3 %split_experts.5 = (bf16[4,384,3072]{2,1,0:T(8,128)(2,1)}, f32[8,128]{1,0:T(8,128)}) custom-call(bf16[256,256]{1,0:T(8,128)(2,1)} %constant.63.clone.sort_ref, bf16[768,24,4,128]{3,2,1,0:T(4,128)(2,1)} %bitcast.46, bf16[64,3072]{1,0:T(8,128)(2,1)} %get-tuple-element.47.refs_0_.refs_5_), custom_call_target="tpu_custom_call" | custom-call | bytes 18874368 | tf_op jit(solution)/shard_map/split_experts/pallas_call | solution.py:186
  62.9 15.2 %forward_tokens.1 = (bf16[640,3072]{1,0:T(8,128)(2,1)}, bf16[4,160,768]{2,1,0:T(8,128)(2,1)}, f32[4,160,768]{2,1,0:T(8,128)}, f32[4,160,768]{2,1,0:T(8,128)}) custom-call(s32[4,1,512]{2,1,0:T(1,128)} %bitcast.49, f32[4,1,512]{2,1,0:T(1,128)} %bitcast.51, bf16[4,3072,768]{2,1,0:T(8,128)(2,1)} %get-tuple-element.44.refs_0_.refs_1_, ...), custom_call_target="tpu_custom_call" | custom-call | flops 5033164800 | bytes 18874368 | tf_op jit(solution)/shard_map/forward_tokens/pallas_call | solution.py:292
  79.2 29.2 %forward_cotangents.1 = (bf16[640,3072]{1,0:T(8,128)(2,1)}, bf16[4,160,768]{2,1,0:T(8,128)(2,1)}, f32[256,3200]{1,0:T(8,128)}, bf16[256,3200]{1,0:T(8,128)(2,1)}) custom-call(s32[4,1,512]{2,1,0:T(1,128)} %bitcast.50, f32[4,160,768]{2,1,0:T(8,128)} %get-tuple-element.50.active_ref, f32[4,160,768]{2,1,0:T(8,128)} %get-tuple-element.51.slope_ref, ...), custom_call_target="tpu_custom_call" | custom-call | flops 10066329600 | bytes 37748736 | tf_op jit(solution)/shard_map/forward_cotangents/pallas_call | solution.py:381
  108.7 2.1 %copy-done = bf16[640,3072]{1,0:T(8,128)(2,1)S(1)} copy-done((bf16[640,3072]{1,0:T(8,128)(2,1)S(1)}, bf16[640,3072]{1,0:T(8,128)(2,1)}, u32[]{:S(2)}) %copy-start) | copy-done | bytes 3932184
  112.0 5.2 %weight_gradient.7 = (bf16[3072,6,4,128]{3,2,1,0:T(4,128)(2,1)}, f32[8,128]{1,0:T(8,128)S(1)}) custom-call(bf16[4,160,3072]{2,1,0:T(8,128)(2,1)S(1)} %bitcast.36, bf16[4,160,768]{2,1,0:T(8,128)(2,1)S(1)} %copy-done.2), custom_call_target="tpu_custom_call" | custom-call | flops 754974720 | bytes 9437184 | tf_op jit(solution)/shard_map/weight_gradient/pallas_call | solution.py:451
  117.2 1.9 %copy-done.4 = f32[256,3200]{1,0:T(8,128)S(1)} copy-done((f32[256,3200]{1,0:T(8,128)S(1)}, f32[256,3200]{1,0:T(8,128)}, u32[]{:S(2)}) %copy-start.4) | copy-done | bytes 3276824
  120.0 1.6 collective-permute-start.14
  123.5 5.2 %weight_gradient.8 = (bf16[3072,6,4,128]{3,2,1,0:T(4,128)(2,1)}, f32[8,128]{1,0:T(8,128)S(1)}) custom-call(bf16[4,160,3072]{2,1,0:T(8,128)(2,1)S(1)} %bitcast.37, bf16[4,160,768]{2,1,0:T(8,128)(2,1)S(1)} %copy-done.2, bf16[3072,6,4,128]{3,2,1,0:T(4,128)(2,1)} %get-tuple-element.63.refs_0_, ...), custom_call_target="tpu_custom_call", output_to_operand_aliasing={{0}: (2, {})} | custom-call | flops 754974720 | bytes 9437184 | tf_op jit(solution)/shard_map/weight_gradient/pallas_call | solution.py:451
  128.7 5.2 %weight_gradient.9 = (bf16[3072,6,4,128]{3,2,1,0:T(4,128)(2,1)}, f32[8,128]{1,0:T(8,128)S(1)}) custom-call(bf16[4,160,3072]{2,1,0:T(8,128)(2,1)S(1)} %bitcast.38, bf16[4,160,768]{2,1,0:T(8,128)(2,1)S(1)} %copy-done.2, bf16[3072,6,4,128]{3,2,1,0:T(4,128)(2,1)} %get-tuple-element.64.refs_0_, ...), custom_call_target="tpu_custom_call", output_to_operand_aliasing={{0}: (2, {})} | custom-call | flops 754974720 | bytes 9437184 | tf_op jit(solution)/shard_map/weight_gradient/pallas_call | solution.py:451
  133.9 5.2 %weight_gradient.10 = (bf16[3072,6,4,128]{3,2,1,0:T(4,128)(2,1)}, f32[8,128]{1,0:T(8,128)S(1)}) custom-call(bf16[4,160,3072]{2,1,0:T(8,128)(2,1)S(1)} %bitcast.39, bf16[4,160,768]{2,1,0:T(8,128)(2,1)S(1)} %copy-done.2, bf16[3072,6,4,128]{3,2,1,0:T(4,128)(2,1)} %get-tuple-element.66.refs_0_, ...), custom_call_target="tpu_custom_call", output_to_operand_aliasing={{0}: (2, {})} | custom-call | flops 754974720 | bytes 9437184 | tf_op jit(solution)/shard_map/weight_gradient/pallas_call | solution.py:451
  139.1 2.5 %collective-permute-done.15.refs_2_ = bf16[64,3200]{1,0:T(8,128)(2,1)S(1)} collective-permute-done((bf16[64,3200]{1,0:T(8,128)(2,1)S(1)}, bf16[64,3200]{1,0:T(8,128)(2,1)S(1)}, u32[]{:S(2)}, u32[]{:S(2)}) %collective-permute-start.15) | collective-permute-done | bytes 409632 | tf_op jit(solution)/shard_map/ppermute | solution.py:28
  142.4 1.6 collective-permute-start.17
  144.0 2.6 %collective-permute-start.18 = (bf16[16,3200]{1,0:T(8,128)(2,1)S(1)}, bf16[16,3200]{1,0:T(8,128)(2,1)S(1)}, u32[]{:S(2)}, u32[]{:S(2)}) collective-permute-start(bf16[16,3200]{1,0:T(8,128)(2,1)S(1)} %get-tuple-element.71), channel_id=1, source_target_pairs={{0,16},{1,17},{2,18},{3,19},{4,20},{5,21},{6,22},{7,23},{8,24},{9,... | collective-permute-start | bytes 307208 | tf_op jit(solution)/shard_map/ppermute | solution.py:28
  146.9 6.7 %weight_gradient.11 = (bf16[768,24,4,128]{3,2,1,0:T(4,128)(2,1)}, f32[8,128]{1,0:T(8,128)S(1)}) custom-call(bf16[4,160,768]{2,1,0:T(8,128)(2,1)S(1)} %copy-done.3, bf16[4,160,3072]{2,1,0:T(8,128)(2,1)S(1)} %bitcast.40, f32[16,3200]{1,0:T(8,128)S(1)} %get-tuple-element.69.refs_0_), custom_call_target="tpu_custom_call" | custom-call | flops 1006632960 | bytes 12582912 | tf_op jit(solution)/shard_map/weight_gradient/pallas_call | solution.py:451
  154.6 3.2 %collective-permute-start.22 = (bf16[16,3200]{1,0:T(8,128)(2,1)S(1)}, bf16[16,3200]{1,0:T(8,128)(2,1)S(1)}, u32[]{:S(2)}, u32[]{:S(2)}) collective-permute-start(bf16[16,3200]{1,0:T(8,128)(2,1)S(1)} %third_sum.1.refs_1_.refs_0_), channel_id=1, source_target_pairs={{0,24},{1,25},{2,26},{3,27},{4,28},{5,29},{6,30},{7,31},{8,16},{9,... | collective-permute-start | bytes 307208 | tf_op jit(solution)/shard_map/ppermute | solution.py:28
  159.1 6.7 %weight_gradient.12 = (bf16[768,24,4,128]{3,2,1,0:T(4,128)(2,1)}, f32[8,128]{1,0:T(8,128)S(1)}) custom-call(bf16[4,160,768]{2,1,0:T(8,128)(2,1)S(1)} %copy-done.3, bf16[4,160,3072]{2,1,0:T(8,128)(2,1)S(1)} %bitcast.41, bf16[768,24,4,128]{3,2,1,0:T(4,128)(2,1)} %get-tuple-element.76.refs_0_, ...), custom_call_target="tpu_custom_call", output_to_operand_aliasing={{0}: (2, {})} | custom-call | flops 1006632960 | bytes 12582912 | tf_op jit(solution)/shard_map/weight_gradient/pallas_call | solution.py:451
  166.3 1.6 collective-permute-start.23
  167.9 6.7 %weight_gradient.13 = (bf16[768,24,4,128]{3,2,1,0:T(4,128)(2,1)}, f32[8,128]{1,0:T(8,128)S(1)}) custom-call(bf16[4,160,768]{2,1,0:T(8,128)(2,1)S(1)} %copy-done.3, bf16[4,160,3072]{2,1,0:T(8,128)(2,1)S(1)} %bitcast.42, bf16[768,24,4,128]{3,2,1,0:T(4,128)(2,1)} %get-tuple-element.78.refs_0_, ...), custom_call_target="tpu_custom_call", output_to_operand_aliasing={{0}: (2, {})} | custom-call | flops 1006632960 | bytes 12582912 | tf_op jit(solution)/shard_map/weight_gradient/pallas_call | solution.py:451
  174.6 2.4 %collective-permute-done.23.refs_1_ = bf16[64,3200]{1,0:T(8,128)(2,1)S(1)} collective-permute-done((bf16[64,3200]{1,0:T(8,128)(2,1)S(1)}, bf16[64,3200]{1,0:T(8,128)(2,1)S(1)}, u32[]{:S(2)}, u32[]{:S(2)}) %collective-permute-start.23) | collective-permute-done | bytes 409632 | tf_op jit(solution)/shard_map/ppermute | solution.py:28
  176.9 1.5 join_x.1
  (94 shorter events, 28.0 us)
Async XLA Ops:
  2.3 29.1 %collective-permute-start.2 = (f32[8,128]{1,0:T(8,128)S(1)}, f32[8,128]{1,0:T(8,128)S(1)}, u32[]{:S(2)}, u32[]{:S(2)}) collective-permute-start(f32[8,128]{1,0:T(8,128)S(1)} %maximum_select_fusion), channel_id=1, source_target_pairs={{0,3},{1,2},{2,1},{3,0},{4,7},{5,6},{6,5},{7,4},{8,11},{9,10},{10,... | collective-permute-start | bytes 12296 | tf_op jit(solution)/shard_map/ppermute | solution.py:28
  4.7 27.3 %collective-permute-start.1 = (f32[8,128]{1,0:T(8,128)S(1)}, f32[8,128]{1,0:T(8,128)}, u32[]{:S(2)}, u32[]{:S(2)}) collective-permute-start(f32[8,128]{1,0:T(8,128)S(1)} %maximum_select_fusion), channel_id=1, source_target_pairs={{0,2},{1,3},{2,0},{3,1},{4,6},{5,7},{6,4},{7,5},{8,10},{9,11},{10,... | collective-permute-start | bytes 12296 | tf_op jit(solution)/shard_map/ppermute | solution.py:28
  5.3 28.2 %collective-permute-start = (f32[8,128]{1,0:T(8,128)S(1)}, f32[8,128]{1,0:T(8,128)}, u32[]{:S(2)}, u32[]{:S(2)}) collective-permute-start(f32[8,128]{1,0:T(8,128)S(1)} %get-tuple-element.95), channel_id=1, source_target_pairs={{0,1},{1,0},{2,3},{3,2},{4,5},{5,4},{6,7},{7,6},{8,9},{9,8},{10,11... | collective-permute-start | bytes 12296 | tf_op jit(solution)/shard_map/ppermute | solution.py:28
  5.3 56.6 %collective-permute-start.3 = (bf16[128,3072]{1,0:T(8,128)(2,1)}, bf16[128,3072]{1,0:T(8,128)(2,1)S(1)}, u32[]{:S(2)}, u32[]{:S(2)}) collective-permute-start(bf16[128,3072]{1,0:T(8,128)(2,1)} %refs_2_.1), channel_id=1, source_target_pairs={{0,1},{1,0},{2,3},{3,2},{4,5},{5,4},{6,7},{7,6},{8,9},{9,8},{10,11... | collective-permute-start | bytes 2359304 | tf_op jit(solution)/shard_map/ppermute | solution.py:28
  6.8 23.8 %collective-permute-start.4 = (bf16[64,3072]{1,0:T(8,128)(2,1)S(1)}, bf16[64,3072]{1,0:T(8,128)(2,1)S(1)}, u32[]{:S(2)}, u32[]{:S(2)}) collective-permute-start(bf16[64,3072]{1,0:T(8,128)(2,1)S(1)} %constant_dynamic-slice_fusion.1), channel_id=1, source_target_pairs={{0,2},{1,3},{2,0},{3,1},{4,6},{5,7},{6,4},{7,5},{8,10},{9,11},{10,... | collective-permute-start | bytes 1179656 | tf_op jit(solution)/shard_map/ppermute | solution.py:28
  30.6 47.5 %collective-permute-start.10 = (bf16[128,3072]{1,0:T(8,128)(2,1)S(1)}, bf16[128,3072]{1,0:T(8,128)(2,1)S(1)}, u32[]{:S(2)}, u32[]{:S(2)}) collective-permute-start(bf16[128,3072]{1,0:T(8,128)(2,1)S(1)} %copy-done.8), channel_id=1, source_target_pairs={{0,1},{1,0},{2,3},{3,2},{4,5},{5,4},{6,7},{7,6},{8,9},{9,8},{10,11... | collective-permute-start | bytes 2359304 | tf_op jit(solution)/shard_map/ppermute | solution.py:28
  31.4 13.9 %collective-permute-start.6 = (bf16[64,3072]{1,0:T(8,128)(2,1)S(1)}, bf16[64,3072]{1,0:T(8,128)(2,1)S(1)}, u32[]{:S(2)}, u32[]{:S(2)}) collective-permute-start(bf16[64,3072]{1,0:T(8,128)(2,1)S(1)} %constant_dynamic-slice_fusion), channel_id=1, source_target_pairs={{0,2},{1,3},{2,0},{3,1},{4,6},{5,7},{6,4},{7,5},{8,10},{9,11},{10,... | collective-permute-start | bytes 1179656 | tf_op jit(solution)/shard_map/ppermute | solution.py:28
  32.0 13.3 %collective-permute-start.5 = (bf16[64,3072]{1,0:T(8,128)(2,1)}, bf16[64,3072]{1,0:T(8,128)(2,1)S(1)}, u32[]{:S(2)}, u32[]{:S(2)}) collective-permute-start(bf16[64,3072]{1,0:T(8,128)(2,1)} %hold.3.refs_0_.refs_4_), channel_id=1, source_target_pairs={{0,4},{1,5},{2,6},{3,7},{4,0},{5,1},{6,2},{7,3},{8,12},{9,13},{10,... | collective-permute-start | bytes 1179656 | tf_op jit(solution)/shard_map/ppermute | solution.py:28
  34.9 27.0 %collective-permute-start.7 = (bf16[64,3072]{1,0:T(8,128)(2,1)}, bf16[64,3072]{1,0:T(8,128)(2,1)}, u32[]{:S(2)}, u32[]{:S(2)}) collective-permute-start(bf16[64,3072]{1,0:T(8,128)(2,1)} %hold.3.refs_0_.refs_4_), channel_id=1, source_target_pairs={{0,1},{1,0},{2,3},{3,2},{4,5},{5,4},{6,7},{7,6},{8,9},{9,8},{10,11... | collective-permute-start | bytes 1179656 | tf_op jit(solution)/shard_map/ppermute | solution.py:28
  46.2 15.7 %collective-permute-start.8 = (bf16[64,3072]{1,0:T(8,128)(2,1)}, bf16[64,3072]{1,0:T(8,128)(2,1)S(1)}, u32[]{:S(2)}, u32[]{:S(2)}) collective-permute-start(bf16[64,3072]{1,0:T(8,128)(2,1)} %get-tuple-element.47.refs_0_.refs_5_), channel_id=1, source_target_pairs={{0,1},{1,0},{2,3},{3,2},{4,5},{5,4},{6,7},{7,6},{8,9},{9,8},{10,11... | collective-permute-start | bytes 1179656 | tf_op jit(solution)/shard_map/ppermute | solution.py:28
  46.7 14.5 %collective-permute-start.9 = (bf16[64,3072]{1,0:T(8,128)(2,1)}, bf16[64,3072]{1,0:T(8,128)(2,1)S(1)}, u32[]{:S(2)}, u32[]{:S(2)}) collective-permute-start(bf16[64,3072]{1,0:T(8,128)(2,1)} %get-tuple-element.48.refs_6_), channel_id=1, source_target_pairs={{0,4},{1,5},{2,6},{3,7},{4,0},{5,1},{6,2},{7,3},{8,12},{9,13},{10,... | collective-permute-start | bytes 1179656 | tf_op jit(solution)/shard_map/ppermute | solution.py:28
  61.2 17.0 %collective-permute-start.11 = (bf16[64,3072]{1,0:T(8,128)(2,1)S(1)}, bf16[64,3072]{1,0:T(8,128)(2,1)}, u32[]{:S(2)}, u32[]{:S(2)}) collective-permute-start(bf16[64,3072]{1,0:T(8,128)(2,1)S(1)} %copy-done.10), channel_id=1, source_target_pairs={{0,1},{1,0},{2,3},{3,2},{4,5},{5,4},{6,7},{7,6},{8,9},{9,8},{10,11... | collective-permute-start | bytes 1179656 | tf_op jit(solution)/shard_map/ppermute | solution.py:28
  61.9 16.2 %collective-permute-start.12 = (bf16[64,3072]{1,0:T(8,128)(2,1)}, bf16[64,3072]{1,0:T(8,128)(2,1)S(1)}, u32[]{:S(2)}, u32[]{:S(2)}) collective-permute-start(bf16[64,3072]{1,0:T(8,128)(2,1)} %hold.5.refs_8_.refs_7_), channel_id=1, source_target_pairs={{0,1},{1,0},{2,3},{3,2},{4,5},{5,4},{6,7},{7,6},{8,9},{9,8},{10,11... | collective-permute-start | bytes 1179656 | tf_op jit(solution)/shard_map/ppermute | solution.py:28
  108.3 8.9 %collective-permute-start.13 = (bf16[256,3200]{1,0:T(8,128)(2,1)}, bf16[256,3200]{1,0:T(8,128)(2,1)S(1)}, u32[]{:S(2)}, u32[]{:S(2)}) collective-permute-start(bf16[256,3200]{1,0:T(8,128)(2,1)} %get-tuple-element.55), channel_id=1, source_target_pairs={{0,1},{1,0},{2,3},{3,2},{4,5},{5,4},{6,7},{7,6},{8,9},{9,8},{10,11... | collective-permute-start | bytes 4915208 | tf_op jit(solution)/shard_map/ppermute | solution.py:28
  120.0 19.1 %collective-permute-start.14 = (bf16[64,3200]{1,0:T(8,128)(2,1)S(1)}, bf16[64,3200]{1,0:T(8,128)(2,1)S(1)}, u32[]{:S(2)}, u32[]{:S(2)}) collective-permute-start(bf16[64,3200]{1,0:T(8,128)(2,1)S(1)} %get-tuple-element.60), channel_id=1, source_target_pairs={{0,4},{1,5},{2,6},{3,7},{4,0},{5,1},{6,2},{7,3},{8,12},{9,13},{10,... | collective-permute-start | bytes 1228808 | tf_op jit(solution)/shard_map/ppermute | solution.py:28
  121.5 20.1 %collective-permute-start.15 = (bf16[64,3200]{1,0:T(8,128)(2,1)S(1)}, bf16[64,3200]{1,0:T(8,128)(2,1)S(1)}, u32[]{:S(2)}, u32[]{:S(2)}) collective-permute-start(bf16[64,3200]{1,0:T(8,128)(2,1)S(1)} %get-tuple-element.61), channel_id=1, source_target_pairs={{0,2},{1,3},{2,0},{3,1},{4,6},{5,7},{6,4},{7,5},{8,10},{9,11},{10,... | collective-permute-start | bytes 1228808 | tf_op jit(solution)/shard_map/ppermute | solution.py:28
  123.0 18.7 %collective-permute-start.16 = (bf16[64,3200]{1,0:T(8,128)(2,1)S(1)}, bf16[64,3200]{1,0:T(8,128)(2,1)S(1)}, u32[]{:S(2)}, u32[]{:S(2)}) collective-permute-start(bf16[64,3200]{1,0:T(8,128)(2,1)S(1)} %get-tuple-element.62), channel_id=1, source_target_pairs={{0,6},{1,7},{2,4},{3,5},{4,2},{5,3},{6,0},{7,1},{8,14},{9,15},{10,... | collective-permute-start | bytes 1228808 | tf_op jit(solution)/shard_map/ppermute | solution.py:28
  142.4 11.1 %collective-permute-start.17 = (bf16[16,3200]{1,0:T(8,128)(2,1)S(1)}, bf16[16,3200]{1,0:T(8,128)(2,1)S(1)}, u32[]{:S(2)}, u32[]{:S(2)}) collective-permute-start(bf16[16,3200]{1,0:T(8,128)(2,1)S(1)} %get-tuple-element.70), channel_id=1, source_target_pairs={{0,8},{1,9},{2,10},{3,11},{4,12},{5,13},{6,14},{7,15},{8,0},{9,1},... | collective-permute-start | bytes 307208 | tf_op jit(solution)/shard_map/ppermute | solution.py:28
  144.0 10.0 %collective-permute-start.18 = (bf16[16,3200]{1,0:T(8,128)(2,1)S(1)}, bf16[16,3200]{1,0:T(8,128)(2,1)S(1)}, u32[]{:S(2)}, u32[]{:S(2)}) collective-permute-start(bf16[16,3200]{1,0:T(8,128)(2,1)S(1)} %get-tuple-element.71), channel_id=1, source_target_pairs={{0,16},{1,17},{2,18},{3,19},{4,20},{5,21},{6,22},{7,23},{8,24},{9,... | collective-permute-start | bytes 307208 | tf_op jit(solution)/shard_map/ppermute | solution.py:28
  146.7 7.3 %collective-permute-start.19 = (bf16[16,3200]{1,0:T(8,128)(2,1)S(1)}, bf16[16,3200]{1,0:T(8,128)(2,1)S(1)}, u32[]{:S(2)}, u32[]{:S(2)}) collective-permute-start(bf16[16,3200]{1,0:T(8,128)(2,1)S(1)} %get-tuple-element.72), channel_id=1, source_target_pairs={{0,24},{1,25},{2,26},{3,27},{4,28},{5,29},{6,30},{7,31},{8,16},{9,... | collective-permute-start | bytes 307208 | tf_op jit(solution)/shard_map/ppermute | solution.py:28
  154.6 11.1 %collective-permute-start.22 = (bf16[16,3200]{1,0:T(8,128)(2,1)S(1)}, bf16[16,3200]{1,0:T(8,128)(2,1)S(1)}, u32[]{:S(2)}, u32[]{:S(2)}) collective-permute-start(bf16[16,3200]{1,0:T(8,128)(2,1)S(1)} %third_sum.1.refs_1_.refs_0_), channel_id=1, source_target_pairs={{0,24},{1,25},{2,26},{3,27},{4,28},{5,29},{6,30},{7,31},{8,16},{9,... | collective-permute-start | bytes 307208 | tf_op jit(solution)/shard_map/ppermute | solution.py:28
  157.9 7.9 %collective-permute-start.21 = (bf16[16,3200]{1,0:T(8,128)(2,1)S(1)}, bf16[16,3200]{1,0:T(8,128)(2,1)S(1)}, u32[]{:S(2)}, u32[]{:S(2)}) collective-permute-start(bf16[16,3200]{1,0:T(8,128)(2,1)S(1)} %third_sum.1.refs_1_.refs_0_), channel_id=1, source_target_pairs={{0,16},{1,17},{2,18},{3,19},{4,20},{5,21},{6,22},{7,23},{8,24},{9,... | collective-permute-start | bytes 307208 | tf_op jit(solution)/shard_map/ppermute | solution.py:28
  157.9 7.9 %collective-permute-start.20 = (bf16[16,3200]{1,0:T(8,128)(2,1)S(1)}, bf16[16,3200]{1,0:T(8,128)(2,1)S(1)}, u32[]{:S(2)}, u32[]{:S(2)}) collective-permute-start(bf16[16,3200]{1,0:T(8,128)(2,1)S(1)} %third_sum.1.refs_1_.refs_0_), channel_id=1, source_target_pairs={{0,8},{1,9},{2,10},{3,11},{4,12},{5,13},{6,14},{7,15},{8,0},{9,1},... | collective-permute-start | bytes 307208 | tf_op jit(solution)/shard_map/ppermute | solution.py:28
  166.3 10.6 %collective-permute-start.23 = (bf16[64,3200]{1,0:T(8,128)(2,1)S(1)}, bf16[64,3200]{1,0:T(8,128)(2,1)S(1)}, u32[]{:S(2)}, u32[]{:S(2)}) collective-permute-start(bf16[64,3200]{1,0:T(8,128)(2,1)S(1)} %join_z.1.refs_1_.refs_0_), channel_id=1, source_target_pairs={{0,4},{1,5},{2,6},{3,7},{4,0},{5,1},{6,2},{7,3},{8,12},{9,13},{10,... | collective-permute-start | bytes 1228808 | tf_op jit(solution)/shard_map/ppermute | solution.py:28
  (15 other events, 83.0 us)

commit v7 on v6

--- a/solution.py
+++ b/solution.py
@@ -204,6 +204,43 @@
     )(sort, view, *after)
 
 
+def route_body(first_ref, *refs):
+    metas, (code_ref, gate_ref) = refs[:-2], refs[-2:]
+    experts = code_ref.shape[0]
+    top_count = metas[0].shape[0] // 2
+    row = lax.broadcasted_iota(jnp.int32, (LANES, LANES), 0)
+    column = lax.broadcasted_iota(jnp.int32, (LANES, LANES), 1)
+    earlier = (row < column).astype(WIDE).astype(NARROW)
+    choice = lax.broadcasted_iota(jnp.int32, (top_count, LANES), 0)
+    for block, meta_ref in enumerate(metas):
+        lanes = slice(block * LANES, (block + 1) * LANES)
+        ids = meta_ref[:top_count, :].astype(jnp.int32)
+        gates = meta_ref[top_count:, :]
+        named = [ids == first_ref[0] + expert for expert in range(experts)]
+        hits = [jnp.sum(name.astype(WIDE), axis=0, keepdims=True) for name in named]
+        before = mm(jnp.concatenate(hits, axis=0).astype(NARROW), earlier, NN).astype(jnp.int32)
+        for expert in range(experts):
+            which = jnp.sum(jnp.where(named[expert], choice, 0), axis=0, keepdims=True)
+            slot = before[expert : expert + 1] + block * CAP
+            code_ref[expert, :, lanes] = jnp.where(hits[expert] > 0.5, slot, 1023) + 1024 * which
+            gate_ref[expert, :, lanes] = jnp.sum(
+                jnp.where(named[expert], gates, 0.0), axis=0, keepdims=True
+            )
+
+
+def route(first, metas, experts):
+    shape = (experts, 1, len(metas) * LANES)
+    return pl.pallas_call(
+        route_body,
+        out_shape=[jax.ShapeDtypeStruct(shape, jnp.int32), jax.ShapeDtypeStruct(shape, WIDE)],
+        in_specs=[pl.BlockSpec(memory_space=pltpu.SMEM)]
+        + [pl.BlockSpec(memory_space=pltpu.VMEM)] * len(metas),
+        out_specs=[pl.BlockSpec(memory_space=pltpu.VMEM)] * 2,
+        cost_estimate=pl.CostEstimate(flops=0, bytes_accessed=1 << 18, transcendentals=0),
+        name="route",
+    )(first, *metas)
+
+
 def fetch(pieces, whole, sem):
     copies, begin = [], 0
     for number, piece in enumerate(pieces):
@@ -237,37 +274,49 @@
     return specs, operands
 
 
-def gather_slots(code_ref, whole_ref, pick_ref, slot_ref):
+def block_picks(code_ref):
     experts, _, tokens = code_ref.shape
-    slots = pick_ref.shape[0] // experts
-    model_width = whole_ref.shape[1]
-    columns = 256
-    for expert in range(experts):
-        pick_ref[expert * slots : (expert + 1) * slots, :] = (
-            chosen(code_ref[expert], slots).astype(WIDE).astype(NARROW)
-        )
-    for begin in range(0, model_width, columns):
+    slot = lax.broadcasted_iota(jnp.int32, (CAP, LANES), 0)
+    picks = []
+    for block in range(tokens // LANES):
+        lanes = slice(block * LANES, (block + 1) * LANES)
+        codes = [jnp.bitwise_and(code_ref[expert, :, lanes], 1023) for expert in range(experts)]
+        found = [(slot + block * CAP == code).astype(WIDE) for code in codes]
+        picks.append(jnp.concatenate(found, axis=0).astype(NARROW))
+    return picks
+
+
+def gather_slots(code_ref, whole_ref, wide_ref, slot_ref):
+    experts = code_ref.shape[0]
+    slots = slot_ref.shape[0] // experts
+    columns = wide_ref.shape[1]
+    picks = block_picks(code_ref)
+    for begin in range(0, whole_ref.shape[1], columns):
         part = slice(begin, begin + columns)
-        slot_ref[:, part] = mm(pick_ref[...], whole_ref[:, part], NN).astype(NARROW)
+        for block, pick in enumerate(picks):
+            found = mm(pick, whole_ref[block * LANES : (block + 1) * LANES, part], NN)
+            for expert in range(experts):
+                row = expert * slots + block * CAP
+                wide_ref[row : row + CAP, :] = found[expert * CAP : (expert + 1) * CAP]
+        slot_ref[:, part] = wide_ref[...].astype(NARROW)
 
 
 def forward_tokens_body(code_ref, gate_ref, *refs):
     w_refs, refs = refs[:2], refs[2:]
-    pieces, refs = refs[:-9], refs[-9:]
-    xs_ref, ag_ref, active_ref, slope_ref, x_ref, slot_ref, pick_ref, sem, out_sem = refs
+    pieces, refs = refs[:-8], refs[-8:]
+    xs_ref, ag_ref, active_ref, slope_ref, x_ref, slot_ref, wide_ref, sem = refs
     step = pl.program_id(0)
     slots = ag_ref.shape[1]
-    out = pltpu.make_async_copy(slot_ref, xs_ref, out_sem)
 
     @pl.when(step == 0)
     def _():
         fetch(pieces, x_ref, sem)
-        gather_slots(code_ref, x_ref, pick_ref, slot_ref)
-        out.start()
+        gather_slots(code_ref, x_ref, wide_ref, slot_ref)
 
     choose = chosen(code_ref[step], slots)
     gate = jnp.sum(jnp.where(choose, gate_ref[step], 0.0), axis=1, keepdims=True)
     rows = pl.ds(pl.multiple_of(step * slots, slots), slots)
+    xs_ref[0] = slot_ref[rows, :]
     pre_act, begin = 0.0, 0
     for w_ref in w_refs:
         end = begin + w_ref.shape[1]
@@ -278,7 +327,6 @@
     active_ref[0] = active
     ag_ref[0] = (gate * active).astype(NARROW)
     slope_ref[0] = gate * squash * (1.0 + pre_act * (1.0 - squash))
-    pl.when(step == pl.num_programs(0) - 1)(out.wait)
 
 
 def forward_tokens(code, gate_tok, x_pieces, w_split):
@@ -288,20 +336,18 @@
     expert = lambda i: (i, 0, 0)
     all_experts = pl.BlockSpec((experts, 1, tokens), lambda i: (0, 0, 0))
     w_specs, w_operands = weight_parts([w_split], 2)
-    shapes = [(hidden, NARROW), (hidden, WIDE), (hidden, WIDE)]
+    shapes = [(model_width, NARROW), (hidden, NARROW), (hidden, WIDE), (hidden, WIDE)]
     return pl.pallas_call(
         forward_tokens_body,
-        out_shape=[jax.ShapeDtypeStruct((experts * slots, model_width), NARROW)]
-        + [jax.ShapeDtypeStruct((experts, slots, width), dtype) for width, dtype in shapes],
+        out_shape=[jax.ShapeDtypeStruct((experts, slots, width), dtype) for width, dtype in shapes],
         grid=(experts,),
         in_specs=[all_experts, all_experts, *w_specs, *[ANY] * len(x_pieces)],
-        out_specs=[ANY] + [pl.BlockSpec((1, slots, width), expert) for width, _ in shapes],
+        out_specs=[pl.BlockSpec((1, slots, width), expert) for width, _ in shapes],
         scratch_shapes=[
             pltpu.VMEM((tokens, model_width), NARROW),
             pltpu.VMEM((experts * slots, model_width), NARROW),
-            pltpu.VMEM((experts * slots, tokens), NARROW),
+            pltpu.VMEM((experts * slots, 512), WIDE),
             pltpu.SemaphoreType.DMA((len(x_pieces),)),
-            pltpu.SemaphoreType.DMA(()),
         ],
         compiler_params=pltpu.CompilerParams(vmem_limit_bytes=56 * MIB),
         cost_estimate=pl.CostEstimate(
@@ -315,22 +361,21 @@
 
 def forward_cotangents_body(code_ref, active_ref, slope_ref, *refs):
     w_refs, v_refs, refs = refs[:2], refs[2:4], refs[4:]
-    pieces, refs = refs[:-10], refs[-10:]
-    gs_ref, gp_ref, keep_ref, send_ref, g_ref, slot_ref, back_ref, pick_ref, sem, out_sem = refs
+    pieces, refs = refs[:-9], refs[-9:]
+    gs_ref, gp_ref, keep_ref, send_ref, g_ref, slot_ref, wide_ref, back_ref, sem = refs
     step = pl.program_id(0)
     slots = gp_ref.shape[1]
     model_width = g_ref.shape[1]
     columns = 512
-    out = pltpu.make_async_copy(slot_ref, gs_ref, out_sem)
 
     @pl.when(step == 0)
     def _():
         fetch(pieces, g_ref, sem)
-        gather_slots(code_ref, g_ref, pick_ref, slot_ref)
-        out.start()
+        gather_slots(code_ref, g_ref, wide_ref, slot_ref)
 
     code = code_ref[step]
     rows = pl.ds(pl.multiple_of(step * slots, slots), slots)
+    gs_ref[0] = slot_ref[rows, :]
     gate_part, begin = 0.0, 0
     for v_ref in v_refs:
         part = slice(begin, begin + v_ref.shape[1])
@@ -342,7 +387,7 @@
         held = w_refs[0].shape[1]
         w_ref, inner = w_refs[begin // held], begin % held
         back = mm(gp_ref[0], w_ref[0, inner : inner + columns, :], NT)
-        back_ref[rows, begin : begin + columns] = back.astype(NARROW)
+        back_ref[rows, begin : begin + columns] = back
     which = jnp.sum(
         jnp.where(chosen(code, slots), jnp.right_shift(code, 10), 0), axis=1, keepdims=True
     )
@@ -350,22 +395,25 @@
     high = gate_part.astype(NARROW).astype(WIDE)
     gates = jnp.where(lane == which, high, 0.0)
     gates = jnp.where(lane == which + LANES // 2, gate_part - high, gates)
-    back_ref[rows, model_width:] = gates.astype(NARROW)
+    back_ref[rows, model_width:] = gates
 
     @pl.when(step == pl.num_programs(0) - 1)
     def _():
-        out.wait()
-        quarter = g_ref.shape[0] // 4
+        experts = code_ref.shape[0]
+        picks = block_picks(code_ref)
         for begin in range(0, model_width + LANES, columns):
             part = slice(begin, min(begin + columns, model_width + LANES))
-            summed = mm(pick_ref[...], back_ref[:, part], TN)
-            if begin == model_width:
-                summed = summed + pltpu.roll(summed, LANES // 2, 1)
-            for pair in range(2):
-                lower = 2 * pair * quarter
-                into = slice(pair * quarter, (pair + 1) * quarter)
-                keep_ref[into, part] = summed[lower : lower + quarter]
-                send_ref[into, part] = summed[lower + quarter : lower + 2 * quarter].astype(NARROW)
+            for block, pick in enumerate(picks):
+                starts = [expert * slots + block * CAP for expert in range(experts)]
+                held = [back_ref[start : start + CAP, part] for start in starts]
+                summed = mm(pick, jnp.concatenate(held, axis=0).astype(NARROW), TN)
+                if begin == model_width:
+                    summed = summed + pltpu.roll(summed, LANES // 2, 1)
+                into = slice(block // 2 * LANES, (block // 2 + 1) * LANES)
+                if block % 2 == 0:
+                    keep_ref[into, part] = summed
+                else:
+                    send_ref[into, part] = summed.astype(NARROW)
 
 
 def forward_cotangents(code, active, slope, g_pieces, w_split, v_split):
@@ -381,7 +429,7 @@
     return pl.pallas_call(
         forward_cotangents_body,
         out_shape=[
-            jax.ShapeDtypeStruct((experts * slots, model_width), NARROW),
+            jax.ShapeDtypeStruct((experts, slots, model_width), NARROW),
             jax.ShapeDtypeStruct((experts, slots, hidden), NARROW),
             jax.ShapeDtypeStruct((tokens // 2, width), WIDE),
             jax.ShapeDtypeStruct((tokens // 2, width), NARROW),
@@ -396,7 +444,7 @@
             *[ANY] * len(g_pieces),
         ],
         out_specs=[
-            ANY,
+            pl.BlockSpec((1, slots, model_width), expert),
             pl.BlockSpec((1, slots, hidden), expert),
             pl.BlockSpec((tokens // 2, width), whole, pipeline_mode=one),
             pl.BlockSpec((tokens // 2, width), whole, pipeline_mode=one),
@@ -404,10 +452,9 @@
         scratch_shapes=[
             pltpu.VMEM((tokens, model_width), NARROW),
             pltpu.VMEM((experts * slots, model_width), NARROW),
-            pltpu.VMEM((experts * slots, width), NARROW),
-            pltpu.VMEM((experts * slots, tokens), NARROW),
+            pltpu.VMEM((experts * slots, 512), WIDE),
+            pltpu.VMEM((experts * slots, width), WIDE),
             pltpu.SemaphoreType.DMA((len(g_pieces),)),
-            pltpu.SemaphoreType.DMA(()),
         ],
         compiler_params=pltpu.CompilerParams(vmem_limit_bytes=56 * MIB),
         cost_estimate=pl.CostEstimate(
@@ -495,34 +542,18 @@
 
     meta = jnp.concatenate([expert_ids.astype(WIDE), gate_values.astype(WIDE)], axis=1).T
     turned = own_order(meta)
-    meta = jnp.stack([meta, swap(meta, CORE), swap(turned, Y), swap(turned, CORE | Y)])
+    metas = [meta, swap(meta, CORE), swap(turned, Y), swap(turned, CORE | Y)]
     w_view, v_view = tiled_view(w_in), tiled_view(w_out)
     x_near = swap(lax.dynamic_slice_in_dim(tokens, x_index * half, half, axis=0), Y)
     g_near = swap(lax.dynamic_slice_in_dim(cotangent, x_index * half, half, axis=0), Y)
     x_core, g_core = swap(tokens, CORE), swap(cotangent, CORE)
-    ids, gates = meta[:, :top_count].astype(jnp.int32), meta[:, top_count:]
-    blocks = ids.shape[0]
-    names = first + jnp.arange(local_count, dtype=jnp.int32)
-    named = ids[:, None] == names[None, :, None, None]
-    hit = jnp.any(named, axis=2)
-    gate_tok = jnp.sum(jnp.where(named, gates[:, None], 0.0), axis=2)
-    earlier = jnp.tril(jnp.ones((tok_rows, tok_rows), WIDE), -1)
-    position = jnp.einsum("tu,blu->blt", earlier, hit.astype(WIDE)).astype(jnp.int32)
-    base = jnp.arange(blocks, dtype=jnp.int32)[:, None, None] * CAP
-    order = jnp.arange(top_count, dtype=jnp.int32)[None, None, :, None]
-    which = jnp.sum(jnp.where(named, order, 0), axis=2)
-    code = jnp.where(hit, base + position, 1023) + 1024 * which
-
-    def by_expert(value):
-        return jnp.swapaxes(value, 0, 1).reshape(local_count, 1, blocks * tok_rows)
-
-    code, gate_tok = by_expert(code), by_expert(gate_tok)
     w_sort, v_sort = sorter(8, 6, local_count), sorter(16, 4, local_count)
     w_split, flag = split_experts(w_view, w_sort, 0, model_width, 256, 6, 8, [])
-    (x_near,) = hold([x_near], [flag])
+    x_near, *others = hold([x_near, *metas[1:]], [flag])
+    code, gate_tok = route(first.astype(jnp.int32).reshape(1), [metas[0], *others], local_count)
     x_far = swap(x_near, X)
     x_near_core = swap(x_near, CORE)
-    v_low, flag = split_experts(v_view, v_sort, 0, hidden // 2, 64, 4, 16, [x_near])
+    v_low, flag = split_experts(v_view, v_sort, 0, hidden // 2, 64, 4, 16, [x_near, code])
     x_far, g_near = hold([x_far, g_near], [flag])
     g_far = swap(g_near, X)
     g_near_core = swap(g_near, CORE)
@@ -536,7 +567,6 @@
     gs, gp, keep, send = forward_cotangents(
         code, active, slope, g_pieces, w_split, [v_low, v_high]
     )
-    xs, gs = xs.reshape(local_count, -1, model_width), gs.reshape(local_count, -1, model_width)
     width = keep.shape[1]
 
     def shape(rows, dtype, columns=width):
@@ -551,13 +581,13 @@
         return outer(ag, gs, holder, number * rows, rows, 128, 8, after)
 
     got = swap(send, CORE)
-    grad_in, flag = in_part(None, 0, [])
     mine, *sends = small_call(
-        first_sum, place, [keep, got], [flag],
+        first_sum, place, [keep, got], [],
         [shape(half, WIDE)] + [shape(half, NARROW)] * 3, "first_sum", 32,
     )
     got = [swap(part, mask) for part, mask in zip(sends, (X, Y, X | Y))]
-    grad_in, flag = in_part(grad_in, 1, [mine])
+    grad_in, flag = in_part(None, 0, [mine])
+    grad_in, flag = in_part(grad_in, 1, [flag])
     grad_in, flag = in_part(grad_in, 2, [flag])
     grad_in, flag = in_part(grad_in, 3, [flag])
     mine, *sends = small_call(

time: 180 us -> 172 us (0.956)
  other arithmetic: 6.24 us -> 1.53 us
  local copies, waits for them, and re-layouts: 13.3 us -> 11.5 us
    pallas_call x1, Pallas kernels: 29.2 us -> 27.1 us  [forward_cotangents(): pl.pallas_call(forward_cotangents_body, out_shape=[jax.ShapeDtypeStruct((...]
    unnamed x31 -> x39, local copies, waits for them, and re-layouts: 9.97 us -> 9.3 us
  transfers between devices with their start and end apart: 24 -> 24, of which waited for: 3 -> 4; matrix products, arithmetic and copies ran while one was open for 5% -> 2% of each run, Pallas kernels for 54% -> 57%
where the time goes in v7:
time: 172 us
  Pallas kernels  129 us (75%)
  starting transfers between devices  22.4 us (13%)
  local copies, waits for them, and re-layouts  11.5 us (7%)
  waiting for transfers between devices  6.63 us (4%)
    pallas_call x7, Pallas kernels, outer(): pl.pallas_call(functools.partial(outer_body, group), out_shape=[jax.Shape...  40.8 us
    pallas_call x3, Pallas kernels, split_experts(): pl.pallas_call(functools.partial(split_body, group, some), out_shape=[jax...  40.2 us
    pallas_call x1, Pallas kernels, forward_cotangents(): pl.pallas_call(forward_cotangents_body, out_shape=[jax.ShapeDtypeStruct((...  27.1 us
    ppermute x24, starting transfers between devices, swap(): return lax.ppermute(value, AXES, [(i, i ^ mask) for i in range(size)])  22.4 us
    pallas_call x1, Pallas kernels, forward_tokens(): pl.pallas_call(forward_tokens_body, out_shape=[jax.ShapeDtypeStruct((expe...  14.9 us
    unnamed x39, local copies, waits for them, and re-layouts  9.3 us
    ppermute x24, waiting for transfers between devices, swap(): return lax.ppermute(value, AXES, [(i, i ^ mask) for i in range(size)])  6.63 us
    pallas_call x5, Pallas kernels, small_call(): pl.pallas_call(run, out_shape=outs, grid=(steps,), in_specs=[pl.BlockSpec...  4.21 us
  transfers between devices with their start and end apart: 24, of which 4 were waited for; matrix products, arithmetic and copies ran while one was open for 2% of the time, Pallas kernels for 57%

profile of v7, /device:TPU:0, one launch (start us, length us, event | category | flops | bytes accessed | tf_op | source)
XLA Modules:
  0.0 171.6 jit_solution(15266650489891495681)
XLA Ops:
  1.8 3.0 %collective-permute-start = (bf16[64,3072]{1,0:T(8,128)(2,1)S(1)}, bf16[64,3072]{1,0:T(8,128)(2,1)S(1)}, u32[]{:S(2)}, u32[]{:S(2)}) collective-permute-start(bf16[64,3072]{1,0:T(8,128)(2,1)S(1)} %constant_dynamic-slice_fusion.1), channel_id=1, source_target_pairs={{0,2},{1,3},{2,0},{3,1},{4,6},{5,7},{6,4},{7,5},{8,10},{9,11},{10,... | collective-permute-start | bytes 1179656 | tf_op jit(solution)/shard_map/ppermute | solution.py:28
  9.6 19.7 %split_experts.3 = (bf16[4,3072,768]{2,1,0:T(8,128)(2,1)}, f32[8,128]{1,0:T(8,128)}) custom-call(bf16[192,192]{1,0:T(8,128)(2,1)} %constant.46.clone.sort_ref, bf16[3072,6,4,128]{3,2,1,0:T(4,128)(2,1)} %bitcast.25), custom_call_target="tpu_custom_call" | custom-call | bytes 37748736 | tf_op jit(solution)/shard_map/split_experts/pallas_call | solution.py:186
  30.0 1.7 collective-permute-start.5
  31.7 1.5 route.1
  33.2 10.3 %split_experts.4 = (bf16[4,384,3072]{2,1,0:T(8,128)(2,1)}, f32[8,128]{1,0:T(8,128)}) custom-call(bf16[256,256]{1,0:T(8,128)(2,1)} %constant.47.clone.sort_ref, bf16[768,24,4,128]{3,2,1,0:T(4,128)(2,1)} %bitcast.22, bf16[64,3072]{1,0:T(8,128)(2,1)} %get-tuple-element.57.refs_0_.refs_4_, s32[4,1,512]{2,1,0:T(1,128)} %get-tuple-element.54.refs_1_.code_ref), custom_call_target="tpu_custom_call" | custom-call | bytes 18874368 | tf_op jit(solution)/shard_map/split_experts/pallas_call | solution.py:186
  45.5 10.3 %split_experts.5 = (bf16[4,384,3072]{2,1,0:T(8,128)(2,1)}, f32[8,128]{1,0:T(8,128)}) custom-call(bf16[256,256]{1,0:T(8,128)(2,1)} %constant.47.clone.sort_ref, bf16[768,24,4,128]{3,2,1,0:T(4,128)(2,1)} %bitcast.23, bf16[64,3072]{1,0:T(8,128)(2,1)} %get-tuple-element.59.refs_0_.refs_5_), custom_call_target="tpu_custom_call" | custom-call | bytes 18874368 | tf_op jit(solution)/shard_map/split_experts/pallas_call | solution.py:186
  56.9 14.9 %forward_tokens.1 = (bf16[4,160,3072]{2,1,0:T(8,128)(2,1)}, bf16[4,160,768]{2,1,0:T(8,128)(2,1)}, f32[4,160,768]{2,1,0:T(8,128)}, f32[4,160,768]{2,1,0:T(8,128)}) custom-call(s32[4,1,512]{2,1,0:T(1,128)} %get-tuple-element.54.refs_1_.code_ref, f32[4,1,512]{2,1,0:T(1,128)} %get-tuple-element.55.gate_ref, ...), custom_call_target="tpu_custom_call" | custom-call | flops 5033164800 | bytes 18874368 | tf_op jit(solution)/shard_map/forward_tokens/pallas_call | solution.py:340
  72.9 27.1 %forward_cotangents.1 = (bf16[4,160,3072]{2,1,0:T(8,128)(2,1)}, bf16[4,160,768]{2,1,0:T(8,128)(2,1)}, f32[256,3200]{1,0:T(8,128)}, bf16[256,3200]{1,0:T(8,128)(2,1)}) custom-call(s32[4,1,512]{2,1,0:T(1,128)} %get-tuple-element.54.refs_1_.code_ref, f32[4,160,768]{2,1,0:T(8,128)} %get-tuple-element.62.active_ref, f32[4,160,768]{2,1,0:T(8,128)} %get-tuple-element.63.slope_ref, ...), custom_call_target="tpu_custom_call" | custom-call | flops 10066329600 | bytes 37748736 | tf_op jit(solution)/shard_map/forward_cotangents/pallas_call | solution.py:429
  100.6 3.3 %collective-permute-done.13.refs_1_ = bf16[256,3200]{1,0:T(8,128)(2,1)S(1)} collective-permute-done((bf16[256,3200]{1,0:T(8,128)(2,1)}, bf16[256,3200]{1,0:T(8,128)(2,1)S(1)}, u32[]{:S(2)}, u32[]{:S(2)}) %collective-permute-start.13) | collective-permute-done | bytes 1638432 | tf_op jit(solution)/shard_map/ppermute | solution.py:28
  103.9 1.9 %copy-done.4 = f32[256,3200]{1,0:T(8,128)S(1)} copy-done((f32[256,3200]{1,0:T(8,128)S(1)}, f32[256,3200]{1,0:T(8,128)}, u32[]{:S(2)}) %copy-start.4) | copy-done | bytes 3276824
  106.6 1.5 collective-permute-start.14
  108.1 1.5 collective-permute-start.15
  110.2 2.1 %copy-done = bf16[4,160,3072]{2,1,0:T(8,128)(2,1)S(1)} copy-done((bf16[4,160,3072]{2,1,0:T(8,128)(2,1)S(1)}, bf16[4,160,3072]{2,1,0:T(8,128)(2,1)}, u32[]{:S(2)}) %copy-start) | copy-done | bytes 3932184
  113.5 5.2 %weight_gradient.7 = (bf16[3072,6,4,128]{3,2,1,0:T(4,128)(2,1)}, f32[8,128]{1,0:T(8,128)S(1)}) custom-call(bf16[4,160,3072]{2,1,0:T(8,128)(2,1)S(1)} %copy-done, bf16[4,160,768]{2,1,0:T(8,128)(2,1)S(1)} %copy-done.2, f32[64,3200]{1,0:T(8,128)S(1)} %get-tuple-element.68.refs_0_), custom_call_target="tpu_custom_call" | custom-call | flops 754974720 | bytes 9437184 | tf_op jit(solution)/shard_map/weight_gradient/pallas_call | solution.py:498
  118.7 5.2 %weight_gradient.8 = (bf16[3072,6,4,128]{3,2,1,0:T(4,128)(2,1)}, f32[8,128]{1,0:T(8,128)S(1)}) custom-call(bf16[4,160,3072]{2,1,0:T(8,128)(2,1)S(1)} %copy-done, bf16[4,160,768]{2,1,0:T(8,128)(2,1)S(1)} %copy-done.2, bf16[3072,6,4,128]{3,2,1,0:T(4,128)(2,1)} %get-tuple-element.74.refs_0_, ...), custom_call_target="tpu_custom_call", output_to_operand_aliasing={{0}: (2, {})} | custom-call | flops 754974720 | bytes 9437184 | tf_op jit(solution)/shard_map/weight_gradient/pallas_call | solution.py:498
  123.9 5.2 %weight_gradient.9 = (bf16[3072,6,4,128]{3,2,1,0:T(4,128)(2,1)}, f32[8,128]{1,0:T(8,128)S(1)}) custom-call(bf16[4,160,3072]{2,1,0:T(8,128)(2,1)S(1)} %copy-done, bf16[4,160,768]{2,1,0:T(8,128)(2,1)S(1)} %copy-done.2, bf16[3072,6,4,128]{3,2,1,0:T(4,128)(2,1)} %get-tuple-element.76.refs_0_, ...), custom_call_target="tpu_custom_call", output_to_operand_aliasing={{0}: (2, {})} | custom-call | flops 754974720 | bytes 9437184 | tf_op jit(solution)/shard_map/weight_gradient/pallas_call | solution.py:498
  129.1 5.2 %weight_gradient.10 = (bf16[3072,6,4,128]{3,2,1,0:T(4,128)(2,1)}, f32[8,128]{1,0:T(8,128)S(1)}) custom-call(bf16[4,160,3072]{2,1,0:T(8,128)(2,1)S(1)} %copy-done, bf16[4,160,768]{2,1,0:T(8,128)(2,1)S(1)} %copy-done.2, bf16[3072,6,4,128]{3,2,1,0:T(4,128)(2,1)} %get-tuple-element.78.refs_0_, ...), custom_call_target="tpu_custom_call", output_to_operand_aliasing={{0}: (2, {})} | custom-call | flops 754974720 | bytes 9437184 | tf_op jit(solution)/shard_map/weight_gradient/pallas_call | solution.py:498
  135.0 1.6 collective-permute-start.17
  136.6 2.6 %collective-permute-start.18 = (bf16[16,3200]{1,0:T(8,128)(2,1)S(1)}, bf16[16,3200]{1,0:T(8,128)(2,1)S(1)}, u32[]{:S(2)}, u32[]{:S(2)}) collective-permute-start(bf16[16,3200]{1,0:T(8,128)(2,1)S(1)} %get-tuple-element.83), channel_id=1, source_target_pairs={{0,16},{1,17},{2,18},{3,19},{4,20},{5,21},{6,22},{7,23},{8,24},{9,... | collective-permute-start | bytes 307208 | tf_op jit(solution)/shard_map/ppermute | solution.py:28
  139.5 6.7 %weight_gradient.11 = (bf16[768,24,4,128]{3,2,1,0:T(4,128)(2,1)}, f32[8,128]{1,0:T(8,128)S(1)}) custom-call(bf16[4,160,768]{2,1,0:T(8,128)(2,1)S(1)} %copy-done.3, bf16[4,160,3072]{2,1,0:T(8,128)(2,1)S(1)} %copy-done.1, f32[16,3200]{1,0:T(8,128)S(1)} %get-tuple-element.81.refs_0_), custom_call_target="tpu_custom_call" | custom-call | flops 1006632960 | bytes 12582912 | tf_op jit(solution)/shard_map/weight_gradient/pallas_call | solution.py:498
  147.7 2.8 %collective-permute-start.22 = (bf16[16,3200]{1,0:T(8,128)(2,1)S(1)}, bf16[16,3200]{1,0:T(8,128)(2,1)S(1)}, u32[]{:S(2)}, u32[]{:S(2)}) collective-permute-start(bf16[16,3200]{1,0:T(8,128)(2,1)S(1)} %third_sum.1.refs_1_.refs_0_), channel_id=1, source_target_pairs={{0,24},{1,25},{2,26},{3,27},{4,28},{5,29},{6,30},{7,31},{8,16},{9,... | collective-permute-start | bytes 307208 | tf_op jit(solution)/shard_map/ppermute | solution.py:28
  152.1 6.7 %weight_gradient.12 = (bf16[768,24,4,128]{3,2,1,0:T(4,128)(2,1)}, f32[8,128]{1,0:T(8,128)S(1)}) custom-call(bf16[4,160,768]{2,1,0:T(8,128)(2,1)S(1)} %copy-done.3, bf16[4,160,3072]{2,1,0:T(8,128)(2,1)S(1)} %copy-done.1, bf16[768,24,4,128]{3,2,1,0:T(4,128)(2,1)} %get-tuple-element.88.refs_0_, ...), custom_call_target="tpu_custom_call", output_to_operand_aliasing={{0}: (2, {})} | custom-call | flops 1006632960 | bytes 12582912 | tf_op jit(solution)/shard_map/weight_gradient/pallas_call | solution.py:498
  160.8 6.7 %weight_gradient.13 = (bf16[768,24,4,128]{3,2,1,0:T(4,128)(2,1)}, f32[8,128]{1,0:T(8,128)S(1)}) custom-call(bf16[4,160,768]{2,1,0:T(8,128)(2,1)S(1)} %copy-done.3, bf16[4,160,3072]{2,1,0:T(8,128)(2,1)S(1)} %copy-done.1, bf16[768,24,4,128]{3,2,1,0:T(4,128)(2,1)} %get-tuple-element.90.refs_0_, ...), custom_call_target="tpu_custom_call", output_to_operand_aliasing={{0}: (2, {})} | custom-call | flops 1006632960 | bytes 12582912 | tf_op jit(solution)/shard_map/weight_gradient/pallas_call | solution.py:498
  167.5 2.0 %collective-permute-done.23.refs_1_ = bf16[64,3200]{1,0:T(8,128)(2,1)S(1)} collective-permute-done((bf16[64,3200]{1,0:T(8,128)(2,1)S(1)}, bf16[64,3200]{1,0:T(8,128)(2,1)S(1)}, u32[]{:S(2)}, u32[]{:S(2)}) %collective-permute-start.23) | collective-permute-done | bytes 409632 | tf_op jit(solution)/shard_map/ppermute | solution.py:28
  (92 shorter events, 22.1 us)
Async XLA Ops:
  1.8 27.5 %collective-permute-start = (bf16[64,3072]{1,0:T(8,128)(2,1)S(1)}, bf16[64,3072]{1,0:T(8,128)(2,1)S(1)}, u32[]{:S(2)}, u32[]{:S(2)}) collective-permute-start(bf16[64,3072]{1,0:T(8,128)(2,1)S(1)} %constant_dynamic-slice_fusion.1), channel_id=1, source_target_pairs={{0,2},{1,3},{2,0},{3,1},{4,6},{5,7},{6,4},{7,5},{8,10},{9,11},{10,... | collective-permute-start | bytes 1179656 | tf_op jit(solution)/shard_map/ppermute | solution.py:28
  6.3 22.9 %collective-permute-start.3 = (f32[8,128]{1,0:T(8,128)S(1)}, f32[8,128]{1,0:T(8,128)S(1)}, u32[]{:S(2)}, u32[]{:S(2)}) collective-permute-start(f32[8,128]{1,0:T(8,128)S(1)} %maximum_select_fusion), channel_id=1, source_target_pairs={{0,3},{1,2},{2,1},{3,0},{4,7},{5,6},{6,5},{7,4},{8,11},{9,10},{10,... | collective-permute-start | bytes 12296 | tf_op jit(solution)/shard_map/ppermute | solution.py:28
  6.3 22.9 %collective-permute-start.2 = (f32[8,128]{1,0:T(8,128)S(1)}, f32[8,128]{1,0:T(8,128)S(1)}, u32[]{:S(2)}, u32[]{:S(2)}) collective-permute-start(f32[8,128]{1,0:T(8,128)S(1)} %maximum_select_fusion), channel_id=1, source_target_pairs={{0,2},{1,3},{2,0},{3,1},{4,6},{5,7},{6,4},{7,5},{8,10},{9,11},{10,... | collective-permute-start | bytes 12296 | tf_op jit(solution)/shard_map/ppermute | solution.py:28
  7.5 21.7 %collective-permute-start.1 = (f32[8,128]{1,0:T(8,128)S(1)}, f32[8,128]{1,0:T(8,128)S(1)}, u32[]{:S(2)}, u32[]{:S(2)}) collective-permute-start(f32[8,128]{1,0:T(8,128)S(1)} %maximum_bitcast_fusion.refs_0_), channel_id=1, source_target_pairs={{0,1},{1,0},{2,3},{3,2},{4,5},{5,4},{6,7},{7,6},{8,9},{9,8},{10,11... | collective-permute-start | bytes 12296 | tf_op jit(solution)/shard_map/ppermute | solution.py:28
  9.2 34.3 %collective-permute-start.6 = (bf16[64,3072]{1,0:T(8,128)(2,1)S(1)}, bf16[64,3072]{1,0:T(8,128)(2,1)S(1)}, u32[]{:S(2)}, u32[]{:S(2)}) collective-permute-start(bf16[64,3072]{1,0:T(8,128)(2,1)S(1)} %constant_dynamic-slice_fusion), channel_id=1, source_target_pairs={{0,2},{1,3},{2,0},{3,1},{4,6},{5,7},{6,4},{7,5},{8,10},{9,11},{10,... | collective-permute-start | bytes 1179656 | tf_op jit(solution)/shard_map/ppermute | solution.py:28
  30.0 13.5 %collective-permute-start.5 = (bf16[64,3072]{1,0:T(8,128)(2,1)}, bf16[64,3072]{1,0:T(8,128)(2,1)S(1)}, u32[]{:S(2)}, u32[]{:S(2)}) collective-permute-start(bf16[64,3072]{1,0:T(8,128)(2,1)} %get-tuple-element.57.refs_0_.refs_4_), channel_id=1, source_target_pairs={{0,4},{1,5},{2,6},{3,7},{4,0},{5,1},{6,2},{7,3},{8,12},{9,13},{10,... | collective-permute-start | bytes 1179656 | tf_op jit(solution)/shard_map/ppermute | solution.py:28
  31.7 25.2 %collective-permute-start.4 = (bf16[128,3072]{1,0:T(8,128)(2,1)S(1)}, bf16[128,3072]{1,0:T(8,128)(2,1)}, u32[]{:S(2)}, u32[]{:S(2)}) collective-permute-start(bf16[128,3072]{1,0:T(8,128)(2,1)S(1)} %copy-done.10), channel_id=1, source_target_pairs={{0,1},{1,0},{2,3},{3,2},{4,5},{5,4},{6,7},{7,6},{8,9},{9,8},{10,11... | collective-permute-start | bytes 2359304 | tf_op jit(solution)/shard_map/ppermute | solution.py:28
  44.4 11.7 %collective-permute-start.9 = (bf16[64,3072]{1,0:T(8,128)(2,1)}, bf16[64,3072]{1,0:T(8,128)(2,1)S(1)}, u32[]{:S(2)}, u32[]{:S(2)}) collective-permute-start(bf16[64,3072]{1,0:T(8,128)(2,1)} %get-tuple-element.60.refs_6_), channel_id=1, source_target_pairs={{0,4},{1,5},{2,6},{3,7},{4,0},{5,1},{6,2},{7,3},{8,12},{9,13},{10,... | collective-permute-start | bytes 1179656 | tf_op jit(solution)/shard_map/ppermute | solution.py:28
  44.8 12.2 %collective-permute-start.7 = (bf16[64,3072]{1,0:T(8,128)(2,1)S(1)}, bf16[64,3072]{1,0:T(8,128)(2,1)}, u32[]{:S(2)}, u32[]{:S(2)}) collective-permute-start(bf16[64,3072]{1,0:T(8,128)(2,1)S(1)} %copy-done.7), channel_id=1, source_target_pairs={{0,1},{1,0},{2,3},{3,2},{4,5},{5,4},{6,7},{7,6},{8,9},{9,8},{10,11... | collective-permute-start | bytes 1179656 | tf_op jit(solution)/shard_map/ppermute | solution.py:28
  45.0 11.9 %collective-permute-start.8 = (bf16[64,3072]{1,0:T(8,128)(2,1)}, bf16[64,3072]{1,0:T(8,128)(2,1)}, u32[]{:S(2)}, u32[]{:S(2)}) collective-permute-start(bf16[64,3072]{1,0:T(8,128)(2,1)} %get-tuple-element.59.refs_0_.refs_5_), channel_id=1, source_target_pairs={{0,1},{1,0},{2,3},{3,2},{4,5},{5,4},{6,7},{7,6},{8,9},{9,8},{10,11... | collective-permute-start | bytes 1179656 | tf_op jit(solution)/shard_map/ppermute | solution.py:28
  45.3 26.6 %collective-permute-start.10 = (bf16[128,3072]{1,0:T(8,128)(2,1)S(1)}, bf16[128,3072]{1,0:T(8,128)(2,1)S(1)}, u32[]{:S(2)}, u32[]{:S(2)}) collective-permute-start(bf16[128,3072]{1,0:T(8,128)(2,1)S(1)} %copy-done.9), channel_id=1, source_target_pairs={{0,1},{1,0},{2,3},{3,2},{4,5},{5,4},{6,7},{7,6},{8,9},{9,8},{10,11... | collective-permute-start | bytes 2359304 | tf_op jit(solution)/shard_map/ppermute | solution.py:28
  56.2 15.7 %collective-permute-start.11 = (bf16[64,3072]{1,0:T(8,128)(2,1)S(1)}, bf16[64,3072]{1,0:T(8,128)(2,1)}, u32[]{:S(2)}, u32[]{:S(2)}) collective-permute-start(bf16[64,3072]{1,0:T(8,128)(2,1)S(1)} %copy-done.12), channel_id=1, source_target_pairs={{0,1},{1,0},{2,3},{3,2},{4,5},{5,4},{6,7},{7,6},{8,9},{9,8},{10,11... | collective-permute-start | bytes 1179656 | tf_op jit(solution)/shard_map/ppermute | solution.py:28
  56.9 14.9 %collective-permute-start.12 = (bf16[64,3072]{1,0:T(8,128)(2,1)}, bf16[64,3072]{1,0:T(8,128)(2,1)S(1)}, u32[]{:S(2)}, u32[]{:S(2)}) collective-permute-start(bf16[64,3072]{1,0:T(8,128)(2,1)} %hold.5.refs_8_.refs_7_), channel_id=1, source_target_pairs={{0,1},{1,0},{2,3},{3,2},{4,5},{5,4},{6,7},{7,6},{8,9},{9,8},{10,11... | collective-permute-start | bytes 1179656 | tf_op jit(solution)/shard_map/ppermute | solution.py:28
  100.0 3.9 %collective-permute-start.13 = (bf16[256,3200]{1,0:T(8,128)(2,1)}, bf16[256,3200]{1,0:T(8,128)(2,1)S(1)}, u32[]{:S(2)}, u32[]{:S(2)}) collective-permute-start(bf16[256,3200]{1,0:T(8,128)(2,1)} %get-tuple-element.67), channel_id=1, source_target_pairs={{0,1},{1,0},{2,3},{3,2},{4,5},{5,4},{6,7},{7,6},{8,9},{9,8},{10,11... | collective-permute-start | bytes 4915208 | tf_op jit(solution)/shard_map/ppermute | solution.py:28
  106.6 27.6 %collective-permute-start.14 = (bf16[64,3200]{1,0:T(8,128)(2,1)S(1)}, bf16[64,3200]{1,0:T(8,128)(2,1)S(1)}, u32[]{:S(2)}, u32[]{:S(2)}) collective-permute-start(bf16[64,3200]{1,0:T(8,128)(2,1)S(1)} %get-tuple-element.69), channel_id=1, source_target_pairs={{0,4},{1,5},{2,6},{3,7},{4,0},{5,1},{6,2},{7,3},{8,12},{9,13},{10,... | collective-permute-start | bytes 1228808 | tf_op jit(solution)/shard_map/ppermute | solution.py:28
  108.1 26.1 %collective-permute-start.15 = (bf16[64,3200]{1,0:T(8,128)(2,1)S(1)}, bf16[64,3200]{1,0:T(8,128)(2,1)S(1)}, u32[]{:S(2)}, u32[]{:S(2)}) collective-permute-start(bf16[64,3200]{1,0:T(8,128)(2,1)S(1)} %get-tuple-element.70), channel_id=1, source_target_pairs={{0,2},{1,3},{2,0},{3,1},{4,6},{5,7},{6,4},{7,5},{8,10},{9,11},{10,... | collective-permute-start | bytes 1228808 | tf_op jit(solution)/shard_map/ppermute | solution.py:28
  109.7 24.6 %collective-permute-start.16 = (bf16[64,3200]{1,0:T(8,128)(2,1)S(1)}, bf16[64,3200]{1,0:T(8,128)(2,1)S(1)}, u32[]{:S(2)}, u32[]{:S(2)}) collective-permute-start(bf16[64,3200]{1,0:T(8,128)(2,1)S(1)} %get-tuple-element.71), channel_id=1, source_target_pairs={{0,6},{1,7},{2,4},{3,5},{4,2},{5,3},{6,0},{7,1},{8,14},{9,15},{10,... | collective-permute-start | bytes 1228808 | tf_op jit(solution)/shard_map/ppermute | solution.py:28
  135.0 11.2 %collective-permute-start.17 = (bf16[16,3200]{1,0:T(8,128)(2,1)S(1)}, bf16[16,3200]{1,0:T(8,128)(2,1)S(1)}, u32[]{:S(2)}, u32[]{:S(2)}) collective-permute-start(bf16[16,3200]{1,0:T(8,128)(2,1)S(1)} %get-tuple-element.82), channel_id=1, source_target_pairs={{0,8},{1,9},{2,10},{3,11},{4,12},{5,13},{6,14},{7,15},{8,0},{9,1},... | collective-permute-start | bytes 307208 | tf_op jit(solution)/shard_map/ppermute | solution.py:28
  136.6 10.4 %collective-permute-start.18 = (bf16[16,3200]{1,0:T(8,128)(2,1)S(1)}, bf16[16,3200]{1,0:T(8,128)(2,1)S(1)}, u32[]{:S(2)}, u32[]{:S(2)}) collective-permute-start(bf16[16,3200]{1,0:T(8,128)(2,1)S(1)} %get-tuple-element.83), channel_id=1, source_target_pairs={{0,16},{1,17},{2,18},{3,19},{4,20},{5,21},{6,22},{7,23},{8,24},{9,... | collective-permute-start | bytes 307208 | tf_op jit(solution)/shard_map/ppermute | solution.py:28
  139.2 7.8 %collective-permute-start.19 = (bf16[16,3200]{1,0:T(8,128)(2,1)S(1)}, bf16[16,3200]{1,0:T(8,128)(2,1)S(1)}, u32[]{:S(2)}, u32[]{:S(2)}) collective-permute-start(bf16[16,3200]{1,0:T(8,128)(2,1)S(1)} %get-tuple-element.84), channel_id=1, source_target_pairs={{0,24},{1,25},{2,26},{3,27},{4,28},{5,29},{6,30},{7,31},{8,16},{9,... | collective-permute-start | bytes 307208 | tf_op jit(solution)/shard_map/ppermute | solution.py:28
  147.7 11.1 %collective-permute-start.22 = (bf16[16,3200]{1,0:T(8,128)(2,1)S(1)}, bf16[16,3200]{1,0:T(8,128)(2,1)S(1)}, u32[]{:S(2)}, u32[]{:S(2)}) collective-permute-start(bf16[16,3200]{1,0:T(8,128)(2,1)S(1)} %third_sum.1.refs_1_.refs_0_), channel_id=1, source_target_pairs={{0,24},{1,25},{2,26},{3,27},{4,28},{5,29},{6,30},{7,31},{8,16},{9,... | collective-permute-start | bytes 307208 | tf_op jit(solution)/shard_map/ppermute | solution.py:28
  150.4 8.4 %collective-permute-start.21 = (bf16[16,3200]{1,0:T(8,128)(2,1)S(1)}, bf16[16,3200]{1,0:T(8,128)(2,1)S(1)}, u32[]{:S(2)}, u32[]{:S(2)}) collective-permute-start(bf16[16,3200]{1,0:T(8,128)(2,1)S(1)} %third_sum.1.refs_1_.refs_0_), channel_id=1, source_target_pairs={{0,16},{1,17},{2,18},{3,19},{4,20},{5,21},{6,22},{7,23},{8,24},{9,... | collective-permute-start | bytes 307208 | tf_op jit(solution)/shard_map/ppermute | solution.py:28
  150.8 8.0 %collective-permute-start.20 = (bf16[16,3200]{1,0:T(8,128)(2,1)S(1)}, bf16[16,3200]{1,0:T(8,128)(2,1)S(1)}, u32[]{:S(2)}, u32[]{:S(2)}) collective-permute-start(bf16[16,3200]{1,0:T(8,128)(2,1)S(1)} %third_sum.1.refs_1_.refs_0_), channel_id=1, source_target_pairs={{0,8},{1,9},{2,10},{3,11},{4,12},{5,13},{6,14},{7,15},{8,0},{9,1},... | collective-permute-start | bytes 307208 | tf_op jit(solution)/shard_map/ppermute | solution.py:28
  159.4 10.1 %collective-permute-start.23 = (bf16[64,3200]{1,0:T(8,128)(2,1)S(1)}, bf16[64,3200]{1,0:T(8,128)(2,1)S(1)}, u32[]{:S(2)}, u32[]{:S(2)}) collective-permute-start(bf16[64,3200]{1,0:T(8,128)(2,1)S(1)} %join_z.1.refs_1_.refs_0_), channel_id=1, source_target_pairs={{0,4},{1,5},{2,6},{3,7},{4,0},{5,1},{6,2},{7,3},{8,12},{9,13},{10,... | collective-permute-start | bytes 1228808 | tf_op jit(solution)/shard_map/ppermute | solution.py:28
  (19 other events, 151.7 us)

commit v8 on v7

--- a/solution.py
+++ b/solution.py
@@ -144,14 +144,21 @@
     return weight.reshape(rows, experts, columns // LANES, LANES).transpose(0, 2, 1, 3)
 
 
+def odd_tiles(rows):
+    tiles = -(-rows // 8)
+    return 8 * (tiles + 1 - tiles % 2)
+
+
 def split_body(group, some, sort_ref, w_ref, *refs):
-    out_ref, flag_ref = refs[-2:]
+    out_ref, flag_ref, wide_ref = refs[-3:]
     flag_ref[...] = jnp.zeros_like(flag_ref)
     rows, tiles, experts, _ = w_ref.shape
     held = group * experts
     flat = w_ref.reshape(rows, tiles * experts, LANES)
-    places = [(row, tile) for row in range(0, rows, some) for tile in range(0, tiles, group)]
-    for pair in zip(places[::2], places[1::2]):
+    stride = wide_ref.shape[1]
+    wide = wide_ref.reshape(wide_ref.shape[0] * stride, LANES)
+
+    def matmul(pair):
         blocks = [
             flat[row : row + some, tile * experts : tile * experts + held, :].reshape(
                 some * held, LANES
@@ -178,6 +185,23 @@
                             NARROW
                         )
 
+    for row in range(0, rows, 32):
+        other, base = row + 16, row // 2
+        wide_ref[base : base + 16, : tiles * experts, :] = flat[other : other + 16].astype(WIDE)
+        places = [
+            (first, tile) for first in range(row, other, some) for tile in range(0, tiles, group)
+        ]
+        pairs = list(zip(places[::2], places[1::2]))
+        combos = [(expert, tile) for expert in range(experts) for tile in range(tiles)]
+        share = len(combos) // len(pairs)
+        for number, pair in enumerate(pairs):
+            matmul(pair)
+            for expert, tile in combos[number * share : (number + 1) * share]:
+                part = wide[pl.ds(base * stride + tile * experts + expert, 16, stride), :]
+                out_ref[expert, other : other + 16, tile * LANES : (tile + 1) * LANES] = (
+                    part.astype(NARROW)
+                )
+
 
 def split_experts(view, sort, start, rows, block, group, some, after):
     _, tiles, experts, _ = view.shape
@@ -196,6 +220,7 @@
             pl.BlockSpec((experts, block, columns), lambda i: (0, i, 0)),
             pl.BlockSpec(FLAG.shape, lambda i: (0, 0)),
         ],
+        scratch_shapes=[pltpu.VMEM((block // 2, odd_tiles(tiles * experts), LANES), WIDE)],
         compiler_params=pltpu.CompilerParams(vmem_limit_bytes=56 * MIB),
         cost_estimate=pl.CostEstimate(
             flops=0, bytes_accessed=4 * experts * rows * columns, transcendentals=0
@@ -456,7 +481,7 @@
             pltpu.VMEM((experts * slots, width), WIDE),
             pltpu.SemaphoreType.DMA((len(g_pieces),)),
         ],
-        compiler_params=pltpu.CompilerParams(vmem_limit_bytes=56 * MIB),
+        compiler_params=pltpu.CompilerParams(vmem_limit_bytes=48 * MIB),
         cost_estimate=pl.CostEstimate(
             flops=2 * slots * experts * model_width * (2 * hidden + 2 * tokens),
             bytes_accessed=4 * experts * model_width * hidden,
@@ -464,11 +489,6 @@
         ),
         name="forward_cotangents",
     )(code, active, slope, *w_operands, *v_operands, *g_pieces)
-
-
-def odd_tiles(rows):
-    tiles = -(-rows // 8)
-    return 8 * (tiles + 1 - tiles % 2)
 
 
 def outer_body(group, a_ref, b_ref, *refs):

time: 172 us -> 171 us (level)
  Pallas kernels: 129 us -> 127 us
    pallas_call x1, Pallas kernels: 27.1 us -> 23.9 us  [forward_cotangents(): pl.pallas_call(forward_cotangents_body, out_shape=[jax.ShapeDtypeStruct((...]
    pallas_call x3, Pallas kernels: 40.2 us -> 42 us  [split_experts(): pl.pallas_call(functools.partial(split_body, group, some), out_shape=[jax...]
  transfers between devices with their start and end apart: 24 -> 24, of which waited for: 4 -> 3; matrix products, arithmetic and copies ran while one was open for 2% -> 2% of each run, Pallas kernels for 57% -> 58%
where the time goes in v8:
time: 171 us; the launch traced here: 170 us
  Pallas kernels  127 us (74%)
  starting transfers between devices  23 us (13%)
  local copies, waits for them, and re-layouts  10.6 us (6%)
  waiting for transfers between devices  6.5 us (4%)
    pallas_call x3, Pallas kernels, split_experts(): pl.pallas_call(functools.partial(split_body, group, some), out_shape=[jax...  42 us
    pallas_call x7, Pallas kernels, outer(): pl.pallas_call(functools.partial(outer_body, group), out_shape=[jax.Shape...  40.8 us
    pallas_call x1, Pallas kernels, forward_cotangents(): pl.pallas_call(forward_cotangents_body, out_shape=[jax.ShapeDtypeStruct((...  23.9 us
    ppermute x24, starting transfers between devices, swap(): return lax.ppermute(value, AXES, [(i, i ^ mask) for i in range(size)])  23 us
    pallas_call x1, Pallas kernels, forward_tokens(): pl.pallas_call(forward_tokens_body, out_shape=[jax.ShapeDtypeStruct((expe...  15 us
    unnamed x39, local copies, waits for them, and re-layouts  8.52 us
    ppermute x24, waiting for transfers between devices, swap(): return lax.ppermute(value, AXES, [(i, i ^ mask) for i in range(size)])  6.5 us
    pallas_call x5, Pallas kernels, small_call(): pl.pallas_call(run, out_shape=outs, grid=(steps,), in_specs=[pl.BlockSpec...  4.21 us
  transfers between devices with their start and end apart: 24, of which 3 were waited for; matrix products, arithmetic and copies ran while one was open for 2% of the time, Pallas kernels for 58%

profile of v8, /device:TPU:0, one launch (start us, length us, event | category | flops | bytes accessed | tf_op | source)
XLA Modules:
  0.0 169.9 jit_solution(3361464475746352836)
XLA Ops:
  1.7 3.0 %collective-permute-start = (bf16[64,3072]{1,0:T(8,128)(2,1)S(1)}, bf16[64,3072]{1,0:T(8,128)(2,1)S(1)}, u32[]{:S(2)}, u32[]{:S(2)}) collective-permute-start(bf16[64,3072]{1,0:T(8,128)(2,1)S(1)} %constant_dynamic-slice_fusion.1), channel_id=1, source_target_pairs={{0,2},{1,3},{2,0},{3,1},{4,6},{5,7},{6,4},{7,5},{8,10},{9,11},{10,... | collective-permute-start | bytes 1179656 | tf_op jit(solution)/shard_map/ppermute | solution.py:28
  9.5 20.6 %split_experts.3 = (bf16[4,3072,768]{2,1,0:T(8,128)(2,1)}, f32[8,128]{1,0:T(8,128)}) custom-call(bf16[192,192]{1,0:T(8,128)(2,1)} %constant.46.clone.sort_ref, bf16[3072,6,4,128]{3,2,1,0:T(4,128)(2,1)} %bitcast.25), custom_call_target="tpu_custom_call" | custom-call | bytes 37748736 | tf_op jit(solution)/shard_map/split_experts/pallas_call | solution.py:210
  30.9 1.7 %collective-permute-start.5 = (bf16[64,3072]{1,0:T(8,128)(2,1)}, bf16[64,3072]{1,0:T(8,128)(2,1)S(1)}, u32[]{:S(2)}, u32[]{:S(2)}) collective-permute-start(bf16[64,3072]{1,0:T(8,128)(2,1)} %get-tuple-element.57.refs_0_.refs_4_), channel_id=1, source_target_pairs={{0,4},{1,5},{2,6},{3,7},{4,0},{5,1},{6,2},{7,3},{8,12},{9,13},{10,... | collective-permute-start | bytes 1179656 | tf_op jit(solution)/shard_map/ppermute | solution.py:28
  34.1 10.7 %split_experts.4 = (bf16[4,384,3072]{2,1,0:T(8,128)(2,1)}, f32[8,128]{1,0:T(8,128)}) custom-call(bf16[256,256]{1,0:T(8,128)(2,1)} %constant.47.clone.sort_ref, bf16[768,24,4,128]{3,2,1,0:T(4,128)(2,1)} %bitcast.22, bf16[64,3072]{1,0:T(8,128)(2,1)} %get-tuple-element.57.refs_0_.refs_4_, s32[4,1,512]{2,1,0:T(1,128)} %get-tuple-element.54.refs_1_.code_ref), custom_call_target="tpu_custom_call" | custom-call | bytes 18874368 | tf_op jit(solution)/shard_map/split_experts/pallas_call | solution.py:210
  46.8 10.7 %split_experts.5 = (bf16[4,384,3072]{2,1,0:T(8,128)(2,1)}, f32[8,128]{1,0:T(8,128)}) custom-call(bf16[256,256]{1,0:T(8,128)(2,1)} %constant.47.clone.sort_ref, bf16[768,24,4,128]{3,2,1,0:T(4,128)(2,1)} %bitcast.23, bf16[64,3072]{1,0:T(8,128)(2,1)} %get-tuple-element.59.refs_0_.refs_5_), custom_call_target="tpu_custom_call" | custom-call | bytes 18874368 | tf_op jit(solution)/shard_map/split_experts/pallas_call | solution.py:210
  58.5 15.0 %forward_tokens.1 = (bf16[4,160,3072]{2,1,0:T(8,128)(2,1)}, bf16[4,160,768]{2,1,0:T(8,128)(2,1)}, f32[4,160,768]{2,1,0:T(8,128)}, f32[4,160,768]{2,1,0:T(8,128)}) custom-call(s32[4,1,512]{2,1,0:T(1,128)} %get-tuple-element.54.refs_1_.code_ref, f32[4,1,512]{2,1,0:T(1,128)} %get-tuple-element.55.gate_ref, ...), custom_call_target="tpu_custom_call" | custom-call | flops 5033164800 | bytes 18874368 | tf_op jit(solution)/shard_map/forward_tokens/pallas_call | solution.py:365
  75.3 23.9 %forward_cotangents.1 = (bf16[4,160,3072]{2,1,0:T(8,128)(2,1)}, bf16[4,160,768]{2,1,0:T(8,128)(2,1)S(1)}, f32[256,3200]{1,0:T(8,128)}, bf16[256,3200]{1,0:T(8,128)(2,1)}) custom-call(s32[4,1,512]{2,1,0:T(1,128)S(1)} %copy-done.11, f32[4,160,768]{2,1,0:T(8,128)} %get-tuple-element.62.active_ref, f32[4,160,768]{2,1,0:T(8,128)} %get-tuple-element.63.slope_ref, ...), custom_call_target="tpu_custom_call" | custom-call | flops 10066329600 | bytes 37748736 | tf_op jit(solution)/shard_map/forward_cotangents/pallas_call | solution.py:454
  99.6 3.3 %collective-permute-done.13.refs_1_ = bf16[256,3200]{1,0:T(8,128)(2,1)S(1)} collective-permute-done((bf16[256,3200]{1,0:T(8,128)(2,1)}, bf16[256,3200]{1,0:T(8,128)(2,1)S(1)}, u32[]{:S(2)}, u32[]{:S(2)}) %collective-permute-start.13) | collective-permute-done | bytes 1638432 | tf_op jit(solution)/shard_map/ppermute | solution.py:28
  102.9 1.9 %copy-done.5 = f32[256,3200]{1,0:T(8,128)S(1)} copy-done((f32[256,3200]{1,0:T(8,128)S(1)}, f32[256,3200]{1,0:T(8,128)}, u32[]{:S(2)}) %copy-start.5) | copy-done | bytes 3276824
  105.7 1.8 %collective-permute-start.14 = (bf16[64,3200]{1,0:T(8,128)(2,1)S(1)}, bf16[64,3200]{1,0:T(8,128)(2,1)S(1)}, u32[]{:S(2)}, u32[]{:S(2)}) collective-permute-start(bf16[64,3200]{1,0:T(8,128)(2,1)S(1)} %get-tuple-element.69), channel_id=1, source_target_pairs={{0,4},{1,5},{2,6},{3,7},{4,0},{5,1},{6,2},{7,3},{8,12},{9,13},{10,... | collective-permute-start | bytes 1228808 | tf_op jit(solution)/shard_map/ppermute | solution.py:28
  107.5 1.5 collective-permute-start.15
  109.2 2.1 %copy-done = bf16[4,160,3072]{2,1,0:T(8,128)(2,1)S(1)} copy-done((bf16[4,160,3072]{2,1,0:T(8,128)(2,1)S(1)}, bf16[4,160,3072]{2,1,0:T(8,128)(2,1)}, u32[]{:S(2)}) %copy-start) | copy-done | bytes 3932184
  111.3 5.2 %weight_gradient.7 = (bf16[3072,6,4,128]{3,2,1,0:T(4,128)(2,1)}, f32[8,128]{1,0:T(8,128)S(1)}) custom-call(bf16[4,160,3072]{2,1,0:T(8,128)(2,1)S(1)} %copy-done, bf16[4,160,768]{2,1,0:T(8,128)(2,1)S(1)} %get-tuple-element.73.b_ref, f32[64,3200]{1,0:T(8,128)S(1)} %get-tuple-element.68.refs_0_), custom_call_target="tpu_custom_call" | custom-call | flops 754974720 | bytes 9437184 | tf_op jit(solution)/shard_map/weight_gradient/pallas_call | solution.py:518
  116.5 5.2 %weight_gradient.8 = (bf16[3072,6,4,128]{3,2,1,0:T(4,128)(2,1)}, f32[8,128]{1,0:T(8,128)S(1)}) custom-call(bf16[4,160,3072]{2,1,0:T(8,128)(2,1)S(1)} %copy-done, bf16[4,160,768]{2,1,0:T(8,128)(2,1)S(1)} %get-tuple-element.73.b_ref, bf16[3072,6,4,128]{3,2,1,0:T(4,128)(2,1)} %get-tuple-element.74.refs_0_, ...), custom_call_target="tpu_custom_call", output_to_operand_aliasing={{0}: (2, {})} | custom-call | flops 754974720 | bytes 9437184 | tf_op jit(solution)/shard_map/weight_gradient/pallas_call | solution.py:518
  121.7 5.2 %weight_gradient.9 = (bf16[3072,6,4,128]{3,2,1,0:T(4,128)(2,1)}, f32[8,128]{1,0:T(8,128)S(1)}) custom-call(bf16[4,160,3072]{2,1,0:T(8,128)(2,1)S(1)} %copy-done, bf16[4,160,768]{2,1,0:T(8,128)(2,1)S(1)} %get-tuple-element.73.b_ref, bf16[3072,6,4,128]{3,2,1,0:T(4,128)(2,1)} %get-tuple-element.76.refs_0_, ...), custom_call_target="tpu_custom_call", output_to_operand_aliasing={{0}: (2, {})} | custom-call | flops 754974720 | bytes 9437184 | tf_op jit(solution)/shard_map/weight_gradient/pallas_call | solution.py:518
  126.9 5.2 %weight_gradient.10 = (bf16[3072,6,4,128]{3,2,1,0:T(4,128)(2,1)}, f32[8,128]{1,0:T(8,128)S(1)}) custom-call(bf16[4,160,3072]{2,1,0:T(8,128)(2,1)S(1)} %copy-done, bf16[4,160,768]{2,1,0:T(8,128)(2,1)S(1)} %get-tuple-element.73.b_ref, bf16[3072,6,4,128]{3,2,1,0:T(4,128)(2,1)} %get-tuple-element.78.refs_0_, ...), custom_call_target="tpu_custom_call", output_to_operand_aliasing={{0}: (2, {})} | custom-call | flops 754974720 | bytes 9437184 | tf_op jit(solution)/shard_map/weight_gradient/pallas_call | solution.py:518
  132.9 1.9 %collective-permute-start.17 = (bf16[16,3200]{1,0:T(8,128)(2,1)S(1)}, bf16[16,3200]{1,0:T(8,128)(2,1)S(1)}, u32[]{:S(2)}, u32[]{:S(2)}) collective-permute-start(bf16[16,3200]{1,0:T(8,128)(2,1)S(1)} %get-tuple-element.82), channel_id=1, source_target_pairs={{0,8},{1,9},{2,10},{3,11},{4,12},{5,13},{6,14},{7,15},{8,0},{9,1},... | collective-permute-start | bytes 307208 | tf_op jit(solution)/shard_map/ppermute | solution.py:28
  134.7 2.6 %collective-permute-start.18 = (bf16[16,3200]{1,0:T(8,128)(2,1)S(1)}, bf16[16,3200]{1,0:T(8,128)(2,1)S(1)}, u32[]{:S(2)}, u32[]{:S(2)}) collective-permute-start(bf16[16,3200]{1,0:T(8,128)(2,1)S(1)} %get-tuple-element.83), channel_id=1, source_target_pairs={{0,16},{1,17},{2,18},{3,19},{4,20},{5,21},{6,22},{7,23},{8,24},{9,... | collective-permute-start | bytes 307208 | tf_op jit(solution)/shard_map/ppermute | solution.py:28
  137.3 6.7 %weight_gradient.11 = (bf16[768,24,4,128]{3,2,1,0:T(4,128)(2,1)}, f32[8,128]{1,0:T(8,128)S(1)}) custom-call(bf16[4,160,768]{2,1,0:T(8,128)(2,1)S(1)} %copy-done.2, bf16[4,160,3072]{2,1,0:T(8,128)(2,1)S(1)} %copy-done.1, f32[16,3200]{1,0:T(8,128)S(1)} %get-tuple-element.81.refs_0_), custom_call_target="tpu_custom_call" | custom-call | flops 1006632960 | bytes 12582912 | tf_op jit(solution)/shard_map/weight_gradient/pallas_call | solution.py:518
  145.6 2.9 %collective-permute-start.22 = (bf16[16,3200]{1,0:T(8,128)(2,1)S(1)}, bf16[16,3200]{1,0:T(8,128)(2,1)S(1)}, u32[]{:S(2)}, u32[]{:S(2)}) collective-permute-start(bf16[16,3200]{1,0:T(8,128)(2,1)S(1)} %third_sum.1.refs_1_.refs_0_), channel_id=1, source_target_pairs={{0,24},{1,25},{2,26},{3,27},{4,28},{5,29},{6,30},{7,31},{8,16},{9,... | collective-permute-start | bytes 307208 | tf_op jit(solution)/shard_map/ppermute | solution.py:28
  150.1 6.7 %weight_gradient.12 = (bf16[768,24,4,128]{3,2,1,0:T(4,128)(2,1)}, f32[8,128]{1,0:T(8,128)S(1)}) custom-call(bf16[4,160,768]{2,1,0:T(8,128)(2,1)S(1)} %copy-done.2, bf16[4,160,3072]{2,1,0:T(8,128)(2,1)S(1)} %copy-done.1, bf16[768,24,4,128]{3,2,1,0:T(4,128)(2,1)} %get-tuple-element.88.refs_0_, ...), custom_call_target="tpu_custom_call", output_to_operand_aliasing={{0}: (2, {})} | custom-call | flops 1006632960 | bytes 12582912 | tf_op jit(solution)/shard_map/weight_gradient/pallas_call | solution.py:518
  157.4 1.6 collective-permute-start.23
  158.9 6.7 %weight_gradient.13 = (bf16[768,24,4,128]{3,2,1,0:T(4,128)(2,1)}, f32[8,128]{1,0:T(8,128)S(1)}) custom-call(bf16[4,160,768]{2,1,0:T(8,128)(2,1)S(1)} %copy-done.2, bf16[4,160,3072]{2,1,0:T(8,128)(2,1)S(1)} %copy-done.1, bf16[768,24,4,128]{3,2,1,0:T(4,128)(2,1)} %get-tuple-element.90.refs_0_, ...), custom_call_target="tpu_custom_call", output_to_operand_aliasing={{0}: (2, {})} | custom-call | flops 1006632960 | bytes 12582912 | tf_op jit(solution)/shard_map/weight_gradient/pallas_call | solution.py:518
  165.6 2.1 %collective-permute-done.23.refs_1_ = bf16[64,3200]{1,0:T(8,128)(2,1)S(1)} collective-permute-done((bf16[64,3200]{1,0:T(8,128)(2,1)S(1)}, bf16[64,3200]{1,0:T(8,128)(2,1)S(1)}, u32[]{:S(2)}, u32[]{:S(2)}) %collective-permute-start.23) | collective-permute-done | bytes 409632 | tf_op jit(solution)/shard_map/ppermute | solution.py:28
  (92 shorter events, 20.8 us)
Async XLA Ops:
  1.7 28.4 %collective-permute-start = (bf16[64,3072]{1,0:T(8,128)(2,1)S(1)}, bf16[64,3072]{1,0:T(8,128)(2,1)S(1)}, u32[]{:S(2)}, u32[]{:S(2)}) collective-permute-start(bf16[64,3072]{1,0:T(8,128)(2,1)S(1)} %constant_dynamic-slice_fusion.1), channel_id=1, source_target_pairs={{0,2},{1,3},{2,0},{3,1},{4,6},{5,7},{6,4},{7,5},{8,10},{9,11},{10,... | collective-permute-start | bytes 1179656 | tf_op jit(solution)/shard_map/ppermute | solution.py:28
  6.2 23.8 %collective-permute-start.3 = (f32[8,128]{1,0:T(8,128)S(1)}, f32[8,128]{1,0:T(8,128)S(1)}, u32[]{:S(2)}, u32[]{:S(2)}) collective-permute-start(f32[8,128]{1,0:T(8,128)S(1)} %maximum_select_fusion), channel_id=1, source_target_pairs={{0,3},{1,2},{2,1},{3,0},{4,7},{5,6},{6,5},{7,4},{8,11},{9,10},{10,... | collective-permute-start | bytes 12296 | tf_op jit(solution)/shard_map/ppermute | solution.py:28
  6.3 23.8 %collective-permute-start.2 = (f32[8,128]{1,0:T(8,128)S(1)}, f32[8,128]{1,0:T(8,128)S(1)}, u32[]{:S(2)}, u32[]{:S(2)}) collective-permute-start(f32[8,128]{1,0:T(8,128)S(1)} %maximum_select_fusion), channel_id=1, source_target_pairs={{0,2},{1,3},{2,0},{3,1},{4,6},{5,7},{6,4},{7,5},{8,10},{9,11},{10,... | collective-permute-start | bytes 12296 | tf_op jit(solution)/shard_map/ppermute | solution.py:28
  7.4 22.7 %collective-permute-start.1 = (f32[8,128]{1,0:T(8,128)S(1)}, f32[8,128]{1,0:T(8,128)S(1)}, u32[]{:S(2)}, u32[]{:S(2)}) collective-permute-start(f32[8,128]{1,0:T(8,128)S(1)} %maximum_bitcast_fusion.refs_0_), channel_id=1, source_target_pairs={{0,1},{1,0},{2,3},{3,2},{4,5},{5,4},{6,7},{7,6},{8,9},{9,8},{10,11... | collective-permute-start | bytes 12296 | tf_op jit(solution)/shard_map/ppermute | solution.py:28
  9.1 35.7 %collective-permute-start.6 = (bf16[64,3072]{1,0:T(8,128)(2,1)S(1)}, bf16[64,3072]{1,0:T(8,128)(2,1)S(1)}, u32[]{:S(2)}, u32[]{:S(2)}) collective-permute-start(bf16[64,3072]{1,0:T(8,128)(2,1)S(1)} %constant_dynamic-slice_fusion), channel_id=1, source_target_pairs={{0,2},{1,3},{2,0},{3,1},{4,6},{5,7},{6,4},{7,5},{8,10},{9,11},{10,... | collective-permute-start | bytes 1179656 | tf_op jit(solution)/shard_map/ppermute | solution.py:28
  30.9 13.9 %collective-permute-start.5 = (bf16[64,3072]{1,0:T(8,128)(2,1)}, bf16[64,3072]{1,0:T(8,128)(2,1)S(1)}, u32[]{:S(2)}, u32[]{:S(2)}) collective-permute-start(bf16[64,3072]{1,0:T(8,128)(2,1)} %get-tuple-element.57.refs_0_.refs_4_), channel_id=1, source_target_pairs={{0,4},{1,5},{2,6},{3,7},{4,0},{5,1},{6,2},{7,3},{8,12},{9,13},{10,... | collective-permute-start | bytes 1179656 | tf_op jit(solution)/shard_map/ppermute | solution.py:28
  32.6 25.7 %collective-permute-start.4 = (bf16[128,3072]{1,0:T(8,128)(2,1)}, bf16[128,3072]{1,0:T(8,128)(2,1)}, u32[]{:S(2)}, u32[]{:S(2)}) collective-permute-start(bf16[128,3072]{1,0:T(8,128)(2,1)} %refs_2_.1), channel_id=1, source_target_pairs={{0,1},{1,0},{2,3},{3,2},{4,5},{5,4},{6,7},{7,6},{8,9},{9,8},{10,11... | collective-permute-start | bytes 2359304 | tf_op jit(solution)/shard_map/ppermute | solution.py:28
  45.7 11.8 %collective-permute-start.9 = (bf16[64,3072]{1,0:T(8,128)(2,1)}, bf16[64,3072]{1,0:T(8,128)(2,1)S(1)}, u32[]{:S(2)}, u32[]{:S(2)}) collective-permute-start(bf16[64,3072]{1,0:T(8,128)(2,1)} %get-tuple-element.60.refs_6_), channel_id=1, source_target_pairs={{0,4},{1,5},{2,6},{3,7},{4,0},{5,1},{6,2},{7,3},{8,12},{9,13},{10,... | collective-permute-start | bytes 1179656 | tf_op jit(solution)/shard_map/ppermute | solution.py:28
  46.0 12.5 %collective-permute-start.7 = (bf16[64,3072]{1,0:T(8,128)(2,1)S(1)}, bf16[64,3072]{1,0:T(8,128)(2,1)}, u32[]{:S(2)}, u32[]{:S(2)}) collective-permute-start(bf16[64,3072]{1,0:T(8,128)(2,1)S(1)} %copy-done.13), channel_id=1, source_target_pairs={{0,1},{1,0},{2,3},{3,2},{4,5},{5,4},{6,7},{7,6},{8,9},{9,8},{10,11... | collective-permute-start | bytes 1179656 | tf_op jit(solution)/shard_map/ppermute | solution.py:28
  46.3 12.2 %collective-permute-start.8 = (bf16[64,3072]{1,0:T(8,128)(2,1)}, bf16[64,3072]{1,0:T(8,128)(2,1)}, u32[]{:S(2)}, u32[]{:S(2)}) collective-permute-start(bf16[64,3072]{1,0:T(8,128)(2,1)} %get-tuple-element.59.refs_0_.refs_5_), channel_id=1, source_target_pairs={{0,1},{1,0},{2,3},{3,2},{4,5},{5,4},{6,7},{7,6},{8,9},{9,8},{10,11... | collective-permute-start | bytes 1179656 | tf_op jit(solution)/shard_map/ppermute | solution.py:28
  46.5 27.0 %collective-permute-start.10 = (bf16[128,3072]{1,0:T(8,128)(2,1)S(1)}, bf16[128,3072]{1,0:T(8,128)(2,1)S(1)}, u32[]{:S(2)}, u32[]{:S(2)}) collective-permute-start(bf16[128,3072]{1,0:T(8,128)(2,1)S(1)} %copy-done.6), channel_id=1, source_target_pairs={{0,1},{1,0},{2,3},{3,2},{4,5},{5,4},{6,7},{7,6},{8,9},{9,8},{10,11... | collective-permute-start | bytes 2359304 | tf_op jit(solution)/shard_map/ppermute | solution.py:28
  57.5 16.0 %collective-permute-start.11 = (bf16[64,3072]{1,0:T(8,128)(2,1)S(1)}, bf16[64,3072]{1,0:T(8,128)(2,1)S(1)}, u32[]{:S(2)}, u32[]{:S(2)}) collective-permute-start(bf16[64,3072]{1,0:T(8,128)(2,1)S(1)} %copy-done.8), channel_id=1, source_target_pairs={{0,1},{1,0},{2,3},{3,2},{4,5},{5,4},{6,7},{7,6},{8,9},{9,8},{10,11... | collective-permute-start | bytes 1179656 | tf_op jit(solution)/shard_map/ppermute | solution.py:28
  58.3 16.0 %collective-permute-start.12 = (bf16[64,3072]{1,0:T(8,128)(2,1)}, bf16[64,3072]{1,0:T(8,128)(2,1)S(1)}, u32[]{:S(2)}, u32[]{:S(2)}) collective-permute-start(bf16[64,3072]{1,0:T(8,128)(2,1)} %hold.5.refs_8_.refs_7_), channel_id=1, source_target_pairs={{0,1},{1,0},{2,3},{3,2},{4,5},{5,4},{6,7},{7,6},{8,9},{9,8},{10,11... | collective-permute-start | bytes 1179656 | tf_op jit(solution)/shard_map/ppermute | solution.py:28
  99.1 3.8 %collective-permute-start.13 = (bf16[256,3200]{1,0:T(8,128)(2,1)}, bf16[256,3200]{1,0:T(8,128)(2,1)S(1)}, u32[]{:S(2)}, u32[]{:S(2)}) collective-permute-start(bf16[256,3200]{1,0:T(8,128)(2,1)} %get-tuple-element.67), channel_id=1, source_target_pairs={{0,1},{1,0},{2,3},{3,2},{4,5},{5,4},{6,7},{7,6},{8,9},{9,8},{10,11... | collective-permute-start | bytes 4915208 | tf_op jit(solution)/shard_map/ppermute | solution.py:28
  105.7 26.4 %collective-permute-start.14 = (bf16[64,3200]{1,0:T(8,128)(2,1)S(1)}, bf16[64,3200]{1,0:T(8,128)(2,1)S(1)}, u32[]{:S(2)}, u32[]{:S(2)}) collective-permute-start(bf16[64,3200]{1,0:T(8,128)(2,1)S(1)} %get-tuple-element.69), channel_id=1, source_target_pairs={{0,4},{1,5},{2,6},{3,7},{4,0},{5,1},{6,2},{7,3},{8,12},{9,13},{10,... | collective-permute-start | bytes 1228808 | tf_op jit(solution)/shard_map/ppermute | solution.py:28
  107.5 24.7 %collective-permute-start.15 = (bf16[64,3200]{1,0:T(8,128)(2,1)S(1)}, bf16[64,3200]{1,0:T(8,128)(2,1)S(1)}, u32[]{:S(2)}, u32[]{:S(2)}) collective-permute-start(bf16[64,3200]{1,0:T(8,128)(2,1)S(1)} %get-tuple-element.70), channel_id=1, source_target_pairs={{0,2},{1,3},{2,0},{3,1},{4,6},{5,7},{6,4},{7,5},{8,10},{9,11},{10,... | collective-permute-start | bytes 1228808 | tf_op jit(solution)/shard_map/ppermute | solution.py:28
  109.0 23.1 %collective-permute-start.16 = (bf16[64,3200]{1,0:T(8,128)(2,1)S(1)}, bf16[64,3200]{1,0:T(8,128)(2,1)S(1)}, u32[]{:S(2)}, u32[]{:S(2)}) collective-permute-start(bf16[64,3200]{1,0:T(8,128)(2,1)S(1)} %get-tuple-element.71), channel_id=1, source_target_pairs={{0,6},{1,7},{2,4},{3,5},{4,2},{5,3},{6,0},{7,1},{8,14},{9,15},{10,... | collective-permute-start | bytes 1228808 | tf_op jit(solution)/shard_map/ppermute | solution.py:28
  132.9 11.2 %collective-permute-start.17 = (bf16[16,3200]{1,0:T(8,128)(2,1)S(1)}, bf16[16,3200]{1,0:T(8,128)(2,1)S(1)}, u32[]{:S(2)}, u32[]{:S(2)}) collective-permute-start(bf16[16,3200]{1,0:T(8,128)(2,1)S(1)} %get-tuple-element.82), channel_id=1, source_target_pairs={{0,8},{1,9},{2,10},{3,11},{4,12},{5,13},{6,14},{7,15},{8,0},{9,1},... | collective-permute-start | bytes 307208 | tf_op jit(solution)/shard_map/ppermute | solution.py:28
  134.7 10.3 %collective-permute-start.18 = (bf16[16,3200]{1,0:T(8,128)(2,1)S(1)}, bf16[16,3200]{1,0:T(8,128)(2,1)S(1)}, u32[]{:S(2)}, u32[]{:S(2)}) collective-permute-start(bf16[16,3200]{1,0:T(8,128)(2,1)S(1)} %get-tuple-element.83), channel_id=1, source_target_pairs={{0,16},{1,17},{2,18},{3,19},{4,20},{5,21},{6,22},{7,23},{8,24},{9,... | collective-permute-start | bytes 307208 | tf_op jit(solution)/shard_map/ppermute | solution.py:28
  137.3 7.7 %collective-permute-start.19 = (bf16[16,3200]{1,0:T(8,128)(2,1)S(1)}, bf16[16,3200]{1,0:T(8,128)(2,1)S(1)}, u32[]{:S(2)}, u32[]{:S(2)}) collective-permute-start(bf16[16,3200]{1,0:T(8,128)(2,1)S(1)} %get-tuple-element.84), channel_id=1, source_target_pairs={{0,24},{1,25},{2,26},{3,27},{4,28},{5,29},{6,30},{7,31},{8,16},{9,... | collective-permute-start | bytes 307208 | tf_op jit(solution)/shard_map/ppermute | solution.py:28
  145.6 11.1 %collective-permute-start.22 = (bf16[16,3200]{1,0:T(8,128)(2,1)S(1)}, bf16[16,3200]{1,0:T(8,128)(2,1)S(1)}, u32[]{:S(2)}, u32[]{:S(2)}) collective-permute-start(bf16[16,3200]{1,0:T(8,128)(2,1)S(1)} %third_sum.1.refs_1_.refs_0_), channel_id=1, source_target_pairs={{0,24},{1,25},{2,26},{3,27},{4,28},{5,29},{6,30},{7,31},{8,16},{9,... | collective-permute-start | bytes 307208 | tf_op jit(solution)/shard_map/ppermute | solution.py:28
  148.6 8.2 %collective-permute-start.21 = (bf16[16,3200]{1,0:T(8,128)(2,1)S(1)}, bf16[16,3200]{1,0:T(8,128)(2,1)S(1)}, u32[]{:S(2)}, u32[]{:S(2)}) collective-permute-start(bf16[16,3200]{1,0:T(8,128)(2,1)S(1)} %third_sum.1.refs_1_.refs_0_), channel_id=1, source_target_pairs={{0,16},{1,17},{2,18},{3,19},{4,20},{5,21},{6,22},{7,23},{8,24},{9,... | collective-permute-start | bytes 307208 | tf_op jit(solution)/shard_map/ppermute | solution.py:28
  148.8 8.0 %collective-permute-start.20 = (bf16[16,3200]{1,0:T(8,128)(2,1)S(1)}, bf16[16,3200]{1,0:T(8,128)(2,1)S(1)}, u32[]{:S(2)}, u32[]{:S(2)}) collective-permute-start(bf16[16,3200]{1,0:T(8,128)(2,1)S(1)} %third_sum.1.refs_1_.refs_0_), channel_id=1, source_target_pairs={{0,8},{1,9},{2,10},{3,11},{4,12},{5,13},{6,14},{7,15},{8,0},{9,1},... | collective-permute-start | bytes 307208 | tf_op jit(solution)/shard_map/ppermute | solution.py:28
  157.4 10.4 %collective-permute-start.23 = (bf16[64,3200]{1,0:T(8,128)(2,1)S(1)}, bf16[64,3200]{1,0:T(8,128)(2,1)S(1)}, u32[]{:S(2)}, u32[]{:S(2)}) collective-permute-start(bf16[64,3200]{1,0:T(8,128)(2,1)S(1)} %join_z.1.refs_1_.refs_0_), channel_id=1, source_target_pairs={{0,4},{1,5},{2,6},{3,7},{4,0},{5,1},{6,2},{7,3},{8,12},{9,13},{10,... | collective-permute-start | bytes 1228808 | tf_op jit(solution)/shard_map/ppermute | solution.py:28
  (19 other events, 153.6 us)

commit v9 on v8

--- a/solution.py
+++ b/solution.py
@@ -203,7 +203,7 @@
                 )
 
 
-def split_experts(view, sort, start, rows, block, group, some, after):
+def split_experts(view, sort, start, rows, block, group, some, after, grant=56):
     _, tiles, experts, _ = view.shape
     columns = tiles * LANES
     first = start // block
@@ -221,7 +221,7 @@
             pl.BlockSpec(FLAG.shape, lambda i: (0, 0)),
         ],
         scratch_shapes=[pltpu.VMEM((block // 2, odd_tiles(tiles * experts), LANES), WIDE)],
-        compiler_params=pltpu.CompilerParams(vmem_limit_bytes=56 * MIB),
+        compiler_params=pltpu.CompilerParams(vmem_limit_bytes=grant * MIB),
         cost_estimate=pl.CostEstimate(
             flops=0, bytes_accessed=4 * experts * rows * columns, transcendentals=0
         ),
@@ -374,7 +374,7 @@
             pltpu.VMEM((experts * slots, 512), WIDE),
             pltpu.SemaphoreType.DMA((len(x_pieces),)),
         ],
-        compiler_params=pltpu.CompilerParams(vmem_limit_bytes=56 * MIB),
+        compiler_params=pltpu.CompilerParams(vmem_limit_bytes=42 * MIB),
         cost_estimate=pl.CostEstimate(
             flops=2 * slots * experts * model_width * (hidden + tokens),
             bytes_accessed=2 * experts * model_width * hidden,
@@ -481,7 +481,7 @@
             pltpu.VMEM((experts * slots, width), WIDE),
             pltpu.SemaphoreType.DMA((len(g_pieces),)),
         ],
-        compiler_params=pltpu.CompilerParams(vmem_limit_bytes=48 * MIB),
+        compiler_params=pltpu.CompilerParams(vmem_limit_bytes=46 * MIB),
         cost_estimate=pl.CostEstimate(
             flops=2 * slots * experts * model_width * (2 * hidden + 2 * tokens),
             bytes_accessed=4 * experts * model_width * hidden,
@@ -578,7 +578,7 @@
     g_far = swap(g_near, X)
     g_near_core = swap(g_near, CORE)
     x_far_core = swap(x_far, CORE)
-    v_high, flag = split_experts(v_view, v_sort, hidden // 2, hidden // 2, 64, 4, 16, [x_far])
+    v_high, flag = split_experts(v_view, v_sort, hidden // 2, hidden // 2, 64, 4, 16, [x_far], 46)
     x_pieces = [tokens, x_core, x_near, x_far, x_near_core, x_far_core]
     (g_far,) = hold([g_far], [flag])
     g_far_core = swap(g_far, CORE)

time: 171 us -> 176 us (1.029)
  local copies, waits for them, and re-layouts: 10.6 us -> 16 us
    unnamed x39 -> x53, local copies, waits for them, and re-layouts: 8.52 us -> 13.8 us
    pallas_call x1, Pallas kernels: 15 us -> 11.8 us  [forward_tokens(): pl.pallas_call(forward_tokens_body, out_shape=[jax.ShapeDtypeStruct((expe...]
  transfers between devices with their start and end apart: 24 -> 24, of which waited for: 3 -> 3; matrix products, arithmetic and copies ran while one was open for 2% -> 1% of each run, Pallas kernels for 58% -> 55%
where the time goes in v9:
time: 176 us; the launch traced here: 175 us
  Pallas kernels  127 us (72%)
  starting transfers between devices  22.9 us (13%)
  local copies, waits for them, and re-layouts  16 us (9%)
  waiting for transfers between devices  6.75 us (4%)
    pallas_call x3, Pallas kernels, split_experts(): pl.pallas_call(functools.partial(split_body, group, some), out_shape=[jax...  42.1 us
    pallas_call x7, Pallas kernels, outer(): pl.pallas_call(functools.partial(outer_body, group), out_shape=[jax.Shape...  40.8 us
    pallas_call x1, Pallas kernels, forward_cotangents(): pl.pallas_call(forward_cotangents_body, out_shape=[jax.ShapeDtypeStruct((...  25.6 us
    ppermute x24, starting transfers between devices, swap(): return lax.ppermute(value, AXES, [(i, i ^ mask) for i in range(size)])  22.9 us
    unnamed x53, local copies, waits for them, and re-layouts  13.8 us
    pallas_call x1, Pallas kernels, forward_tokens(): pl.pallas_call(forward_tokens_body, out_shape=[jax.ShapeDtypeStruct((expe...  11.8 us
    ppermute x24, waiting for transfers between devices, swap(): return lax.ppermute(value, AXES, [(i, i ^ mask) for i in range(size)])  6.75 us
    pallas_call x5, Pallas kernels, small_call(): pl.pallas_call(run, out_shape=outs, grid=(steps,), in_specs=[pl.BlockSpec...  5.11 us
  transfers between devices with their start and end apart: 24, of which 3 were waited for; matrix products, arithmetic and copies ran while one was open for 1% of the time, Pallas kernels for 55%

profile of v9, /device:TPU:0, one launch (start us, length us, event | category | flops | bytes accessed | tf_op | source)
XLA Modules:
  0.0 175.0 jit_solution(8542329364446839724)
XLA Ops:
  1.8 3.0 %collective-permute-start = (bf16[64,3072]{1,0:T(8,128)(2,1)S(1)}, bf16[64,3072]{1,0:T(8,128)(2,1)S(1)}, u32[]{:S(2)}, u32[]{:S(2)}) collective-permute-start(bf16[64,3072]{1,0:T(8,128)(2,1)S(1)} %constant_dynamic-slice_fusion.1), channel_id=1, source_target_pairs={{0,2},{1,3},{2,0},{3,1},{4,6},{5,7},{6,4},{7,5},{8,10},{9,11},{10,... | collective-permute-start | bytes 1179656 | tf_op jit(solution)/shard_map/ppermute | solution.py:28
  9.6 20.6 %split_experts.3 = (bf16[4,3072,768]{2,1,0:T(8,128)(2,1)}, f32[8,128]{1,0:T(8,128)}) custom-call(bf16[192,192]{1,0:T(8,128)(2,1)} %constant.46.clone.sort_ref, bf16[3072,6,4,128]{3,2,1,0:T(4,128)(2,1)} %bitcast.25), custom_call_target="tpu_custom_call" | custom-call | bytes 37748736 | tf_op jit(solution)/shard_map/split_experts/pallas_call | solution.py:210
  31.0 1.7 collective-permute-start.5
  34.2 10.7 %split_experts.4 = (bf16[4,384,3072]{2,1,0:T(8,128)(2,1)}, f32[8,128]{1,0:T(8,128)}) custom-call(bf16[256,256]{1,0:T(8,128)(2,1)} %constant.47.clone.sort_ref, bf16[768,24,4,128]{3,2,1,0:T(4,128)(2,1)} %bitcast.22, bf16[64,3072]{1,0:T(8,128)(2,1)} %get-tuple-element.57.refs_0_.refs_4_, s32[4,1,512]{2,1,0:T(1,128)} %get-tuple-element.54.refs_1_.code_ref), custom_call_target="tpu_custom_call" | custom-call | bytes 18874368 | tf_op jit(solution)/shard_map/split_experts/pallas_call | solution.py:210
  47.8 10.8 %split_experts.5 = (bf16[4,384,3072]{2,1,0:T(8,128)(2,1)}, f32[8,128]{1,0:T(8,128)S(1)}) custom-call(bf16[256,256]{1,0:T(8,128)(2,1)S(1)} %copy-done.18, bf16[768,24,4,128]{3,2,1,0:T(4,128)(2,1)} %bitcast.23, bf16[64,3072]{1,0:T(8,128)(2,1)S(1)} %copy-done.9), custom_call_target="tpu_custom_call" | custom-call | bytes 18874368 | tf_op jit(solution)/shard_map/split_experts/pallas_call | solution.py:210
  62.4 11.8 %forward_tokens.1 = (bf16[4,160,3072]{2,1,0:T(8,128)(2,1)S(1)}, bf16[4,160,768]{2,1,0:T(8,128)(2,1)S(1)}, f32[4,160,768]{2,1,0:T(8,128)S(1)}, f32[4,160,768]{2,1,0:T(8,128)S(1)}) custom-call(s32[4,1,512]{2,1,0:T(1,128)S(1)} %copy-done.19, f32[4,1,512]{2,1,0:T(1,128)S(1)} %copy-done.20, bf16[4,3072,768]{2,1,0:T(8,128)(2,1)} %get-tuple-element.56.refs_0_.refs_1_, ...), custom_call_target="tpu_custom_call" | custom-call | flops 5033164800 | bytes 18874368 | tf_op jit(solution)/shard_map/forward_tokens/pallas_call | solution.py:365
  74.2 2.0 %copy-done = bf16[4,160,3072]{2,1,0:T(8,128)(2,1)} copy-done((bf16[4,160,3072]{2,1,0:T(8,128)(2,1)}, bf16[4,160,3072]{2,1,0:T(8,128)(2,1)S(1)}, u32[]{:S(2)}) %copy-start) | copy-done | bytes 3932184
  77.6 25.6 %forward_cotangents.1 = (bf16[4,160,3072]{2,1,0:T(8,128)(2,1)}, bf16[4,160,768]{2,1,0:T(8,128)(2,1)S(1)}, f32[256,3200]{1,0:T(8,128)}, bf16[256,3200]{1,0:T(8,128)(2,1)}) custom-call(s32[4,1,512]{2,1,0:T(1,128)S(1)} %copy-done.19, f32[4,160,768]{2,1,0:T(8,128)S(1)} %get-tuple-element.62.active_ref, f32[4,160,768]{2,1,0:T(8,128)} %copy-done.12, ...), custom_call_target="tpu_custom_call" | custom-call | flops 10066329600 | bytes 37748736 | tf_op jit(solution)/shard_map/forward_cotangents/pallas_call | solution.py:454
  103.6 3.5 %collective-permute-done.13.refs_1_ = bf16[256,3200]{1,0:T(8,128)(2,1)} collective-permute-done((bf16[256,3200]{1,0:T(8,128)(2,1)}, bf16[256,3200]{1,0:T(8,128)(2,1)}, u32[]{:S(2)}, u32[]{:S(2)}) %collective-permute-start.13) | collective-permute-done | bytes 1638432 | tf_op jit(solution)/shard_map/ppermute | solution.py:28
  107.1 1.9 %copy-done.11 = f32[256,3200]{1,0:T(8,128)S(1)} copy-done((f32[256,3200]{1,0:T(8,128)S(1)}, f32[256,3200]{1,0:T(8,128)}, u32[]{:S(2)}) %copy-start.11) | copy-done | bytes 3276824
  109.1 1.7 first_sum.1
  110.8 1.8 %collective-permute-start.14 = (bf16[64,3200]{1,0:T(8,128)(2,1)S(1)}, bf16[64,3200]{1,0:T(8,128)(2,1)S(1)}, u32[]{:S(2)}, u32[]{:S(2)}) collective-permute-start(bf16[64,3200]{1,0:T(8,128)(2,1)S(1)} %get-tuple-element.69), channel_id=1, source_target_pairs={{0,4},{1,5},{2,6},{3,7},{4,0},{5,1},{6,2},{7,3},{8,12},{9,13},{10,... | collective-permute-start | bytes 1228808 | tf_op jit(solution)/shard_map/ppermute | solution.py:28
  114.3 2.1 %copy-done.1 = bf16[4,160,3072]{2,1,0:T(8,128)(2,1)S(1)} copy-done((bf16[4,160,3072]{2,1,0:T(8,128)(2,1)S(1)}, bf16[4,160,3072]{2,1,0:T(8,128)(2,1)}, u32[]{:S(2)}) %copy-start.1) | copy-done | bytes 3932184
  116.5 5.2 %weight_gradient.7 = (bf16[3072,6,4,128]{3,2,1,0:T(4,128)(2,1)}, f32[8,128]{1,0:T(8,128)S(1)}) custom-call(bf16[4,160,3072]{2,1,0:T(8,128)(2,1)S(1)} %copy-done.1, bf16[4,160,768]{2,1,0:T(8,128)(2,1)S(1)} %get-tuple-element.73.b_ref, f32[64,3200]{1,0:T(8,128)S(1)} %get-tuple-element.68.refs_0_), custom_call_target="tpu_custom_call" | custom-call | flops 754974720 | bytes 9437184 | tf_op jit(solution)/shard_map/weight_gradient/pallas_call | solution.py:518
  121.6 5.2 %weight_gradient.8 = (bf16[3072,6,4,128]{3,2,1,0:T(4,128)(2,1)}, f32[8,128]{1,0:T(8,128)S(1)}) custom-call(bf16[4,160,3072]{2,1,0:T(8,128)(2,1)S(1)} %copy-done.1, bf16[4,160,768]{2,1,0:T(8,128)(2,1)S(1)} %get-tuple-element.73.b_ref, bf16[3072,6,4,128]{3,2,1,0:T(4,128)(2,1)} %get-tuple-element.74.refs_0_, ...), custom_call_target="tpu_custom_call", output_to_operand_aliasing={{0}: (2, {})} | custom-call | flops 754974720 | bytes 9437184 | tf_op jit(solution)/shard_map/weight_gradient/pallas_call | solution.py:518
  126.8 5.2 %weight_gradient.9 = (bf16[3072,6,4,128]{3,2,1,0:T(4,128)(2,1)}, f32[8,128]{1,0:T(8,128)S(1)}) custom-call(bf16[4,160,3072]{2,1,0:T(8,128)(2,1)S(1)} %copy-done.1, bf16[4,160,768]{2,1,0:T(8,128)(2,1)S(1)} %get-tuple-element.73.b_ref, bf16[3072,6,4,128]{3,2,1,0:T(4,128)(2,1)} %get-tuple-element.76.refs_0_, ...), custom_call_target="tpu_custom_call", output_to_operand_aliasing={{0}: (2, {})} | custom-call | flops 754974720 | bytes 9437184 | tf_op jit(solution)/shard_map/weight_gradient/pallas_call | solution.py:518
  132.0 5.2 %weight_gradient.10 = (bf16[3072,6,4,128]{3,2,1,0:T(4,128)(2,1)}, f32[8,128]{1,0:T(8,128)S(1)}) custom-call(bf16[4,160,3072]{2,1,0:T(8,128)(2,1)S(1)} %copy-done.1, bf16[4,160,768]{2,1,0:T(8,128)(2,1)S(1)} %get-tuple-element.73.b_ref, bf16[3072,6,4,128]{3,2,1,0:T(4,128)(2,1)} %get-tuple-element.78.refs_0_, ...), custom_call_target="tpu_custom_call", output_to_operand_aliasing={{0}: (2, {})} | custom-call | flops 754974720 | bytes 9437184 | tf_op jit(solution)/shard_map/weight_gradient/pallas_call | solution.py:518
  138.0 1.9 %collective-permute-start.17 = (bf16[16,3200]{1,0:T(8,128)(2,1)S(1)}, bf16[16,3200]{1,0:T(8,128)(2,1)S(1)}, u32[]{:S(2)}, u32[]{:S(2)}) collective-permute-start(bf16[16,3200]{1,0:T(8,128)(2,1)S(1)} %get-tuple-element.82), channel_id=1, source_target_pairs={{0,8},{1,9},{2,10},{3,11},{4,12},{5,13},{6,14},{7,15},{8,0},{9,1},... | collective-permute-start | bytes 307208 | tf_op jit(solution)/shard_map/ppermute | solution.py:28
  139.8 2.6 %collective-permute-start.18 = (bf16[16,3200]{1,0:T(8,128)(2,1)S(1)}, bf16[16,3200]{1,0:T(8,128)(2,1)S(1)}, u32[]{:S(2)}, u32[]{:S(2)}) collective-permute-start(bf16[16,3200]{1,0:T(8,128)(2,1)S(1)} %get-tuple-element.83), channel_id=1, source_target_pairs={{0,16},{1,17},{2,18},{3,19},{4,20},{5,21},{6,22},{7,23},{8,24},{9,... | collective-permute-start | bytes 307208 | tf_op jit(solution)/shard_map/ppermute | solution.py:28
  142.4 6.7 %weight_gradient.11 = (bf16[768,24,4,128]{3,2,1,0:T(4,128)(2,1)}, f32[8,128]{1,0:T(8,128)S(1)}) custom-call(bf16[4,160,768]{2,1,0:T(8,128)(2,1)S(1)} %get-tuple-element.85.a_ref, bf16[4,160,3072]{2,1,0:T(8,128)(2,1)S(1)} %copy-done.2, f32[16,3200]{1,0:T(8,128)S(1)} %get-tuple-element.81.refs_0_), custom_call_target="tpu_custom_call" | custom-call | flops 1006632960 | bytes 12582912 | tf_op jit(solution)/shard_map/weight_gradient/pallas_call | solution.py:518
  150.7 2.9 %collective-permute-start.22 = (bf16[16,3200]{1,0:T(8,128)(2,1)S(1)}, bf16[16,3200]{1,0:T(8,128)(2,1)S(1)}, u32[]{:S(2)}, u32[]{:S(2)}) collective-permute-start(bf16[16,3200]{1,0:T(8,128)(2,1)S(1)} %third_sum.1.refs_1_.refs_0_), channel_id=1, source_target_pairs={{0,24},{1,25},{2,26},{3,27},{4,28},{5,29},{6,30},{7,31},{8,16},{9,... | collective-permute-start | bytes 307208 | tf_op jit(solution)/shard_map/ppermute | solution.py:28
  155.2 6.7 %weight_gradient.12 = (bf16[768,24,4,128]{3,2,1,0:T(4,128)(2,1)}, f32[8,128]{1,0:T(8,128)S(1)}) custom-call(bf16[4,160,768]{2,1,0:T(8,128)(2,1)S(1)} %get-tuple-element.85.a_ref, bf16[4,160,3072]{2,1,0:T(8,128)(2,1)S(1)} %copy-done.2, bf16[768,24,4,128]{3,2,1,0:T(4,128)(2,1)} %get-tuple-element.88.refs_0_, ...), custom_call_target="tpu_custom_call", output_to_operand_aliasing={{0}: (2, {})} | custom-call | flops 1006632960 | bytes 12582912 | tf_op jit(solution)/shard_map/weight_gradient/pallas_call | solution.py:518
  164.0 6.7 %weight_gradient.13 = (bf16[768,24,4,128]{3,2,1,0:T(4,128)(2,1)}, f32[8,128]{1,0:T(8,128)S(1)}) custom-call(bf16[4,160,768]{2,1,0:T(8,128)(2,1)S(1)} %get-tuple-element.85.a_ref, bf16[4,160,3072]{2,1,0:T(8,128)(2,1)S(1)} %copy-done.2, bf16[768,24,4,128]{3,2,1,0:T(4,128)(2,1)} %get-tuple-element.90.refs_0_, ...), custom_call_target="tpu_custom_call", output_to_operand_aliasing={{0}: (2, {})} | custom-call | flops 1006632960 | bytes 12582912 | tf_op jit(solution)/shard_map/weight_gradient/pallas_call | solution.py:518
  170.7 2.2 %collective-permute-done.23.refs_1_ = bf16[64,3200]{1,0:T(8,128)(2,1)S(1)} collective-permute-done((bf16[64,3200]{1,0:T(8,128)(2,1)S(1)}, bf16[64,3200]{1,0:T(8,128)(2,1)S(1)}, u32[]{:S(2)}, u32[]{:S(2)}) %collective-permute-start.23) | collective-permute-done | bytes 409632 | tf_op jit(solution)/shard_map/ppermute | solution.py:28
  (106 shorter events, 26.4 us)
Async XLA Ops:
  1.8 28.4 %collective-permute-start = (bf16[64,3072]{1,0:T(8,128)(2,1)S(1)}, bf16[64,3072]{1,0:T(8,128)(2,1)S(1)}, u32[]{:S(2)}, u32[]{:S(2)}) collective-permute-start(bf16[64,3072]{1,0:T(8,128)(2,1)S(1)} %constant_dynamic-slice_fusion.1), channel_id=1, source_target_pairs={{0,2},{1,3},{2,0},{3,1},{4,6},{5,7},{6,4},{7,5},{8,10},{9,11},{10,... | collective-permute-start | bytes 1179656 | tf_op jit(solution)/shard_map/ppermute | solution.py:28
  6.3 23.8 %collective-permute-start.3 = (f32[8,128]{1,0:T(8,128)S(1)}, f32[8,128]{1,0:T(8,128)S(1)}, u32[]{:S(2)}, u32[]{:S(2)}) collective-permute-start(f32[8,128]{1,0:T(8,128)S(1)} %maximum_select_fusion), channel_id=1, source_target_pairs={{0,3},{1,2},{2,1},{3,0},{4,7},{5,6},{6,5},{7,4},{8,11},{9,10},{10,... | collective-permute-start | bytes 12296 | tf_op jit(solution)/shard_map/ppermute | solution.py:28
  6.3 23.8 %collective-permute-start.2 = (f32[8,128]{1,0:T(8,128)S(1)}, f32[8,128]{1,0:T(8,128)S(1)}, u32[]{:S(2)}, u32[]{:S(2)}) collective-permute-start(f32[8,128]{1,0:T(8,128)S(1)} %maximum_select_fusion), channel_id=1, source_target_pairs={{0,2},{1,3},{2,0},{3,1},{4,6},{5,7},{6,4},{7,5},{8,10},{9,11},{10,... | collective-permute-start | bytes 12296 | tf_op jit(solution)/shard_map/ppermute | solution.py:28
  7.5 22.7 %collective-permute-start.1 = (f32[8,128]{1,0:T(8,128)S(1)}, f32[8,128]{1,0:T(8,128)S(1)}, u32[]{:S(2)}, u32[]{:S(2)}) collective-permute-start(f32[8,128]{1,0:T(8,128)S(1)} %maximum_bitcast_fusion.refs_0_), channel_id=1, source_target_pairs={{0,1},{1,0},{2,3},{3,2},{4,5},{5,4},{6,7},{7,6},{8,9},{9,8},{10,11... | collective-permute-start | bytes 12296 | tf_op jit(solution)/shard_map/ppermute | solution.py:28
  9.2 35.7 %collective-permute-start.6 = (bf16[64,3072]{1,0:T(8,128)(2,1)S(1)}, bf16[64,3072]{1,0:T(8,128)(2,1)S(1)}, u32[]{:S(2)}, u32[]{:S(2)}) collective-permute-start(bf16[64,3072]{1,0:T(8,128)(2,1)S(1)} %constant_dynamic-slice_fusion), channel_id=1, source_target_pairs={{0,2},{1,3},{2,0},{3,1},{4,6},{5,7},{6,4},{7,5},{8,10},{9,11},{10,... | collective-permute-start | bytes 1179656 | tf_op jit(solution)/shard_map/ppermute | solution.py:28
  31.0 13.9 %collective-permute-start.5 = (bf16[64,3072]{1,0:T(8,128)(2,1)}, bf16[64,3072]{1,0:T(8,128)(2,1)S(1)}, u32[]{:S(2)}, u32[]{:S(2)}) collective-permute-start(bf16[64,3072]{1,0:T(8,128)(2,1)} %get-tuple-element.57.refs_0_.refs_4_), channel_id=1, source_target_pairs={{0,4},{1,5},{2,6},{3,7},{4,0},{5,1},{6,2},{7,3},{8,12},{9,13},{10,... | collective-permute-start | bytes 1179656 | tf_op jit(solution)/shard_map/ppermute | solution.py:28
  32.7 27.3 %collective-permute-start.4 = (bf16[128,3072]{1,0:T(8,128)(2,1)S(1)}, bf16[128,3072]{1,0:T(8,128)(2,1)}, u32[]{:S(2)}, u32[]{:S(2)}) collective-permute-start(bf16[128,3072]{1,0:T(8,128)(2,1)S(1)} %copy-done.14), channel_id=1, source_target_pairs={{0,1},{1,0},{2,3},{3,2},{4,5},{5,4},{6,7},{7,6},{8,9},{9,8},{10,11... | collective-permute-start | bytes 2359304 | tf_op jit(solution)/shard_map/ppermute | solution.py:28
  45.8 13.5 %collective-permute-start.9 = (bf16[64,3072]{1,0:T(8,128)(2,1)}, bf16[64,3072]{1,0:T(8,128)(2,1)S(1)}, u32[]{:S(2)}, u32[]{:S(2)}) collective-permute-start(bf16[64,3072]{1,0:T(8,128)(2,1)} %get-tuple-element.60.refs_6_), channel_id=1, source_target_pairs={{0,4},{1,5},{2,6},{3,7},{4,0},{5,1},{6,2},{7,3},{8,12},{9,13},{10,... | collective-permute-start | bytes 1179656 | tf_op jit(solution)/shard_map/ppermute | solution.py:28
  46.1 14.2 %collective-permute-start.7 = (bf16[64,3072]{1,0:T(8,128)(2,1)S(1)}, bf16[64,3072]{1,0:T(8,128)(2,1)}, u32[]{:S(2)}, u32[]{:S(2)}) collective-permute-start(bf16[64,3072]{1,0:T(8,128)(2,1)S(1)} %copy-done.7), channel_id=1, source_target_pairs={{0,1},{1,0},{2,3},{3,2},{4,5},{5,4},{6,7},{7,6},{8,9},{9,8},{10,11... | collective-permute-start | bytes 1179656 | tf_op jit(solution)/shard_map/ppermute | solution.py:28
  46.3 14.0 %collective-permute-start.8 = (bf16[64,3072]{1,0:T(8,128)(2,1)}, bf16[64,3072]{1,0:T(8,128)(2,1)}, u32[]{:S(2)}, u32[]{:S(2)}) collective-permute-start(bf16[64,3072]{1,0:T(8,128)(2,1)} %get-tuple-element.59.refs_0_.refs_5_), channel_id=1, source_target_pairs={{0,1},{1,0},{2,3},{3,2},{4,5},{5,4},{6,7},{7,6},{8,9},{9,8},{10,11... | collective-permute-start | bytes 1179656 | tf_op jit(solution)/shard_map/ppermute | solution.py:28
  46.6 31.0 %collective-permute-start.10 = (bf16[128,3072]{1,0:T(8,128)(2,1)S(1)}, bf16[128,3072]{1,0:T(8,128)(2,1)}, u32[]{:S(2)}, u32[]{:S(2)}) collective-permute-start(bf16[128,3072]{1,0:T(8,128)(2,1)S(1)} %copy-done.13), channel_id=1, source_target_pairs={{0,1},{1,0},{2,3},{3,2},{4,5},{5,4},{6,7},{7,6},{8,9},{9,8},{10,11... | collective-permute-start | bytes 2359304 | tf_op jit(solution)/shard_map/ppermute | solution.py:28
  59.3 18.3 %collective-permute-start.11 = (bf16[64,3072]{1,0:T(8,128)(2,1)S(1)}, bf16[64,3072]{1,0:T(8,128)(2,1)}, u32[]{:S(2)}, u32[]{:S(2)}) collective-permute-start(bf16[64,3072]{1,0:T(8,128)(2,1)S(1)} %copy-done.17), channel_id=1, source_target_pairs={{0,1},{1,0},{2,3},{3,2},{4,5},{5,4},{6,7},{7,6},{8,9},{9,8},{10,11... | collective-permute-start | bytes 1179656 | tf_op jit(solution)/shard_map/ppermute | solution.py:28
  60.0 17.6 %collective-permute-start.12 = (bf16[64,3072]{1,0:T(8,128)(2,1)}, bf16[64,3072]{1,0:T(8,128)(2,1)S(1)}, u32[]{:S(2)}, u32[]{:S(2)}) collective-permute-start(bf16[64,3072]{1,0:T(8,128)(2,1)} %hold.5.refs_8_.refs_7_), channel_id=1, source_target_pairs={{0,1},{1,0},{2,3},{3,2},{4,5},{5,4},{6,7},{7,6},{8,9},{9,8},{10,11... | collective-permute-start | bytes 1179656 | tf_op jit(solution)/shard_map/ppermute | solution.py:28
  103.2 3.9 %collective-permute-start.13 = (bf16[256,3200]{1,0:T(8,128)(2,1)}, bf16[256,3200]{1,0:T(8,128)(2,1)}, u32[]{:S(2)}, u32[]{:S(2)}) collective-permute-start(bf16[256,3200]{1,0:T(8,128)(2,1)} %get-tuple-element.67), channel_id=1, source_target_pairs={{0,1},{1,0},{2,3},{3,2},{4,5},{5,4},{6,7},{7,6},{8,9},{9,8},{10,11... | collective-permute-start | bytes 4915208 | tf_op jit(solution)/shard_map/ppermute | solution.py:28
  110.8 26.4 %collective-permute-start.14 = (bf16[64,3200]{1,0:T(8,128)(2,1)S(1)}, bf16[64,3200]{1,0:T(8,128)(2,1)S(1)}, u32[]{:S(2)}, u32[]{:S(2)}) collective-permute-start(bf16[64,3200]{1,0:T(8,128)(2,1)S(1)} %get-tuple-element.69), channel_id=1, source_target_pairs={{0,4},{1,5},{2,6},{3,7},{4,0},{5,1},{6,2},{7,3},{8,12},{9,13},{10,... | collective-permute-start | bytes 1228808 | tf_op jit(solution)/shard_map/ppermute | solution.py:28
  112.6 24.6 %collective-permute-start.15 = (bf16[64,3200]{1,0:T(8,128)(2,1)S(1)}, bf16[64,3200]{1,0:T(8,128)(2,1)S(1)}, u32[]{:S(2)}, u32[]{:S(2)}) collective-permute-start(bf16[64,3200]{1,0:T(8,128)(2,1)S(1)} %get-tuple-element.70), channel_id=1, source_target_pairs={{0,2},{1,3},{2,0},{3,1},{4,6},{5,7},{6,4},{7,5},{8,10},{9,11},{10,... | collective-permute-start | bytes 1228808 | tf_op jit(solution)/shard_map/ppermute | solution.py:28
  114.1 23.1 %collective-permute-start.16 = (bf16[64,3200]{1,0:T(8,128)(2,1)S(1)}, bf16[64,3200]{1,0:T(8,128)(2,1)S(1)}, u32[]{:S(2)}, u32[]{:S(2)}) collective-permute-start(bf16[64,3200]{1,0:T(8,128)(2,1)S(1)} %get-tuple-element.71), channel_id=1, source_target_pairs={{0,6},{1,7},{2,4},{3,5},{4,2},{5,3},{6,0},{7,1},{8,14},{9,15},{10,... | collective-permute-start | bytes 1228808 | tf_op jit(solution)/shard_map/ppermute | solution.py:28
  138.0 11.1 %collective-permute-start.17 = (bf16[16,3200]{1,0:T(8,128)(2,1)S(1)}, bf16[16,3200]{1,0:T(8,128)(2,1)S(1)}, u32[]{:S(2)}, u32[]{:S(2)}) collective-permute-start(bf16[16,3200]{1,0:T(8,128)(2,1)S(1)} %get-tuple-element.82), channel_id=1, source_target_pairs={{0,8},{1,9},{2,10},{3,11},{4,12},{5,13},{6,14},{7,15},{8,0},{9,1},... | collective-permute-start | bytes 307208 | tf_op jit(solution)/shard_map/ppermute | solution.py:28
  139.8 10.3 %collective-permute-start.18 = (bf16[16,3200]{1,0:T(8,128)(2,1)S(1)}, bf16[16,3200]{1,0:T(8,128)(2,1)S(1)}, u32[]{:S(2)}, u32[]{:S(2)}) collective-permute-start(bf16[16,3200]{1,0:T(8,128)(2,1)S(1)} %get-tuple-element.83), channel_id=1, source_target_pairs={{0,16},{1,17},{2,18},{3,19},{4,20},{5,21},{6,22},{7,23},{8,24},{9,... | collective-permute-start | bytes 307208 | tf_op jit(solution)/shard_map/ppermute | solution.py:28
  142.4 7.7 %collective-permute-start.19 = (bf16[16,3200]{1,0:T(8,128)(2,1)S(1)}, bf16[16,3200]{1,0:T(8,128)(2,1)S(1)}, u32[]{:S(2)}, u32[]{:S(2)}) collective-permute-start(bf16[16,3200]{1,0:T(8,128)(2,1)S(1)} %get-tuple-element.84), channel_id=1, source_target_pairs={{0,24},{1,25},{2,26},{3,27},{4,28},{5,29},{6,30},{7,31},{8,16},{9,... | collective-permute-start | bytes 307208 | tf_op jit(solution)/shard_map/ppermute | solution.py:28
  150.7 11.1 %collective-permute-start.22 = (bf16[16,3200]{1,0:T(8,128)(2,1)S(1)}, bf16[16,3200]{1,0:T(8,128)(2,1)S(1)}, u32[]{:S(2)}, u32[]{:S(2)}) collective-permute-start(bf16[16,3200]{1,0:T(8,128)(2,1)S(1)} %third_sum.1.refs_1_.refs_0_), channel_id=1, source_target_pairs={{0,24},{1,25},{2,26},{3,27},{4,28},{5,29},{6,30},{7,31},{8,16},{9,... | collective-permute-start | bytes 307208 | tf_op jit(solution)/shard_map/ppermute | solution.py:28
  153.6 8.2 %collective-permute-start.21 = (bf16[16,3200]{1,0:T(8,128)(2,1)S(1)}, bf16[16,3200]{1,0:T(8,128)(2,1)S(1)}, u32[]{:S(2)}, u32[]{:S(2)}) collective-permute-start(bf16[16,3200]{1,0:T(8,128)(2,1)S(1)} %third_sum.1.refs_1_.refs_0_), channel_id=1, source_target_pairs={{0,16},{1,17},{2,18},{3,19},{4,20},{5,21},{6,22},{7,23},{8,24},{9,... | collective-permute-start | bytes 307208 | tf_op jit(solution)/shard_map/ppermute | solution.py:28
  153.9 8.0 %collective-permute-start.20 = (bf16[16,3200]{1,0:T(8,128)(2,1)S(1)}, bf16[16,3200]{1,0:T(8,128)(2,1)S(1)}, u32[]{:S(2)}, u32[]{:S(2)}) collective-permute-start(bf16[16,3200]{1,0:T(8,128)(2,1)S(1)} %third_sum.1.refs_1_.refs_0_), channel_id=1, source_target_pairs={{0,8},{1,9},{2,10},{3,11},{4,12},{5,13},{6,14},{7,15},{8,0},{9,1},... | collective-permute-start | bytes 307208 | tf_op jit(solution)/shard_map/ppermute | solution.py:28
  162.5 10.4 %collective-permute-start.23 = (bf16[64,3200]{1,0:T(8,128)(2,1)S(1)}, bf16[64,3200]{1,0:T(8,128)(2,1)S(1)}, u32[]{:S(2)}, u32[]{:S(2)}) collective-permute-start(bf16[64,3200]{1,0:T(8,128)(2,1)S(1)} %join_z.1.refs_1_.refs_0_), channel_id=1, source_target_pairs={{0,4},{1,5},{2,6},{3,7},{4,0},{5,1},{6,2},{7,3},{8,12},{9,13},{10,... | collective-permute-start | bytes 1228808 | tf_op jit(solution)/shard_map/ppermute | solution.py:28
  (26 other events, 265.7 us)
